TPU v7x, 32 devices: a whole 2x2x4 slice. The times are simulated.
32 devices in a mesh: dp: 2 (over x), tile: 16 (over z, y, core).
Axes of the slice: x: 2, y: 2, z: 4, core: 2. Of those that a mesh axis runs over, the one named last changes fastest.
Arguments:
- grad_out: bfloat16 [2, 64, 640, 512], P('dp', 'tile'), may hold values from -6 to 6
- bev_act: bfloat16 [2, 64, 640, 512], P('dp', 'tile'), may hold values from -6 to 6
- conv_weight: bfloat16 [512, 3, 3, 512], replicated, may hold values from -0.09375 to 0.09375
- img_in: bfloat16 [2, 8192, 512], P('dp', 'tile'), may hold values from -6 to 6
- backbone_weight: bfloat16 [512, 512], replicated, may hold values from -0.25 to 0.25
- route: int32 [2, 640], P('dp'), may hold values from 0 to 63, as said below
- offsets: int32 [2, 40960], P('dp', 'tile'), may hold values from 0 to 62
- frac_x: int32 [2, 40960], P('dp', 'tile'), may hold values from 0 to 255
- frac_y: int32 [2, 40960], P('dp', 'tile'), may hold values from 0 to 255
Outputs:
- image_grad: bfloat16 [2, 8192, 512], P('dp', 'tile')
- conv_grad: bfloat16 [512, 3, 3, 512], replicated
- backbone_grad: bfloat16 [512, 512], replicated
Inputs may be any that keep to these rules, and one draw needn't show every extreme that they name: `route`: owner of image block id is id // 4. Among the 40 ground blocks k * 40 to k * 40 + 39 of one sample, at most 5 have sources with one owner; in every sample some owner has exactly 5 such blocks from every device.
All inputs are finite; a program needn't handle non-finite values.
Results may differ from a plain program's by a relative error of at most 0.0073.
Values may be sent and summed in bfloat16 or wider, within the bound.
No kernel may reach another device: no remote copies, remote signals or barrier semaphores. Data moves between devices by JAX's collectives and lax.ppermute only.
A program may use at most 192 MiB of HBM per device.

v0:
```python
import math

import jax
import jax.numpy as jnp
from jax import lax
from jax.sharding import PartitionSpec as P

BLK = 64
IMGW = 64


def extended(block, sides, width):
    for axis, dim in sides:
        count = lax.axis_size(axis)
        forward = [(i, i + 1) for i in range(count - 1)]
        backward = [(target, source) for source, target in forward]
        low = lax.ppermute(
            lax.slice_in_dim(block, block.shape[dim] - width, None, axis=dim), axis, forward
        )
        high = lax.ppermute(lax.slice_in_dim(block, 0, width, axis=dim), axis, backward)
        block = jnp.concatenate([low, block, high], axis=dim)
    return block


def make_band(offsets, frac_x, frac_y, blocks, width):
    columns = lax.broadcasted_iota(jnp.int32, (1, 1, width), 2)
    shaped = offsets.reshape(blocks, -1, 1)
    right_w = frac_x.reshape(blocks, -1, 1).astype(jnp.float32) / 256.0
    lower_w = frac_y.reshape(blocks, -1, 1).astype(jnp.float32) / 256.0
    across = jnp.where(columns == shaped, 1.0 - right_w, 0.0) + jnp.where(
        columns == shaped + 1, right_w, 0.0
    )
    return jnp.concatenate([(1.0 - lower_w) * across, lower_w * across], axis=2).astype(
        jnp.bfloat16
    )


def silu_slope(value):
    sigma = jax.nn.sigmoid(value)
    return sigma * (1.0 + value * (1.0 - sigma))


def warp_items(parts):
    return jnp.einsum(
        "skmp,skmc->skpc", parts[1], parts[0], preferred_element_type=jnp.float32
    ).astype(jnp.bfloat16)


def body(grad_out, bev_act, conv_weight, img_in, backbone_weight, route, offsets, frac_x, frac_y):
    tiles = lax.axis_size("tile")
    my_tile = lax.axis_index("tile")
    rows = grad_out.shape[1]
    cols = grad_out.shape[2]
    chans = grad_out.shape[3]
    stacked = jnp.stack([grad_out[0], bev_act[0]])
    framed = extended(stacked, (("tile", 1),), 1)
    framed = jnp.pad(framed, ((0, 0), (0, 0), (1, 1), (0, 0)))
    out_frame = framed[0]
    act_frame = framed[1]
    center = grad_out[0]
    bev_sum = jnp.zeros((rows, cols, chans), jnp.float32)
    conv_parts = []
    for row_tap in range(3):
        tap_terms = []
        for col_tap in range(3):
            shifted = out_frame[2 - row_tap : 2 - row_tap + rows, 2 - col_tap : 2 - col_tap + cols]
            bev_sum = bev_sum + jnp.einsum(
                "rvo,co->rvc",
                shifted,
                conv_weight[:, row_tap, col_tap, :],
                preferred_element_type=jnp.float32,
            )
            moved = act_frame[row_tap : row_tap + rows, col_tap : col_tap + cols]
            tap_terms.append(
                jnp.einsum("rvc,rvo->co", moved, center, preferred_element_type=jnp.float32)
            )
        conv_parts.append(jnp.stack(tap_terms, axis=1))
    conv_local = jnp.stack(conv_parts, axis=1)
    bev_grad = bev_sum.astype(jnp.bfloat16)
    block_count = rows * cols // BLK
    blocks = bev_grad.reshape(block_count, BLK, chans)
    band = make_band(offsets[0], frac_x[0], frac_y[0], block_count, IMGW)
    capacity = max(2, 2 * block_count // tiles)
    image = img_in[0]
    per_device = image.shape[0] // (2 * IMGW)
    owners = (route[0] // per_device).reshape(tiles, block_count)
    local_ids = (route[0] % per_device).reshape(tiles, block_count)
    same_owner = owners[:, :, None] == owners[:, None, :]
    earlier = lax.broadcasted_iota(
        jnp.int32, (1, block_count, block_count), 2
    ) < lax.broadcasted_iota(jnp.int32, (1, block_count, block_count), 1)
    ranks = jnp.sum((same_owner & earlier).astype(jnp.int32), axis=2)
    slots = owners * capacity + ranks
    my_slots = lax.dynamic_index_in_dim(slots, my_tile, 0, keepdims=False)
    slot_total = tiles * capacity
    sent_blocks = jnp.zeros((slot_total, BLK, chans), jnp.bfloat16).at[my_slots].set(blocks)
    sent_bands = jnp.zeros((slot_total, BLK, 2 * IMGW), jnp.bfloat16).at[my_slots].set(band)
    arrived = warp_items(
        (
            lax.all_to_all(
                sent_blocks.reshape(tiles, capacity, BLK, chans),
                "tile",
                split_axis=0,
                concat_axis=0,
                tiled=True,
            ),
            lax.all_to_all(
                sent_bands.reshape(tiles, capacity, BLK, 2 * IMGW),
                "tile",
                split_axis=0,
                concat_axis=0,
                tiled=True,
            ),
        )
    )
    mine = owners == my_tile
    block_iota = lax.broadcasted_iota(jnp.int32, (per_device, 1, 1, 1), 0)
    slot_iota = lax.broadcasted_iota(jnp.int32, (1, 1, 1, capacity), 3)
    picks = (
        mine[None, :, :, None]
        & (local_ids[None, :, :, None] == block_iota)
        & (ranks[None, :, :, None] == slot_iota)
    )
    gather_table = (
        jnp.sum(picks.astype(jnp.int32), axis=2)
        .astype(jnp.bfloat16)
        .reshape(per_device, slot_total)
    )
    feature_grad = jnp.dot(
        gather_table,
        arrived.reshape(slot_total, 2 * IMGW * chans),
        preferred_element_type=jnp.float32,
    ).reshape(image.shape[0], chans)
    pre_act = jnp.dot(image, backbone_weight, preferred_element_type=jnp.float32)
    scaled = (feature_grad * silu_slope(pre_act)).astype(jnp.bfloat16)
    image_grad = lax.dot_general(
        scaled, backbone_weight, (((1,), (1,)), ((), ())), preferred_element_type=jnp.float32
    ).astype(jnp.bfloat16)
    backbone_local = lax.dot_general(
        image, scaled, (((0,), (0,)), ((), ())), preferred_element_type=jnp.float32
    )
    cell_scale = 1.0 / math.sqrt(lax.axis_size("dp") * tiles * rows * cols)
    pixel_scale = 1.0 / math.sqrt(lax.axis_size("dp") * tiles * image.shape[0])
    conv_total, backbone_total = lax.psum((conv_local, backbone_local), ("dp", "tile"))
    conv_grad = (conv_total * cell_scale).astype(jnp.bfloat16)
    backbone_grad = (backbone_total * pixel_scale).astype(jnp.bfloat16)
    return (image_grad[None], conv_grad, backbone_grad)


def solution(mesh):
    return jax.shard_map(
        body,
        mesh=mesh,
        in_specs=(
            P("dp", "tile", None, None),
            P("dp", "tile", None, None),
            P(),
            P("dp", "tile", None),
            P(),
            P("dp", None),
            P("dp", "tile"),
            P("dp", "tile"),
            P("dp", "tile"),
        ),
        out_specs=(P("dp", "tile", None), P(), P()),
        check_vma=False,
    )
```

profile of v0, /device:TPU:0, one launch (start us, length us, event | category | flops | bytes accessed | tf_op | source)
XLA Modules:
  0.0 498.5 jit_solution(7476630493773151393)
XLA Ops:
  7.2 2.1 constant_dynamic-update-slice_fusion.1
  9.3 0.5 copy-done.4
  10.0 2.3 copy-done.2
  12.2 1.2 fusion.127
  13.5 3.4 collective-permute-start
  16.9 1.3 collective-permute-start.1
  18.7 0.5 convert_reduce_fusion
  19.2 2.7 multiply_convert_fusion.2
  22.3 1.4 broadcast_in_dim.31
  23.7 6.3 %scatter_fusion = bf16[80,64,128]{2,1,0:T(8,128)(2,1)} fusion(bf16[80,64,128]{2,1,0:T(8,128)(2,1)} %broadcast_in_dim.31, s32[40]{0:T(128)S(1)} %fusion.125, bf16[40,64,128]{2,1,0:T(8,128)(2,1)S(1)} %pad_maximum_fusion.1), kind=kCustom, calls=%fused_computation | custom fusion | bytes 1966240 | tf_op jit(solution)/shard_map/scatter | solution.py:97
  29.9 8.3 %all-to-all-start = ((bf16[16,5,64,128]{3,2,1,0:T(8,128)(2,1)}), bf16[16,5,64,128]{3,2,1,0:T(8,128)(2,1)}, u32[]{:S(2)}, u32[]{:S(2)}) async-start(bf16[16,5,64,128]{3,2,1,0:T(8,128)(2,1)} %bitcast.2), calls=%async_computation | async-start | bytes 2621440 | tf_op jit(solution)/shard_map/all_to_all | solution.py:107
  38.3 5.2 %fusion.5 = bf16[2,6,642,512]{3,2,1,0:T(8,128)(2,1)S(1)} fusion(bf16[2,1,640,512]{3,2,1,0:T(8,128)(2,1)} %collective-permute-done.1, bf16[2,4,640,512]{3,2,1,0:T(8,128)(2,1)} %copy-done.2, bf16[2,1,640,512]{3,2,1,0:T(8,128)(2,1)} %collective-permute-done), kind=kLoop, calls=%fused_computation.11 | loop fusion | flops 47333376 | bytes 15753216 | tf_op jit(solution)/shard_map/concatenate | solution.py:21
  43.6 2.4 slice_bitcast_fusion
  46.0 3.9 fusion.26
  49.9 3.9 fusion.28
  53.9 4.0 fusion.30
  57.9 3.9 fusion.32
  61.7 3.9 fusion.34
  65.7 4.0 fusion.36
  69.7 3.9 fusion.38
  73.6 3.9 fusion.40
  77.5 17.3 %add_convert_fusion = bf16[4,640,512]{2,1,0:T(8,128)(2,1)S(1)} fusion(f32[4,640,512]{2,1,0:T(8,128)} %fusion.26, f32[4,640,512]{2,1,0:T(8,128)} %fusion.28, f32[4,640,512]{2,1,0:T(8,128)} %fusion.30, f32[4,640,512]{2,1,0:T(8,128)} %fusion.32, f32[4,640,512]{2,1,0:T(8,128)} %fusion.34, f32[4,640,512]{2,1,0:T(8,128)} %fusion.36, f32[4,640,512]{2,1,0:T(8,128)} %fusion.40, ...), kind=kOutput, calls=%fused_computation.13 | convolution fusion | flops 1353973760 | bytes 47710208 | tf_op jit(solution)/shard_map/rvo,co->rvc/dot_general | solution.py:67
  94.8 2.9 broadcast_in_dim.35
  97.7 7.9 %scatter_fusion.1 = bf16[80,64,512]{2,1,0:T(8,128)(2,1)} fusion(bf16[80,64,512]{2,1,0:T(8,128)(2,1)} %broadcast_in_dim.35, s32[40]{0:T(128)S(1)} %fusion.125, bf16[40,64,512]{2,1,0:T(8,128)(2,1)S(1)} %bitcast.153), kind=kCustom, calls=%fused_computation.1 | custom fusion | bytes 7864480 | tf_op jit(solution)/shard_map/scatter | solution.py:96
  105.5 26.1 %all-to-all-start.1 = ((bf16[16,5,64,512]{3,2,1,0:T(8,128)(2,1)}), bf16[16,5,64,512]{3,2,1,0:T(8,128)(2,1)}, u32[]{:S(2)}, u32[]{:S(2)}) async-start(bf16[16,5,64,512]{3,2,1,0:T(8,128)(2,1)} %bitcast.152), calls=%async_computation.1 | async-start | bytes 10485760 | tf_op jit(solution)/shard_map/all_to_all | solution.py:100
  131.7 0.4 convert_reduce_fusion.1
  132.4 3.4 fusion.93
  135.8 1.6 fusion.73
  137.4 1.6 fusion.78
  139.3 1.5 fusion.83
  140.8 1.5 fusion.88
  142.4 1.6 fusion.53
  143.9 1.6 fusion.63
  145.5 1.6 fusion.58
  147.0 1.6 fusion.68
  148.6 1.4 maximum_bitcast_fusion
  150.0 4.9 pad_maximum_fusion
  154.9 72.7 %all-to-all-done.1 = bf16[16,5,64,512]{3,2,1,0:T(8,128)(2,1)} async-done(((bf16[16,5,64,512]{3,2,1,0:T(8,128)(2,1)}), bf16[16,5,64,512]{3,2,1,0:T(8,128)(2,1)}, u32[]{:S(2)}, u32[]{:S(2)}) %all-to-all-start.1) | async-done | bytes 5242912 | tf_op jit(solution)/shard_map/all_to_all | solution.py:100
  227.6 9.8 %convolution_convert_fusion = bf16[16,5,128,512]{3,2,1,0:T(8,128)(2,1)} fusion(bf16[16,5,64,128]{3,2,1,0:T(8,128)(2,1)} %all-to-all-done, bf16[16,5,64,512]{3,2,1,0:T(8,128)(2,1)} %all-to-all-done.1), kind=kOutput, calls=%fused_computation.12 | convolution fusion | flops 676331520 | bytes 17039360 | tf_op jit(solution)/shard_map/skmp,skmc->skpc/dot_general | solution.py:44
  237.4 14.6 %copy.64 = bf16[10,8,128,512]{3,1,2,0:T(8,128)(2,1)} copy(bf16[10,8,128,512]{3,2,1,0:T(8,128)(2,1)} %bitcast.150) | data formatting | bytes 20971520
  251.9 5.7 %fusion.128 = f32[4,65536]{1,0:T(4,128)S(1)} fusion(bf16[4,80]{1,0:T(4,128)(2,1)S(1)} %convert_element_type.67, bf16[80,65536]{1,0:T(8,128)(2,1)} %bitcast.151), kind=kOutput, calls=%fused_computation.133 | convolution fusion | flops 41943040 | bytes 11534976 | tf_op jit(solution)/shard_map/dot_general | solution.py:129
  257.6 0.7 reshape.239
  258.4 0.7 multiply_convert_fusion.4
  259.1 1.4 convolution_bitcast_fusion
  260.5 1.3 fusion.98
  261.8 221.1 %all-reduce.4.cloned.1.call-done = (f32[512,3,3,512]{3,0,2,1:T(8,128)}, f32[512,512]{0,1:T(8,128)}) async-done(((f32[512,3,3,512]{3,0,2,1:T(8,128)}, f32[512,512]{0,1:T(8,128)}), (f32[512,3,3,512]{3,0,2,1:T(8,128)}, f32[512,512]{0,1:T(8,128)})) %all-reduce.4.cloned.1.call-update) | async-done | bytes 10485776 | tf_op jit(solution)/shard_map/psum | solution.py:144
  482.9 7.3 %multiply_convert_fusion = bf16[512,3,3,512]{3,0,2,1:T(8,128)(2,1)} fusion(f32[512,3,3,512]{3,0,2,1:T(8,128)} %get-tuple-element.15), kind=kLoop, calls=%fused_computation.6 | loop fusion | flops 4718592 | bytes 14155776 | tf_op jit(solution)/shard_map/convert_element_type | solution.py:145
  490.4 1.0 copy.54
  (55 shorter events, 1.8 us)
Async XLA Ops:
  7.2 251.2 %copy-start = (bf16[1,512,512]{2,1,0:T(8,128)(2,1)S(1)}, bf16[1,512,512]{2,1,0:T(8,128)(2,1)}, u32[]{:S(2)}) copy-start(bf16[1,512,512]{2,1,0:T(8,128)(2,1)} %param.12) | copy-start | bytes 1572868
  7.2 2.6 copy-start.4
  9.8 8.4 %copy-start.8 = (s32[1,2560]{1,0:T(1,128)S(1)}, s32[1,2560]{1,0:T(1,128)}, u32[]{:S(2)}) copy-start(s32[1,2560]{1,0:T(1,128)} %param.17) | copy-start | bytes 30724
  9.8 8.5 %copy-start.9 = (s32[1,2560]{1,0:T(1,128)S(1)}, s32[1,2560]{1,0:T(1,128)}, u32[]{:S(2)}) copy-start(s32[1,2560]{1,0:T(1,128)} %param.16) | copy-start | bytes 30724
  9.8 8.5 %copy-start.11 = (s32[1,640]{1,0:T(1,128)S(1)}, s32[1,640]{1,0:T(1,128)}, u32[]{:S(2)}) copy-start(s32[1,640]{1,0:T(1,128)} %param.14) | copy-start | bytes 7684
  9.9 2.3 copy-start.2
  12.2 6.3 %copy-start.10 = (s32[1,2560]{1,0:T(1,128)S(1)}, s32[1,2560]{1,0:T(1,128)}, u32[]{:S(2)}) copy-start(s32[1,2560]{1,0:T(1,128)} %param.15) | copy-start | bytes 30724
  13.5 24.8 %collective-permute-start = (bf16[2,1,640,512]{3,2,1,0:T(8,128)(2,1)}, bf16[2,1,640,512]{3,2,1,0:T(8,128)(2,1)}, u32[]{:S(2)}, u32[]{:S(2)}) collective-permute-start(bf16[2,1,640,512]{3,2,1,0:T(8,128)(2,1)} %get-tuple-element.21), channel_id=1, source_target_pairs={{0,1},{1,2},{2,3},{3,4},{4,5},{5,6},{6,7},{7,8},{8,9},{9,10},{10,1... | collective-permute-start | bytes 3932168 | tf_op jit(solution)/shard_map/ppermute | solution.py:17
  16.9 21.4 %collective-permute-start.1 = (bf16[2,1,640,512]{3,2,1,0:T(8,128)(2,1)S(1)}, bf16[2,1,640,512]{3,2,1,0:T(8,128)(2,1)}, u32[]{:S(2)}, u32[]{:S(2)}) collective-permute-start(bf16[2,1,640,512]{3,2,1,0:T(8,128)(2,1)S(1)} %get-tuple-element.22), channel_id=1, source_target_pairs={{1,0},{2,1},{3,2},{4,3},{5,4},{6,5},{7,6},{8,7},{9,8},{10,9},{11,1... | collective-permute-start | bytes 3932168 | tf_op jit(solution)/shard_map/ppermute | solution.py:20
  29.9 75.6 %all-to-all-start = ((bf16[16,5,64,128]{3,2,1,0:T(8,128)(2,1)}), bf16[16,5,64,128]{3,2,1,0:T(8,128)(2,1)}, u32[]{:S(2)}, u32[]{:S(2)}) async-start(bf16[16,5,64,128]{3,2,1,0:T(8,128)(2,1)} %bitcast.2), calls=%async_computation | async-start | bytes 2621440 | tf_op jit(solution)/shard_map/all_to_all | solution.py:107
  38.3 7.7 %slice-start = ((s8[4718592]{0:T(1024)(128)(4,1)}), s8[4194304]{0:T(1024)(128)(4,1)S(1)}, s32[]{:S(2)}) async-start(s8[4718592]{0:T(1024)(128)(4,1)} %bitcast.154), calls=%async_computation.3 | async-start | bytes 8388608
  43.6 2.4 slice-start.1
  46.0 27.6 %copy-start.1 = (bf16[6,642,512]{2,1,0:T(8,128)(2,1)}, bf16[6,642,512]{2,1,0:T(8,128)(2,1)S(1)}, u32[]{:S(2)}) copy-start(bf16[6,642,512]{2,1,0:T(8,128)(2,1)S(1)} %get-tuple-element.20) | copy-start | bytes 11833348
  105.5 26.8 %copy-start.5 = (bf16[1,4,640,512]{3,2,1,0:T(8,128)(2,1)S(1)}, bf16[1,4,640,512]{3,2,1,0:T(8,128)(2,1)}, u32[]{:S(2)}) copy-start(bf16[1,4,640,512]{3,2,1,0:T(8,128)(2,1)} %param.9) | copy-start | bytes 7864324
  105.5 122.0 %all-to-all-start.1 = ((bf16[16,5,64,512]{3,2,1,0:T(8,128)(2,1)}), bf16[16,5,64,512]{3,2,1,0:T(8,128)(2,1)}, u32[]{:S(2)}, u32[]{:S(2)}) async-start(bf16[16,5,64,512]{3,2,1,0:T(8,128)(2,1)} %bitcast.152), calls=%async_computation.1 | async-start | bytes 10485760 | tf_op jit(solution)/shard_map/all_to_all | solution.py:100
  131.6 351.3 %all-reduce.4.cloned.1.call-start = ((), (), s32[]{:S(2)}) async-start(), calls=%async_computation.2 | async-start | bytes 20971520 | tf_op jit(solution)/shard_map/psum | solution.py:144
  132.4 3.5 copy-start.3
  251.9 6.5 %copy-start.7 = (bf16[512,512]{1,0:T(8,128)(2,1)S(1)}, bf16[512,512]{1,0:T(8,128)(2,1)}, u32[]{:S(2)}) copy-start(bf16[512,512]{1,0:T(8,128)(2,1)} %param.13) | copy-start | bytes 1572868
  482.9 7.3 %copy-start.6 = (f32[512,512]{0,1:T(8,128)S(1)}, f32[512,512]{0,1:T(8,128)}, u32[]{:S(2)}) copy-start(f32[512,512]{0,1:T(8,128)} %get-tuple-element.16) | copy-start | bytes 3145732
Sparse Core Ops, SparseCore 0:
  260.7 222.2 all-reduce.3
where the time goes:
time: 503 us; the launch traced here: 498 us
  waiting for transfers between devices  294 us (58%)
  matrix products  83.5 us (17%)
  local copies, waits for them, and re-layouts  43.9 us (9%)
  starting transfers between devices  39.1 us (8%)
  other arithmetic  23.5 us (5%)
  between operations  14.7 us (3%)
    psum x1, waiting for transfers between devices, body(): lax.psum((conv_local, backbone_local), ('dp', 'tile'))  221 us
    all_to_all x1, waiting for transfers between devices, body(): lax.all_to_all(sent_blocks.reshape(tiles, capacity, BLK, chans), 'tile',...  72.7 us
    dot_general x9, matrix products, body(): jnp.einsum('rvo,co->rvc', shifted, conv_weight[:, row_tap, col_tap, :], p...  48.7 us
    all_to_all x1, starting transfers between devices, body(): lax.all_to_all(sent_blocks.reshape(tiles, capacity, BLK, chans), 'tile',...  26.1 us
    unnamed x31, local copies, waits for them, and re-layouts  20.5 us
    dot_general x9, matrix products, body(): jnp.einsum('rvc,rvo->co', moved, center, preferred_element_type=jnp.float32)  15.8 us
  transfers between devices with their start and end apart: 5, of which 2 were waited for; matrix products, arithmetic and copies ran while one was open for 21% of the time, Pallas kernels for 0%

commit v1 on v0

v1 whole, which is shorter than its diff:
```python
import functools
import math

import jax
import jax.numpy as jnp
from jax import lax
from jax.experimental import pallas as pl
from jax.experimental.pallas import tpu as pltpu
from jax.sharding import PartitionSpec as P

BLK = 64
IMGW = 64
GROUP = 4
VMEM_BYTES = 56 * 1024 * 1024
F32 = jnp.float32
BF16 = jnp.bfloat16
VMEM = pl.BlockSpec(memory_space=pltpu.VMEM)
SMEM = pl.BlockSpec(memory_space=pltpu.SMEM)
ANY = pl.BlockSpec(memory_space=pl.ANY)


def params(**extra):
    return pltpu.CompilerParams(vmem_limit_bytes=VMEM_BYTES, **extra)


def cost(flops, nbytes):
    return pl.CostEstimate(flops=int(flops), bytes_accessed=int(nbytes), transcendentals=0)


def nt_dot(a, b):
    return lax.dot_general(a, b, (((1,), (1,)), ((), ())), preferred_element_type=F32)


def column_shift(value, by):
    if by == 0:
        return value
    length = value.shape[0]
    place = lax.broadcasted_iota(jnp.int32, value.shape, 0)
    edge = length - 1 if by > 0 else 0
    return jnp.where(place == edge, 0.0, pltpu.roll(value, (-by) % length, 0))


def bev_inner_kernel(g_ref, w_ref, inner_ref, edge_ref, acc_ref):
    rows = g_ref.shape[0]
    step = pl.program_id(0)

    def row_terms(u, taps, j, first):
        lhs = jnp.concatenate([g_ref[u - i + 1] for i in taps], axis=1)
        rhs = jnp.concatenate([w_ref[i, 0] for i in taps], axis=1)
        term = column_shift(nt_dot(lhs, rhs), 1 - j)
        if first:
            acc_ref[u] = term
        else:
            acc_ref[u] = acc_ref[u] + term

    for order, j in enumerate((1, 0, 2)):
        @pl.when(step == order)
        def _(j=j, order=order):
            row_terms(0, (0, 1), j, order == 0)
            row_terms(rows - 1, (1, 2), j, order == 0)

            @pl.loop(1, rows - 1)
            def _(u):
                row_terms(u, (0, 1, 2), j, order == 0)

    @pl.when(step == 2)
    def _():
        edge_ref[0] = acc_ref[0]
        edge_ref[1] = acc_ref[rows - 1]

        @pl.loop(1, rows - 1)
        def _(u):
            inner_ref[u - 1] = acc_ref[u].astype(BF16)


def col_tap(step):
    return jnp.where(step == 0, 1, jnp.where(step == 1, 0, 2))


def bev_inner(grad, weight):
    rows, cols, chans = grad.shape
    whole = lambda *shape: pl.BlockSpec(shape, lambda s: (0,) * len(shape))
    return pl.pallas_call(
        bev_inner_kernel,
        grid=(3,),
        in_specs=[
            whole(rows, cols, chans),
            pl.BlockSpec((3, 1, chans, chans), lambda s: (0, col_tap(s), 0, 0)),
        ],
        out_specs=[whole(rows - 2, cols, chans), whole(2, cols, chans)],
        out_shape=[
            jax.ShapeDtypeStruct((rows - 2, cols, chans), BF16),
            jax.ShapeDtypeStruct((2, cols, chans), F32),
        ],
        scratch_shapes=[pltpu.VMEM((rows, cols, chans), F32)],
        compiler_params=params(),
        cost_estimate=cost(2 * (3 * rows - 2) * 3 * cols * chans * chans, 2 * (rows * cols * chans * 2 + 9 * chans * chans)),
        name="bev_inner",
    )(grad, weight)


def bev_edge_kernel(edge_ref, low_ref, high_ref, wl_ref, wh_ref, out_ref, acc_ref):
    step = pl.program_id(0)
    for order, j in enumerate((1, 0, 2)):
        @pl.when(step == order)
        def _(j=j, order=order):
            for side, (halo, w) in enumerate(((low_ref, wl_ref), (high_ref, wh_ref))):
                term = column_shift(nt_dot(halo[...], w[0, 0]), 1 - j)
                base = edge_ref[side] if order == 0 else acc_ref[side]
                if order == 2:
                    out_ref[side] = (base + term).astype(BF16)
                else:
                    acc_ref[side] = base + term


def bev_edge(edge, low, high, weight):
    _, cols, chans = edge.shape
    whole = lambda *shape: pl.BlockSpec(shape, lambda s: (0,) * len(shape))
    return pl.pallas_call(
        bev_edge_kernel,
        grid=(3,),
        in_specs=[
            whole(2, cols, chans),
            whole(cols, chans),
            whole(cols, chans),
            pl.BlockSpec((1, 1, chans, chans), lambda s: (2, col_tap(s), 0, 0)),
            pl.BlockSpec((1, 1, chans, chans), lambda s: (0, col_tap(s), 0, 0)),
        ],
        out_specs=whole(2, cols, chans),
        out_shape=jax.ShapeDtypeStruct((2, cols, chans), BF16),
        scratch_shapes=[pltpu.VMEM((2, cols, chans), F32)],
        compiler_params=params(),
        cost_estimate=cost(2 * 6 * cols * chans * chans, 2 * (8 * cols * chans + 6 * chans * chans)),
        name="bev_edge",
    )(edge, low, high, weight, weight)


def turn_kernel(parts, order_ref, a_ref, out_ref, wide_ref):
    chans, cols = wide_ref.shape
    size = chans // parts
    flat = a_ref[0].astype(F32).T
    place = lax.broadcasted_iota(jnp.int32, flat.shape, 1)
    for j in range(3):
        if j == 0:
            moved = jnp.where(place == 0, 0.0, pltpu.roll(flat, 1, 1))
        elif j == 1:
            moved = flat
        else:
            moved = jnp.where(place == cols - 1, 0.0, pltpu.roll(flat, cols - 1, 1))
        wide_ref[...] = moved

        for s in range(parts):
            source = pl.multiple_of(order_ref[s] * size, size)
            out_ref[j, s * size : (s + 1) * size, :] = wide_ref[pl.ds(source, size), :].astype(BF16)


def turn(act, order):
    rows, cols, chans = act.shape
    parts = order.shape[0]
    return pl.pallas_call(
        functools.partial(turn_kernel, parts),
        grid=(rows,),
        in_specs=[SMEM, pl.BlockSpec((1, cols, chans), lambda u: (u, 0, 0))],
        out_specs=pl.BlockSpec((3, chans, cols), lambda u: (0, 0, u)),
        out_shape=jax.ShapeDtypeStruct((3, chans, rows * cols), BF16),
        scratch_shapes=[pltpu.VMEM((chans, cols), F32)],
        compiler_params=params(),
        cost_estimate=cost(0, 16 * rows * cols * chans),
        name="turn",
    )(order, act)


def wgrad_kernel(taps, cols, a_ref, g_ref, low_ref, high_ref, keep_ref, send_ref):
    step = pl.program_id(0)
    half = pl.program_id(1)
    total = a_ref.shape[2]

    def product(tap):
        a = a_ref[0]
        g = g_ref[...]
        if tap == 1:
            return jnp.dot(a, g, preferred_element_type=F32)
        if tap == 0:
            return jnp.dot(a[:, : total - cols], g[cols:], preferred_element_type=F32) + jnp.dot(
                a[:, total - cols :], high_ref[...], preferred_element_type=F32
            )
        return jnp.dot(a[:, cols:], g[: total - cols], preferred_element_type=F32) + jnp.dot(
            a[:, :cols], low_ref[...], preferred_element_type=F32
        )

    for place, tap in enumerate(taps):
        @pl.when(step // 3 == place)
        def _(tap=tap):
            term = product(tap).astype(BF16)

            @pl.when(half == 0)
            def _():
                send_ref[0] = term

            @pl.when(half == 1)
            def _():
                keep_ref[0] = term


def wgrad(turned, grad, low, high, taps):
    rows, cols, chans = grad.shape
    flat = grad.reshape(rows * cols, chans)
    count = 3 * len(taps)
    half_rows = chans // 2
    whole = lambda *shape: pl.BlockSpec(shape, lambda t, h: (0,) * len(shape))
    in_specs = [
        pl.BlockSpec((1, half_rows, rows * cols), lambda t, h: (t % 3, 1 - h, 0)),
        whole(rows * cols, chans),
    ]
    operands = [turned, flat]
    if taps == (1,):
        kernel = lambda a, g, keep, send: wgrad_kernel(taps, cols, a, g, None, None, keep, send)
    else:
        kernel = functools.partial(wgrad_kernel, taps, cols)
        in_specs += [whole(cols, chans), whole(cols, chans)]
        operands += [low, high]
    half_spec = pl.BlockSpec((1, half_rows, chans), lambda t, h: (t, 0, 0))
    shape = jax.ShapeDtypeStruct((count, half_rows, chans), BF16)
    return pl.pallas_call(
        kernel,
        grid=(count, 2),
        in_specs=in_specs,
        out_specs=[half_spec, half_spec],
        out_shape=[shape, shape],
        compiler_params=params(),
        cost_estimate=cost(2 * count * rows * cols * chans * chans, 2 * (4 * rows * cols * chans + count * chans * chans)),
        name="wgrad",
    )(*operands)


def fold_kernel(keep_ref, recv_ref, first_ref, second_ref):
    cut = first_ref.shape[1]
    first_ref[...] = (keep_ref[:, :cut].astype(F32) + recv_ref[:, :cut].astype(F32)).astype(BF16)
    second_ref[...] = (keep_ref[:, cut:].astype(F32) + recv_ref[:, cut:].astype(F32)).astype(BF16)


def fold(keep, recv):
    n, m = keep.shape[:2]
    rest = keep.shape[2:]
    block = pl.BlockSpec((1, m) + rest, lambda t: (t,) + (0,) * (1 + len(rest)))
    half = pl.BlockSpec((1, m // 2) + rest, lambda t: (t,) + (0,) * (1 + len(rest)))
    shape = jax.ShapeDtypeStruct((n, m // 2) + rest, BF16)
    return pl.pallas_call(
        fold_kernel,
        grid=(n,),
        in_specs=[block, block],
        out_specs=[half, half],
        out_shape=[shape, shape],
        compiler_params=params(),
        cost_estimate=cost(0, 6 * keep.size),
        name="fold",
    )(keep, recv)


def pieces_kernel(
    plan, info_ref, route_ref, off_ref, fx_ref, fy_ref, *refs
):
    own_blocks, per, tile_bits, edge = plan
    sources = refs[:4]
    outs = refs[4:8]
    blocks_ref, acc_ref, count_ref, list_ref, sems = refs[8:]
    copies = []
    start = 0
    for n, source in enumerate(sources):
        size = source.shape[0]
        copies.append(pltpu.make_async_copy(source, blocks_ref.at[pl.ds(start, size)], sems.at[n]))
        start += size
    for copy in copies:
        copy.start()
    tile = info_ref[0]
    core = tile & 1
    slots = outs[0].shape[0] * 2
    half_per = outs[0].shape[1]
    wide = 2 * own_blocks
    inner = own_blocks - 2 * edge

    @pl.loop(0, slots * per)
    def _(n):
        count_ref[n] = 0

    @pl.loop(0, wide)
    def _(n):
        other = n // own_blocks
        k = n - other * own_blocks
        ident = route_ref[(tile ^ other) * own_blocks + k]
        owner = ident // per
        local = ident - owner * per
        away = (owner ^ tile) >> 1

        @pl.when(((owner ^ tile) & 1) == 0)
        def _():
            place = slot_of(away, core, tile_bits)
            at = place * per + local
            have = count_ref[at]
            list_ref[at * wide + have] = n
            count_ref[at] = have + 1

    for copy in copies:
        copy.wait()

    lanes = lax.broadcasted_iota(jnp.int32, (1, 2 * BLK), 1)
    low_lane = lanes < BLK

    def group_product(at, first, have):
        picked = []
        for g in range(GROUP):
            there = first + g < have
            n = jnp.where(there, list_ref[at * wide + jnp.minimum(first + g, wide - 1)], 0)
            other = n // own_blocks
            k = n - other * own_blocks
            spot = jnp.where(
                k < edge, inner + k, jnp.where(k >= own_blocks - edge, inner + k - inner, k - edge)
            )
            picked.append((there, n, other * own_blocks + spot))
        rhs = jnp.concatenate([blocks_ref[spot] for _, _, spot in picked], axis=0)

        def lane_row(ref):
            halves = []
            for p in range(0, GROUP, 2):
                a = ref[pl.ds(picked[p][1], 1), :]
                b = ref[pl.ds(picked[p + 1][1], 1), :]
                halves.append(jnp.where(low_lane, a, b))
            return jnp.concatenate(halves, axis=1)

        valid = jnp.concatenate(
            [
                jnp.where(
                    low_lane,
                    jnp.where(picked[p][0], 1.0, 0.0),
                    jnp.where(picked[p + 1][0], 1.0, 0.0),
                )
                for p in range(0, GROUP, 2)
            ],
            axis=1,
        ).astype(F32)
        left = lane_row(off_ref)
        right_w = lane_row(fx_ref).astype(F32) / 256.0
        lower_w = lane_row(fy_ref).astype(F32) / 256.0
        column = lax.broadcasted_iota(jnp.int32, (IMGW, GROUP * BLK), 0)
        across = jnp.where(column == left, 1.0 - right_w, 0.0) + jnp.where(
            column == left + 1, right_w, 0.0
        )
        band = jnp.concatenate(
            [((1.0 - lower_w) * valid) * across, (lower_w * valid) * across], axis=0
        ).astype(BF16)
        return jnp.dot(band, rhs, preferred_element_type=F32)

    def fill(out, place, local, inside):
        at = place * per + local
        have = count_ref[at]
        value = group_product(at, 0, have)
        out[inside[0], inside[1]] = value.astype(BF16)

        @pl.when(have > GROUP)
        def _():
            acc_ref[...] = value

            @pl.loop(1, (have + GROUP - 1) // GROUP)
            def _(m):
                acc_ref[...] = acc_ref[...] + group_product(at, m * GROUP, have)

            out[inside[0], inside[1]] = acc_ref[...].astype(BF16)

    for chunk in range(2):
        for half in (1, 0):
            out = outs[2 * chunk + half]

            @pl.loop(0, (slots // 2) * half_per, unroll=2)
            def _(n, out=out, half=half, chunk=chunk):
                place = n // half_per
                local = n - place * half_per
                fill(out, half * (slots // 2) + place, chunk * half_per + local, (place, local))


def swap_low_bits(value):
    return (value & ~3) | ((value & 1) << 1) | ((value >> 1) & 1)


def slot_of(away, core, bits):
    place = 0
    first = jnp.where((core == 1) & (bits >= 2), swap_low_bits(away), away)
    for n in range(bits):
        place = place | (((first >> n) & 1) << (bits - 1 - n))
    return place


def warp_pieces(info, route, off, fx, fy, sources, tiles, per, edge):
    own = sources[0].shape[0] + sources[1].shape[0]
    chans = sources[0].shape[2]
    bits = int(math.log2(tiles)) - 1
    slots = tiles // 2
    shape = jax.ShapeDtypeStruct((slots // 2, per // 2, 2 * IMGW, chans), BF16)
    return pl.pallas_call(
        functools.partial(pieces_kernel, (own, per, bits, edge)),
        in_specs=[SMEM, SMEM, VMEM, VMEM, VMEM] + [ANY] * 4,
        out_specs=[VMEM] * 4,
        out_shape=[shape] * 4,
        scratch_shapes=[
            pltpu.VMEM((2 * own, BLK, chans), BF16),
            pltpu.VMEM((2 * IMGW, chans), F32),
            pltpu.SMEM((slots * per,), jnp.int32),
            pltpu.SMEM((slots * per * 2 * own,), jnp.int32),
            pltpu.SemaphoreType.DMA((4,)),
        ],
        compiler_params=params(),
        cost_estimate=cost(
            2 * slots * per * 2 * IMGW * GROUP * BLK * chans, 2 * (own * 2 * BLK * chans + slots * per * 2 * IMGW * chans)
        ),
        name="warp_pieces",
    )(info, route, off, fx, fy, *sources)


def slope_kernel(order_ref, img_ref, w_ref, slope_ref, turned_ref, wide_ref):
    value = jnp.dot(img_ref[...], w_ref[...], preferred_element_type=F32)
    sigma = jax.nn.sigmoid(value)
    slope_ref[...] = sigma * (1.0 + value * (1.0 - sigma))
    wide_ref[...] = img_ref[...].astype(F32).T
    parts = order_ref.shape[0]
    size = wide_ref.shape[0] // parts
    for s in range(parts):
        source = pl.multiple_of(order_ref[s] * size, size)
        turned_ref[s * size : (s + 1) * size, :] = wide_ref[pl.ds(source, size), :].astype(BF16)


def image_slope(order, image, weight):
    pixels, chans = image.shape
    return pl.pallas_call(
        slope_kernel,
        in_specs=[SMEM, VMEM, VMEM],
        out_specs=[VMEM, VMEM],
        out_shape=[
            jax.ShapeDtypeStruct((pixels, chans), F32),
            jax.ShapeDtypeStruct((chans, pixels), BF16),
        ],
        scratch_shapes=[pltpu.VMEM((chans, pixels), F32)],
        compiler_params=params(),
        cost_estimate=cost(2 * pixels * chans * chans, 10 * pixels * chans),
        name="image_slope",
    )(order, image, weight)


def image_kernel(ka, ra, kb, rb, slope_ref, turned_ref, w_ref, img_out, keep_ref, send_ref):
    half = ka.shape[0]
    feature = jnp.concatenate(
        [ka[...].astype(F32) + ra[...].astype(F32), kb[...].astype(F32) + rb[...].astype(F32)], axis=0
    )
    scaled = (feature * slope_ref[...]).astype(BF16)
    grad = jnp.dot(turned_ref[...], scaled, preferred_element_type=F32).astype(BF16)
    cut = keep_ref.shape[1]
    keep_ref[0] = grad[:cut]
    send_ref[0] = grad[cut:]
    img_out[...] = nt_dot(scaled, w_ref[...]).astype(BF16)


def image_layer(ka, ra, kb, rb, slope, turned, weight):
    pixels, chans = slope.shape
    half = jax.ShapeDtypeStruct((1, chans // 2, chans), BF16)
    return pl.pallas_call(
        image_kernel,
        in_specs=[VMEM] * 7,
        out_specs=[VMEM] * 3,
        out_shape=[jax.ShapeDtypeStruct((pixels, chans), BF16), half, half],
        compiler_params=params(),
        cost_estimate=cost(4 * pixels * chans * chans, 16 * pixels * chans),
        name="image_layer",
    )(ka, ra, kb, rb, slope, turned, weight)


def exchange(value, size_dp, size_tile, flip):
    pairs = []
    for d in range(size_dp):
        for t in range(size_tile):
            dm, tm = flip(t & 1)
            pairs.append((d * size_tile + t, (d ^ dm) * size_tile + (t ^ tm)))
    return lax.ppermute(value, ("dp", "tile"), pairs)


def step_masks(size_dp, size_tile, core):
    dp_masks = [(1 << n, 0) for n in range(int(math.log2(size_dp)))]
    tile_masks = [(0, 1 << n) for n in range(1, int(math.log2(size_tile)))]
    masks = dp_masks + tile_masks
    if core == 1 and len(masks) >= 2:
        masks = [masks[1], masks[0]] + masks[2:]
    return masks


def canonical(masks, size_dp, size_tile):
    dp_bits = int(math.log2(size_dp))
    out = []
    for dm, tm in masks:
        out.append(int(math.log2(dm)) if dm else dp_bits + int(math.log2(tm)) - 1)
    return out


def part_order(me_dp, me_tile, size_dp, size_tile, levels):
    core = me_tile & 1
    dp_bits = int(math.log2(size_dp))
    me = me_dp | ((me_tile >> 1) << dp_bits)
    mine = []
    for which in (0, 1):
        masks = step_masks(size_dp, size_tile, which)[: levels - 1]
        bits = canonical(masks, size_dp, size_tile)
        table = []
        for t in range(1 << (levels - 1)):
            value = 0
            for n, bit in enumerate(bits):
                value |= ((t >> (levels - 2 - n)) & 1) << bit
            table.append(value)
        mine.append(table)
    low_mask = (1 << (levels - 1)) - 1
    tables = jnp.array(mine, jnp.int32)
    same = jnp.where(core == 0, tables[0], tables[1]) ^ (me & low_mask)
    flipped = jnp.where(core == 0, tables[1], tables[0]) ^ (me & low_mask)
    top = 1 << (levels - 1)
    return jnp.concatenate([same + core * top, flipped + (1 - core) * top])


def reduce_parts(keep, send, size_dp, size_tile, levels, scale):
    masks = [step_masks(size_dp, size_tile, core) for core in (0, 1)]
    recv = exchange(send, size_dp, size_tile, lambda core: (0, 1))
    for n in range(levels - 1):
        keep, send = fold(keep, recv)
        recv = exchange(send, size_dp, size_tile, lambda core, n=n: masks[core][n])
    total = keep.astype(F32) + recv.astype(F32)
    for n in range(levels - 1, len(masks[0])):
        value = total.astype(BF16)
        recv = exchange(value, size_dp, size_tile, lambda core, n=n: masks[core][n])
        total = value.astype(F32) + recv.astype(F32)
    return (total * scale).astype(BF16)


def gather_parts(part, size_dp, size_tile, levels):
    masks = [step_masks(size_dp, size_tile, core) for core in (0, 1)]
    for n in reversed(range(levels - 1)):
        recv = exchange(part, size_dp, size_tile, lambda core, n=n: masks[core][n])
        part = jnp.concatenate([part, recv], axis=1)
    recv = exchange(part, size_dp, size_tile, lambda core: (0, 1))
    return part, recv


def place_kernel(parts, shapes, order_ref, *refs):
    count = len(shapes)
    sources = refs[: 2 * count]
    outs = refs[2 * count : 2 * count + 2]
    sem = refs[-1]
    copies = []
    for n, (which, taps) in enumerate(shapes):
        for side in range(2):
            source = sources[2 * n + side]
            size = 2 * source.shape[1] // parts
            for s in range(parts // 2):
                target = pl.multiple_of(order_ref[side * (parts // 2) + s] * size, size)
                for place, tap in enumerate(taps):
                    copies.append(
                        pltpu.make_async_copy(
                            source.at[pl.ds(place * 3, 3), pl.ds(s * size, size)]
                            if which == 0
                            else source.at[0, pl.ds(s * size, size)],
                            outs[0].at[pl.ds(tap * 3, 3), pl.ds(target, size)]
                            if which == 0
                            else outs[1].at[pl.ds(target, size)],
                            sem,
                        )
                    )
    for copy in copies:
        copy.start()
    for copy in copies:
        copy.wait()


def place_parts(order, groups, chans):
    operands = []
    shapes = []
    for which, taps, mine, other in groups:
        operands += [mine, other]
        shapes.append((which, taps))
    return pl.pallas_call(
        functools.partial(place_kernel, order.shape[0], tuple(shapes)),
        in_specs=[SMEM] + [ANY] * len(operands),
        out_specs=[ANY, ANY],
        out_shape=[
            jax.ShapeDtypeStruct((9, chans, chans), BF16),
            jax.ShapeDtypeStruct((chans, chans), BF16),
        ],
        scratch_shapes=[pltpu.SemaphoreType.DMA],
        compiler_params=params(),
        cost_estimate=cost(0, 40 * chans * chans),
        name="place_parts",
    )(order, *operands)


def body(grad_out, bev_act, conv_weight, img_in, backbone_weight, route, offsets, frac_x, frac_y):
    tiles = lax.axis_size("tile")
    pods = lax.axis_size("dp")
    my_tile = lax.axis_index("tile")
    my_pod = lax.axis_index("dp")
    grad = grad_out[0]
    rows, cols, chans = grad.shape
    image = img_in[0]
    weight = jnp.transpose(conv_weight, (1, 2, 0, 3))
    per = image.shape[0] // (2 * IMGW)
    own = rows * cols // BLK
    edge_blocks = cols // BLK
    levels = min(int(math.log2(pods * tiles)), int(math.log2(chans // 16)))
    order = part_order(my_pod, my_tile, pods, tiles, levels)
    cell_scale = 1.0 / math.sqrt(pods * tiles * rows * cols)
    pixel_scale = 1.0 / math.sqrt(pods * tiles * image.shape[0])

    forward = [(i, i + 1) for i in range(tiles - 1)]
    backward = [(b, a) for a, b in forward]
    low = lax.ppermute(grad[rows - 1], "tile", forward)
    high = lax.ppermute(grad[0], "tile", backward)

    core_swap = [(t, t ^ 1) for t in range(tiles)]
    cells = jnp.stack([offsets[0], frac_x[0], frac_y[0]]).reshape(3, own, BLK)
    cells_other = lax.ppermute(cells, "tile", core_swap)
    cells = jnp.concatenate([cells, cells_other], axis=1)
    cells = jnp.concatenate([cells, cells], axis=2)

    inner, edge = bev_inner(grad, weight)
    inner_other = lax.ppermute(inner, "tile", core_swap)
    turned = turn(bev_act[0], order)
    edge = bev_edge(edge, low, high, weight)
    edge_other = lax.ppermute(edge, "tile", core_swap)
    keep_mid, send_mid = wgrad(turned, grad, None, None, (1,))
    as_blocks = lambda value: value.reshape(-1, BLK, chans)
    info = jnp.reshape(my_tile, (1,)).astype(jnp.int32)
    keep_a, send_a, keep_b, send_b = warp_pieces(
        info,
        route[0],
        cells[0],
        cells[1],
        cells[2],
        [as_blocks(v) for v in (inner, edge, inner_other, edge_other)],
        tiles,
        per,
        edge_blocks,
    )
    slope, image_turned = image_slope(order, image, backbone_weight)
    keep_out, send_out = wgrad(turned, grad, low, high, (0, 2))

    tile_masks = [(0, 1 << n) for n in range(1, int(math.log2(tiles)))]
    swapped = [tile_masks[1], tile_masks[0]] + tile_masks[2:] if len(tile_masks) > 1 else tile_masks
    both = (tile_masks, swapped)

    def warp_steps(keep, send):
        for n in range(len(tile_masks)):
            recv = exchange(send, pods, tiles, lambda core, n=n: both[core][n])
            if n == len(tile_masks) - 1:
                return keep.reshape(-1, chans), recv.reshape(-1, chans)
            shape = keep.shape
            keep, send = fold(
                keep.reshape((1, shape[0]) + (shape[1] * shape[2], chans)),
                recv.reshape((1, shape[0]) + (shape[1] * shape[2], chans)),
            )
            keep = keep.reshape((shape[0] // 2,) + shape[1:])
            send = send.reshape((shape[0] // 2,) + shape[1:])

    pair_a = warp_steps(keep_a, send_a)
    pair_b = warp_steps(keep_b, send_b)

    mid = reduce_parts(keep_mid, send_mid, pods, tiles, levels, cell_scale)
    mid = gather_parts(mid, pods, tiles, levels)
    outer = reduce_parts(keep_out, send_out, pods, tiles, levels, cell_scale)
    outer = gather_parts(outer, pods, tiles, levels)

    image_grad, keep_img, send_img = image_layer(*pair_a, *pair_b, slope, image_turned, backbone_weight)
    back = reduce_parts(keep_img, send_img, pods, tiles, levels, pixel_scale)
    back = gather_parts(back, pods, tiles, levels)

    conv_grad, backbone_grad = place_parts(
        order, [(0, (1,)) + mid, (0, (0, 2)) + outer, (1, (0,)) + back], chans
    )
    conv_grad = jnp.transpose(conv_grad.reshape(3, 3, chans, chans), (2, 0, 1, 3))
    return (image_grad[None], conv_grad, backbone_grad)


def solution(mesh):
    return jax.shard_map(
        body,
        mesh=mesh,
        in_specs=(
            P("dp", "tile", None, None),
            P("dp", "tile", None, None),
            P(),
            P("dp", "tile", None),
            P(),
            P("dp", None),
            P("dp", "tile"),
            P("dp", "tile"),
            P("dp", "tile"),
        ),
        out_specs=(P("dp", "tile", None), P(), P()),
        check_vma=False,
    )
```

time: 503 us -> 429 us (0.85)
  Pallas kernels: 0 us -> 280 us
  waiting for transfers between devices: 294 us -> 71.9 us
  matrix products: 83.5 us -> 0 us
  local copies, waits for them, and re-layouts: 43.9 us -> 19.5 us
  other arithmetic: 23.5 us -> 1.63 us
  between operations: 14.7 us -> 1.23 us
  starting transfers between devices: 39.1 us -> 51.6 us
    pallas_call x0 -> x25, Pallas kernels: none -> 280 us  [the longest x1 161 us: place_parts(): pl.pallas_call(functools.partial(place_kernel, order.shape[0], tuple(shap...]
    psum x1 -> x0, waiting for transfers between devices: 221 us -> none  [body(): lax.psum((conv_local, backbone_local), ('dp', 'tile'))]
    dot_general x23 -> x0, matrix products: 83.5 us -> none  [the longest x9 48.7 us: body(): jnp.einsum('rvo,co->rvc', shifted, conv_weight[:, row_tap, col_tap, :], p...]
    all_to_all x2 -> x0, waiting for transfers between devices: 72.7 us -> none  [the longest x1 72.7 us: body(): lax.all_to_all(sent_blocks.reshape(tiles, capacity, BLK, chans), 'tile',...]
    ppermute x2 -> x41, waiting for transfers between devices: 0.01 us -> 71.9 us  [the longest x36 71.9 us: exchange(): return lax.ppermute(value, ('dp', 'tile'), pairs)]
    ppermute x2 -> x41, starting transfers between devices: 4.69 us -> 51.6 us  [the longest x36 47.4 us: exchange(): return lax.ppermute(value, ('dp', 'tile'), pairs)]
    all_to_all x2 -> x0, starting transfers between devices: 34.4 us -> none  [the longest x1 26.1 us: body(): lax.all_to_all(sent_blocks.reshape(tiles, capacity, BLK, chans), 'tile',...]
    scatter x2 -> x0, local copies, waits for them, and re-layouts: 14.1 us -> none  [the longest x1 7.89 us: body(): jnp.zeros((slot_total, BLK, chans), jnp.bfloat16).at[my_slots].set(blocks)]
  transfers between devices with their start and end apart: 5 -> 41, of which waited for: 2 -> 16; matrix products, arithmetic and copies ran while one was open for 21% -> 1% of each run, Pallas kernels for 0% -> 24%
where the time goes in v1:
time: 429 us; the launch traced here: 426 us
  Pallas kernels  280 us (65%)
  waiting for transfers between devices  71.9 us (17%)
  starting transfers between devices  51.6 us (12%)
  local copies, waits for them, and re-layouts  19.5 us (5%)
    pallas_call x1, Pallas kernels, place_parts(): pl.pallas_call(functools.partial(place_kernel, order.shape[0], tuple(shap...  161 us
    ppermute x36, waiting for transfers between devices, exchange(): return lax.ppermute(value, ('dp', 'tile'), pairs)  71.9 us
    ppermute x36, starting transfers between devices, exchange(): return lax.ppermute(value, ('dp', 'tile'), pairs)  47.4 us
    pallas_call x16, Pallas kernels, fold(): pl.pallas_call(fold_kernel, grid=(n,), in_specs=[block, block], out_specs...  43 us
    pallas_call x2, Pallas kernels, wgrad(): pl.pallas_call(kernel, grid=(count, 2), in_specs=in_specs, out_specs=[hal...  27.2 us
    unnamed x81, local copies, waits for them, and re-layouts  17.3 us
    pallas_call x1, Pallas kernels, bev_inner(): pl.pallas_call(bev_inner_kernel, grid=(3,), in_specs=[whole(rows, cols, c...  16.5 us
    pallas_call x1, Pallas kernels, warp_pieces(): pl.pallas_call(functools.partial(pieces_kernel, (own, per, bits, edge)),...  13.4 us
  transfers between devices with their start and end apart: 41, of which 16 were waited for; matrix products, arithmetic and copies ran while one was open for 1% of the time, Pallas kernels for 24%

profile of v1, /device:TPU:0, one launch (start us, length us, event | category | flops | bytes accessed | tf_op | source)
XLA Modules:
  0.0 426.4 jit_solution(14883715393885142929)
XLA Ops:
  2.0 2.4 collective-permute-start.1
  6.4 7.0 %turn.1.a.a_ref = bf16[3,512,2560]{2,1,0:T(8,128)(2,1)} custom-call(s32[32]{0:T(128)} %pad_add_fusion.1.order_ref, bf16[4,640,512]{2,1,0:T(8,128)(2,1)} %bitcast.46), custom_call_target="tpu_custom_call" | custom-call | bytes 20971520 | tf_op jit(solution)/shard_map/turn/pallas_call | solution.py:160
  14.5 17.6 %wgrad.3 = (bf16[6,256,512]{2,1,0:T(8,128)(2,1)}, bf16[6,256,512]{2,1,0:T(8,128)(2,1)}) custom-call(bf16[3,512,2560]{2,1,0:T(8,128)(2,1)} %turn.1.a.a_ref, bf16[2560,512]{1,0:T(8,128)(2,1)} %bitcast.53, bf16[640,512]{1,0:T(8,128)(2,1)} %copy-done.10, bf16[640,512]{1,0:T(8,128)(2,1)} %copy-done.11), custom_call_target="tpu_custom_call" | custom-call | flops 8053063680 | bytes 13631488 | tf_op jit(solution)/shard_map/wgrad/pallas_call | solution.py:224
  32.2 8.1 %collective-permute-start.21 = (bf16[6,256,512]{2,1,0:T(8,128)(2,1)}, bf16[6,256,512]{2,1,0:T(8,128)(2,1)S(1)}, u32[]{:S(2)}, u32[]{:S(2)}) collective-permute-start(bf16[6,256,512]{2,1,0:T(8,128)(2,1)} %get-tuple-element.80), channel_id=1, source_target_pairs={{0,1},{1,0},{2,3},{3,2},{4,5},{5,4},{6,7},{7,6},{8,9},{9,8},{10,11... | collective-permute-start | bytes 4718600 | tf_op jit(solution)/shard_map/ppermute | solution.py:480
  40.3 16.5 %bev_inner.1 = (bf16[2,640,512]{2,1,0:T(8,128)(2,1)}, f32[2,640,512]{2,1,0:T(8,128)}) custom-call(bf16[4,640,512]{2,1,0:T(8,128)(2,1)} %bitcast.54, bf16[3,3,512,512]{3,2,1,0:T(8,128)(2,1)} %bitcast.42), custom_call_target="tpu_custom_call" | custom-call | flops 10066329600 | bytes 9961472 | tf_op jit(solution)/shard_map/bev_inner/pallas_call | solution.py:83
  56.7 6.5 %bev_edge.1 = bf16[2,640,512]{2,1,0:T(8,128)(2,1)} custom-call(f32[2,640,512]{2,1,0:T(8,128)} %get-tuple-element.53.edge_ref, bf16[640,512]{1,0:T(8,128)(2,1)} %copy-done.10, bf16[640,512]{1,0:T(8,128)(2,1)} %copy-done.11, bf16[3,3,512,512]{3,2,1,0:T(8,128)(2,1)} %bitcast.43, bf16[3,3,512,512]{3,2,1,0:T(8,128)(2,1)} %bitcast.44), custom_call_target="tpu_custom_call" | custom-call | flops 2013265920 | bytes 8388608 | tf_op jit(solution)/shard_map/bev_edge/pallas_call | solution.py:119
  65.0 4.9 %fold.24 = (bf16[6,128,512]{2,1,0:T(8,128)(2,1)}, bf16[6,128,512]{2,1,0:T(8,128)(2,1)}) custom-call(bf16[6,256,512]{2,1,0:T(8,128)(2,1)} %get-tuple-element.79.keep_ref, bf16[6,256,512]{2,1,0:T(8,128)(2,1)} %copy-done.1), custom_call_target="tpu_custom_call" | custom-call | bytes 4718592 | tf_op jit(solution)/shard_map/fold/pallas_call | solution.py:248
  71.4 9.6 %wgrad.2 = (bf16[3,256,512]{2,1,0:T(8,128)(2,1)}, bf16[3,256,512]{2,1,0:T(8,128)(2,1)}) custom-call(bf16[3,512,2560]{2,1,0:T(8,128)(2,1)} %turn.1.a.a_ref, bf16[2560,512]{1,0:T(8,128)(2,1)} %bitcast.55), custom_call_target="tpu_custom_call" | custom-call | flops 4026531840 | bytes 12058624 | tf_op jit(solution)/shard_map/wgrad/pallas_call | solution.py:224
  84.5 13.4 %warp_pieces.1 = (bf16[4,2,128,512]{3,2,1,0:T(8,128)(2,1)}, bf16[4,2,128,512]{3,2,1,0:T(8,128)(2,1)}, bf16[4,2,128,512]{3,2,1,0:T(8,128)(2,1)}, bf16[4,2,128,512]{3,2,1,0:T(8,128)(2,1)}) custom-call(s32[1]{0:T(128)} %bitcast.info_ref, s32[640]{0:T(1024)} %reduce.route_ref, s32[80,128]{1,0:T(8,128)} %get-tuple-element.111.off_ref, ...), custom_call_target="tpu_custom_call" | custom-call | flops 1073741824 | bytes 9437184 | tf_op jit(solution)/shard_map/warp_pieces/pallas_call | solution.py:398
  98.0 1.8 collective-permute-start.8
  100.9 4.4 %fold.25 = (bf16[6,64,512]{2,1,0:T(8,128)(2,1)}, bf16[6,64,512]{2,1,0:T(8,128)(2,1)}) custom-call(bf16[6,128,512]{2,1,0:T(8,128)(2,1)} %get-tuple-element.81.keep_ref, bf16[6,128,512]{2,1,0:T(8,128)(2,1)} %copy-done.8), custom_call_target="tpu_custom_call" | custom-call | bytes 2359296 | tf_op jit(solution)/shard_map/fold/pallas_call | solution.py:248
  107.1 21.4 %collective-permute-done.23.recv_ref = bf16[6,64,512]{2,1,0:T(8,128)(2,1)S(1)} collective-permute-done((bf16[6,64,512]{2,1,0:T(8,128)(2,1)}, bf16[6,64,512]{2,1,0:T(8,128)(2,1)S(1)}, u32[]{:S(2)}, u32[]{:S(2)}) %collective-permute-start.23) | collective-permute-done | bytes 393248 | tf_op jit(solution)/shard_map/ppermute | solution.py:480
  129.2 4.0 fold.26
  133.2 1.8 collective-permute-start.24
  135.0 4.0 collective-permute-done.24.recv_ref
  139.8 3.6 fold.27
  143.4 2.8 collective-permute-start.25
  147.1 3.1 fold.20
  153.1 2.7 fold.18
  155.8 2.4 collective-permute-start.9
  159.2 2.6 fold.16
  162.6 2.8 fold.21
  166.5 1.8 collective-permute-start.27
  168.3 2.9 collective-permute-done.13.recv_ref
  171.9 2.5 fold.22
  174.3 2.0 collective-permute-start.14
  177.3 1.9 collective-permute-done.14.recv_ref
  179.9 2.2 fold.23
  182.1 2.7 collective-permute-start.15
  185.6 2.1 fold.19
  188.7 2.1 fold.17
  190.7 2.7 collective-permute-start.7
  193.4 2.8 image_slope.1
  196.6 3.6 collective-permute-done.10
  200.2 3.3 collective-permute-done.7
  204.2 3.4 image_layer.1
  207.7 2.0 collective-permute-start.29
  215.5 7.8 %collective-permute-done.32.recv_ref = bf16[1,128,512]{2,1,0:T(8,128)(2,1)S(1)} collective-permute-done((bf16[1,128,512]{2,1,0:T(8,128)(2,1)}, bf16[1,128,512]{2,1,0:T(8,128)(2,1)S(1)}, u32[]{:S(2)}, u32[]{:S(2)}) %collective-permute-start.32) | collective-permute-done | bytes 131104 | tf_op jit(solution)/shard_map/ppermute | solution.py:480
  225.6 2.3 collective-permute-start.33
  227.9 2.4 collective-permute-done.33.recv_ref
  232.5 4.1 collective-permute-done.34.recv_ref
  240.5 2.9 collective-permute-done.35
  243.6 4.6 %collective-permute-done.36 = bf16[1,16,512]{2,1,0:T(8,128)(2,1)S(1)} collective-permute-done((bf16[1,16,512]{2,1,0:T(8,128)(2,1)S(1)}, bf16[1,16,512]{2,1,0:T(8,128)(2,1)S(1)}, u32[]{:S(2)}, u32[]{:S(2)}) %collective-permute-start.36) | collective-permute-done | bytes 16416 | tf_op jit(solution)/shard_map/ppermute | solution.py:480
  248.3 3.8 collective-permute-done.37
  252.1 2.2 collective-permute-start.38
  254.2 2.9 collective-permute-done.38
  258.7 3.4 collective-permute-done.39
  265.6 160.6 %place_parts.1 = (bf16[9,512,512]{2,1,0:T(8,128)(2,1)}, bf16[512,512]{1,0:T(8,128)(2,1)}) custom-call(s32[32]{0:T(128)} %pad_add_fusion.1.order_ref, bf16[3,256,512]{2,1,0:T(8,128)(2,1)} %copy-done.6, bf16[3,256,512]{2,1,0:T(8,128)(2,1)} %copy-done.9, bf16[6,256,512]{2,1,0:T(8,128)(2,1)} %copy-done, bf16[6,256,512]{2,1,0:T(8,128)(2,1)} %copy-done.2, ...), custom_call_target="tpu_custom_call" | custom-call | bytes 10485760 | tf_op jit(solution)/shard_map/place_parts/pallas_call | solution.py:582
  (163 shorter events, 46.8 us)
Async XLA Ops:
  2.0 11.4 %collective-permute-start.1 = (bf16[640,512]{1,0:T(8,128)(2,1)S(1)}, bf16[640,512]{1,0:T(8,128)(2,1)S(1)}, u32[]{:S(2)}, u32[]{:S(2)}) collective-permute-start(bf16[640,512]{1,0:T(8,128)(2,1)S(1)} %get-tuple-element.108), channel_id=1, source_target_pairs={{0,1},{1,2},{2,3},{3,4},{4,5},{5,6},{6,7},{7,8},{8,9},{9,10},{10,1... | collective-permute-start | bytes 1966088 | tf_op jit(solution)/shard_map/ppermute | solution.py:616
  4.4 9.0 %collective-permute-start.2 = (bf16[640,512]{1,0:T(8,128)(2,1)S(1)}, bf16[640,512]{1,0:T(8,128)(2,1)S(1)}, u32[]{:S(2)}, u32[]{:S(2)}) collective-permute-start(bf16[640,512]{1,0:T(8,128)(2,1)S(1)} %get-tuple-element.107), channel_id=1, source_target_pairs={{1,0},{2,1},{3,2},{4,3},{5,4},{6,5},{7,6},{8,7},{9,8},{10,9},{11,1... | collective-permute-start | bytes 1966088 | tf_op jit(solution)/shard_map/ppermute | solution.py:617
  32.2 31.7 %collective-permute-start.21 = (bf16[6,256,512]{2,1,0:T(8,128)(2,1)}, bf16[6,256,512]{2,1,0:T(8,128)(2,1)S(1)}, u32[]{:S(2)}, u32[]{:S(2)}) collective-permute-start(bf16[6,256,512]{2,1,0:T(8,128)(2,1)} %get-tuple-element.80), channel_id=1, source_target_pairs={{0,1},{1,0},{2,3},{3,2},{4,5},{5,4},{6,7},{7,6},{8,9},{9,8},{10,11... | collective-permute-start | bytes 4718600 | tf_op jit(solution)/shard_map/ppermute | solution.py:480
  56.7 26.8 %collective-permute-start.3 = (bf16[2,640,512]{2,1,0:T(8,128)(2,1)}, bf16[2,640,512]{2,1,0:T(8,128)(2,1)S(1)}, u32[]{:S(2)}, u32[]{:S(2)}) collective-permute-start(bf16[2,640,512]{2,1,0:T(8,128)(2,1)} %get-tuple-element.52), channel_id=1, source_target_pairs={{0,1},{1,0},{2,3},{3,2},{4,5},{5,4},{6,7},{7,6},{8,9},{9,8},{10,11... | collective-permute-start | bytes 3932168 | tf_op jit(solution)/shard_map/ppermute | solution.py:626
  56.7 7.0 %copy-start.31 = (s32[1,2560]{1,0:T(1,128)S(1)}, s32[1,2560]{1,0:T(1,128)}, u32[]{:S(2)}) copy-start(s32[1,2560]{1,0:T(1,128)} %param.17) | copy-start | bytes 30724
  56.7 7.0 %copy-start.32 = (s32[1,2560]{1,0:T(1,128)S(1)}, s32[1,2560]{1,0:T(1,128)}, u32[]{:S(2)}) copy-start(s32[1,2560]{1,0:T(1,128)} %param.16) | copy-start | bytes 30724
  63.2 20.3 %collective-permute-start.4 = (bf16[2,640,512]{2,1,0:T(8,128)(2,1)}, bf16[2,640,512]{2,1,0:T(8,128)(2,1)}, u32[]{:S(2)}, u32[]{:S(2)}) collective-permute-start(bf16[2,640,512]{2,1,0:T(8,128)(2,1)} %bev_edge.1), channel_id=1, source_target_pairs={{0,1},{1,0},{2,3},{3,2},{4,5},{5,4},{6,7},{7,6},{8,9},{9,8},{10,11... | collective-permute-start | bytes 3932168 | tf_op jit(solution)/shard_map/ppermute | solution.py:629
  63.9 18.9 %collective-permute-start = (s32[3,40,64]{2,1,0:T(8,128)S(1)}, s32[3,40,64]{2,1,0:T(8,128)S(1)}, u32[]{:S(2)}, u32[]{:S(2)}) collective-permute-start(s32[3,40,64]{2,1,0:T(8,128)S(1)} %reshape.80), channel_id=1, source_target_pairs={{0,1},{1,0},{2,3},{3,2},{4,5},{5,4},{6,7},{7,6},{8,9},{9,8},{10,11... | collective-permute-start | bytes 92168 | tf_op jit(solution)/shard_map/ppermute | solution.py:621
  69.9 12.2 %copy-start.33 = (s32[1,640]{1,0:T(1,128)S(1)}, s32[1,640]{1,0:T(1,128)}, u32[]{:S(2)}) copy-start(s32[1,640]{1,0:T(1,128)} %param.15) | copy-start | bytes 7684
  69.9 30.2 %collective-permute-start.22 = (bf16[6,128,512]{2,1,0:T(8,128)(2,1)}, bf16[6,128,512]{2,1,0:T(8,128)(2,1)S(1)}, u32[]{:S(2)}, u32[]{:S(2)}) collective-permute-start(bf16[6,128,512]{2,1,0:T(8,128)(2,1)} %get-tuple-element.82), channel_id=1, source_target_pairs={{0,16},{1,3},{2,18},{3,1},{4,20},{5,7},{6,22},{7,5},{8,24},{9,11},... | collective-permute-start | bytes 2359304 | tf_op jit(solution)/shard_map/ppermute | solution.py:480
  81.0 65.2 %collective-permute-start.11 = (bf16[3,256,512]{2,1,0:T(8,128)(2,1)}, bf16[3,256,512]{2,1,0:T(8,128)(2,1)S(1)}, u32[]{:S(2)}, u32[]{:S(2)}) collective-permute-start(bf16[3,256,512]{2,1,0:T(8,128)(2,1)} %get-tuple-element.70), channel_id=1, source_target_pairs={{0,1},{1,0},{2,3},{3,2},{4,5},{5,4},{6,7},{7,6},{8,9},{9,8},{10,11... | collective-permute-start | bytes 2359304 | tf_op jit(solution)/shard_map/ppermute | solution.py:480
  98.0 54.2 %collective-permute-start.8 = (bf16[4,2,128,512]{3,2,1,0:T(8,128)(2,1)}, bf16[4,2,128,512]{3,2,1,0:T(8,128)(2,1)S(1)}, u32[]{:S(2)}, u32[]{:S(2)}) collective-permute-start(bf16[4,2,128,512]{3,2,1,0:T(8,128)(2,1)} %get-tuple-element.61), channel_id=1, source_target_pairs={{0,2},{1,5},{2,0},{3,7},{4,6},{5,1},{6,4},{7,3},{8,10},{9,13},{10,... | collective-permute-start | bytes 3145736 | tf_op jit(solution)/shard_map/ppermute | solution.py:480
  99.8 58.4 %collective-permute-start.5 = (bf16[4,2,128,512]{3,2,1,0:T(8,128)(2,1)}, bf16[4,2,128,512]{3,2,1,0:T(8,128)(2,1)S(1)}, u32[]{:S(2)}, u32[]{:S(2)}) collective-permute-start(bf16[4,2,128,512]{3,2,1,0:T(8,128)(2,1)} %get-tuple-element.55), channel_id=1, source_target_pairs={{0,2},{1,5},{2,0},{3,7},{4,6},{5,1},{6,4},{7,3},{8,10},{9,13},{10,... | collective-permute-start | bytes 3145736 | tf_op jit(solution)/shard_map/ppermute | solution.py:480
  105.4 23.1 %collective-permute-start.23 = (bf16[6,64,512]{2,1,0:T(8,128)(2,1)}, bf16[6,64,512]{2,1,0:T(8,128)(2,1)S(1)}, u32[]{:S(2)}, u32[]{:S(2)}) collective-permute-start(bf16[6,64,512]{2,1,0:T(8,128)(2,1)} %get-tuple-element.84), channel_id=1, source_target_pairs={{0,2},{1,17},{2,0},{3,19},{4,6},{5,21},{6,4},{7,23},{8,10},{9,25},... | collective-permute-start | bytes 1179656 | tf_op jit(solution)/shard_map/ppermute | solution.py:480
  133.2 5.9 %collective-permute-start.24 = (bf16[6,32,512]{2,1,0:T(8,128)(2,1)}, bf16[6,32,512]{2,1,0:T(8,128)(2,1)S(1)}, u32[]{:S(2)}, u32[]{:S(2)}) collective-permute-start(bf16[6,32,512]{2,1,0:T(8,128)(2,1)} %get-tuple-element.86), channel_id=1, source_target_pairs={{0,4},{1,5},{2,6},{3,7},{4,0},{5,1},{6,2},{7,3},{8,12},{9,13},{10,... | collective-permute-start | bytes 589832 | tf_op jit(solution)/shard_map/ppermute | solution.py:480
  143.4 8.0 %copy-start.25 = (bf16[6,16,512]{2,1,0:T(8,128)(2,1)S(1)}, bf16[6,16,512]{2,1,0:T(8,128)(2,1)}, u32[]{:S(2)}) copy-start(bf16[6,16,512]{2,1,0:T(8,128)(2,1)} %get-tuple-element.87) | copy-start | bytes 294916
  143.4 8.0 %collective-permute-start.25 = (bf16[6,16,512]{2,1,0:T(8,128)(2,1)}, bf16[6,16,512]{2,1,0:T(8,128)(2,1)S(1)}, u32[]{:S(2)}, u32[]{:S(2)}) collective-permute-start(bf16[6,16,512]{2,1,0:T(8,128)(2,1)} %get-tuple-element.88), channel_id=1, source_target_pairs={{0,8},{1,9},{2,10},{3,11},{4,12},{5,13},{6,14},{7,15},{8,0},{9,1},... | collective-permute-start | bytes 294920 | tf_op jit(solution)/shard_map/ppermute | solution.py:480
  150.1 11.7 %collective-permute-start.12 = (bf16[3,128,512]{2,1,0:T(8,128)(2,1)}, bf16[3,128,512]{2,1,0:T(8,128)(2,1)S(1)}, u32[]{:S(2)}, u32[]{:S(2)}) collective-permute-start(bf16[3,128,512]{2,1,0:T(8,128)(2,1)} %get-tuple-element.72), channel_id=1, source_target_pairs={{0,16},{1,3},{2,18},{3,1},{4,20},{5,7},{6,22},{7,5},{8,24},{9,11},... | collective-permute-start | bytes 1179656 | tf_op jit(solution)/shard_map/ppermute | solution.py:480
  151.4 15.0 %collective-permute-start.26 = (bf16[6,16,512]{2,1,0:T(8,128)(2,1)S(1)}, bf16[6,16,512]{2,1,0:T(8,128)(2,1)S(1)}, u32[]{:S(2)}, u32[]{:S(2)}) collective-permute-start(bf16[6,16,512]{2,1,0:T(8,128)(2,1)S(1)} %get-tuple-element.104), channel_id=1, source_target_pairs={{0,8},{1,9},{2,10},{3,11},{4,12},{5,13},{6,14},{7,15},{8,0},{9,1},... | collective-permute-start | bytes 294920 | tf_op jit(solution)/shard_map/ppermute | solution.py:480
  155.8 29.0 %collective-permute-start.9 = (bf16[2,2,128,512]{3,2,1,0:T(8,128)(2,1)}, bf16[2,2,128,512]{3,2,1,0:T(8,128)(2,1)S(1)}, u32[]{:S(2)}, u32[]{:S(2)}) collective-permute-start(bf16[2,2,128,512]{3,2,1,0:T(8,128)(2,1)} %bitcast.65), channel_id=1, source_target_pairs={{0,4},{1,3},{2,6},{3,1},{4,0},{5,7},{6,2},{7,5},{8,12},{9,11},{10,... | collective-permute-start | bytes 1572872 | tf_op jit(solution)/shard_map/ppermute | solution.py:480
  161.8 26.1 %collective-permute-start.6 = (bf16[2,2,128,512]{3,2,1,0:T(8,128)(2,1)}, bf16[2,2,128,512]{3,2,1,0:T(8,128)(2,1)S(1)}, u32[]{:S(2)}, u32[]{:S(2)}) collective-permute-start(bf16[2,2,128,512]{3,2,1,0:T(8,128)(2,1)} %bitcast.66), channel_id=1, source_target_pairs={{0,4},{1,3},{2,6},{3,1},{4,0},{5,7},{6,2},{7,5},{8,12},{9,11},{10,... | collective-permute-start | bytes 1572872 | tf_op jit(solution)/shard_map/ppermute | solution.py:480
  165.3 5.9 %collective-permute-start.13 = (bf16[3,64,512]{2,1,0:T(8,128)(2,1)}, bf16[3,64,512]{2,1,0:T(8,128)(2,1)S(1)}, u32[]{:S(2)}, u32[]{:S(2)}) collective-permute-start(bf16[3,64,512]{2,1,0:T(8,128)(2,1)} %get-tuple-element.74), channel_id=1, source_target_pairs={{0,2},{1,17},{2,0},{3,19},{4,6},{5,21},{6,4},{7,23},{8,10},{9,25},... | collective-permute-start | bytes 589832 | tf_op jit(solution)/shard_map/ppermute | solution.py:480
  166.5 9.9 %collective-permute-start.27 = (bf16[6,32,512]{2,1,0:T(8,128)(2,1)S(1)}, bf16[6,32,512]{2,1,0:T(8,128)(2,1)S(1)}, u32[]{:S(2)}, u32[]{:S(2)}) collective-permute-start(bf16[6,32,512]{2,1,0:T(8,128)(2,1)S(1)} %pad_maximum_fusion.4), channel_id=1, source_target_pairs={{0,4},{1,5},{2,6},{3,7},{4,0},{5,1},{6,2},{7,3},{8,12},{9,13},{10,... | collective-permute-start | bytes 589832 | tf_op jit(solution)/shard_map/ppermute | solution.py:480
  174.3 4.9 %collective-permute-start.14 = (bf16[3,32,512]{2,1,0:T(8,128)(2,1)}, bf16[3,32,512]{2,1,0:T(8,128)(2,1)S(1)}, u32[]{:S(2)}, u32[]{:S(2)}) collective-permute-start(bf16[3,32,512]{2,1,0:T(8,128)(2,1)} %get-tuple-element.76), channel_id=1, source_target_pairs={{0,4},{1,5},{2,6},{3,7},{4,0},{5,1},{6,2},{7,3},{8,12},{9,13},{10,... | collective-permute-start | bytes 294920 | tf_op jit(solution)/shard_map/ppermute | solution.py:480
  176.4 31.2 %collective-permute-start.28 = (bf16[6,64,512]{2,1,0:T(8,128)(2,1)S(1)}, bf16[6,64,512]{2,1,0:T(8,128)(2,1)S(1)}, u32[]{:S(2)}, u32[]{:S(2)}) collective-permute-start(bf16[6,64,512]{2,1,0:T(8,128)(2,1)S(1)} %pad_maximum_fusion.2), channel_id=1, source_target_pairs={{0,2},{1,17},{2,0},{3,19},{4,6},{5,21},{6,4},{7,23},{8,10},{9,25},... | collective-permute-start | bytes 1179656 | tf_op jit(solution)/shard_map/ppermute | solution.py:480
  182.1 14.2 %collective-permute-start.15 = (bf16[3,16,512]{2,1,0:T(8,128)(2,1)}, bf16[3,16,512]{2,1,0:T(8,128)(2,1)S(1)}, u32[]{:S(2)}, u32[]{:S(2)}) collective-permute-start(bf16[3,16,512]{2,1,0:T(8,128)(2,1)} %get-tuple-element.78), channel_id=1, source_target_pairs={{0,8},{1,9},{2,10},{3,11},{4,12},{5,13},{6,14},{7,15},{8,0},{9,1},... | collective-permute-start | bytes 147464 | tf_op jit(solution)/shard_map/ppermute | solution.py:480
  185.6 10.7 %copy-start.27 = (bf16[3,16,512]{2,1,0:T(8,128)(2,1)S(1)}, bf16[3,16,512]{2,1,0:T(8,128)(2,1)}, u32[]{:S(2)}) copy-start(bf16[3,16,512]{2,1,0:T(8,128)(2,1)} %get-tuple-element.77) | copy-start | bytes 147460
  187.7 12.5 %collective-permute-start.10 = (bf16[1,2,128,512]{3,2,1,0:T(8,128)(2,1)}, bf16[1,2,128,512]{3,2,1,0:T(8,128)(2,1)S(1)}, u32[]{:S(2)}, u32[]{:S(2)}) collective-permute-start(bf16[1,2,128,512]{3,2,1,0:T(8,128)(2,1)} %bitcast.67), channel_id=1, source_target_pairs={{0,8},{1,9},{2,10},{3,11},{4,12},{5,13},{6,14},{7,15},{8,0},{9,1},... | collective-permute-start | bytes 786440 | tf_op jit(solution)/shard_map/ppermute | solution.py:480
  190.7 12.8 %collective-permute-start.7 = (bf16[1,2,128,512]{3,2,1,0:T(8,128)(2,1)}, bf16[1,2,128,512]{3,2,1,0:T(8,128)(2,1)S(1)}, u32[]{:S(2)}, u32[]{:S(2)}) collective-permute-start(bf16[1,2,128,512]{3,2,1,0:T(8,128)(2,1)} %bitcast.68), channel_id=1, source_target_pairs={{0,8},{1,9},{2,10},{3,11},{4,12},{5,13},{6,14},{7,15},{8,0},{9,1},... | collective-permute-start | bytes 786440 | tf_op jit(solution)/shard_map/ppermute | solution.py:480
  196.3 13.4 %collective-permute-start.16 = (bf16[3,16,512]{2,1,0:T(8,128)(2,1)S(1)}, bf16[3,16,512]{2,1,0:T(8,128)(2,1)S(1)}, u32[]{:S(2)}, u32[]{:S(2)}) collective-permute-start(bf16[3,16,512]{2,1,0:T(8,128)(2,1)S(1)} %get-tuple-element.106), channel_id=1, source_target_pairs={{0,8},{1,9},{2,10},{3,11},{4,12},{5,13},{6,14},{7,15},{8,0},{9,1},... | collective-permute-start | bytes 147464 | tf_op jit(solution)/shard_map/ppermute | solution.py:480
  207.6 2.2 collective-permute-start.31
  207.7 30.9 %collective-permute-start.29 = (bf16[6,128,512]{2,1,0:T(8,128)(2,1)S(1)}, bf16[6,128,512]{2,1,0:T(8,128)(2,1)S(1)}, u32[]{:S(2)}, u32[]{:S(2)}) collective-permute-start(bf16[6,128,512]{2,1,0:T(8,128)(2,1)S(1)} %pad_maximum_fusion), channel_id=1, source_target_pairs={{0,16},{1,3},{2,18},{3,1},{4,20},{5,7},{6,22},{7,5},{8,24},{9,11},... | collective-permute-start | bytes 2359304 | tf_op jit(solution)/shard_map/ppermute | solution.py:480
  209.7 5.4 %collective-permute-start.17 = (bf16[3,32,512]{2,1,0:T(8,128)(2,1)S(1)}, bf16[3,32,512]{2,1,0:T(8,128)(2,1)S(1)}, u32[]{:S(2)}, u32[]{:S(2)}) collective-permute-start(bf16[3,32,512]{2,1,0:T(8,128)(2,1)S(1)} %pad_maximum_fusion.6), channel_id=1, source_target_pairs={{0,4},{1,5},{2,6},{3,7},{4,0},{5,1},{6,2},{7,3},{8,12},{9,13},{10,... | collective-permute-start | bytes 294920 | tf_op jit(solution)/shard_map/ppermute | solution.py:480
  212.3 11.0 %collective-permute-start.32 = (bf16[1,128,512]{2,1,0:T(8,128)(2,1)}, bf16[1,128,512]{2,1,0:T(8,128)(2,1)S(1)}, u32[]{:S(2)}, u32[]{:S(2)}) collective-permute-start(bf16[1,128,512]{2,1,0:T(8,128)(2,1)} %get-tuple-element.92), channel_id=1, source_target_pairs={{0,16},{1,3},{2,18},{3,1},{4,20},{5,7},{6,22},{7,5},{8,24},{9,11},... | collective-permute-start | bytes 393224 | tf_op jit(solution)/shard_map/ppermute | solution.py:480
  215.1 23.7 %collective-permute-start.18 = (bf16[3,64,512]{2,1,0:T(8,128)(2,1)S(1)}, bf16[3,64,512]{2,1,0:T(8,128)(2,1)S(1)}, u32[]{:S(2)}, u32[]{:S(2)}) collective-permute-start(bf16[3,64,512]{2,1,0:T(8,128)(2,1)S(1)} %pad_maximum_fusion.3), channel_id=1, source_target_pairs={{0,2},{1,17},{2,0},{3,19},{4,6},{5,21},{6,4},{7,23},{8,10},{9,25},... | collective-permute-start | bytes 589832 | tf_op jit(solution)/shard_map/ppermute | solution.py:480
  225.6 4.8 %collective-permute-start.33 = (bf16[1,64,512]{2,1,0:T(8,128)(2,1)}, bf16[1,64,512]{2,1,0:T(8,128)(2,1)S(1)}, u32[]{:S(2)}, u32[]{:S(2)}) collective-permute-start(bf16[1,64,512]{2,1,0:T(8,128)(2,1)} %get-tuple-element.94), channel_id=1, source_target_pairs={{0,2},{1,17},{2,0},{3,19},{4,6},{5,21},{6,4},{7,23},{8,10},{9,25},... | collective-permute-start | bytes 196616 | tf_op jit(solution)/shard_map/ppermute | solution.py:480
  232.4 4.1 collective-permute-start.34
  238.6 4.8 %collective-permute-start.35 = (bf16[1,16,512]{2,1,0:T(8,128)(2,1)}, bf16[1,16,512]{2,1,0:T(8,128)(2,1)S(1)}, u32[]{:S(2)}, u32[]{:S(2)}) collective-permute-start(bf16[1,16,512]{2,1,0:T(8,128)(2,1)} %get-tuple-element.98), channel_id=1, source_target_pairs={{0,8},{1,9},{2,10},{3,11},{4,12},{5,13},{6,14},{7,15},{8,0},{9,1},... | collective-permute-start | bytes 49160 | tf_op jit(solution)/shard_map/ppermute | solution.py:480
  238.7 25.1 %copy-start = (bf16[6,256,512]{2,1,0:T(8,128)(2,1)}, bf16[6,256,512]{2,1,0:T(8,128)(2,1)S(1)}, u32[]{:S(2)}) copy-start(bf16[6,256,512]{2,1,0:T(8,128)(2,1)S(1)} %constant_dynamic-update-slice_fusion.5.refs_2_) | copy-start | bytes 4718596
  238.7 25.1 %collective-permute-start.30 = (bf16[6,256,512]{2,1,0:T(8,128)(2,1)S(1)}, bf16[6,256,512]{2,1,0:T(8,128)(2,1)S(1)}, u32[]{:S(2)}, u32[]{:S(2)}) collective-permute-start(bf16[6,256,512]{2,1,0:T(8,128)(2,1)S(1)} %constant_dynamic-update-slice_fusion.5.refs_2_), channel_id=1, source_target_pairs={{0,1},{1,0},{2,3},{3,2},{4,5},{5,4},{6,7},{7,6},{8,9},{9,8},{10,11... | collective-permute-start | bytes 4718600 | tf_op jit(solution)/shard_map/ppermute | solution.py:480
  238.8 9.3 %collective-permute-start.19 = (bf16[3,128,512]{2,1,0:T(8,128)(2,1)S(1)}, bf16[3,128,512]{2,1,0:T(8,128)(2,1)S(1)}, u32[]{:S(2)}, u32[]{:S(2)}) collective-permute-start(bf16[3,128,512]{2,1,0:T(8,128)(2,1)S(1)} %pad_maximum_fusion.1), channel_id=1, source_target_pairs={{0,16},{1,3},{2,18},{3,1},{4,20},{5,7},{6,22},{7,5},{8,24},{9,11},... | collective-permute-start | bytes 1179656 | tf_op jit(solution)/shard_map/ppermute | solution.py:480
  243.4 4.7 %collective-permute-start.36 = (bf16[1,16,512]{2,1,0:T(8,128)(2,1)S(1)}, bf16[1,16,512]{2,1,0:T(8,128)(2,1)S(1)}, u32[]{:S(2)}, u32[]{:S(2)}) collective-permute-start(bf16[1,16,512]{2,1,0:T(8,128)(2,1)S(1)} %get-tuple-element.102), channel_id=1, source_target_pairs={{0,8},{1,9},{2,10},{3,11},{4,12},{5,13},{6,14},{7,15},{8,0},{9,1},... | collective-permute-start | bytes 49160 | tf_op jit(solution)/shard_map/ppermute | solution.py:480
  248.1 3.9 collective-permute-start.37
  248.2 15.6 %copy-start.6 = (bf16[3,256,512]{2,1,0:T(8,128)(2,1)}, bf16[3,256,512]{2,1,0:T(8,128)(2,1)S(1)}, u32[]{:S(2)}) copy-start(bf16[3,256,512]{2,1,0:T(8,128)(2,1)S(1)} %constant_dynamic-update-slice_fusion.refs_0_) | copy-start | bytes 2359300
  248.2 14.1 %collective-permute-start.20 = (bf16[3,256,512]{2,1,0:T(8,128)(2,1)S(1)}, bf16[3,256,512]{2,1,0:T(8,128)(2,1)S(1)}, u32[]{:S(2)}, u32[]{:S(2)}) collective-permute-start(bf16[3,256,512]{2,1,0:T(8,128)(2,1)S(1)} %constant_dynamic-update-slice_fusion.refs_0_), channel_id=1, source_target_pairs={{0,1},{1,0},{2,3},{3,2},{4,5},{5,4},{6,7},{7,6},{8,9},{9,8},{10,11... | collective-permute-start | bytes 2359304 | tf_op jit(solution)/shard_map/ppermute | solution.py:480
  252.1 5.0 %collective-permute-start.38 = (bf16[1,64,512]{2,1,0:T(8,128)(2,1)S(1)}, bf16[1,64,512]{2,1,0:T(8,128)(2,1)S(1)}, u32[]{:S(2)}, u32[]{:S(2)}) collective-permute-start(bf16[1,64,512]{2,1,0:T(8,128)(2,1)S(1)} %pad_maximum_fusion.7), channel_id=1, source_target_pairs={{0,2},{1,17},{2,0},{3,19},{4,6},{5,21},{6,4},{7,23},{8,10},{9,25},... | collective-permute-start | bytes 196616 | tf_op jit(solution)/shard_map/ppermute | solution.py:480
  257.1 5.0 %collective-permute-start.39 = (bf16[1,128,512]{2,1,0:T(8,128)(2,1)S(1)}, bf16[1,128,512]{2,1,0:T(8,128)(2,1)S(1)}, u32[]{:S(2)}, u32[]{:S(2)}) collective-permute-start(bf16[1,128,512]{2,1,0:T(8,128)(2,1)S(1)} %pad_maximum_fusion.5), channel_id=1, source_target_pairs={{0,16},{1,3},{2,18},{3,1},{4,20},{5,7},{6,22},{7,5},{8,24},{9,11},... | collective-permute-start | bytes 393224 | tf_op jit(solution)/shard_map/ppermute | solution.py:480
  262.2 1.6 collective-permute-start.40
  (29 other events, 46.7 us)

commit v2 on v1

--- a/solution.py
+++ b/solution.py
@@ -56,12 +56,9 @@
     for order, j in enumerate((1, 0, 2)):
         @pl.when(step == order)
         def _(j=j, order=order):
-            row_terms(0, (0, 1), j, order == 0)
-            row_terms(rows - 1, (1, 2), j, order == 0)
-
-            @pl.loop(1, rows - 1)
-            def _(u):
-                row_terms(u, (0, 1, 2), j, order == 0)
+            for u in range(rows):
+                taps = (0, 1) if u == 0 else (1, 2) if u == rows - 1 else (0, 1, 2)
+                row_terms(u, taps, j, order == 0)
 
     @pl.when(step == 2)
     def _():
@@ -135,126 +132,76 @@
     )(edge, low, high, weight, weight)
 
 
-def turn_kernel(parts, order_ref, a_ref, out_ref, wide_ref):
-    chans, cols = wide_ref.shape
-    size = chans // parts
-    flat = a_ref[0].astype(F32).T
-    place = lax.broadcasted_iota(jnp.int32, flat.shape, 1)
-    for j in range(3):
-        if j == 0:
-            moved = jnp.where(place == 0, 0.0, pltpu.roll(flat, 1, 1))
-        elif j == 1:
-            moved = flat
-        else:
-            moved = jnp.where(place == cols - 1, 0.0, pltpu.roll(flat, cols - 1, 1))
-        wide_ref[...] = moved
-
-        for s in range(parts):
-            source = pl.multiple_of(order_ref[s] * size, size)
-            out_ref[j, s * size : (s + 1) * size, :] = wide_ref[pl.ds(source, size), :].astype(BF16)
-
-
-def turn(act, order):
-    rows, cols, chans = act.shape
-    parts = order.shape[0]
+def tn_dot(a, b):
+    return lax.dot_general(a, b, (((0,), (0,)), ((), ())), preferred_element_type=F32)
+
+
+def spread(value_ref, order_ref, keep_ref, send_ref):
+    parts = order_ref.shape[0]
+    size = value_ref.shape[0] // parts
+    for half, target in enumerate((keep_ref, send_ref)):
+        for s in range(parts // 2):
+            source = pl.multiple_of(order_ref[half * (parts // 2) + s] * size, size)
+            target[0, s * size : (s + 1) * size, :] = value_ref[pl.ds(source, size), :].astype(BF16)
+
+
+def wgrad_kernel(taps, halo, order_ref, a_ref, g_ref, *refs):
+    if halo:
+        low_ref, high_ref = refs[:2]
+        refs = refs[2:]
+    keep_ref, send_ref, moved_ref, wide_ref = refs[-4:]
+    rows, cols, chans = a_ref.shape
+    total = rows * cols
+    step = pl.program_id(0)
+    last = None
+    for t, (i, j) in enumerate(taps):
+        fresh = j != last
+        last = j
+
+        @pl.when(step == t)
+        def _(i=i, j=j, fresh=fresh):
+            if fresh:
+                for u in range(rows):
+                    if j == 1:
+                        moved_ref[u * cols : (u + 1) * cols, :] = a_ref[u]
+                    else:
+                        moved_ref[u * cols : (u + 1) * cols, :] = column_shift(
+                            a_ref[u].astype(F32), j - 1
+                        ).astype(BF16)
+            if i == 1:
+                wide_ref[...] = tn_dot(moved_ref[...], g_ref[...])
+            elif i == 0:
+                wide_ref[...] = tn_dot(moved_ref[: total - cols, :], g_ref[cols:, :]) + tn_dot(
+                    moved_ref[total - cols :, :], high_ref[...]
+                )
+            else:
+                wide_ref[...] = tn_dot(moved_ref[cols:, :], g_ref[: total - cols, :]) + tn_dot(
+                    moved_ref[:cols, :], low_ref[...]
+                )
+            spread(wide_ref, order_ref, keep_ref, send_ref)
+
+
+def wgrad(order, act, grad, halos, after, taps):
+    rows, cols, chans = grad.shape
+    count = len(taps)
+    whole = lambda *shape: pl.BlockSpec(shape, lambda t: (0,) * len(shape))
+    half_spec = pl.BlockSpec((1, chans // 2, chans), lambda t: (t, 0, 0))
+    shape = jax.ShapeDtypeStruct((count, chans // 2, chans), BF16)
     return pl.pallas_call(
-        functools.partial(turn_kernel, parts),
-        grid=(rows,),
-        in_specs=[SMEM, pl.BlockSpec((1, cols, chans), lambda u: (u, 0, 0))],
-        out_specs=pl.BlockSpec((3, chans, cols), lambda u: (0, 0, u)),
-        out_shape=jax.ShapeDtypeStruct((3, chans, rows * cols), BF16),
-        scratch_shapes=[pltpu.VMEM((chans, cols), F32)],
-        compiler_params=params(),
-        cost_estimate=cost(0, 16 * rows * cols * chans),
-        name="turn",
-    )(order, act)
-
-
-def wgrad_kernel(taps, cols, a_ref, g_ref, low_ref, high_ref, keep_ref, send_ref):
-    step = pl.program_id(0)
-    half = pl.program_id(1)
-    total = a_ref.shape[2]
-
-    def product(tap):
-        a = a_ref[0]
-        g = g_ref[...]
-        if tap == 1:
-            return jnp.dot(a, g, preferred_element_type=F32)
-        if tap == 0:
-            return jnp.dot(a[:, : total - cols], g[cols:], preferred_element_type=F32) + jnp.dot(
-                a[:, total - cols :], high_ref[...], preferred_element_type=F32
-            )
-        return jnp.dot(a[:, cols:], g[: total - cols], preferred_element_type=F32) + jnp.dot(
-            a[:, :cols], low_ref[...], preferred_element_type=F32
-        )
-
-    for place, tap in enumerate(taps):
-        @pl.when(step // 3 == place)
-        def _(tap=tap):
-            term = product(tap).astype(BF16)
-
-            @pl.when(half == 0)
-            def _():
-                send_ref[0] = term
-
-            @pl.when(half == 1)
-            def _():
-                keep_ref[0] = term
-
-
-def wgrad(turned, grad, low, high, taps):
-    rows, cols, chans = grad.shape
-    flat = grad.reshape(rows * cols, chans)
-    count = 3 * len(taps)
-    half_rows = chans // 2
-    whole = lambda *shape: pl.BlockSpec(shape, lambda t, h: (0,) * len(shape))
-    in_specs = [
-        pl.BlockSpec((1, half_rows, rows * cols), lambda t, h: (t % 3, 1 - h, 0)),
-        whole(rows * cols, chans),
-    ]
-    operands = [turned, flat]
-    if taps == (1,):
-        kernel = lambda a, g, keep, send: wgrad_kernel(taps, cols, a, g, None, None, keep, send)
-    else:
-        kernel = functools.partial(wgrad_kernel, taps, cols)
-        in_specs += [whole(cols, chans), whole(cols, chans)]
-        operands += [low, high]
-    half_spec = pl.BlockSpec((1, half_rows, chans), lambda t, h: (t, 0, 0))
-    shape = jax.ShapeDtypeStruct((count, half_rows, chans), BF16)
-    return pl.pallas_call(
-        kernel,
-        grid=(count, 2),
-        in_specs=in_specs,
+        functools.partial(wgrad_kernel, taps, len(halos) > 0),
+        grid=(count,),
+        in_specs=[SMEM, whole(rows, cols, chans), whole(rows * cols, chans)]
+        + [whole(cols, chans)] * len(halos)
+        + [ANY] * len(after),
         out_specs=[half_spec, half_spec],
         out_shape=[shape, shape],
+        scratch_shapes=[pltpu.VMEM((rows * cols, chans), BF16), pltpu.VMEM((chans, chans), F32)],
         compiler_params=params(),
-        cost_estimate=cost(2 * count * rows * cols * chans * chans, 2 * (4 * rows * cols * chans + count * chans * chans)),
+        cost_estimate=cost(
+            2 * count * rows * cols * chans * chans, 2 * (2 * rows * cols * chans + count * chans * chans)
+        ),
         name="wgrad",
-    )(*operands)
-
-
-def fold_kernel(keep_ref, recv_ref, first_ref, second_ref):
-    cut = first_ref.shape[1]
-    first_ref[...] = (keep_ref[:, :cut].astype(F32) + recv_ref[:, :cut].astype(F32)).astype(BF16)
-    second_ref[...] = (keep_ref[:, cut:].astype(F32) + recv_ref[:, cut:].astype(F32)).astype(BF16)
-
-
-def fold(keep, recv):
-    n, m = keep.shape[:2]
-    rest = keep.shape[2:]
-    block = pl.BlockSpec((1, m) + rest, lambda t: (t,) + (0,) * (1 + len(rest)))
-    half = pl.BlockSpec((1, m // 2) + rest, lambda t: (t,) + (0,) * (1 + len(rest)))
-    shape = jax.ShapeDtypeStruct((n, m // 2) + rest, BF16)
-    return pl.pallas_call(
-        fold_kernel,
-        grid=(n,),
-        in_specs=[block, block],
-        out_specs=[half, half],
-        out_shape=[shape, shape],
-        compiler_params=params(),
-        cost_estimate=cost(0, 6 * keep.size),
-        name="fold",
-    )(keep, recv)
+    )(order, act, grad.reshape(rows * cols, chans), *halos, *after)
 
 
 def pieces_kernel(
@@ -353,14 +300,17 @@
     def fill(out, place, local, inside):
         at = place * per + local
         have = count_ref[at]
-        value = group_product(at, 0, have)
-        out[inside[0], inside[1]] = value.astype(BF16)
+        out[inside[0], inside[1]] = group_product(at, 0, have).astype(BF16)
+
+    def overfill(out, place, local, inside):
+        at = place * per + local
+        have = count_ref[at]
 
         @pl.when(have > GROUP)
         def _():
-            acc_ref[...] = value
-
-            @pl.loop(1, (have + GROUP - 1) // GROUP)
+            acc_ref[...] = jnp.zeros_like(acc_ref)
+
+            @pl.loop(0, (have + GROUP - 1) // GROUP)
             def _(m):
                 acc_ref[...] = acc_ref[...] + group_product(at, m * GROUP, have)
 
@@ -370,11 +320,13 @@
         for half in (1, 0):
             out = outs[2 * chunk + half]
 
-            @pl.loop(0, (slots // 2) * half_per, unroll=2)
-            def _(n, out=out, half=half, chunk=chunk):
+            def visit(n, step, out=out, half=half, chunk=chunk):
                 place = n // half_per
                 local = n - place * half_per
-                fill(out, half * (slots // 2) + place, chunk * half_per + local, (place, local))
+                step(out, half * (slots // 2) + place, chunk * half_per + local, (place, local))
+
+            pl.loop(0, (slots // 2) * half_per, unroll=4)(functools.partial(visit, step=fill))
+            pl.loop(0, (slots // 2) * half_per)(functools.partial(visit, step=overfill))
 
 
 def swap_low_bits(value):
@@ -415,60 +367,61 @@
     )(info, route, off, fx, fy, *sources)
 
 
-def slope_kernel(order_ref, img_ref, w_ref, slope_ref, turned_ref, wide_ref):
+def slope_kernel(img_ref, w_ref, slope_ref):
     value = jnp.dot(img_ref[...], w_ref[...], preferred_element_type=F32)
     sigma = jax.nn.sigmoid(value)
     slope_ref[...] = sigma * (1.0 + value * (1.0 - sigma))
-    wide_ref[...] = img_ref[...].astype(F32).T
-    parts = order_ref.shape[0]
-    size = wide_ref.shape[0] // parts
-    for s in range(parts):
-        source = pl.multiple_of(order_ref[s] * size, size)
-        turned_ref[s * size : (s + 1) * size, :] = wide_ref[pl.ds(source, size), :].astype(BF16)
-
-
-def image_slope(order, image, weight):
+
+
+def image_slope(image, weight):
     pixels, chans = image.shape
     return pl.pallas_call(
         slope_kernel,
-        in_specs=[SMEM, VMEM, VMEM],
-        out_specs=[VMEM, VMEM],
-        out_shape=[
-            jax.ShapeDtypeStruct((pixels, chans), F32),
-            jax.ShapeDtypeStruct((chans, pixels), BF16),
-        ],
-        scratch_shapes=[pltpu.VMEM((chans, pixels), F32)],
+        in_specs=[VMEM, VMEM],
+        out_specs=VMEM,
+        out_shape=jax.ShapeDtypeStruct((pixels, chans), F32),
         compiler_params=params(),
         cost_estimate=cost(2 * pixels * chans * chans, 10 * pixels * chans),
         name="image_slope",
-    )(order, image, weight)
-
-
-def image_kernel(ka, ra, kb, rb, slope_ref, turned_ref, w_ref, img_out, keep_ref, send_ref):
-    half = ka.shape[0]
-    feature = jnp.concatenate(
-        [ka[...].astype(F32) + ra[...].astype(F32), kb[...].astype(F32) + rb[...].astype(F32)], axis=0
-    )
+    )(image, weight)
+
+
+def image_kernel(chunks, order_ref, *refs):
+    terms = refs[: sum(chunks)]
+    slope_ref, image_ref, w_ref, img_out, keep_ref, send_ref, wide_ref = refs[sum(chunks) :]
+    feature = []
+    start = 0
+    for size in chunks:
+        total = terms[start][0].astype(F32)
+        for term in terms[start + 1 : start + size]:
+            total = total + term[0].astype(F32)
+        feature.append(total.reshape(-1, total.shape[-1]))
+        start += size
+    feature = jnp.concatenate(feature, axis=0)
     scaled = (feature * slope_ref[...]).astype(BF16)
-    grad = jnp.dot(turned_ref[...], scaled, preferred_element_type=F32).astype(BF16)
-    cut = keep_ref.shape[1]
-    keep_ref[0] = grad[:cut]
-    send_ref[0] = grad[cut:]
+    wide_ref[...] = tn_dot(image_ref[...], scaled)
+    spread(wide_ref, order_ref, keep_ref, send_ref)
     img_out[...] = nt_dot(scaled, w_ref[...]).astype(BF16)
 
 
-def image_layer(ka, ra, kb, rb, slope, turned, weight):
+def image_layer(order, chunks, slope, image, weight):
     pixels, chans = slope.shape
     half = jax.ShapeDtypeStruct((1, chans // 2, chans), BF16)
+    whole = lambda *shape: pl.BlockSpec(shape, lambda n: (0,) * len(shape))
+    terms = [term for chunk in chunks for term in chunk]
     return pl.pallas_call(
-        image_kernel,
-        in_specs=[VMEM] * 7,
-        out_specs=[VMEM] * 3,
+        functools.partial(image_kernel, tuple(len(chunk) for chunk in chunks)),
+        grid=(1,),
+        in_specs=[SMEM]
+        + [whole(1, *term.shape[1:]) for term in terms]
+        + [whole(pixels, chans), whole(pixels, chans), whole(chans, chans)],
+        out_specs=[whole(pixels, chans), whole(1, chans // 2, chans), whole(1, chans // 2, chans)],
         out_shape=[jax.ShapeDtypeStruct((pixels, chans), BF16), half, half],
+        scratch_shapes=[pltpu.VMEM((chans, chans), F32)],
         compiler_params=params(),
         cost_estimate=cost(4 * pixels * chans * chans, 16 * pixels * chans),
         name="image_layer",
-    )(ka, ra, kb, rb, slope, turned, weight)
+    )(order, *terms, slope, image, weight)
 
 
 def exchange(value, size_dp, size_tile, flip):
@@ -520,13 +473,22 @@
     return jnp.concatenate([same + core * top, flipped + (1 - core) * top])
 
 
+def region_sum(terms, axis, low, high):
+    total = lax.slice_in_dim(terms[0], low, high, axis=axis).astype(F32)
+    for term in terms[1:]:
+        total = total + lax.slice_in_dim(term, low, high, axis=axis).astype(F32)
+    return total
+
+
 def reduce_parts(keep, send, size_dp, size_tile, levels, scale):
     masks = [step_masks(size_dp, size_tile, core) for core in (0, 1)]
-    recv = exchange(send, size_dp, size_tile, lambda core: (0, 1))
+    terms = [keep, exchange(send, size_dp, size_tile, lambda core: (0, 1))]
+    extent = keep.shape[1]
     for n in range(levels - 1):
-        keep, send = fold(keep, recv)
-        recv = exchange(send, size_dp, size_tile, lambda core, n=n: masks[core][n])
-    total = keep.astype(F32) + recv.astype(F32)
+        send = region_sum(terms, 1, extent // 2, extent).astype(BF16)
+        extent //= 2
+        terms.append(exchange(send, size_dp, size_tile, lambda core, n=n: masks[core][n]))
+    total = region_sum(terms, 1, 0, extent)
     for n in range(levels - 1, len(masks[0])):
         value = total.astype(BF16)
         recv = exchange(value, size_dp, size_tile, lambda core, n=n: masks[core][n])
@@ -543,55 +505,51 @@
     return part, recv
 
 
-def place_kernel(parts, shapes, order_ref, *refs):
-    count = len(shapes)
-    sources = refs[: 2 * count]
-    outs = refs[2 * count : 2 * count + 2]
-    sem = refs[-1]
-    copies = []
-    for n, (which, taps) in enumerate(shapes):
-        for side in range(2):
-            source = sources[2 * n + side]
-            size = 2 * source.shape[1] // parts
-            for s in range(parts // 2):
-                target = pl.multiple_of(order_ref[side * (parts // 2) + s] * size, size)
-                for place, tap in enumerate(taps):
-                    copies.append(
-                        pltpu.make_async_copy(
-                            source.at[pl.ds(place * 3, 3), pl.ds(s * size, size)]
-                            if which == 0
-                            else source.at[0, pl.ds(s * size, size)],
-                            outs[0].at[pl.ds(tap * 3, 3), pl.ds(target, size)]
-                            if which == 0
-                            else outs[1].at[pl.ds(target, size)],
-                            sem,
-                        )
-                    )
-    for copy in copies:
-        copy.start()
-    for copy in copies:
-        copy.wait()
-
-
-def place_parts(order, groups, chans):
-    operands = []
-    shapes = []
-    for which, taps, mine, other in groups:
-        operands += [mine, other]
-        shapes.append((which, taps))
+def warp_steps(keep, send, size_dp, size_tile):
+    tile_masks = [(0, 1 << n) for n in range(1, int(math.log2(size_tile)))]
+    swapped = [tile_masks[1], tile_masks[0]] + tile_masks[2:] if len(tile_masks) > 1 else tile_masks
+    both = (tile_masks, swapped)
+    terms = [keep]
+    extent = keep.shape[0]
+    for n in range(len(tile_masks)):
+        if n > 0:
+            send = region_sum(terms, 0, extent // 2, extent).astype(BF16)
+            extent //= 2
+        terms.append(exchange(send, size_dp, size_tile, lambda core, n=n: both[core][n]))
+    return terms
+
+
+def place_kernel(order_ref, mine_ref, other_ref, *refs):
+    out_ref = refs[-1]
+    parts = order_ref.shape[0]
+    size = out_ref.shape[1] // parts
+    for half, source in enumerate((mine_ref, other_ref)):
+        for s in range(parts // 2):
+            target = pl.multiple_of(order_ref[half * (parts // 2) + s] * size, size)
+            out_ref[0, pl.ds(target, size), :] = source[0, s * size : (s + 1) * size, :]
+
+
+def place_parts(order, mine, other, places, count, before):
+    chans = mine.shape[2]
+
+    def target(t):
+        place = places[0]
+        for n, value in enumerate(places):
+            place = jnp.where(t == n, value, place)
+        return (place, 0, 0)
+
+    half_spec = pl.BlockSpec((1, chans // 2, chans), lambda t: (t, 0, 0))
     return pl.pallas_call(
-        functools.partial(place_kernel, order.shape[0], tuple(shapes)),
-        in_specs=[SMEM] + [ANY] * len(operands),
-        out_specs=[ANY, ANY],
-        out_shape=[
-            jax.ShapeDtypeStruct((9, chans, chans), BF16),
-            jax.ShapeDtypeStruct((chans, chans), BF16),
-        ],
-        scratch_shapes=[pltpu.SemaphoreType.DMA],
+        place_kernel,
+        grid=(len(places),),
+        in_specs=[SMEM, half_spec, half_spec] + [ANY] * len(before),
+        out_specs=pl.BlockSpec((1, chans, chans), target),
+        out_shape=jax.ShapeDtypeStruct((count, chans, chans), BF16),
+        input_output_aliases={3: 0} if before else {},
         compiler_params=params(),
-        cost_estimate=cost(0, 40 * chans * chans),
+        cost_estimate=cost(0, 4 * len(places) * chans * chans),
         name="place_parts",
-    )(order, *operands)
+    )(order, mine, other, *before)
 
 
 def body(grad_out, bev_act, conv_weight, img_in, backbone_weight, route, offsets, frac_x, frac_y):
@@ -624,10 +582,12 @@
 
     inner, edge = bev_inner(grad, weight)
     inner_other = lax.ppermute(inner, "tile", core_swap)
-    turned = turn(bev_act[0], order)
+    mid_taps = ((1, 1), (1, 0), (1, 2))
+    outer_taps = ((0, 1), (2, 1), (0, 0), (2, 0), (0, 2), (2, 2))
+    keep_mid, send_mid = wgrad(order, bev_act[0], grad, [], [inner], mid_taps)
     edge = bev_edge(edge, low, high, weight)
     edge_other = lax.ppermute(edge, "tile", core_swap)
-    keep_mid, send_mid = wgrad(turned, grad, None, None, (1,))
+    slope = image_slope(image, backbone_weight)
     as_blocks = lambda value: value.reshape(-1, BLK, chans)
     info = jnp.reshape(my_tile, (1,)).astype(jnp.int32)
     keep_a, send_a, keep_b, send_b = warp_pieces(
@@ -641,41 +601,25 @@
         per,
         edge_blocks,
     )
-    slope, image_turned = image_slope(order, image, backbone_weight)
-    keep_out, send_out = wgrad(turned, grad, low, high, (0, 2))
-
-    tile_masks = [(0, 1 << n) for n in range(1, int(math.log2(tiles)))]
-    swapped = [tile_masks[1], tile_masks[0]] + tile_masks[2:] if len(tile_masks) > 1 else tile_masks
-    both = (tile_masks, swapped)
-
-    def warp_steps(keep, send):
-        for n in range(len(tile_masks)):
-            recv = exchange(send, pods, tiles, lambda core, n=n: both[core][n])
-            if n == len(tile_masks) - 1:
-                return keep.reshape(-1, chans), recv.reshape(-1, chans)
-            shape = keep.shape
-            keep, send = fold(
-                keep.reshape((1, shape[0]) + (shape[1] * shape[2], chans)),
-                recv.reshape((1, shape[0]) + (shape[1] * shape[2], chans)),
-            )
-            keep = keep.reshape((shape[0] // 2,) + shape[1:])
-            send = send.reshape((shape[0] // 2,) + shape[1:])
-
-    pair_a = warp_steps(keep_a, send_a)
-    pair_b = warp_steps(keep_b, send_b)
+    keep_out, send_out = wgrad(order, bev_act[0], grad, [low, high], [keep_a], outer_taps)
+    chunk_a = warp_steps(keep_a, send_a, pods, tiles)
+    chunk_b = warp_steps(keep_b, send_b, pods, tiles)
 
     mid = reduce_parts(keep_mid, send_mid, pods, tiles, levels, cell_scale)
     mid = gather_parts(mid, pods, tiles, levels)
     outer = reduce_parts(keep_out, send_out, pods, tiles, levels, cell_scale)
     outer = gather_parts(outer, pods, tiles, levels)
 
-    image_grad, keep_img, send_img = image_layer(*pair_a, *pair_b, slope, image_turned, backbone_weight)
+    image_grad, keep_img, send_img = image_layer(
+        order, [chunk_a, chunk_b], slope, image, backbone_weight
+    )
     back = reduce_parts(keep_img, send_img, pods, tiles, levels, pixel_scale)
     back = gather_parts(back, pods, tiles, levels)
 
-    conv_grad, backbone_grad = place_parts(
-        order, [(0, (1,)) + mid, (0, (0, 2)) + outer, (1, (0,)) + back], chans
-    )
+    tap_place = lambda taps: [3 * i + j for i, j in taps]
+    conv_grad = place_parts(order, *mid, tap_place(mid_taps), 9, [])
+    conv_grad = place_parts(order, *outer, tap_place(outer_taps), 9, [conv_grad])
+    backbone_grad = place_parts(order, *back, [0], 1, [])[0]
     conv_grad = jnp.transpose(conv_grad.reshape(3, 3, chans, chans), (2, 0, 1, 3))
     return (image_grad[None], conv_grad, backbone_grad)
 

time: 429 us -> 230 us (0.54)
  Pallas kernels: 280 us -> 72.2 us
  waiting for transfers between devices: 71.9 us -> 85.9 us
  other arithmetic: 1.63 us -> 14.2 us
  local copies, waits for them, and re-layouts: 19.5 us -> 8.41 us
  starting transfers between devices: 51.6 us -> 47.1 us
    pallas_call x22 -> x7, Pallas kernels: 244 us -> 40.1 us  [the longest x2 22.9 us: wgrad(): pl.pallas_call(functools.partial(wgrad_kernel, taps, len(halos) > 0), gri...]
    ppermute x36, waiting for transfers between devices: 71.9 us -> 85.9 us  [exchange(): return lax.ppermute(value, ('dp', 'tile'), pairs)]
    unnamed x81 -> x69, local copies, waits for them, and re-layouts: 17.3 us -> 6.2 us
    convert_element_type x0 -> x16, other arithmetic: none -> 10.6 us  [the longest x12 10.2 us: reduce_parts(): send = region_sum(terms, 1, extent // 2, extent).astype(BF16)]
    ppermute x36, starting transfers between devices: 47.4 us -> 39.7 us  [exchange(): return lax.ppermute(value, ('dp', 'tile'), pairs)]
  transfers between devices with their start and end apart: 41 -> 41, of which waited for: 16 -> 17; matrix products, arithmetic and copies ran while one was open for 1% -> 7% of each run, Pallas kernels for 24% -> 29%
where the time goes in v2:
time: 230 us; the launch traced here: 229 us
  waiting for transfers between devices  85.9 us (37%)
  Pallas kernels  72.2 us (31%)
  starting transfers between devices  47.1 us (20%)
  other arithmetic  14.2 us (6%)
  local copies, waits for them, and re-layouts  8.41 us (4%)
    ppermute x36, waiting for transfers between devices, exchange(): return lax.ppermute(value, ('dp', 'tile'), pairs)  85.9 us
    ppermute x36, starting transfers between devices, exchange(): return lax.ppermute(value, ('dp', 'tile'), pairs)  39.7 us
    pallas_call x2, Pallas kernels, wgrad(): pl.pallas_call(functools.partial(wgrad_kernel, taps, len(halos) > 0), gri...  22.9 us
    pallas_call x1, Pallas kernels, bev_inner(): pl.pallas_call(bev_inner_kernel, grid=(3,), in_specs=[whole(rows, cols, c...  15.1 us
    pallas_call x3, Pallas kernels, place_parts(): pl.pallas_call(place_kernel, grid=(len(places),), in_specs=[SMEM, half_sp...  10.5 us
    pallas_call x1, Pallas kernels, warp_pieces(): pl.pallas_call(functools.partial(pieces_kernel, (own, per, bits, edge)),...  10.4 us
    convert_element_type x12, other arithmetic, reduce_parts(): send = region_sum(terms, 1, extent // 2, extent).astype(BF16)  10.2 us
    pallas_call x1, Pallas kernels, bev_edge(): pl.pallas_call(bev_edge_kernel, grid=(3,), in_specs=[whole(2, cols, chans...  6.52 us
  transfers between devices with their start and end apart: 41, of which 17 were waited for; matrix products, arithmetic and copies ran while one was open for 7% of the time, Pallas kernels for 29%

profile of v2, /device:TPU:0, one launch (start us, length us, event | category | flops | bytes accessed | tf_op | source)
XLA Modules:
  0.0 228.9 jit_solution(18116057295551695147)
XLA Ops:
  0.6 1.4 slice_bitcast_fusion
  2.0 1.3 collective-permute-start.2
  3.3 3.1 %collective-permute-start.1 = (bf16[640,512]{1,0:T(8,128)(2,1)S(1)}, bf16[640,512]{1,0:T(8,128)(2,1)S(1)}, u32[]{:S(2)}, u32[]{:S(2)}) collective-permute-start(bf16[640,512]{1,0:T(8,128)(2,1)S(1)} %get-tuple-element.36), channel_id=1, source_target_pairs={{0,1},{1,2},{2,3},{3,4},{4,5},{5,6},{6,7},{7,8},{8,9},{9,10},{10,1... | collective-permute-start | bytes 1966088 | tf_op jit(solution)/shard_map/ppermute | solution.py:574
  6.4 15.1 %bev_inner.1 = (bf16[2,640,512]{2,1,0:T(8,128)(2,1)}, f32[2,640,512]{2,1,0:T(8,128)}) custom-call(bf16[4,640,512]{2,1,0:T(8,128)(2,1)} %bitcast.39, bf16[3,3,512,512]{3,2,1,0:T(8,128)(2,1)} %bitcast.29), custom_call_target="tpu_custom_call" | custom-call | flops 10066329600 | bytes 9961472 | tf_op jit(solution)/shard_map/bev_inner/pallas_call | solution.py:80
  21.5 2.5 %collective-permute-start.3 = (bf16[2,640,512]{2,1,0:T(8,128)(2,1)}, bf16[2,640,512]{2,1,0:T(8,128)(2,1)S(1)}, u32[]{:S(2)}, u32[]{:S(2)}) collective-permute-start(bf16[2,640,512]{2,1,0:T(8,128)(2,1)} %get-tuple-element.16.refs_0_), channel_id=1, source_target_pairs={{0,1},{1,0},{2,3},{3,2},{4,5},{5,4},{6,7},{7,6},{8,9},{9,8},{10,11... | collective-permute-start | bytes 3932168 | tf_op jit(solution)/shard_map/ppermute | solution.py:584
  25.2 6.5 %bev_edge.1 = bf16[2,640,512]{2,1,0:T(8,128)(2,1)} custom-call(f32[2,640,512]{2,1,0:T(8,128)} %get-tuple-element.17.edge_ref, bf16[640,512]{1,0:T(8,128)(2,1)} %copy-done.15, bf16[640,512]{1,0:T(8,128)(2,1)} %copy-done.14, bf16[3,3,512,512]{3,2,1,0:T(8,128)(2,1)} %bitcast.30, bf16[3,3,512,512]{3,2,1,0:T(8,128)(2,1)} %bitcast.31), custom_call_target="tpu_custom_call" | custom-call | flops 2013265920 | bytes 8388608 | tf_op jit(solution)/shard_map/bev_edge/pallas_call | solution.py:116
  33.0 8.3 %wgrad.3 = (bf16[3,256,512]{2,1,0:T(8,128)(2,1)}, bf16[3,256,512]{2,1,0:T(8,128)(2,1)}) custom-call(s32[32]{0:T(128)} %pad_add_fusion.1.order_ref, bf16[4,640,512]{2,1,0:T(8,128)(2,1)} %bitcast.43, bf16[2560,512]{1,0:T(8,128)(2,1)} %bitcast.40, bf16[2,640,512]{2,1,0:T(8,128)(2,1)} %get-tuple-element.16.refs_0_), custom_call_target="tpu_custom_call" | custom-call | flops 4026531840 | bytes 6815744 | tf_op jit(solution)/shard_map/wgrad/pallas_call | solution.py:190
  44.2 10.4 %warp_pieces.1 = (bf16[4,2,128,512]{3,2,1,0:T(8,128)(2,1)}, bf16[4,2,128,512]{3,2,1,0:T(8,128)(2,1)}, bf16[4,2,128,512]{3,2,1,0:T(8,128)(2,1)}, bf16[4,2,128,512]{3,2,1,0:T(8,128)(2,1)}) custom-call(s32[1]{0:T(128)} %bitcast.2.info_ref, s32[640]{0:T(1024)} %reduce.route_ref, s32[80,128]{1,0:T(8,128)} %get-tuple-element.39.off_ref, ...), custom_call_target="tpu_custom_call" | custom-call | flops 1073741824 | bytes 9437184 | tf_op jit(solution)/shard_map/warp_pieces/pallas_call | solution.py:350
  54.7 14.6 %wgrad.2 = (bf16[6,256,512]{2,1,0:T(8,128)(2,1)}, bf16[6,256,512]{2,1,0:T(8,128)(2,1)}) custom-call(s32[32]{0:T(128)} %pad_add_fusion.1.order_ref, bf16[4,640,512]{2,1,0:T(8,128)(2,1)} %bitcast.44, bf16[2560,512]{1,0:T(8,128)(2,1)} %bitcast.41, bf16[640,512]{1,0:T(8,128)(2,1)} %copy-done.15, bf16[640,512]{1,0:T(8,128)(2,1)} %copy-done.14, ...), custom_call_target="tpu_custom_call" | custom-call | flops 8053063680 | bytes 8388608 | tf_op jit(solution)/shard_map/wgrad/pallas_call | solution.py:190
  72.4 2.8 %collective-permute-start.5 = (bf16[4,2,128,512]{3,2,1,0:T(8,128)(2,1)}, bf16[4,2,128,512]{3,2,1,0:T(8,128)(2,1)S(1)}, u32[]{:S(2)}, u32[]{:S(2)}) collective-permute-start(bf16[4,2,128,512]{3,2,1,0:T(8,128)(2,1)} %get-tuple-element.19), channel_id=1, source_target_pairs={{0,2},{1,5},{2,0},{3,7},{4,6},{5,1},{6,4},{7,3},{8,10},{9,13},{10,... | collective-permute-start | bytes 3145736 | tf_op jit(solution)/shard_map/ppermute | solution.py:433
  75.3 3.9 %collective-permute-done.22 = bf16[3,128,512]{2,1,0:T(8,128)(2,1)S(1)} collective-permute-done((bf16[3,128,512]{2,1,0:T(8,128)(2,1)S(1)}, bf16[3,128,512]{2,1,0:T(8,128)(2,1)S(1)}, u32[]{:S(2)}, u32[]{:S(2)}) %collective-permute-start.22) | collective-permute-done | bytes 393248 | tf_op jit(solution)/shard_map/ppermute | solution.py:433
  79.2 1.8 add_convert_fusion.7
  81.0 1.9 collective-permute-start.23
  84.0 2.0 collective-permute-start.12
  86.0 2.8 %image_slope.1.refs_8_ = f32[512,512]{1,0:T(8,128)} custom-call(bf16[512,512]{1,0:T(8,128)(2,1)} %bitcast.34, bf16[512,512]{1,0:T(8,128)(2,1)} %refs_10_.1), custom_call_target="tpu_custom_call" | custom-call | flops 268435456 | bytes 2621440 | tf_op jit(solution)/shard_map/image_slope/pallas_call | solution.py:378
  88.9 27.9 %collective-permute-done.23 = bf16[3,64,512]{2,1,0:T(8,128)(2,1)S(1)} collective-permute-done((bf16[3,64,512]{2,1,0:T(8,128)(2,1)}, bf16[3,64,512]{2,1,0:T(8,128)(2,1)S(1)}, u32[]{:S(2)}, u32[]{:S(2)}) %collective-permute-start.23) | collective-permute-done | bytes 196640 | tf_op jit(solution)/shard_map/ppermute | solution.py:433
  117.9 2.6 %collective-permute-start.24 = (bf16[3,32,512]{2,1,0:T(8,128)(2,1)S(1)}, bf16[3,32,512]{2,1,0:T(8,128)(2,1)S(1)}, u32[]{:S(2)}, u32[]{:S(2)}) collective-permute-start(bf16[3,32,512]{2,1,0:T(8,128)(2,1)S(1)} %add_convert_fusion.10), channel_id=1, source_target_pairs={{0,4},{1,5},{2,6},{3,7},{4,0},{5,1},{6,2},{7,3},{8,12},{9,13},{10,... | collective-permute-start | bytes 294920 | tf_op jit(solution)/shard_map/ppermute | solution.py:433
  120.8 2.0 collective-permute-start.9
  122.9 1.2 add_convert_fusion.4
  124.1 2.1 collective-permute-start.13
  127.1 1.8 collective-permute-start.25
  128.9 7.0 %collective-permute-done.6.refs_2_ = bf16[2,2,128,512]{3,2,1,0:T(8,128)(2,1)S(1)} collective-permute-done((bf16[2,2,128,512]{3,2,1,0:T(8,128)(2,1)S(1)}, bf16[2,2,128,512]{3,2,1,0:T(8,128)(2,1)S(1)}, u32[]{:S(2)}, u32[]{:S(2)}) %collective-permute-start.6) | collective-permute-done | bytes 524320 | tf_op jit(solution)/shard_map/ppermute | solution.py:433
  136.1 2.8 %collective-permute-start.7 = (bf16[1,2,128,512]{3,2,1,0:T(8,128)(2,1)S(1)}, bf16[1,2,128,512]{3,2,1,0:T(8,128)(2,1)S(1)}, u32[]{:S(2)}, u32[]{:S(2)}) collective-permute-start(bf16[1,2,128,512]{3,2,1,0:T(8,128)(2,1)S(1)} %add_convert_fusion.6), channel_id=1, source_target_pairs={{0,8},{1,9},{2,10},{3,11},{4,12},{5,13},{6,14},{7,15},{8,0},{9,1},... | collective-permute-start | bytes 786440 | tf_op jit(solution)/shard_map/ppermute | solution.py:433
  139.9 1.8 collective-permute-start.14
  141.7 3.9 %collective-permute-done.9.refs_6_ = bf16[2,2,128,512]{3,2,1,0:T(8,128)(2,1)S(1)} collective-permute-done((bf16[2,2,128,512]{3,2,1,0:T(8,128)(2,1)S(1)}, bf16[2,2,128,512]{3,2,1,0:T(8,128)(2,1)S(1)}, u32[]{:S(2)}, u32[]{:S(2)}) %collective-permute-start.9) | collective-permute-done | bytes 524320 | tf_op jit(solution)/shard_map/ppermute | solution.py:433
  145.8 1.9 collective-permute-done.14
  148.6 2.1 collective-permute-start.15
  152.6 3.8 %collective-permute-done.10.refs_7_ = bf16[1,2,128,512]{3,2,1,0:T(8,128)(2,1)S(1)} collective-permute-done((bf16[1,2,128,512]{3,2,1,0:T(8,128)(2,1)S(1)}, bf16[1,2,128,512]{3,2,1,0:T(8,128)(2,1)S(1)}, u32[]{:S(2)}, u32[]{:S(2)}) %collective-permute-start.10) | collective-permute-done | bytes 262176 | tf_op jit(solution)/shard_map/ppermute | solution.py:433
  157.1 3.8 %image_layer.1 = (bf16[512,512]{1,0:T(8,128)(2,1)}, bf16[1,256,512]{2,1,0:T(8,128)(2,1)}, bf16[1,256,512]{2,1,0:T(8,128)(2,1)}) custom-call(s32[32]{0:T(128)} %pad_add_fusion.1.order_ref, bf16[4,2,128,512]{3,2,1,0:T(8,128)(2,1)} %get-tuple-element.18.refs_0_.refs_2_, bf16[4,2,128,512]{3,2,1,0:T(8,128)(2,1)} %copy-done.2, bf16[2,2,128,512]{3,2,1,0:T(8,128)(2,1)} %copy-done.9, ...), custom_call_target="tpu_custom_call" | custom-call | flops 536870912 | bytes 4194304 | tf_op jit(solution)/shard_map/image_layer/pallas_call | solution.py:412
  162.0 2.1 collective-permute-start.27
  164.2 5.0 %collective-permute-done.16 = bf16[6,16,512]{2,1,0:T(8,128)(2,1)S(1)} collective-permute-done((bf16[6,16,512]{2,1,0:T(8,128)(2,1)S(1)}, bf16[6,16,512]{2,1,0:T(8,128)(2,1)S(1)}, u32[]{:S(2)}, u32[]{:S(2)}) %collective-permute-start.16) | collective-permute-done | bytes 98336 | tf_op jit(solution)/shard_map/ppermute | solution.py:433
  171.2 4.9 %collective-permute-done.17 = bf16[6,32,512]{2,1,0:T(8,128)(2,1)S(1)} collective-permute-done((bf16[6,32,512]{2,1,0:T(8,128)(2,1)S(1)}, bf16[6,32,512]{2,1,0:T(8,128)(2,1)S(1)}, u32[]{:S(2)}, u32[]{:S(2)}) %collective-permute-start.17) | collective-permute-done | bytes 196640 | tf_op jit(solution)/shard_map/ppermute | solution.py:433
  176.1 1.9 collective-permute-start.18
  178.3 1.9 collective-permute-start.33
  180.2 3.7 %collective-permute-done.18 = bf16[6,64,512]{2,1,0:T(8,128)(2,1)S(1)} collective-permute-done((bf16[6,64,512]{2,1,0:T(8,128)(2,1)S(1)}, bf16[6,64,512]{2,1,0:T(8,128)(2,1)S(1)}, u32[]{:S(2)}, u32[]{:S(2)}) %collective-permute-start.18) | collective-permute-done | bytes 393248 | tf_op jit(solution)/shard_map/ppermute | solution.py:433
  184.9 3.5 %collective-permute-done.33 = bf16[1,64,512]{2,1,0:T(8,128)(2,1)S(1)} collective-permute-done((bf16[1,64,512]{2,1,0:T(8,128)(2,1)S(1)}, bf16[1,64,512]{2,1,0:T(8,128)(2,1)S(1)}, u32[]{:S(2)}, u32[]{:S(2)}) %collective-permute-start.33) | collective-permute-done | bytes 65568 | tf_op jit(solution)/shard_map/ppermute | solution.py:433
  188.6 3.9 %collective-permute-done.34 = bf16[1,32,512]{2,1,0:T(8,128)(2,1)S(1)} collective-permute-done((bf16[1,32,512]{2,1,0:T(8,128)(2,1)S(1)}, bf16[1,32,512]{2,1,0:T(8,128)(2,1)S(1)}, u32[]{:S(2)}, u32[]{:S(2)}) %collective-permute-start.34) | collective-permute-done | bytes 32800 | tf_op jit(solution)/shard_map/ppermute | solution.py:433
  193.4 2.6 %collective-permute-done.19 = bf16[6,128,512]{2,1,0:T(8,128)(2,1)S(1)} collective-permute-done((bf16[6,128,512]{2,1,0:T(8,128)(2,1)S(1)}, bf16[6,128,512]{2,1,0:T(8,128)(2,1)S(1)}, u32[]{:S(2)}, u32[]{:S(2)}) %collective-permute-start.19) | collective-permute-done | bytes 786464 | tf_op jit(solution)/shard_map/ppermute | solution.py:433
  198.2 3.9 %collective-permute-done.36 = bf16[1,16,512]{2,1,0:T(8,128)(2,1)S(1)} collective-permute-done((bf16[1,16,512]{2,1,0:T(8,128)(2,1)S(1)}, bf16[1,16,512]{2,1,0:T(8,128)(2,1)S(1)}, u32[]{:S(2)}, u32[]{:S(2)}) %collective-permute-start.36) | collective-permute-done | bytes 16416 | tf_op jit(solution)/shard_map/ppermute | solution.py:433
  202.2 1.9 collective-permute-done.29
  204.2 1.8 collective-permute-done.37
  206.0 2.1 collective-permute-start.38
  208.1 2.2 collective-permute-done.38
  211.4 4.0 %collective-permute-done.39 = bf16[1,128,512]{2,1,0:T(8,128)(2,1)S(1)} collective-permute-done((bf16[1,128,512]{2,1,0:T(8,128)(2,1)S(1)}, bf16[1,128,512]{2,1,0:T(8,128)(2,1)S(1)}, u32[]{:S(2)}, u32[]{:S(2)}) %collective-permute-start.39) | collective-permute-done | bytes 131104 | tf_op jit(solution)/shard_map/ppermute | solution.py:433
  216.4 3.4 %place_parts.3.refs_0_ = bf16[9,512,512]{2,1,0:T(8,128)(2,1)} custom-call(s32[32]{0:T(128)} %pad_add_fusion.1.order_ref, bf16[3,256,512]{2,1,0:T(8,128)(2,1)} %copy-done.11, bf16[3,256,512]{2,1,0:T(8,128)(2,1)} %copy-done.12), custom_call_target="tpu_custom_call" | custom-call | bytes 3145728 | tf_op jit(solution)/shard_map/place_parts/pallas_call | solution.py:542
  220.5 1.9 place_parts.5
  222.4 1.2 copy-done.5
  223.6 5.3 %place_parts.4 = bf16[9,512,512]{2,1,0:T(8,128)(2,1)} custom-call(s32[32]{0:T(128)} %pad_add_fusion.1.order_ref, bf16[6,256,512]{2,1,0:T(8,128)(2,1)} %copy-done.4, bf16[6,256,512]{2,1,0:T(8,128)(2,1)} %copy-done.5, bf16[9,512,512]{2,1,0:T(8,128)(2,1)} %place_parts.3.refs_0_), custom_call_target="tpu_custom_call", output_to_operand_aliasing={{}: (3, {})} | custom-call | bytes 6291456 | tf_op jit(solution)/shard_map/place_parts/pallas_call | solution.py:542
  (152 shorter events, 27.3 us)
Async XLA Ops:
  2.0 22.1 %collective-permute-start.2 = (bf16[640,512]{1,0:T(8,128)(2,1)S(1)}, bf16[640,512]{1,0:T(8,128)(2,1)S(1)}, u32[]{:S(2)}, u32[]{:S(2)}) collective-permute-start(bf16[640,512]{1,0:T(8,128)(2,1)S(1)} %get-tuple-element.35), channel_id=1, source_target_pairs={{1,0},{2,1},{3,2},{4,3},{5,4},{6,5},{7,6},{8,7},{9,8},{10,9},{11,1... | collective-permute-start | bytes 1966088 | tf_op jit(solution)/shard_map/ppermute | solution.py:575
  3.3 20.8 %collective-permute-start.1 = (bf16[640,512]{1,0:T(8,128)(2,1)S(1)}, bf16[640,512]{1,0:T(8,128)(2,1)S(1)}, u32[]{:S(2)}, u32[]{:S(2)}) collective-permute-start(bf16[640,512]{1,0:T(8,128)(2,1)S(1)} %get-tuple-element.36), channel_id=1, source_target_pairs={{0,1},{1,2},{2,3},{3,4},{4,5},{5,6},{6,7},{7,8},{8,9},{9,10},{10,1... | collective-permute-start | bytes 1966088 | tf_op jit(solution)/shard_map/ppermute | solution.py:574
  21.5 21.2 %collective-permute-start.3 = (bf16[2,640,512]{2,1,0:T(8,128)(2,1)}, bf16[2,640,512]{2,1,0:T(8,128)(2,1)S(1)}, u32[]{:S(2)}, u32[]{:S(2)}) collective-permute-start(bf16[2,640,512]{2,1,0:T(8,128)(2,1)} %get-tuple-element.16.refs_0_), channel_id=1, source_target_pairs={{0,1},{1,0},{2,3},{3,2},{4,5},{5,4},{6,7},{7,6},{8,9},{9,8},{10,11... | collective-permute-start | bytes 3932168 | tf_op jit(solution)/shard_map/ppermute | solution.py:584
  31.7 11.0 %collective-permute-start.4 = (bf16[2,640,512]{2,1,0:T(8,128)(2,1)}, bf16[2,640,512]{2,1,0:T(8,128)(2,1)S(1)}, u32[]{:S(2)}, u32[]{:S(2)}) collective-permute-start(bf16[2,640,512]{2,1,0:T(8,128)(2,1)} %bev_edge.1), channel_id=1, source_target_pairs={{0,1},{1,0},{2,3},{3,2},{4,5},{5,4},{6,7},{7,6},{8,9},{9,8},{10,11... | collective-permute-start | bytes 3932168 | tf_op jit(solution)/shard_map/ppermute | solution.py:589
  31.9 10.1 %collective-permute-start = (s32[3,40,64]{2,1,0:T(8,128)S(1)}, s32[3,40,64]{2,1,0:T(8,128)S(1)}, u32[]{:S(2)}, u32[]{:S(2)}) collective-permute-start(s32[3,40,64]{2,1,0:T(8,128)S(1)} %reshape.44), channel_id=1, source_target_pairs={{0,1},{1,0},{2,3},{3,2},{4,5},{5,4},{6,7},{7,6},{8,9},{9,8},{10,11... | collective-permute-start | bytes 92168 | tf_op jit(solution)/shard_map/ppermute | solution.py:579
  41.3 29.0 %collective-permute-start.21 = (bf16[3,256,512]{2,1,0:T(8,128)(2,1)}, bf16[3,256,512]{2,1,0:T(8,128)(2,1)}, u32[]{:S(2)}, u32[]{:S(2)}) collective-permute-start(bf16[3,256,512]{2,1,0:T(8,128)(2,1)} %get-tuple-element.26), channel_id=1, source_target_pairs={{0,1},{1,0},{2,3},{3,2},{4,5},{5,4},{6,7},{7,6},{8,9},{9,8},{10,11... | collective-permute-start | bytes 2359304 | tf_op jit(solution)/shard_map/ppermute | solution.py:433
  54.7 15.6 %copy-start.13 = (bf16[3,256,512]{2,1,0:T(8,128)(2,1)S(1)}, bf16[3,256,512]{2,1,0:T(8,128)(2,1)}, u32[]{:S(2)}) copy-start(bf16[3,256,512]{2,1,0:T(8,128)(2,1)} %get-tuple-element.25) | copy-start | bytes 2359300
  69.3 13.6 %collective-permute-start.11 = (bf16[6,256,512]{2,1,0:T(8,128)(2,1)}, bf16[6,256,512]{2,1,0:T(8,128)(2,1)S(1)}, u32[]{:S(2)}, u32[]{:S(2)}) collective-permute-start(bf16[6,256,512]{2,1,0:T(8,128)(2,1)} %get-tuple-element.24), channel_id=1, source_target_pairs={{0,1},{1,0},{2,3},{3,2},{4,5},{5,4},{6,7},{7,6},{8,9},{9,8},{10,11... | collective-permute-start | bytes 4718600 | tf_op jit(solution)/shard_map/ppermute | solution.py:433
  71.4 7.8 %collective-permute-start.22 = (bf16[3,128,512]{2,1,0:T(8,128)(2,1)S(1)}, bf16[3,128,512]{2,1,0:T(8,128)(2,1)S(1)}, u32[]{:S(2)}, u32[]{:S(2)}) collective-permute-start(bf16[3,128,512]{2,1,0:T(8,128)(2,1)S(1)} %add_convert_fusion.3), channel_id=1, source_target_pairs={{0,16},{1,3},{2,18},{3,1},{4,20},{5,7},{6,22},{7,5},{8,24},{9,11},... | collective-permute-start | bytes 1179656 | tf_op jit(solution)/shard_map/ppermute | solution.py:433
  72.4 48.0 %collective-permute-start.5 = (bf16[4,2,128,512]{3,2,1,0:T(8,128)(2,1)}, bf16[4,2,128,512]{3,2,1,0:T(8,128)(2,1)S(1)}, u32[]{:S(2)}, u32[]{:S(2)}) collective-permute-start(bf16[4,2,128,512]{3,2,1,0:T(8,128)(2,1)} %get-tuple-element.19), channel_id=1, source_target_pairs={{0,2},{1,5},{2,0},{3,7},{4,6},{5,1},{6,4},{7,3},{8,10},{9,13},{10,... | collective-permute-start | bytes 3145736 | tf_op jit(solution)/shard_map/ppermute | solution.py:433
  75.3 45.4 %collective-permute-start.8 = (bf16[4,2,128,512]{3,2,1,0:T(8,128)(2,1)}, bf16[4,2,128,512]{3,2,1,0:T(8,128)(2,1)S(1)}, u32[]{:S(2)}, u32[]{:S(2)}) collective-permute-start(bf16[4,2,128,512]{3,2,1,0:T(8,128)(2,1)} %get-tuple-element.21), channel_id=1, source_target_pairs={{0,2},{1,5},{2,0},{3,7},{4,6},{5,1},{6,4},{7,3},{8,10},{9,13},{10,... | collective-permute-start | bytes 3145736 | tf_op jit(solution)/shard_map/ppermute | solution.py:433
  81.0 35.8 %collective-permute-start.23 = (bf16[3,64,512]{2,1,0:T(8,128)(2,1)}, bf16[3,64,512]{2,1,0:T(8,128)(2,1)S(1)}, u32[]{:S(2)}, u32[]{:S(2)}) collective-permute-start(bf16[3,64,512]{2,1,0:T(8,128)(2,1)} %add_convert_fusion.7), channel_id=1, source_target_pairs={{0,2},{1,17},{2,0},{3,19},{4,6},{5,21},{6,4},{7,23},{8,10},{9,25},... | collective-permute-start | bytes 589832 | tf_op jit(solution)/shard_map/ppermute | solution.py:433
  84.0 36.4 %copy-start = (bf16[4,2,128,512]{3,2,1,0:T(8,128)(2,1)S(1)}, bf16[4,2,128,512]{3,2,1,0:T(8,128)(2,1)}, u32[]{:S(2)}) copy-start(bf16[4,2,128,512]{3,2,1,0:T(8,128)(2,1)} %get-tuple-element.18.refs_0_.refs_2_) | copy-start | bytes 3145732
  84.0 38.8 %collective-permute-start.12 = (bf16[6,128,512]{2,1,0:T(8,128)(2,1)}, bf16[6,128,512]{2,1,0:T(8,128)(2,1)}, u32[]{:S(2)}, u32[]{:S(2)}) collective-permute-start(bf16[6,128,512]{2,1,0:T(8,128)(2,1)} %add_convert_fusion), channel_id=1, source_target_pairs={{0,16},{1,3},{2,18},{3,1},{4,20},{5,7},{6,22},{7,5},{8,24},{9,11},... | collective-permute-start | bytes 2359304 | tf_op jit(solution)/shard_map/ppermute | solution.py:433
  86.0 34.6 %copy-start.1 = (bf16[4,2,128,512]{3,2,1,0:T(8,128)(2,1)S(1)}, bf16[4,2,128,512]{3,2,1,0:T(8,128)(2,1)}, u32[]{:S(2)}) copy-start(bf16[4,2,128,512]{3,2,1,0:T(8,128)(2,1)} %get-tuple-element.20.refs_4_) | copy-start | bytes 3145732
  117.9 8.4 %collective-permute-start.24 = (bf16[3,32,512]{2,1,0:T(8,128)(2,1)S(1)}, bf16[3,32,512]{2,1,0:T(8,128)(2,1)S(1)}, u32[]{:S(2)}, u32[]{:S(2)}) collective-permute-start(bf16[3,32,512]{2,1,0:T(8,128)(2,1)S(1)} %add_convert_fusion.10), channel_id=1, source_target_pairs={{0,4},{1,5},{2,6},{3,7},{4,0},{5,1},{6,2},{7,3},{8,12},{9,13},{10,... | collective-permute-start | bytes 294920 | tf_op jit(solution)/shard_map/ppermute | solution.py:433
  120.4 15.6 %copy-start.2 = (bf16[4,2,128,512]{3,2,1,0:T(8,128)(2,1)}, bf16[4,2,128,512]{3,2,1,0:T(8,128)(2,1)S(1)}, u32[]{:S(2)}) copy-start(bf16[4,2,128,512]{3,2,1,0:T(8,128)(2,1)S(1)} %collective-permute-done.5.refs_1_) | copy-start | bytes 3145732
  120.6 15.4 %collective-permute-start.6 = (bf16[2,2,128,512]{3,2,1,0:T(8,128)(2,1)S(1)}, bf16[2,2,128,512]{3,2,1,0:T(8,128)(2,1)S(1)}, u32[]{:S(2)}, u32[]{:S(2)}) collective-permute-start(bf16[2,2,128,512]{3,2,1,0:T(8,128)(2,1)S(1)} %add_convert_fusion.2), channel_id=1, source_target_pairs={{0,4},{1,3},{2,6},{3,1},{4,0},{5,7},{6,2},{7,5},{8,12},{9,11},{10,... | collective-permute-start | bytes 1572872 | tf_op jit(solution)/shard_map/ppermute | solution.py:433
  120.7 24.9 %copy-start.3 = (bf16[4,2,128,512]{3,2,1,0:T(8,128)(2,1)}, bf16[4,2,128,512]{3,2,1,0:T(8,128)(2,1)S(1)}, u32[]{:S(2)}) copy-start(bf16[4,2,128,512]{3,2,1,0:T(8,128)(2,1)S(1)} %collective-permute-done.8.refs_5_) | copy-start | bytes 3145732
  120.8 24.7 %collective-permute-start.9 = (bf16[2,2,128,512]{3,2,1,0:T(8,128)(2,1)S(1)}, bf16[2,2,128,512]{3,2,1,0:T(8,128)(2,1)S(1)}, u32[]{:S(2)}, u32[]{:S(2)}) collective-permute-start(bf16[2,2,128,512]{3,2,1,0:T(8,128)(2,1)S(1)} %add_convert_fusion.1), channel_id=1, source_target_pairs={{0,4},{1,3},{2,6},{3,1},{4,0},{5,7},{6,2},{7,5},{8,12},{9,11},{10,... | collective-permute-start | bytes 1572872 | tf_op jit(solution)/shard_map/ppermute | solution.py:433
  124.1 14.8 %collective-permute-start.13 = (bf16[6,64,512]{2,1,0:T(8,128)(2,1)S(1)}, bf16[6,64,512]{2,1,0:T(8,128)(2,1)S(1)}, u32[]{:S(2)}, u32[]{:S(2)}) collective-permute-start(bf16[6,64,512]{2,1,0:T(8,128)(2,1)S(1)} %add_convert_fusion.4), channel_id=1, source_target_pairs={{0,2},{1,17},{2,0},{3,19},{4,6},{5,21},{6,4},{7,23},{8,10},{9,25},... | collective-permute-start | bytes 1179656 | tf_op jit(solution)/shard_map/ppermute | solution.py:433
  127.1 23.7 %collective-permute-start.25 = (bf16[3,16,512]{2,1,0:T(8,128)(2,1)S(1)}, bf16[3,16,512]{2,1,0:T(8,128)(2,1)S(1)}, u32[]{:S(2)}, u32[]{:S(2)}) collective-permute-start(bf16[3,16,512]{2,1,0:T(8,128)(2,1)S(1)} %add_convert_fusion.13), channel_id=1, source_target_pairs={{0,8},{1,9},{2,10},{3,11},{4,12},{5,13},{6,14},{7,15},{8,0},{9,1},... | collective-permute-start | bytes 147464 | tf_op jit(solution)/shard_map/ppermute | solution.py:433
  136.1 16.5 %collective-permute-start.7 = (bf16[1,2,128,512]{3,2,1,0:T(8,128)(2,1)S(1)}, bf16[1,2,128,512]{3,2,1,0:T(8,128)(2,1)S(1)}, u32[]{:S(2)}, u32[]{:S(2)}) collective-permute-start(bf16[1,2,128,512]{3,2,1,0:T(8,128)(2,1)S(1)} %add_convert_fusion.6), channel_id=1, source_target_pairs={{0,8},{1,9},{2,10},{3,11},{4,12},{5,13},{6,14},{7,15},{8,0},{9,1},... | collective-permute-start | bytes 786440 | tf_op jit(solution)/shard_map/ppermute | solution.py:433
  139.9 7.8 %collective-permute-start.14 = (bf16[6,32,512]{2,1,0:T(8,128)(2,1)S(1)}, bf16[6,32,512]{2,1,0:T(8,128)(2,1)S(1)}, u32[]{:S(2)}, u32[]{:S(2)}) collective-permute-start(bf16[6,32,512]{2,1,0:T(8,128)(2,1)S(1)} %add_convert_fusion.8), channel_id=1, source_target_pairs={{0,4},{1,5},{2,6},{3,7},{4,0},{5,1},{6,2},{7,3},{8,12},{9,13},{10,... | collective-permute-start | bytes 589832 | tf_op jit(solution)/shard_map/ppermute | solution.py:433
  145.7 10.7 %collective-permute-start.10 = (bf16[1,2,128,512]{3,2,1,0:T(8,128)(2,1)S(1)}, bf16[1,2,128,512]{3,2,1,0:T(8,128)(2,1)S(1)}, u32[]{:S(2)}, u32[]{:S(2)}) collective-permute-start(bf16[1,2,128,512]{3,2,1,0:T(8,128)(2,1)S(1)} %add_convert_fusion.5), channel_id=1, source_target_pairs={{0,8},{1,9},{2,10},{3,11},{4,12},{5,13},{6,14},{7,15},{8,0},{9,1},... | collective-permute-start | bytes 786440 | tf_op jit(solution)/shard_map/ppermute | solution.py:433
  148.6 12.2 %collective-permute-start.15 = (bf16[6,16,512]{2,1,0:T(8,128)(2,1)S(1)}, bf16[6,16,512]{2,1,0:T(8,128)(2,1)S(1)}, u32[]{:S(2)}, u32[]{:S(2)}) collective-permute-start(bf16[6,16,512]{2,1,0:T(8,128)(2,1)S(1)} %add_convert_fusion.11), channel_id=1, source_target_pairs={{0,8},{1,9},{2,10},{3,11},{4,12},{5,13},{6,14},{7,15},{8,0},{9,1},... | collective-permute-start | bytes 294920 | tf_op jit(solution)/shard_map/ppermute | solution.py:433
  151.7 10.3 %collective-permute-start.26 = (bf16[3,16,512]{2,1,0:T(8,128)(2,1)S(1)}, bf16[3,16,512]{2,1,0:T(8,128)(2,1)S(1)}, u32[]{:S(2)}, u32[]{:S(2)}) collective-permute-start(bf16[3,16,512]{2,1,0:T(8,128)(2,1)S(1)} %get-tuple-element.32), channel_id=1, source_target_pairs={{0,8},{1,9},{2,10},{3,11},{4,12},{5,13},{6,14},{7,15},{8,0},{9,1},... | collective-permute-start | bytes 147464 | tf_op jit(solution)/shard_map/ppermute | solution.py:433
  160.9 17.4 %copy-start.20 = (bf16[1,256,512]{2,1,0:T(8,128)(2,1)S(1)}, bf16[1,256,512]{2,1,0:T(8,128)(2,1)}, u32[]{:S(2)}) copy-start(bf16[1,256,512]{2,1,0:T(8,128)(2,1)} %get-tuple-element.27) | copy-start | bytes 786436
  160.9 8.4 %collective-permute-start.31 = (bf16[1,256,512]{2,1,0:T(8,128)(2,1)}, bf16[1,256,512]{2,1,0:T(8,128)(2,1)S(1)}, u32[]{:S(2)}, u32[]{:S(2)}) collective-permute-start(bf16[1,256,512]{2,1,0:T(8,128)(2,1)} %get-tuple-element.28), channel_id=1, source_target_pairs={{0,1},{1,0},{2,3},{3,2},{4,5},{5,4},{6,7},{7,6},{8,9},{9,8},{10,11... | collective-permute-start | bytes 786440 | tf_op jit(solution)/shard_map/ppermute | solution.py:433
  161.9 7.2 %collective-permute-start.16 = (bf16[6,16,512]{2,1,0:T(8,128)(2,1)S(1)}, bf16[6,16,512]{2,1,0:T(8,128)(2,1)S(1)}, u32[]{:S(2)}, u32[]{:S(2)}) collective-permute-start(bf16[6,16,512]{2,1,0:T(8,128)(2,1)S(1)} %get-tuple-element.34), channel_id=1, source_target_pairs={{0,8},{1,9},{2,10},{3,11},{4,12},{5,13},{6,14},{7,15},{8,0},{9,1},... | collective-permute-start | bytes 294920 | tf_op jit(solution)/shard_map/ppermute | solution.py:433
  162.0 15.9 %collective-permute-start.27 = (bf16[3,32,512]{2,1,0:T(8,128)(2,1)S(1)}, bf16[3,32,512]{2,1,0:T(8,128)(2,1)S(1)}, u32[]{:S(2)}, u32[]{:S(2)}) collective-permute-start(bf16[3,32,512]{2,1,0:T(8,128)(2,1)S(1)} %pad_maximum_fusion.6), channel_id=1, source_target_pairs={{0,4},{1,5},{2,6},{3,7},{4,0},{5,1},{6,2},{7,3},{8,12},{9,13},{10,... | collective-permute-start | bytes 294920 | tf_op jit(solution)/shard_map/ppermute | solution.py:433
  169.2 6.9 %collective-permute-start.17 = (bf16[6,32,512]{2,1,0:T(8,128)(2,1)S(1)}, bf16[6,32,512]{2,1,0:T(8,128)(2,1)S(1)}, u32[]{:S(2)}, u32[]{:S(2)}) collective-permute-start(bf16[6,32,512]{2,1,0:T(8,128)(2,1)S(1)} %pad_maximum_fusion.3), channel_id=1, source_target_pairs={{0,4},{1,5},{2,6},{3,7},{4,0},{5,1},{6,2},{7,3},{8,12},{9,13},{10,... | collective-permute-start | bytes 589832 | tf_op jit(solution)/shard_map/ppermute | solution.py:433
  170.2 8.1 %collective-permute-start.32 = (bf16[1,128,512]{2,1,0:T(8,128)(2,1)S(1)}, bf16[1,128,512]{2,1,0:T(8,128)(2,1)S(1)}, u32[]{:S(2)}, u32[]{:S(2)}) collective-permute-start(bf16[1,128,512]{2,1,0:T(8,128)(2,1)S(1)} %add_convert_fusion.9), channel_id=1, source_target_pairs={{0,16},{1,3},{2,18},{3,1},{4,20},{5,7},{6,22},{7,5},{8,24},{9,11},... | collective-permute-start | bytes 393224 | tf_op jit(solution)/shard_map/ppermute | solution.py:433
  176.1 7.8 %collective-permute-start.18 = (bf16[6,64,512]{2,1,0:T(8,128)(2,1)S(1)}, bf16[6,64,512]{2,1,0:T(8,128)(2,1)S(1)}, u32[]{:S(2)}, u32[]{:S(2)}) collective-permute-start(bf16[6,64,512]{2,1,0:T(8,128)(2,1)S(1)} %pad_maximum_fusion.1), channel_id=1, source_target_pairs={{0,2},{1,17},{2,0},{3,19},{4,6},{5,21},{6,4},{7,23},{8,10},{9,25},... | collective-permute-start | bytes 1179656 | tf_op jit(solution)/shard_map/ppermute | solution.py:433
  178.0 18.2 %collective-permute-start.28 = (bf16[3,64,512]{2,1,0:T(8,128)(2,1)S(1)}, bf16[3,64,512]{2,1,0:T(8,128)(2,1)S(1)}, u32[]{:S(2)}, u32[]{:S(2)}) collective-permute-start(bf16[3,64,512]{2,1,0:T(8,128)(2,1)S(1)} %pad_maximum_fusion.4), channel_id=1, source_target_pairs={{0,2},{1,17},{2,0},{3,19},{4,6},{5,21},{6,4},{7,23},{8,10},{9,25},... | collective-permute-start | bytes 589832 | tf_op jit(solution)/shard_map/ppermute | solution.py:433
  178.3 10.2 %collective-permute-start.33 = (bf16[1,64,512]{2,1,0:T(8,128)(2,1)S(1)}, bf16[1,64,512]{2,1,0:T(8,128)(2,1)S(1)}, u32[]{:S(2)}, u32[]{:S(2)}) collective-permute-start(bf16[1,64,512]{2,1,0:T(8,128)(2,1)S(1)} %add_convert_fusion.12), channel_id=1, source_target_pairs={{0,2},{1,17},{2,0},{3,19},{4,6},{5,21},{6,4},{7,23},{8,10},{9,25},... | collective-permute-start | bytes 196616 | tf_op jit(solution)/shard_map/ppermute | solution.py:433
  184.0 12.1 %collective-permute-start.19 = (bf16[6,128,512]{2,1,0:T(8,128)(2,1)S(1)}, bf16[6,128,512]{2,1,0:T(8,128)(2,1)S(1)}, u32[]{:S(2)}, u32[]{:S(2)}) collective-permute-start(bf16[6,128,512]{2,1,0:T(8,128)(2,1)S(1)} %pad_maximum_fusion), channel_id=1, source_target_pairs={{0,16},{1,3},{2,18},{3,1},{4,20},{5,7},{6,22},{7,5},{8,24},{9,11},... | collective-permute-start | bytes 2359304 | tf_op jit(solution)/shard_map/ppermute | solution.py:433
  188.5 4.0 %collective-permute-start.34 = (bf16[1,32,512]{2,1,0:T(8,128)(2,1)S(1)}, bf16[1,32,512]{2,1,0:T(8,128)(2,1)S(1)}, u32[]{:S(2)}, u32[]{:S(2)}) collective-permute-start(bf16[1,32,512]{2,1,0:T(8,128)(2,1)S(1)} %add_convert_fusion.14), channel_id=1, source_target_pairs={{0,4},{1,5},{2,6},{3,7},{4,0},{5,1},{6,2},{7,3},{8,12},{9,13},{10,... | collective-permute-start | bytes 98312 | tf_op jit(solution)/shard_map/ppermute | solution.py:433
  192.5 4.7 %collective-permute-start.35 = (bf16[1,16,512]{2,1,0:T(8,128)(2,1)S(1)}, bf16[1,16,512]{2,1,0:T(8,128)(2,1)S(1)}, u32[]{:S(2)}, u32[]{:S(2)}) collective-permute-start(bf16[1,16,512]{2,1,0:T(8,128)(2,1)S(1)} %add_convert_fusion.15), channel_id=1, source_target_pairs={{0,8},{1,9},{2,10},{3,11},{4,12},{5,13},{6,14},{7,15},{8,0},{9,1},... | collective-permute-start | bytes 49160 | tf_op jit(solution)/shard_map/ppermute | solution.py:433
  196.1 23.7 %copy-start.4 = (bf16[6,256,512]{2,1,0:T(8,128)(2,1)}, bf16[6,256,512]{2,1,0:T(8,128)(2,1)S(1)}, u32[]{:S(2)}) copy-start(bf16[6,256,512]{2,1,0:T(8,128)(2,1)S(1)} %constant_dynamic-update-slice_fusion.mine_ref) | copy-start | bytes 4718596
  196.1 26.3 %collective-permute-start.20 = (bf16[6,256,512]{2,1,0:T(8,128)(2,1)S(1)}, bf16[6,256,512]{2,1,0:T(8,128)(2,1)S(1)}, u32[]{:S(2)}, u32[]{:S(2)}) collective-permute-start(bf16[6,256,512]{2,1,0:T(8,128)(2,1)S(1)} %constant_dynamic-update-slice_fusion.mine_ref), channel_id=1, source_target_pairs={{0,1},{1,0},{2,3},{3,2},{4,5},{5,4},{6,7},{7,6},{8,9},{9,8},{10,11... | collective-permute-start | bytes 4718600 | tf_op jit(solution)/shard_map/ppermute | solution.py:433
  196.3 7.8 %collective-permute-start.29 = (bf16[3,128,512]{2,1,0:T(8,128)(2,1)S(1)}, bf16[3,128,512]{2,1,0:T(8,128)(2,1)S(1)}, u32[]{:S(2)}, u32[]{:S(2)}) collective-permute-start(bf16[3,128,512]{2,1,0:T(8,128)(2,1)S(1)} %pad_maximum_fusion.2), channel_id=1, source_target_pairs={{0,16},{1,3},{2,18},{3,1},{4,20},{5,7},{6,22},{7,5},{8,24},{9,11},... | collective-permute-start | bytes 1179656 | tf_op jit(solution)/shard_map/ppermute | solution.py:433
  197.2 4.9 %collective-permute-start.36 = (bf16[1,16,512]{2,1,0:T(8,128)(2,1)S(1)}, bf16[1,16,512]{2,1,0:T(8,128)(2,1)S(1)}, u32[]{:S(2)}, u32[]{:S(2)}) collective-permute-start(bf16[1,16,512]{2,1,0:T(8,128)(2,1)S(1)} %get-tuple-element.30), channel_id=1, source_target_pairs={{0,8},{1,9},{2,10},{3,11},{4,12},{5,13},{6,14},{7,15},{8,0},{9,1},... | collective-permute-start | bytes 49160 | tf_op jit(solution)/shard_map/ppermute | solution.py:433
  202.1 3.9 %collective-permute-start.37 = (bf16[1,32,512]{2,1,0:T(8,128)(2,1)S(1)}, bf16[1,32,512]{2,1,0:T(8,128)(2,1)S(1)}, u32[]{:S(2)}, u32[]{:S(2)}) collective-permute-start(bf16[1,32,512]{2,1,0:T(8,128)(2,1)S(1)} %pad_maximum_fusion.8), channel_id=1, source_target_pairs={{0,4},{1,5},{2,6},{3,7},{4,0},{5,1},{6,2},{7,3},{8,12},{9,13},{10,... | collective-permute-start | bytes 98312 | tf_op jit(solution)/shard_map/ppermute | solution.py:433
  204.2 11.4 %collective-permute-start.30 = (bf16[3,256,512]{2,1,0:T(8,128)(2,1)S(1)}, bf16[3,256,512]{2,1,0:T(8,128)(2,1)S(1)}, u32[]{:S(2)}, u32[]{:S(2)}) collective-permute-start(bf16[3,256,512]{2,1,0:T(8,128)(2,1)S(1)} %constant_dynamic-update-slice_fusion.5.mine_ref), channel_id=1, source_target_pairs={{0,1},{1,0},{2,3},{3,2},{4,5},{5,4},{6,7},{7,6},{8,9},{9,8},{10,11... | collective-permute-start | bytes 2359304 | tf_op jit(solution)/shard_map/ppermute | solution.py:433
  206.0 4.3 %collective-permute-start.38 = (bf16[1,64,512]{2,1,0:T(8,128)(2,1)S(1)}, bf16[1,64,512]{2,1,0:T(8,128)(2,1)S(1)}, u32[]{:S(2)}, u32[]{:S(2)}) collective-permute-start(bf16[1,64,512]{2,1,0:T(8,128)(2,1)S(1)} %pad_maximum_fusion.7), channel_id=1, source_target_pairs={{0,2},{1,17},{2,0},{3,19},{4,6},{5,21},{6,4},{7,23},{8,10},{9,25},... | collective-permute-start | bytes 196616 | tf_op jit(solution)/shard_map/ppermute | solution.py:433
  210.4 5.0 %collective-permute-start.39 = (bf16[1,128,512]{2,1,0:T(8,128)(2,1)S(1)}, bf16[1,128,512]{2,1,0:T(8,128)(2,1)S(1)}, u32[]{:S(2)}, u32[]{:S(2)}) collective-permute-start(bf16[1,128,512]{2,1,0:T(8,128)(2,1)S(1)} %pad_maximum_fusion.5), channel_id=1, source_target_pairs={{0,16},{1,3},{2,18},{3,1},{4,20},{5,7},{6,22},{7,5},{8,24},{9,11},... | collective-permute-start | bytes 393224 | tf_op jit(solution)/shard_map/ppermute | solution.py:433
  215.4 4.4 %collective-permute-start.40 = (bf16[1,256,512]{2,1,0:T(8,128)(2,1)S(1)}, bf16[1,256,512]{2,1,0:T(8,128)(2,1)S(1)}, u32[]{:S(2)}, u32[]{:S(2)}) collective-permute-start(bf16[1,256,512]{2,1,0:T(8,128)(2,1)S(1)} %constant_dynamic-update-slice_fusion.10.mine_ref), channel_id=1, source_target_pairs={{0,1},{1,0},{2,3},{3,2},{4,5},{5,4},{6,7},{7,6},{8,9},{9,8},{10,11... | collective-permute-start | bytes 786440 | tf_op jit(solution)/shard_map/ppermute | solution.py:433
  (23 other events, 112.4 us)

commit v3 on v2

v3 whole, which is shorter than its diff:
```python
import functools
import math

import jax
import jax.numpy as jnp
from jax import lax
from jax.experimental import pallas as pl
from jax.experimental.pallas import tpu as pltpu
from jax.sharding import PartitionSpec as P

BLK = 64
IMGW = 64
GROUP = 4
BATCH = 4
CONV_LEVELS = 3
VMEM_BYTES = 63 * 1024 * 1024
F32 = jnp.float32
BF16 = jnp.bfloat16
VMEM = pl.BlockSpec(memory_space=pltpu.VMEM)
SMEM = pl.BlockSpec(memory_space=pltpu.SMEM)
ANY = pl.BlockSpec(memory_space=pl.ANY)


def params(**extra):
    return pltpu.CompilerParams(vmem_limit_bytes=VMEM_BYTES, **extra)


def cost(flops, nbytes):
    return pl.CostEstimate(flops=int(flops), bytes_accessed=int(nbytes), transcendentals=0)


def nt_dot(a, b):
    return lax.dot_general(a, b, (((1,), (1,)), ((), ())), preferred_element_type=F32)


def column_shift(value, by):
    if by == 0:
        return value
    length = value.shape[0]
    place = lax.broadcasted_iota(jnp.int32, value.shape, 0)
    edge = length - 1 if by > 0 else 0
    return jnp.where(place == edge, 0.0, pltpu.roll(value, (-by) % length, 0))


def bev_kernel(targets, halo, g_ref, *refs):
    if halo:
        low_ref, high_ref = refs[:2]
        refs = refs[2:]
    w_ref, out_ref, acc_ref = refs
    rows = g_ref.shape[0]
    step = pl.program_id(0)

    def frame(u):
        if u < 0:
            return low_ref[...]
        if u >= rows:
            return high_ref[...]
        return g_ref[u]

    for order, j in enumerate((1, 0, 2)):
        @pl.when(step == order)
        def _(j=j, order=order):
            rhs = jnp.concatenate([w_ref[i, 0] for i in range(3)], axis=1)
            for n, u in enumerate(targets):
                lhs = jnp.concatenate([frame(u - i + 1) for i in range(3)], axis=1)
                term = column_shift(nt_dot(lhs, rhs), 1 - j)
                if order == 0:
                    acc_ref[n] = term
                elif order == 1:
                    acc_ref[n] = acc_ref[n] + term
                else:
                    out_ref[n] = (acc_ref[n] + term).astype(BF16)


def col_tap(step):
    return jnp.where(step == 0, 1, jnp.where(step == 1, 0, 2))


def bev_rows(grad, halos, weight, targets, after):
    rows, cols, chans = grad.shape
    whole = lambda *shape: pl.BlockSpec(shape, lambda s: (0,) * len(shape))
    count = len(targets)

    def kernel(g_ref, *refs):
        n = len(halos) + 1
        bev_kernel(targets, len(halos) > 0, g_ref, *refs[:n], *refs[n + len(after) :])

    return pl.pallas_call(
        kernel,
        grid=(3,),
        in_specs=[whole(rows, cols, chans)]
        + [whole(cols, chans)] * len(halos)
        + [pl.BlockSpec((3, 1, chans, chans), lambda s: (0, col_tap(s), 0, 0))]
        + [ANY] * len(after),
        out_specs=whole(count, cols, chans),
        out_shape=jax.ShapeDtypeStruct((count, cols, chans), BF16),
        scratch_shapes=[pltpu.VMEM((count, cols, chans), F32)],
        compiler_params=params(),
        cost_estimate=cost(18 * count * cols * chans * chans, 2 * (2 * rows * cols * chans + 9 * chans * chans)),
        name="bev_rows",
    )(grad, *halos, weight, *after)


def tn_dot(a, b):
    return lax.dot_general(a, b, (((0,), (0,)), ((), ())), preferred_element_type=F32)


def spread(value_ref, order_ref, keep_ref, send_ref):
    parts = order_ref.shape[0]
    size = value_ref.shape[0] // parts
    for half, target in enumerate((keep_ref, send_ref)):
        for s in range(parts // 2):
            source = pl.multiple_of(order_ref[half * (parts // 2) + s] * size, size)
            target[0, s * size : (s + 1) * size, :] = value_ref[pl.ds(source, size), :].astype(BF16)


def wgrad_kernel(taps, halo, order_ref, a_ref, g_ref, *refs):
    if halo:
        low_ref, high_ref = refs[:2]
    keep_ref, send_ref, moved_ref, wide_ref = refs[-4:]
    rows, cols, chans = a_ref.shape
    total = rows * cols
    step = pl.program_id(0)
    for t, (i, j) in enumerate(taps):
        fresh = j != 1 and (t == 0 or taps[t - 1][1] != j)

        @pl.when(step == t)
        def _(i=i, j=j, fresh=fresh):
            if fresh:
                for u in range(rows):
                    moved_ref[u * cols : (u + 1) * cols, :] = column_shift(
                        a_ref[u].astype(F32), j - 1
                    ).astype(BF16)
            if j == 1:
                act = lambda low, high: a_ref[low:high].reshape((high - low) * cols, chans)
            else:
                act = lambda low, high: moved_ref[low * cols : high * cols, :]
            if i == 1:
                wide_ref[...] = tn_dot(act(0, rows), g_ref[...])
            elif i == 0:
                wide_ref[...] = tn_dot(act(0, rows - 1), g_ref[cols:, :]) + tn_dot(
                    act(rows - 1, rows), high_ref[...]
                )
            else:
                wide_ref[...] = tn_dot(act(1, rows), g_ref[: total - cols, :]) + tn_dot(
                    act(0, 1), low_ref[...]
                )
            spread(wide_ref, order_ref, keep_ref, send_ref)


def pick(index, values):
    result = values[0]
    for n, value in enumerate(values):
        result = jnp.where(index == n, value, result)
    return result


def wgrad(order, act, grad, halos, taps, places, count, before, after):
    rows, cols, chans = grad.shape
    whole = lambda *shape: pl.BlockSpec(shape, lambda t: (0,) * len(shape))
    half_spec = pl.BlockSpec((1, chans // 2, chans), lambda t: (pick(t, places), 0, 0))
    shape = jax.ShapeDtypeStruct((count, chans // 2, chans), BF16)
    ahead = 3 + len(halos)
    return pl.pallas_call(
        functools.partial(wgrad_kernel, taps, len(halos) > 0),
        grid=(len(taps),),
        in_specs=[SMEM, whole(rows, cols, chans), whole(rows * cols, chans)]
        + [whole(cols, chans)] * len(halos)
        + [ANY] * (len(before) + len(after)),
        out_specs=[half_spec, half_spec],
        out_shape=[shape, shape],
        scratch_shapes=[pltpu.VMEM((rows * cols, chans), BF16), pltpu.VMEM((chans, chans), F32)],
        input_output_aliases={ahead: 0, ahead + 1: 1} if before else {},
        compiler_params=params(),
        cost_estimate=cost(
            2 * len(taps) * rows * cols * chans * chans,
            2 * (2 * rows * cols * chans + len(taps) * chans * chans),
        ),
        name="wgrad",
    )(order, act, grad.reshape(rows * cols, chans), *halos, *before, *after)


def pieces_kernel(
    plan, info_ref, route_ref, mine_ref, other_ref, *refs
):
    own_blocks, per, tile_bits, edge, after = plan
    sources = refs[:4]
    outs = refs[4 + after : 6 + after]
    blocks_ref, cells_ref, acc_ref, count_ref, list_ref, sems = refs[6 + after :]
    off_ref, fx_ref, fy_ref = cells_ref.at[0], cells_ref.at[1], cells_ref.at[2]
    copies = []
    start = 0
    for n, source in enumerate(sources):
        size = source.shape[0]
        copies.append(pltpu.make_async_copy(source, blocks_ref.at[pl.ds(start, size)], sems.at[n]))
        start += size
    for copy in copies:
        copy.start()
    for n in range(3):
        for start, cells in ((0, mine_ref), (own_blocks, other_ref)):
            cells_ref[n, start : start + own_blocks, :] = jnp.concatenate([cells[n], cells[n]], axis=1)
    tile = info_ref[0]
    core = tile & 1
    slots = outs[0].shape[0] * 2
    wide = 2 * own_blocks
    inner = own_blocks - 2 * edge

    @pl.loop(0, slots * per)
    def _(n):
        count_ref[n] = 0

    @pl.loop(0, wide)
    def _(n):
        other = n // own_blocks
        k = n - other * own_blocks
        ident = route_ref[(tile ^ other) * own_blocks + k]
        owner = ident // per
        local = ident - owner * per
        away = (owner ^ tile) >> 1

        @pl.when(((owner ^ tile) & 1) == 0)
        def _():
            place = slot_of(away, core, tile_bits)
            at = place * per + local
            have = count_ref[at]
            list_ref[at * wide + have] = n
            count_ref[at] = have + 1

    for copy in copies:
        copy.wait()

    lanes = lax.broadcasted_iota(jnp.int32, (1, 2 * BLK), 1)
    low_lane = lanes < BLK

    def group_product(at, first, have):
        picked = []
        for g in range(GROUP):
            there = first + g < have
            n = jnp.where(there, list_ref[at * wide + jnp.minimum(first + g, wide - 1)], 0)
            other = n // own_blocks
            k = n - other * own_blocks
            spot = jnp.where(
                k < edge, inner + k, jnp.where(k >= own_blocks - edge, inner + k - inner, k - edge)
            )
            picked.append((there, n, other * own_blocks + spot))
        rhs = jnp.concatenate([blocks_ref[spot] for _, _, spot in picked], axis=0)

        def lane_row(ref):
            halves = []
            for p in range(0, GROUP, 2):
                a = ref[pl.ds(picked[p][1], 1), :]
                b = ref[pl.ds(picked[p + 1][1], 1), :]
                halves.append(jnp.where(low_lane, a, b))
            return jnp.concatenate(halves, axis=1)

        valid = jnp.concatenate(
            [
                jnp.where(
                    low_lane,
                    jnp.where(picked[p][0], 1.0, 0.0),
                    jnp.where(picked[p + 1][0], 1.0, 0.0),
                )
                for p in range(0, GROUP, 2)
            ],
            axis=1,
        ).astype(F32)
        left = lane_row(off_ref)
        right_w = lane_row(fx_ref).astype(F32) / 256.0
        lower_w = lane_row(fy_ref).astype(F32) / 256.0
        column = lax.broadcasted_iota(jnp.int32, (IMGW, GROUP * BLK), 0)
        across = jnp.where(column == left, 1.0 - right_w, 0.0) + jnp.where(
            column == left + 1, right_w, 0.0
        )
        band = jnp.concatenate(
            [((1.0 - lower_w) * valid) * across, (lower_w * valid) * across], axis=0
        ).astype(BF16)
        return jnp.dot(band, rhs, preferred_element_type=F32)

    def overfill(out, place, local, inside):
        at = place * per + local
        have = count_ref[at]

        @pl.when(have > GROUP)
        def _():
            acc_ref[...] = jnp.zeros_like(acc_ref)

            @pl.loop(0, (have + GROUP - 1) // GROUP)
            def _(m):
                acc_ref[...] = acc_ref[...] + group_product(at, m * GROUP, have)

            out[inside[0], inside[1]] = acc_ref[...].astype(BF16)

    for half in (1, 0):
        out = outs[half]
        base = half * (slots // 2)

        @pl.loop(0, (slots // 2) * per // BATCH)
        def _(m, out=out, base=base):
            values = []
            for n in range(BATCH):
                at = base * per + m * BATCH + n
                values.append(group_product(at, 0, count_ref[at]).astype(BF16))
            for n in range(BATCH):
                spot = m * BATCH + n
                out[spot // per, spot % per] = values[n]

        @pl.loop(0, (slots // 2) * per)
        def _(spot, out=out, base=base):
            overfill(out, base + spot // per, spot % per, (spot // per, spot % per))


def swap_low_bits(value):
    return (value & ~3) | ((value & 1) << 1) | ((value >> 1) & 1)


def slot_of(away, core, bits):
    place = 0
    first = jnp.where((core == 1) & (bits >= 2), swap_low_bits(away), away)
    for n in range(bits):
        place = place | (((first >> n) & 1) << (bits - 1 - n))
    return place


def warp_pieces(info, route, cells, cells_other, sources, tiles, per, edge, after):
    own = sources[0].shape[0] + sources[1].shape[0]
    chans = sources[0].shape[2]
    bits = int(math.log2(tiles)) - 1
    slots = tiles // 2
    shape = jax.ShapeDtypeStruct((slots // 2, per, 2 * IMGW, chans), BF16)
    return pl.pallas_call(
        functools.partial(pieces_kernel, (own, per, bits, edge, len(after))),
        in_specs=[SMEM, SMEM, VMEM, VMEM] + [ANY] * (4 + len(after)),
        out_specs=[VMEM] * 2,
        out_shape=[shape] * 2,
        scratch_shapes=[
            pltpu.VMEM((2 * own, BLK, chans), BF16),
            pltpu.VMEM((3, 2 * own, 2 * BLK), jnp.int32),
            pltpu.VMEM((2 * IMGW, chans), F32),
            pltpu.SMEM((slots * per,), jnp.int32),
            pltpu.SMEM((slots * per * 2 * own,), jnp.int32),
            pltpu.SemaphoreType.DMA((4,)),
        ],
        compiler_params=params(),
        cost_estimate=cost(
            2 * slots * per * 2 * IMGW * GROUP * BLK * chans, 2 * (own * 2 * BLK * chans + slots * per * 2 * IMGW * chans)
        ),
        name="warp_pieces",
    )(info, route, cells, cells_other, *sources, *after)


def slope_kernel(img_ref, w_ref, *refs):
    slope_ref = refs[-1]
    value = jnp.dot(img_ref[...], w_ref[...], preferred_element_type=F32)
    sigma = jax.nn.sigmoid(value)
    slope_ref[...] = sigma * (1.0 + value * (1.0 - sigma))


def image_slope(image, weight, after):
    pixels, chans = image.shape
    return pl.pallas_call(
        slope_kernel,
        in_specs=[VMEM, VMEM] + [ANY] * len(after),
        out_specs=VMEM,
        out_shape=jax.ShapeDtypeStruct((pixels, chans), F32),
        compiler_params=params(),
        cost_estimate=cost(2 * pixels * chans * chans, 10 * pixels * chans),
        name="image_slope",
    )(image, weight, *after)


def image_kernel(chunks, order_ref, *refs):
    terms = refs[: sum(chunks)]
    slope_ref, image_ref, w_ref, img_out, keep_ref, send_ref, wide_ref = refs[sum(chunks) :]
    feature = []
    start = 0
    for size in chunks:
        total = terms[start][0].astype(F32)
        for term in terms[start + 1 : start + size]:
            total = total + term[0].astype(F32)
        feature.append(total.reshape(-1, total.shape[-1]))
        start += size
    feature = jnp.concatenate(feature, axis=0)
    scaled = (feature * slope_ref[...]).astype(BF16)
    wide_ref[...] = tn_dot(image_ref[...], scaled)
    spread(wide_ref, order_ref, keep_ref, send_ref)
    img_out[...] = nt_dot(scaled, w_ref[...]).astype(BF16)


def image_layer(order, chunks, slope, image, weight):
    pixels, chans = slope.shape
    half = jax.ShapeDtypeStruct((1, chans // 2, chans), BF16)
    whole = lambda *shape: pl.BlockSpec(shape, lambda n: (0,) * len(shape))
    terms = [term for chunk in chunks for term in chunk]
    return pl.pallas_call(
        functools.partial(image_kernel, tuple(len(chunk) for chunk in chunks)),
        grid=(1,),
        in_specs=[SMEM]
        + [whole(1, *term.shape[1:]) for term in terms]
        + [whole(pixels, chans), whole(pixels, chans), whole(chans, chans)],
        out_specs=[whole(pixels, chans), whole(1, chans // 2, chans), whole(1, chans // 2, chans)],
        out_shape=[jax.ShapeDtypeStruct((pixels, chans), BF16), half, half],
        scratch_shapes=[pltpu.VMEM((chans, chans), F32)],
        compiler_params=params(),
        cost_estimate=cost(4 * pixels * chans * chans, 16 * pixels * chans),
        name="image_layer",
    )(order, *terms, slope, image, weight)


def exchange(value, size_dp, size_tile, flip):
    pairs = []
    for d in range(size_dp):
        for t in range(size_tile):
            dm, tm = flip(t & 1)
            pairs.append((d * size_tile + t, (d ^ dm) * size_tile + (t ^ tm)))
    return lax.ppermute(value, ("dp", "tile"), pairs)


def step_masks(size_dp, size_tile, core):
    dp_masks = [(1 << n, 0) for n in range(int(math.log2(size_dp)))]
    tile_masks = [(0, 1 << n) for n in range(1, int(math.log2(size_tile)))]
    masks = dp_masks + tile_masks
    if core == 1 and len(masks) >= 2:
        masks = [masks[1], masks[0]] + masks[2:]
    return masks


def part_order(me_dp, me_tile, size_dp, size_tile, levels):
    core = me_tile & 1
    kept = []
    for which in (0, 1):
        value = 0
        for dm, tm in step_masks(size_dp, size_tile, which)[: levels - 1]:
            bit = ((me_dp & dm) | (me_tile & tm)) != 0
            value = 2 * value + bit.astype(jnp.int32)
        kept.append(value)
    top = 1 << (levels - 1)
    places = jnp.arange(top, dtype=jnp.int32)
    same = (places ^ jnp.where(core == 0, kept[0], kept[1])) + core * top
    flipped = (places ^ jnp.where(core == 0, kept[1], kept[0])) + (1 - core) * top
    return jnp.concatenate([same, flipped])


def region_sum(terms, axis, low, high):
    total = lax.slice_in_dim(terms[0], low, high, axis=axis).astype(F32)
    for term in terms[1:]:
        total = total + lax.slice_in_dim(term, low, high, axis=axis).astype(F32)
    return total


class Chain:
    def __init__(self, keep, send, sizes, levels, scale):
        self.sizes = sizes
        self.masks = [step_masks(*sizes, core) for core in (0, 1)]
        self.steps = len(self.masks[0])
        self.levels = levels
        self.scale = scale
        self.terms = [keep]
        self.sent = send
        self.recv = None
        self.extent = keep.shape[1]
        self.count = 1 + self.steps + levels
        self.done = 0

    def total(self):
        if self.done <= self.levels:
            return region_sum(self.terms[:-1] + [self.recv], 1, 0, self.extent)
        return self.sent.astype(F32) + self.recv.astype(F32)

    def step(self, *after):
        n = self.done
        which = n
        if n == 0:
            send = self.sent
        elif n < self.levels:
            self.terms[-1] = self.recv
            send = region_sum(self.terms, 1, self.extent // 2, self.extent).astype(BF16)
            self.extent //= 2
        elif n <= self.steps:
            send = self.total().astype(BF16)
        else:
            which = self.levels - (n - self.steps)
            if n == self.steps + 1:
                send = (self.total() * self.scale).astype(BF16)
            else:
                send = jnp.concatenate([self.sent, self.recv], axis=1)
        if after:
            send = together(send, *after)[0]
        flip = lambda core: (0, 1) if which == 0 else self.masks[core][which - 1]
        self.sent = send
        self.recv = exchange(send, *self.sizes, flip)
        if n < self.levels:
            self.terms.append(self.recv)
        self.done += 1

    def more(self):
        return self.done < self.count

    def tie(self, value):
        self.recv, value = together(self.recv, value)
        return value


def place_kernel(halves, order_ref, info_ref, *refs):
    out_ref = refs[-1]
    parts = order_ref.shape[0]
    size = out_ref.shape[1] // (len(halves) * parts // 2)
    for source_ref, half in zip(refs, halves):
        for s in range(parts // 2):
            place = order_ref[half * (parts // 2) + s]
            if len(halves) == 1:
                place = place & (parts // 2 - 1)
            target = pl.multiple_of(place * size, size)
            out_ref[:, pl.ds(target, size), :] = source_ref[:, s * size : (s + 1) * size, :]


def place_parts(order, info, halves, sources, blocks, count, before):
    taps, rows, chans = sources[0].shape
    group = taps // len(blocks)

    def target(t, order_ref, info_ref):
        side = (info_ref[0] & 1) ^ halves[0] if len(halves) == 1 else 0
        return (pick(t, blocks), side, 0)

    return pl.pallas_call(
        functools.partial(place_kernel, halves),
        grid_spec=pltpu.PrefetchScalarGridSpec(
            num_scalar_prefetch=2,
            grid=(len(blocks),),
            in_specs=[pl.BlockSpec((group, rows, chans), lambda t, o, i: (t, 0, 0))] * len(sources)
            + [ANY] * len(before),
            out_specs=pl.BlockSpec((group, len(halves) * rows, chans), target),
        ),
        out_shape=jax.ShapeDtypeStruct((count, 2 * rows, chans), BF16),
        input_output_aliases={2 + len(sources): 0} if before else {},
        compiler_params=params(),
        cost_estimate=cost(0, 4 * taps * len(halves) * rows * chans),
        name="place_parts",
    )(order, info, *sources, *before)


def together(*values):
    return lax.optimization_barrier(values)


def body(grad_out, bev_act, conv_weight, img_in, backbone_weight, route, offsets, frac_x, frac_y):
    tiles = lax.axis_size("tile")
    pods = lax.axis_size("dp")
    my_tile = lax.axis_index("tile")
    my_pod = lax.axis_index("dp")
    grad = grad_out[0]
    rows, cols, chans = grad.shape
    image = img_in[0]
    weight = jnp.transpose(conv_weight, (1, 2, 0, 3))
    per = image.shape[0] // (2 * IMGW)
    own = rows * cols // BLK
    edge_blocks = cols // BLK
    steps = int(math.log2(pods * tiles))
    levels = min(CONV_LEVELS, steps, int(math.log2(chans // 16)))
    back_levels = min(2, levels)
    order = part_order(my_pod, my_tile, pods, tiles, levels)
    back_order = part_order(my_pod, my_tile, pods, tiles, back_levels)
    cell_scale = 1.0 / math.sqrt(pods * tiles * rows * cols)
    pixel_scale = 1.0 / math.sqrt(pods * tiles * image.shape[0])

    forward = [(i, i + 1) for i in range(tiles - 1)]
    backward = [(b, a) for a, b in forward]
    low = lax.ppermute(grad[rows - 1], "tile", forward)
    high = lax.ppermute(grad[0], "tile", backward)

    core_swap = [(t, t ^ 1) for t in range(tiles)]
    cells = jnp.stack([offsets[0], frac_x[0], frac_y[0]]).reshape(3, own, BLK)
    cells_other = lax.ppermute(cells, "tile", core_swap)

    info = jnp.reshape(my_tile, (1,)).astype(jnp.int32)
    inner = bev_rows(grad, [], weight, tuple(range(1, rows - 1)), [])
    inner_other = lax.ppermute(inner, "tile", core_swap)
    sizes = (pods, tiles)
    act = bev_act[0]
    edge = bev_rows(grad, [low, high], weight, (0, rows - 1), [inner, cells_other])
    edge_other = lax.ppermute(edge, "tile", core_swap)
    slope = image_slope(image, backbone_weight, [edge])
    as_blocks = lambda value: value.reshape(-1, BLK, chans)
    keep, send = warp_pieces(
        info,
        route[0],
        cells,
        cells_other,
        [as_blocks(v) for v in (inner, edge, inner_other, edge_other)],
        tiles,
        per,
        edge_blocks,
        [slope],
    )

    tile_masks = [(0, 1 << n) for n in range(1, int(math.log2(tiles)))]
    swapped = [tile_masks[1], tile_masks[0]] + tile_masks[2:] if len(tile_masks) > 1 else tile_masks
    warp_masks = (tile_masks, swapped)
    warp = [keep]
    extent = keep.shape[0]
    last = len(tile_masks) - 1

    def warp_step(n, send):
        nonlocal extent
        if n > 0:
            send = region_sum(warp, 0, extent // 2, extent).astype(BF16)
            extent //= 2
        warp.append(exchange(send, *sizes, lambda core: warp_masks[core][n]))

    warp_step(0, send)
    early_taps = tuple((i, j) for j in (1, 0, 2) for i in (1, 0))
    late_taps = tuple((2, j) for j in (1, 0, 2))
    outs = wgrad(
        order, act, grad, [low, high], early_taps, tuple(3 * i + j for i, j in early_taps), 6, [], [keep]
    )
    early = Chain(*outs, sizes, levels, cell_scale)
    early.step()
    outs = list(wgrad(order, act, grad, [low, high], late_taps, (1, 0, 2), 3, [], [outs[0]]))
    outs[0] = early.tie(outs[0])
    late = Chain(*outs, sizes, levels, cell_scale)
    warp[1], late.sent = together(warp[1], late.sent)

    warp_step(1, None)
    late.step()
    early.step(warp[1])
    warp[2] = late.tie(warp[2])

    warp_step(2, None)
    late.step(warp[2])
    early.step()
    late.step()
    warp[3] = early.tie(warp[3])
    warp[3] = late.tie(warp[3])
    for n in range(3, last + 1):
        warp_step(n, None)

    image_grad, keep_img, send_img = image_layer(back_order, [warp], slope, image, backbone_weight)
    back = Chain(keep_img, send_img, sizes, back_levels, pixel_scale)
    chains = [back, early, late]
    before = [send_img]
    while any(chain.more() for chain in chains):
        for chain in chains:
            if chain.more():
                held = chain.recv
                chain.step(*before)
                before = [] if held is None else [held]

    conv_grad = place_parts(order, info, (0,), [early.sent], (0, 1), 9, [])
    conv_grad = place_parts(order, info, (1,), [early.recv], (0, 1), 9, [conv_grad])
    conv_grad = place_parts(order, info, (0, 1), [late.sent, late.recv], (2,), 9, [conv_grad])
    backbone_grad = place_parts(back_order, info, (0, 1), [back.sent, back.recv], (0,), 1, [])[0]
    conv_grad = jnp.transpose(conv_grad.reshape(3, 3, chans, chans), (2, 0, 1, 3))
    return (image_grad[None], conv_grad, backbone_grad)


def solution(mesh):
    return jax.shard_map(
        body,
        mesh=mesh,
        in_specs=(
            P("dp", "tile", None, None),
            P("dp", "tile", None, None),
            P(),
            P("dp", "tile", None),
            P(),
            P("dp", None),
            P("dp", "tile"),
            P("dp", "tile"),
            P("dp", "tile"),
        ),
        out_specs=(P("dp", "tile", None), P(), P()),
        check_vma=False,
    )
```

time: 230 us -> 211 us (0.917)
  starting transfers between devices: 47.1 us -> 36.8 us
  waiting for transfers between devices: 85.9 us -> 79.3 us
  local copies, waits for them, and re-layouts: 8.41 us -> 2.97 us
  other arithmetic: 14.2 us -> 18.6 us
    ppermute x36 -> x26, starting transfers between devices: 39.7 us -> 27 us  [exchange(): return lax.ppermute(value, ('dp', 'tile'), pairs)]
    ppermute x36 -> x26, waiting for transfers between devices: 85.9 us -> 79.3 us  [exchange(): return lax.ppermute(value, ('dp', 'tile'), pairs)]
    unnamed x69 -> x30, local copies, waits for them, and re-layouts: 6.2 us -> 0.66 us
    convert_element_type x16 -> x17, other arithmetic: 10.6 us -> 14.6 us  [the longest x5 6.39 us: step(): send = region_sum(self.terms, 1, self.extent // 2, self.extent).astype(BF16)]
    ppermute x1, starting transfers between devices: 0.01 us -> 2.78 us  [body(): edge_other = lax.ppermute(edge, 'tile', core_swap)]
    ppermute x1, starting transfers between devices: 2.55 us -> 0.03 us  [body(): inner_other = lax.ppermute(inner, 'tile', core_swap)]
    concatenate x11 -> x7, other arithmetic: 0.92 us -> 3.39 us  [the longest x5 2.28 us: step(): send = jnp.concatenate([self.sent, self.recv], axis=1)]
    pallas_call x7 -> x8, Pallas kernels: 45.5 us -> 45.4 us  [the longest x2 20.5 us: bev_rows(): pl.pallas_call(kernel, grid=(3,), in_specs=[whole(rows, cols, chans)] + [...]
  transfers between devices with their start and end apart: 41 -> 31, of which waited for: 17 -> 16; matrix products, arithmetic and copies ran while one was open for 7% -> 9% of each run, Pallas kernels for 29% -> 28%
where the time goes in v3:
time: 211 us
  waiting for transfers between devices  79.3 us (38%)
  Pallas kernels  72.2 us (34%)
  starting transfers between devices  36.8 us (17%)
  other arithmetic  18.6 us (9%)
  local copies, waits for them, and re-layouts  2.97 us (1%)
    ppermute x26, waiting for transfers between devices, exchange(): return lax.ppermute(value, ('dp', 'tile'), pairs)  79.3 us
    ppermute x26, starting transfers between devices, exchange(): return lax.ppermute(value, ('dp', 'tile'), pairs)  27 us
    pallas_call x2, Pallas kernels, wgrad(): pl.pallas_call(functools.partial(wgrad_kernel, taps, len(halos) > 0), gri...  23 us
    pallas_call x2, Pallas kernels, bev_rows(): pl.pallas_call(kernel, grid=(3,), in_specs=[whole(rows, cols, chans)] + [...  20.5 us
    pallas_call x4, Pallas kernels, place_parts(): pl.pallas_call(functools.partial(place_kernel, halves), grid_spec=pltpu.P...  11.8 us
    pallas_call x1, Pallas kernels, warp_pieces(): pl.pallas_call(functools.partial(pieces_kernel, (own, per, bits, edge, le...  10.3 us
    convert_element_type x5, other arithmetic, step(): send = region_sum(self.terms, 1, self.extent // 2, self.extent).astype(BF16)  6.39 us
  transfers between devices with their start and end apart: 31, of which 16 were waited for; matrix products, arithmetic and copies ran while one was open for 9% of the time, Pallas kernels for 28%

profile of v3, /device:TPU:0, one launch (start us, length us, event | category | flops | bytes accessed | tf_op | source)
XLA Modules:
  0.0 210.8 jit_solution(7536489144312035257)
XLA Ops:
  0.7 2.2 %slice_bitcast_fusion = (bf16[640,512]{1,0:T(8,128)(2,1)}, bf16[640,512]{1,0:T(8,128)(2,1)S(1)}) fusion(bf16[1,4,640,512]{3,2,1,0:T(8,128)(2,1)} %param.9), kind=kLoop, calls=%fused_computation.11 | loop fusion | bytes 2621440 | tf_op jit(solution)/shard_map/squeeze | solution.py:568
  2.9 1.3 collective-permute-start.2
  4.2 3.9 %collective-permute-start.1 = (bf16[640,512]{1,0:T(8,128)(2,1)S(1)}, bf16[640,512]{1,0:T(8,128)(2,1)}, u32[]{:S(2)}, u32[]{:S(2)}) collective-permute-start(bf16[640,512]{1,0:T(8,128)(2,1)S(1)} %get-tuple-element.76), channel_id=1, source_target_pairs={{0,1},{1,2},{2,3},{3,4},{4,5},{5,6},{6,7},{7,8},{8,9},{9,10},{10,1... | collective-permute-start | bytes 1966088 | tf_op jit(solution)/shard_map/ppermute | solution.py:567
  8.2 1.8 collective-permute-start
  10.0 10.1 %bev_rows.2.refs_3_ = bf16[2,640,512]{2,1,0:T(8,128)(2,1)} custom-call(bf16[4,640,512]{2,1,0:T(8,128)(2,1)} %bitcast.24, bf16[3,3,512,512]{3,2,1,0:T(8,128)(2,1)} %bitcast.29), custom_call_target="tpu_custom_call" | custom-call | flops 6039797760 | bytes 9961472 | tf_op jit(solution)/shard_map/bev_rows/pallas_call | solution.py:88
  20.8 10.4 %bev_rows.3.refs_0_ = bf16[2,640,512]{2,1,0:T(8,128)(2,1)} custom-call(bf16[4,640,512]{2,1,0:T(8,128)(2,1)} %bitcast.25, bf16[640,512]{1,0:T(8,128)(2,1)} %collective-permute-done.1.refs_0_, bf16[640,512]{1,0:T(8,128)(2,1)} %collective-permute-done.2.refs_1_, bf16[3,3,512,512]{3,2,1,0:T(8,128)(2,1)} %bitcast.30, bf16[2,640,512]{2,1,0:T(8,128)(2,1)} %bev_rows.2.refs_3_, ...), custom_call_target="tpu_custom_call" | custom-call | flops 6039797760 | bytes 9961472 | tf_op jit(solution)/shard_map/bev_rows/pallas_call | solution.py:88
  31.1 2.8 %collective-permute-start.4 = (bf16[2,640,512]{2,1,0:T(8,128)(2,1)}, bf16[2,640,512]{2,1,0:T(8,128)(2,1)}, u32[]{:S(2)}, u32[]{:S(2)}) collective-permute-start(bf16[2,640,512]{2,1,0:T(8,128)(2,1)} %bev_rows.3.refs_0_), channel_id=1, source_target_pairs={{0,1},{1,0},{2,3},{3,2},{4,5},{5,4},{6,7},{7,6},{8,9},{9,8},{10,11... | collective-permute-start | bytes 3932168 | tf_op jit(solution)/shard_map/ppermute | solution.py:580
  34.5 2.8 %image_slope.1.refs_4_ = f32[512,512]{1,0:T(8,128)} custom-call(bf16[512,512]{1,0:T(8,128)(2,1)} %bitcast.21, bf16[512,512]{1,0:T(8,128)(2,1)} %refs_6_.1, bf16[2,640,512]{2,1,0:T(8,128)(2,1)} %bev_rows.3.refs_0_), custom_call_target="tpu_custom_call" | custom-call | flops 268435456 | bytes 2621440 | tf_op jit(solution)/shard_map/image_slope/pallas_call | solution.py:360
  37.3 10.3 %warp_pieces.1 = (bf16[4,4,128,512]{3,2,1,0:T(8,128)(2,1)}, bf16[4,4,128,512]{3,2,1,0:T(8,128)(2,1)}) custom-call(s32[1]{0:T(128)} %bitcast.info_ref, s32[640]{0:T(1024)} %reduce.route_ref, s32[3,40,64]{2,1,0:T(8,128)} %copy-done.8, s32[3,40,64]{2,1,0:T(8,128)} %copy-done.9, bf16[20,64,512]{2,1,0:T(8,128)(2,1)} %bitcast.23, bf16[20,64,512]{2,1,0:T(8,128)(2,1)} %bitcast.20, ...), custom_call_target="tpu_custom_call" | custom-call | flops 1073741824 | bytes 9437184 | tf_op jit(solution)/shard_map/warp_pieces/pallas_call | solution.py:330
  47.6 2.6 %collective-permute-start.5 = (bf16[4,4,128,512]{3,2,1,0:T(8,128)(2,1)}, bf16[4,4,128,512]{3,2,1,0:T(8,128)(2,1)}, u32[]{:S(2)}, u32[]{:S(2)}) collective-permute-start(bf16[4,4,128,512]{3,2,1,0:T(8,128)(2,1)} %get-tuple-element.40), channel_id=1, source_target_pairs={{0,2},{1,5},{2,0},{3,7},{4,6},{5,1},{6,4},{7,3},{8,10},{9,13},{10,... | collective-permute-start | bytes 6291464 | tf_op jit(solution)/shard_map/ppermute | solution.py:415
  50.7 14.0 %wgrad.2 = (bf16[6,256,512]{2,1,0:T(8,128)(2,1)}, bf16[6,256,512]{2,1,0:T(8,128)(2,1)}) custom-call(s32[8]{0:T(128)} %pad_add_fusion.2.order_ref, bf16[4,640,512]{2,1,0:T(8,128)(2,1)} %bitcast.31, bf16[2560,512]{1,0:T(8,128)(2,1)} %bitcast.26, bf16[640,512]{1,0:T(8,128)(2,1)} %collective-permute-done.1.refs_0_, ...), custom_call_target="tpu_custom_call" | custom-call | flops 8053063680 | bytes 8388608 | tf_op jit(solution)/shard_map/wgrad/pallas_call | solution.py:164
  64.8 9.0 %wgrad.3 = (bf16[3,256,512]{2,1,0:T(8,128)(2,1)}, bf16[3,256,512]{2,1,0:T(8,128)(2,1)}) custom-call(s32[8]{0:T(128)} %pad_add_fusion.2.order_ref, bf16[4,640,512]{2,1,0:T(8,128)(2,1)} %bitcast.32, bf16[2560,512]{1,0:T(8,128)(2,1)} %bitcast.27, bf16[640,512]{1,0:T(8,128)(2,1)} %collective-permute-done.1.refs_0_, ...), custom_call_target="tpu_custom_call" | custom-call | flops 4026531840 | bytes 6815744 | tf_op jit(solution)/shard_map/wgrad/pallas_call | solution.py:164
  74.5 2.0 add_convert_fusion
  76.5 1.6 collective-permute-start.7
  78.2 1.3 add_convert_fusion.1
  79.6 2.4 %collective-permute-start.11 = (bf16[6,128,512]{2,1,0:T(8,128)(2,1)S(1)}, bf16[6,128,512]{2,1,0:T(8,128)(2,1)S(1)}, u32[]{:S(2)}, u32[]{:S(2)}) collective-permute-start(bf16[6,128,512]{2,1,0:T(8,128)(2,1)S(1)} %add_convert_fusion.1), channel_id=1, source_target_pairs={{0,16},{1,3},{2,18},{3,1},{4,20},{5,7},{6,22},{7,5},{8,24},{9,11},... | collective-permute-start | bytes 2359304 | tf_op jit(solution)/shard_map/ppermute | solution.py:415
  82.0 9.4 %collective-permute-done.7.refs_2_ = bf16[2,4,128,512]{3,2,1,0:T(8,128)(2,1)S(1)} collective-permute-done((bf16[2,4,128,512]{3,2,1,0:T(8,128)(2,1)S(1)}, bf16[2,4,128,512]{3,2,1,0:T(8,128)(2,1)S(1)}, u32[]{:S(2)}, u32[]{:S(2)}) %collective-permute-start.7) | collective-permute-done | bytes 1048608 | tf_op jit(solution)/shard_map/ppermute | solution.py:415
  91.4 1.8 add_convert_fusion.2
  93.1 2.7 %collective-permute-start.13 = (bf16[1,4,128,512]{3,2,1,0:T(8,128)(2,1)S(1)}, bf16[1,4,128,512]{3,2,1,0:T(8,128)(2,1)S(1)}, u32[]{:S(2)}, u32[]{:S(2)}) collective-permute-start(bf16[1,4,128,512]{3,2,1,0:T(8,128)(2,1)S(1)} %add_convert_fusion.2), channel_id=1, source_target_pairs={{0,8},{1,9},{2,10},{3,11},{4,12},{5,13},{6,14},{7,15},{8,0},{9,1},... | collective-permute-start | bytes 1572872 | tf_op jit(solution)/shard_map/ppermute | solution.py:415
  95.8 2.2 %add_convert_fusion.5 = bf16[6,64,512]{2,1,0:T(8,128)(2,1)} fusion(bf16[6,128,512]{2,1,0:T(8,128)(2,1)S(1)} %collective-permute-done.11, bf16[6,256,512]{2,1,0:T(8,128)(2,1)} %collective-permute-done.8, bf16[6,256,512]{2,1,0:T(8,128)(2,1)S(1)} %copy-done.2), kind=kLoop, calls=%fused_computation.9 | loop fusion | flops 1179648 | bytes 1572864 | tf_op jit(solution)/shard_map/convert_element_type | solution.py:476
  98.0 2.0 collective-permute-start.12
  100.8 1.5 collective-permute-start.9
  102.3 3.9 %collective-permute-done.12 = bf16[6,64,512]{2,1,0:T(8,128)(2,1)} collective-permute-done((bf16[6,64,512]{2,1,0:T(8,128)(2,1)}, bf16[6,64,512]{2,1,0:T(8,128)(2,1)}, u32[]{:S(2)}, u32[]{:S(2)}) %collective-permute-start.12) | collective-permute-done | bytes 393248 | tf_op jit(solution)/shard_map/ppermute | solution.py:415
  106.2 12.3 %collective-permute-done.13.refs_3_ = bf16[1,4,128,512]{3,2,1,0:T(8,128)(2,1)S(1)} collective-permute-done((bf16[1,4,128,512]{3,2,1,0:T(8,128)(2,1)S(1)}, bf16[1,4,128,512]{3,2,1,0:T(8,128)(2,1)S(1)}, u32[]{:S(2)}, u32[]{:S(2)}) %collective-permute-start.13) | collective-permute-done | bytes 524320 | tf_op jit(solution)/shard_map/ppermute | solution.py:415
  118.5 1.6 add_convert_fusion.4
  120.2 1.1 add_convert_fusion.9
  121.4 1.8 collective-permute-start.10
  123.7 3.5 %collective-permute-done.10 = bf16[3,64,512]{2,1,0:T(8,128)(2,1)} collective-permute-done((bf16[3,64,512]{2,1,0:T(8,128)(2,1)S(1)}, bf16[3,64,512]{2,1,0:T(8,128)(2,1)}, u32[]{:S(2)}, u32[]{:S(2)}) %collective-permute-start.10) | collective-permute-done | bytes 196640 | tf_op jit(solution)/shard_map/ppermute | solution.py:415
  127.2 3.8 %image_layer.1 = (bf16[512,512]{1,0:T(8,128)(2,1)}, bf16[1,256,512]{2,1,0:T(8,128)(2,1)}, bf16[1,256,512]{2,1,0:T(8,128)(2,1)}) custom-call(s32[4]{0:T(128)} %pad_add_fusion.1.order_ref, bf16[4,4,128,512]{3,2,1,0:T(8,128)(2,1)} %get-tuple-element.39.refs_2_.refs_0_, bf16[4,4,128,512]{3,2,1,0:T(8,128)(2,1)} %collective-permute-done.5.refs_1_, ...), custom_call_target="tpu_custom_call" | custom-call | flops 536870912 | bytes 4194304 | tf_op jit(solution)/shard_map/image_layer/pallas_call | solution.py:394
  131.0 1.1 add_convert_fusion.3
  132.7 2.6 %collective-permute-start.18 = (bf16[6,64,512]{2,1,0:T(8,128)(2,1)S(1)}, bf16[6,64,512]{2,1,0:T(8,128)(2,1)S(1)}, u32[]{:S(2)}, u32[]{:S(2)}) collective-permute-start(bf16[6,64,512]{2,1,0:T(8,128)(2,1)S(1)} %add_convert_fusion.3), channel_id=1, source_target_pairs={{0,8},{1,9},{2,10},{3,11},{4,12},{5,13},{6,14},{7,15},{8,0},{9,1},... | collective-permute-start | bytes 1179656 | tf_op jit(solution)/shard_map/ppermute | solution.py:415
  135.3 0.9 add_convert_fusion.13
  136.3 2.0 collective-permute-start.20
  138.3 15.0 %collective-permute-done.18 = bf16[6,64,512]{2,1,0:T(8,128)(2,1)S(1)} collective-permute-done((bf16[6,64,512]{2,1,0:T(8,128)(2,1)S(1)}, bf16[6,64,512]{2,1,0:T(8,128)(2,1)S(1)}, u32[]{:S(2)}, u32[]{:S(2)}) %collective-permute-start.18) | collective-permute-done | bytes 393248 | tf_op jit(solution)/shard_map/ppermute | solution.py:415
  153.4 1.8 collective-permute-start.21
  155.2 1.3 add_convert_fusion.8
  156.6 6.2 %collective-permute-done.14 = bf16[3,64,512]{2,1,0:T(8,128)(2,1)S(1)} collective-permute-done((bf16[3,64,512]{2,1,0:T(8,128)(2,1)S(1)}, bf16[3,64,512]{2,1,0:T(8,128)(2,1)S(1)}, u32[]{:S(2)}, u32[]{:S(2)}) %collective-permute-start.14) | collective-permute-done | bytes 196640 | tf_op jit(solution)/shard_map/ppermute | solution.py:415
  163.7 4.1 %collective-permute-done.23 = bf16[1,128,512]{2,1,0:T(8,128)(2,1)S(1)} collective-permute-done((bf16[1,128,512]{2,1,0:T(8,128)(2,1)S(1)}, bf16[1,128,512]{2,1,0:T(8,128)(2,1)S(1)}, u32[]{:S(2)}, u32[]{:S(2)}) %collective-permute-start.23) | collective-permute-done | bytes 131104 | tf_op jit(solution)/shard_map/ppermute | solution.py:415
  169.1 9.2 %collective-permute-done.16 = bf16[3,64,512]{2,1,0:T(8,128)(2,1)S(1)} collective-permute-done((bf16[3,64,512]{2,1,0:T(8,128)(2,1)S(1)}, bf16[3,64,512]{2,1,0:T(8,128)(2,1)S(1)}, u32[]{:S(2)}, u32[]{:S(2)}) %collective-permute-start.16) | collective-permute-done | bytes 196640 | tf_op jit(solution)/shard_map/ppermute | solution.py:415
  179.8 1.4 pad_maximum_fusion.refs_0_
  181.2 2.2 %collective-permute-done.26 = bf16[1,128,512]{2,1,0:T(8,128)(2,1)S(1)} collective-permute-done((bf16[1,128,512]{2,1,0:T(8,128)(2,1)S(1)}, bf16[1,128,512]{2,1,0:T(8,128)(2,1)S(1)}, u32[]{:S(2)}, u32[]{:S(2)}) %collective-permute-start.26) | collective-permute-done | bytes 131104 | tf_op jit(solution)/shard_map/ppermute | solution.py:415
  184.6 2.5 %collective-permute-start.28 = (bf16[1,128,512]{2,1,0:T(8,128)(2,1)S(1)}, bf16[1,128,512]{2,1,0:T(8,128)(2,1)S(1)}, u32[]{:S(2)}, u32[]{:S(2)}) collective-permute-start(bf16[1,128,512]{2,1,0:T(8,128)(2,1)S(1)} %add_convert_fusion.10), channel_id=1, source_target_pairs={{0,8},{1,9},{2,10},{3,11},{4,12},{5,13},{6,14},{7,15},{8,0},{9,1},... | collective-permute-start | bytes 393224 | tf_op jit(solution)/shard_map/ppermute | solution.py:415
  187.1 4.9 %collective-permute-done.22 = bf16[3,128,512]{2,1,0:T(8,128)(2,1)S(1)} collective-permute-done((bf16[3,128,512]{2,1,0:T(8,128)(2,1)S(1)}, bf16[3,128,512]{2,1,0:T(8,128)(2,1)S(1)}, u32[]{:S(2)}, u32[]{:S(2)}) %collective-permute-start.22) | collective-permute-done | bytes 393248 | tf_op jit(solution)/shard_map/ppermute | solution.py:415
  193.3 5.0 %collective-permute-done.29 = bf16[1,128,512]{2,1,0:T(8,128)(2,1)S(1)} collective-permute-done((bf16[1,128,512]{2,1,0:T(8,128)(2,1)S(1)}, bf16[1,128,512]{2,1,0:T(8,128)(2,1)S(1)}, u32[]{:S(2)}, u32[]{:S(2)}) %collective-permute-start.29) | collective-permute-done | bytes 131104 | tf_op jit(solution)/shard_map/ppermute | solution.py:415
  199.0 3.0 %place_parts.4.refs_1_ = bf16[9,512,512]{2,1,0:T(8,128)(2,1)} custom-call(s32[8]{0:T(128)} %pad_add_fusion.2.order_ref, s32[1]{0:T(128)} %bitcast.info_ref, bf16[6,256,512]{2,1,0:T(8,128)(2,1)} %pad_maximum_fusion.refs_0_), custom_call_target="tpu_custom_call" | custom-call | bytes 3145728 | tf_op jit(solution)/shard_map/place_parts/pallas_call | solution.py:524
  202.0 2.5 %place_parts.7 = bf16[1,512,512]{2,1,0:T(8,128)(2,1)} custom-call(s32[4]{0:T(128)} %pad_add_fusion.1.order_ref, s32[1]{0:T(128)} %bitcast.info_ref, bf16[1,256,512]{2,1,0:T(8,128)(2,1)} %pad_maximum_fusion.4.refs_0_, bf16[1,256,512]{2,1,0:T(8,128)(2,1)} %collective-permute-done.30.refs_1_), custom_call_target="tpu_custom_call" | custom-call | bytes 1048576 | tf_op jit(solution)/shard_map/place_parts/pallas_call | solution.py:524
  204.5 3.0 %place_parts.5.refs_2_ = bf16[9,512,512]{2,1,0:T(8,128)(2,1)} custom-call(s32[8]{0:T(128)} %pad_add_fusion.2.order_ref, s32[1]{0:T(128)} %bitcast.info_ref, bf16[6,256,512]{2,1,0:T(8,128)(2,1)} %collective-permute-done.27.refs_0_, bf16[9,512,512]{2,1,0:T(8,128)(2,1)} %place_parts.4.refs_1_), custom_call_target="tpu_custom_call", output_to_operand_aliasing={{}: (3, {})} | custom-call | bytes 3145728 | tf_op jit(solution)/shard_map/place_parts/pallas_call | solution.py:524
  207.5 3.3 %place_parts.6 = bf16[9,512,512]{2,1,0:T(8,128)(2,1)} custom-call(s32[8]{0:T(128)} %pad_add_fusion.2.order_ref, s32[1]{0:T(128)} %bitcast.info_ref, bf16[3,256,512]{2,1,0:T(8,128)(2,1)} %copy-done, bf16[3,256,512]{2,1,0:T(8,128)(2,1)} %collective-permute-done.25.refs_1_, bf16[9,512,512]{2,1,0:T(8,128)(2,1)} %place_parts.5.refs_2_), custom_call_target="tpu_custom_call", output_to_operand_aliasing={{}: (4, {})} | custom-call | bytes 3145728 | tf_op jit(solution)/shard_map/place_parts/pallas_call | solution.py:524
  (85 shorter events, 11.9 us)
Async XLA Ops:
  0.6 7.4 %copy-start.10 = (s32[1,2560]{1,0:T(1,128)S(1)}, s32[1,2560]{1,0:T(1,128)}, u32[]{:S(2)}) copy-start(s32[1,2560]{1,0:T(1,128)} %param.17) | copy-start | bytes 30724
  0.6 7.4 %copy-start.11 = (s32[1,2560]{1,0:T(1,128)S(1)}, s32[1,2560]{1,0:T(1,128)}, u32[]{:S(2)}) copy-start(s32[1,2560]{1,0:T(1,128)} %param.16) | copy-start | bytes 30724
  0.7 7.4 %copy-start.12 = (s32[1,2560]{1,0:T(1,128)S(1)}, s32[1,2560]{1,0:T(1,128)}, u32[]{:S(2)}) copy-start(s32[1,2560]{1,0:T(1,128)} %param.15) | copy-start | bytes 30724
  2.9 17.2 %collective-permute-start.2 = (bf16[640,512]{1,0:T(8,128)(2,1)}, bf16[640,512]{1,0:T(8,128)(2,1)}, u32[]{:S(2)}, u32[]{:S(2)}) collective-permute-start(bf16[640,512]{1,0:T(8,128)(2,1)} %get-tuple-element.75), channel_id=1, source_target_pairs={{1,0},{2,1},{3,2},{4,3},{5,4},{6,5},{7,6},{8,7},{9,8},{10,9},{11,1... | collective-permute-start | bytes 1966088 | tf_op jit(solution)/shard_map/ppermute | solution.py:568
  4.2 16.0 %collective-permute-start.1 = (bf16[640,512]{1,0:T(8,128)(2,1)S(1)}, bf16[640,512]{1,0:T(8,128)(2,1)}, u32[]{:S(2)}, u32[]{:S(2)}) collective-permute-start(bf16[640,512]{1,0:T(8,128)(2,1)S(1)} %get-tuple-element.76), channel_id=1, source_target_pairs={{0,1},{1,2},{2,3},{3,4},{4,5},{5,6},{6,7},{7,8},{8,9},{9,10},{10,1... | collective-permute-start | bytes 1966088 | tf_op jit(solution)/shard_map/ppermute | solution.py:567
  8.2 11.9 %copy-start.8 = (s32[3,40,64]{2,1,0:T(8,128)}, s32[3,40,64]{2,1,0:T(8,128)S(1)}, u32[]{:S(2)}) copy-start(s32[3,40,64]{2,1,0:T(8,128)S(1)} %reshape.32.mine_ref) | copy-start | bytes 92164
  8.2 11.9 %collective-permute-start = (s32[3,40,64]{2,1,0:T(8,128)S(1)}, s32[3,40,64]{2,1,0:T(8,128)S(1)}, u32[]{:S(2)}, u32[]{:S(2)}) collective-permute-start(s32[3,40,64]{2,1,0:T(8,128)S(1)} %reshape.32.mine_ref), channel_id=1, source_target_pairs={{0,1},{1,0},{2,3},{3,2},{4,5},{5,4},{6,7},{7,6},{8,9},{9,8},{10,11... | collective-permute-start | bytes 92168 | tf_op jit(solution)/shard_map/ppermute | solution.py:572
  20.1 13.8 %copy-start.13 = (s32[1,640]{1,0:T(1,128)S(1)}, s32[1,640]{1,0:T(1,128)}, u32[]{:S(2)}) copy-start(s32[1,640]{1,0:T(1,128)} %param.14) | copy-start | bytes 7684
  20.1 17.2 %collective-permute-start.3 = (bf16[2,640,512]{2,1,0:T(8,128)(2,1)}, bf16[2,640,512]{2,1,0:T(8,128)(2,1)}, u32[]{:S(2)}, u32[]{:S(2)}) collective-permute-start(bf16[2,640,512]{2,1,0:T(8,128)(2,1)} %bev_rows.2.refs_3_), channel_id=1, source_target_pairs={{0,1},{1,0},{2,3},{3,2},{4,5},{5,4},{6,7},{7,6},{8,9},{9,8},{10,11... | collective-permute-start | bytes 3932168 | tf_op jit(solution)/shard_map/ppermute | solution.py:576
  20.1 0.6 copy-start.9
  31.1 6.1 %collective-permute-start.4 = (bf16[2,640,512]{2,1,0:T(8,128)(2,1)}, bf16[2,640,512]{2,1,0:T(8,128)(2,1)}, u32[]{:S(2)}, u32[]{:S(2)}) collective-permute-start(bf16[2,640,512]{2,1,0:T(8,128)(2,1)} %bev_rows.3.refs_0_), channel_id=1, source_target_pairs={{0,1},{1,0},{2,3},{3,2},{4,5},{5,4},{6,7},{7,6},{8,9},{9,8},{10,11... | collective-permute-start | bytes 3932168 | tf_op jit(solution)/shard_map/ppermute | solution.py:580
  47.6 26.9 %collective-permute-start.5 = (bf16[4,4,128,512]{3,2,1,0:T(8,128)(2,1)}, bf16[4,4,128,512]{3,2,1,0:T(8,128)(2,1)}, u32[]{:S(2)}, u32[]{:S(2)}) collective-permute-start(bf16[4,4,128,512]{3,2,1,0:T(8,128)(2,1)} %get-tuple-element.40), channel_id=1, source_target_pairs={{0,2},{1,5},{2,0},{3,7},{4,6},{5,1},{6,4},{7,3},{8,10},{9,13},{10,... | collective-permute-start | bytes 6291464 | tf_op jit(solution)/shard_map/ppermute | solution.py:415
  64.8 13.4 %collective-permute-start.8 = (bf16[6,256,512]{2,1,0:T(8,128)(2,1)}, bf16[6,256,512]{2,1,0:T(8,128)(2,1)}, u32[]{:S(2)}, u32[]{:S(2)}) collective-permute-start(bf16[6,256,512]{2,1,0:T(8,128)(2,1)} %get-tuple-element.46), channel_id=1, source_target_pairs={{0,1},{1,0},{2,3},{3,2},{4,5},{5,4},{6,7},{7,6},{8,9},{9,8},{10,11... | collective-permute-start | bytes 4718600 | tf_op jit(solution)/shard_map/ppermute | solution.py:415
  74.5 3.6 %copy-start.14 = (bf16[3,256,512]{2,1,0:T(8,128)(2,1)S(1)}, bf16[3,256,512]{2,1,0:T(8,128)(2,1)}, u32[]{:S(2)}) copy-start(bf16[3,256,512]{2,1,0:T(8,128)(2,1)} %get-tuple-element.44) | copy-start | bytes 2359300
  74.5 3.7 %copy-start.2 = (bf16[6,256,512]{2,1,0:T(8,128)(2,1)S(1)}, bf16[6,256,512]{2,1,0:T(8,128)(2,1)}, u32[]{:S(2)}) copy-start(bf16[6,256,512]{2,1,0:T(8,128)(2,1)} %get-tuple-element.41.refs_2_) | copy-start | bytes 4718596
  76.5 14.9 %collective-permute-start.7 = (bf16[2,4,128,512]{3,2,1,0:T(8,128)(2,1)S(1)}, bf16[2,4,128,512]{3,2,1,0:T(8,128)(2,1)S(1)}, u32[]{:S(2)}, u32[]{:S(2)}) collective-permute-start(bf16[2,4,128,512]{3,2,1,0:T(8,128)(2,1)S(1)} %add_convert_fusion), channel_id=1, source_target_pairs={{0,4},{1,3},{2,6},{3,1},{4,0},{5,7},{6,2},{7,5},{8,12},{9,11},{10,... | collective-permute-start | bytes 3145736 | tf_op jit(solution)/shard_map/ppermute | solution.py:415
  78.1 3.8 %collective-permute-start.6 = (bf16[3,256,512]{2,1,0:T(8,128)(2,1)S(1)}, bf16[3,256,512]{2,1,0:T(8,128)(2,1)S(1)}, u32[]{:S(2)}, u32[]{:S(2)}) collective-permute-start(bf16[3,256,512]{2,1,0:T(8,128)(2,1)S(1)} %copy-done.14), channel_id=1, source_target_pairs={{0,1},{1,0},{2,3},{3,2},{4,5},{5,4},{6,7},{7,6},{8,9},{9,8},{10,11... | collective-permute-start | bytes 2359304 | tf_op jit(solution)/shard_map/ppermute | solution.py:415
  79.6 20.4 %copy-start.3 = (bf16[3,256,512]{2,1,0:T(8,128)(2,1)S(1)}, bf16[3,256,512]{2,1,0:T(8,128)(2,1)}, u32[]{:S(2)}) copy-start(bf16[3,256,512]{2,1,0:T(8,128)(2,1)} %get-tuple-element.48) | copy-start | bytes 2359300
  79.6 16.2 %collective-permute-start.11 = (bf16[6,128,512]{2,1,0:T(8,128)(2,1)S(1)}, bf16[6,128,512]{2,1,0:T(8,128)(2,1)S(1)}, u32[]{:S(2)}, u32[]{:S(2)}) collective-permute-start(bf16[6,128,512]{2,1,0:T(8,128)(2,1)S(1)} %add_convert_fusion.1), channel_id=1, source_target_pairs={{0,16},{1,3},{2,18},{3,1},{4,20},{5,7},{6,22},{7,5},{8,24},{9,11},... | collective-permute-start | bytes 2359304 | tf_op jit(solution)/shard_map/ppermute | solution.py:415
  82.0 18.0 %copy-start.4 = (bf16[3,256,512]{2,1,0:T(8,128)(2,1)}, bf16[3,256,512]{2,1,0:T(8,128)(2,1)S(1)}, u32[]{:S(2)}) copy-start(bf16[3,256,512]{2,1,0:T(8,128)(2,1)S(1)} %collective-permute-done.6) | copy-start | bytes 2359300
  91.4 6.6 %copy-start.1 = (bf16[2,4,128,512]{3,2,1,0:T(8,128)(2,1)}, bf16[2,4,128,512]{3,2,1,0:T(8,128)(2,1)S(1)}, u32[]{:S(2)}) copy-start(bf16[2,4,128,512]{3,2,1,0:T(8,128)(2,1)S(1)} %collective-permute-done.7.refs_2_) | copy-start | bytes 3145732
  93.1 25.4 %collective-permute-start.13 = (bf16[1,4,128,512]{3,2,1,0:T(8,128)(2,1)S(1)}, bf16[1,4,128,512]{3,2,1,0:T(8,128)(2,1)S(1)}, u32[]{:S(2)}, u32[]{:S(2)}) collective-permute-start(bf16[1,4,128,512]{3,2,1,0:T(8,128)(2,1)S(1)} %add_convert_fusion.2), channel_id=1, source_target_pairs={{0,8},{1,9},{2,10},{3,11},{4,12},{5,13},{6,14},{7,15},{8,0},{9,1},... | collective-permute-start | bytes 1572872 | tf_op jit(solution)/shard_map/ppermute | solution.py:415
  95.8 5.0 %copy-start.5 = (bf16[6,128,512]{2,1,0:T(8,128)(2,1)}, bf16[6,128,512]{2,1,0:T(8,128)(2,1)S(1)}, u32[]{:S(2)}) copy-start(bf16[6,128,512]{2,1,0:T(8,128)(2,1)S(1)} %collective-permute-done.11) | copy-start | bytes 2359300
  98.0 8.2 %collective-permute-start.12 = (bf16[6,64,512]{2,1,0:T(8,128)(2,1)}, bf16[6,64,512]{2,1,0:T(8,128)(2,1)}, u32[]{:S(2)}, u32[]{:S(2)}) collective-permute-start(bf16[6,64,512]{2,1,0:T(8,128)(2,1)} %add_convert_fusion.5), channel_id=1, source_target_pairs={{0,2},{1,17},{2,0},{3,19},{4,6},{5,21},{6,4},{7,23},{8,10},{9,25},... | collective-permute-start | bytes 1179656 | tf_op jit(solution)/shard_map/ppermute | solution.py:415
  100.8 19.4 %collective-permute-start.9 = (bf16[3,128,512]{2,1,0:T(8,128)(2,1)}, bf16[3,128,512]{2,1,0:T(8,128)(2,1)}, u32[]{:S(2)}, u32[]{:S(2)}) collective-permute-start(bf16[3,128,512]{2,1,0:T(8,128)(2,1)} %add_convert_fusion.6), channel_id=1, source_target_pairs={{0,16},{1,3},{2,18},{3,1},{4,20},{5,7},{6,22},{7,5},{8,24},{9,11},... | collective-permute-start | bytes 1179656 | tf_op jit(solution)/shard_map/ppermute | solution.py:415
  118.5 8.7 %copy-start.6 = (bf16[1,4,128,512]{3,2,1,0:T(8,128)(2,1)}, bf16[1,4,128,512]{3,2,1,0:T(8,128)(2,1)S(1)}, u32[]{:S(2)}) copy-start(bf16[1,4,128,512]{3,2,1,0:T(8,128)(2,1)S(1)} %collective-permute-done.13.refs_3_) | copy-start | bytes 1572868
  120.2 10.8 %collective-permute-start.15 = (bf16[6,64,512]{2,1,0:T(8,128)(2,1)S(1)}, bf16[6,64,512]{2,1,0:T(8,128)(2,1)}, u32[]{:S(2)}, u32[]{:S(2)}) collective-permute-start(bf16[6,64,512]{2,1,0:T(8,128)(2,1)S(1)} %add_convert_fusion.4), channel_id=1, source_target_pairs={{0,4},{1,5},{2,6},{3,7},{4,0},{5,1},{6,2},{7,3},{8,12},{9,13},{10,... | collective-permute-start | bytes 1179656 | tf_op jit(solution)/shard_map/ppermute | solution.py:415
  121.4 5.8 %collective-permute-start.10 = (bf16[3,64,512]{2,1,0:T(8,128)(2,1)S(1)}, bf16[3,64,512]{2,1,0:T(8,128)(2,1)}, u32[]{:S(2)}, u32[]{:S(2)}) collective-permute-start(bf16[3,64,512]{2,1,0:T(8,128)(2,1)S(1)} %add_convert_fusion.9), channel_id=1, source_target_pairs={{0,2},{1,17},{2,0},{3,19},{4,6},{5,21},{6,4},{7,23},{8,10},{9,25},... | collective-permute-start | bytes 589832 | tf_op jit(solution)/shard_map/ppermute | solution.py:415
  131.0 1.7 collective-permute-start.17
  132.1 24.5 %copy-start.7 = (bf16[1,256,512]{2,1,0:T(8,128)(2,1)S(1)}, bf16[1,256,512]{2,1,0:T(8,128)(2,1)}, u32[]{:S(2)}) copy-start(bf16[1,256,512]{2,1,0:T(8,128)(2,1)} %get-tuple-element.63) | copy-start | bytes 786436
  132.7 20.5 %collective-permute-start.18 = (bf16[6,64,512]{2,1,0:T(8,128)(2,1)S(1)}, bf16[6,64,512]{2,1,0:T(8,128)(2,1)S(1)}, u32[]{:S(2)}, u32[]{:S(2)}) collective-permute-start(bf16[6,64,512]{2,1,0:T(8,128)(2,1)S(1)} %add_convert_fusion.3), channel_id=1, source_target_pairs={{0,8},{1,9},{2,10},{3,11},{4,12},{5,13},{6,14},{7,15},{8,0},{9,1},... | collective-permute-start | bytes 1179656 | tf_op jit(solution)/shard_map/ppermute | solution.py:415
  136.3 17.1 %collective-permute-start.20 = (bf16[1,128,512]{2,1,0:T(8,128)(2,1)S(1)}, bf16[1,128,512]{2,1,0:T(8,128)(2,1)S(1)}, u32[]{:S(2)}, u32[]{:S(2)}) collective-permute-start(bf16[1,128,512]{2,1,0:T(8,128)(2,1)S(1)} %add_convert_fusion.13), channel_id=1, source_target_pairs={{0,16},{1,3},{2,18},{3,1},{4,20},{5,7},{6,22},{7,5},{8,24},{9,11},... | collective-permute-start | bytes 393224 | tf_op jit(solution)/shard_map/ppermute | solution.py:415
  153.4 10.2 %collective-permute-start.21 = (bf16[6,64,512]{2,1,0:T(8,128)(2,1)S(1)}, bf16[6,64,512]{2,1,0:T(8,128)(2,1)S(1)}, u32[]{:S(2)}, u32[]{:S(2)}) collective-permute-start(bf16[6,64,512]{2,1,0:T(8,128)(2,1)S(1)} %multiply_convert_fusion), channel_id=1, source_target_pairs={{0,2},{1,17},{2,0},{3,19},{4,6},{5,21},{6,4},{7,23},{8,10},{9,25},... | collective-permute-start | bytes 1179656 | tf_op jit(solution)/shard_map/ppermute | solution.py:415
  156.5 6.3 %collective-permute-start.14 = (bf16[3,64,512]{2,1,0:T(8,128)(2,1)S(1)}, bf16[3,64,512]{2,1,0:T(8,128)(2,1)S(1)}, u32[]{:S(2)}, u32[]{:S(2)}) collective-permute-start(bf16[3,64,512]{2,1,0:T(8,128)(2,1)S(1)} %add_convert_fusion.8), channel_id=1, source_target_pairs={{0,4},{1,5},{2,6},{3,7},{4,0},{5,1},{6,2},{7,3},{8,12},{9,13},{10,... | collective-permute-start | bytes 589832 | tf_op jit(solution)/shard_map/ppermute | solution.py:415
  162.8 5.0 %collective-permute-start.23 = (bf16[1,128,512]{2,1,0:T(8,128)(2,1)S(1)}, bf16[1,128,512]{2,1,0:T(8,128)(2,1)S(1)}, u32[]{:S(2)}, u32[]{:S(2)}) collective-permute-start(bf16[1,128,512]{2,1,0:T(8,128)(2,1)S(1)} %add_convert_fusion.12), channel_id=1, source_target_pairs={{0,2},{1,17},{2,0},{3,19},{4,6},{5,21},{6,4},{7,23},{8,10},{9,25},... | collective-permute-start | bytes 393224 | tf_op jit(solution)/shard_map/ppermute | solution.py:415
  167.8 12.0 %collective-permute-start.24 = (bf16[6,128,512]{2,1,0:T(8,128)(2,1)S(1)}, bf16[6,128,512]{2,1,0:T(8,128)(2,1)S(1)}, u32[]{:S(2)}, u32[]{:S(2)}) collective-permute-start(bf16[6,128,512]{2,1,0:T(8,128)(2,1)S(1)} %pad_maximum_fusion.2), channel_id=1, source_target_pairs={{0,16},{1,3},{2,18},{3,1},{4,20},{5,7},{6,22},{7,5},{8,24},{9,11},... | collective-permute-start | bytes 2359304 | tf_op jit(solution)/shard_map/ppermute | solution.py:415
  168.7 9.5 %collective-permute-start.16 = (bf16[3,64,512]{2,1,0:T(8,128)(2,1)S(1)}, bf16[3,64,512]{2,1,0:T(8,128)(2,1)S(1)}, u32[]{:S(2)}, u32[]{:S(2)}) collective-permute-start(bf16[3,64,512]{2,1,0:T(8,128)(2,1)S(1)} %add_convert_fusion.7), channel_id=1, source_target_pairs={{0,8},{1,9},{2,10},{3,11},{4,12},{5,13},{6,14},{7,15},{8,0},{9,1},... | collective-permute-start | bytes 589832 | tf_op jit(solution)/shard_map/ppermute | solution.py:415
  178.4 5.0 %collective-permute-start.26 = (bf16[1,128,512]{2,1,0:T(8,128)(2,1)S(1)}, bf16[1,128,512]{2,1,0:T(8,128)(2,1)S(1)}, u32[]{:S(2)}, u32[]{:S(2)}) collective-permute-start(bf16[1,128,512]{2,1,0:T(8,128)(2,1)S(1)} %add_convert_fusion.11), channel_id=1, source_target_pairs={{0,4},{1,5},{2,6},{3,7},{4,0},{5,1},{6,2},{7,3},{8,12},{9,13},{10,... | collective-permute-start | bytes 393224 | tf_op jit(solution)/shard_map/ppermute | solution.py:415
  178.4 5.7 %collective-permute-start.19 = (bf16[3,64,512]{2,1,0:T(8,128)(2,1)S(1)}, bf16[3,64,512]{2,1,0:T(8,128)(2,1)S(1)}, u32[]{:S(2)}, u32[]{:S(2)}) collective-permute-start(bf16[3,64,512]{2,1,0:T(8,128)(2,1)S(1)} %multiply_convert_fusion.1), channel_id=1, source_target_pairs={{0,2},{1,17},{2,0},{3,19},{4,6},{5,21},{6,4},{7,23},{8,10},{9,25},... | collective-permute-start | bytes 589832 | tf_op jit(solution)/shard_map/ppermute | solution.py:415
  183.4 21.1 %collective-permute-start.27 = (bf16[6,256,512]{2,1,0:T(8,128)(2,1)}, bf16[6,256,512]{2,1,0:T(8,128)(2,1)}, u32[]{:S(2)}, u32[]{:S(2)}) collective-permute-start(bf16[6,256,512]{2,1,0:T(8,128)(2,1)} %pad_maximum_fusion.refs_0_), channel_id=1, source_target_pairs={{0,1},{1,0},{2,3},{3,2},{4,5},{5,4},{6,7},{7,6},{8,9},{9,8},{10,11... | collective-permute-start | bytes 4718600 | tf_op jit(solution)/shard_map/ppermute | solution.py:415
  184.2 7.8 %collective-permute-start.22 = (bf16[3,128,512]{2,1,0:T(8,128)(2,1)S(1)}, bf16[3,128,512]{2,1,0:T(8,128)(2,1)S(1)}, u32[]{:S(2)}, u32[]{:S(2)}) collective-permute-start(bf16[3,128,512]{2,1,0:T(8,128)(2,1)S(1)} %pad_maximum_fusion.3), channel_id=1, source_target_pairs={{0,16},{1,3},{2,18},{3,1},{4,20},{5,7},{6,22},{7,5},{8,24},{9,11},... | collective-permute-start | bytes 1179656 | tf_op jit(solution)/shard_map/ppermute | solution.py:415
  184.6 8.5 %collective-permute-start.28 = (bf16[1,128,512]{2,1,0:T(8,128)(2,1)S(1)}, bf16[1,128,512]{2,1,0:T(8,128)(2,1)S(1)}, u32[]{:S(2)}, u32[]{:S(2)}) collective-permute-start(bf16[1,128,512]{2,1,0:T(8,128)(2,1)S(1)} %add_convert_fusion.10), channel_id=1, source_target_pairs={{0,8},{1,9},{2,10},{3,11},{4,12},{5,13},{6,14},{7,15},{8,0},{9,1},... | collective-permute-start | bytes 393224 | tf_op jit(solution)/shard_map/ppermute | solution.py:415
  192.1 9.9 %copy-start = (bf16[3,256,512]{2,1,0:T(8,128)(2,1)}, bf16[3,256,512]{2,1,0:T(8,128)(2,1)S(1)}, u32[]{:S(2)}) copy-start(bf16[3,256,512]{2,1,0:T(8,128)(2,1)S(1)} %pad_maximum_fusion.1.refs_0_) | copy-start | bytes 2359300
  192.1 15.4 %collective-permute-start.25 = (bf16[3,256,512]{2,1,0:T(8,128)(2,1)S(1)}, bf16[3,256,512]{2,1,0:T(8,128)(2,1)}, u32[]{:S(2)}, u32[]{:S(2)}) collective-permute-start(bf16[3,256,512]{2,1,0:T(8,128)(2,1)S(1)} %pad_maximum_fusion.1.refs_0_), channel_id=1, source_target_pairs={{0,1},{1,0},{2,3},{3,2},{4,5},{5,4},{6,7},{7,6},{8,9},{9,8},{10,11... | collective-permute-start | bytes 2359304 | tf_op jit(solution)/shard_map/ppermute | solution.py:415
  193.2 5.0 %collective-permute-start.29 = (bf16[1,128,512]{2,1,0:T(8,128)(2,1)S(1)}, bf16[1,128,512]{2,1,0:T(8,128)(2,1)S(1)}, u32[]{:S(2)}, u32[]{:S(2)}) collective-permute-start(bf16[1,128,512]{2,1,0:T(8,128)(2,1)S(1)} %multiply_convert_fusion.2), channel_id=1, source_target_pairs={{0,16},{1,3},{2,18},{3,1},{4,20},{5,7},{6,22},{7,5},{8,24},{9,11},... | collective-permute-start | bytes 393224 | tf_op jit(solution)/shard_map/ppermute | solution.py:415
  199.0 3.0 %collective-permute-start.30 = (bf16[1,256,512]{2,1,0:T(8,128)(2,1)}, bf16[1,256,512]{2,1,0:T(8,128)(2,1)}, u32[]{:S(2)}, u32[]{:S(2)}) collective-permute-start(bf16[1,256,512]{2,1,0:T(8,128)(2,1)} %pad_maximum_fusion.4.refs_0_), channel_id=1, source_target_pairs={{0,1},{1,0},{2,3},{3,2},{4,5},{5,4},{6,7},{7,6},{8,9},{9,8},{10,11... | collective-permute-start | bytes 786440 | tf_op jit(solution)/shard_map/ppermute | solution.py:415

commit v4 on v3

--- a/solution.py
+++ b/solution.py
@@ -12,7 +12,9 @@
 IMGW = 64
 GROUP = 4
 BATCH = 4
-CONV_LEVELS = 3
+EARLY_LEVELS = 4
+LATE_LEVELS = 3
+BACK_LEVELS = 2
 VMEM_BYTES = 63 * 1024 * 1024
 F32 = jnp.float32
 BF16 = jnp.bfloat16
@@ -208,23 +210,33 @@
     @pl.loop(0, slots * per)
     def _(n):
         count_ref[n] = 0
-
-    @pl.loop(0, wide)
-    def _(n):
-        other = n // own_blocks
-        k = n - other * own_blocks
-        ident = route_ref[(tile ^ other) * own_blocks + k]
-        owner = ident // per
-        local = ident - owner * per
-        away = (owner ^ tile) >> 1
-
-        @pl.when(((owner ^ tile) & 1) == 0)
-        def _():
-            place = slot_of(away, core, tile_bits)
-            at = place * per + local
-            have = count_ref[at]
-            list_ref[at * wide + have] = n
-            count_ref[at] = have + 1
+        for g in range(GROUP):
+            list_ref[n * wide + g] = wide
+
+    per_bits = int(math.log2(per))
+    for other in range(2):
+        for first, last, shift in (
+            (0, edge, inner),
+            (edge, own_blocks - edge, -edge),
+            (own_blocks - edge, own_blocks, 0),
+        ):
+            @pl.loop(first, last)
+            def _(k, other=other, shift=shift):
+                ident = route_ref[0, (tile ^ other) * own_blocks + k]
+                owner = ident >> per_bits
+                local = ident & (per - 1)
+
+                @pl.when(((owner ^ tile) & 1) == 0)
+                def _():
+                    at = slot_of((owner ^ tile) >> 1, core, tile_bits) * per + local
+                    have = count_ref[at]
+                    spot = other * own_blocks + shift + k
+                    list_ref[at * wide + have] = (spot << 16) + (other * own_blocks + k)
+                    count_ref[at] = have + 1
+
+    cells_ref[0, wide : wide + 8, :] = jnp.full((8, 2 * BLK), -2 * IMGW, jnp.int32)
+    for n in range(1, 3):
+        cells_ref[n, wide : wide + 8, :] = jnp.zeros((8, 2 * BLK), jnp.int32)
 
     for copy in copies:
         copy.wait()
@@ -232,38 +244,18 @@
     lanes = lax.broadcasted_iota(jnp.int32, (1, 2 * BLK), 1)
     low_lane = lanes < BLK
 
-    def group_product(at, first, have):
-        picked = []
-        for g in range(GROUP):
-            there = first + g < have
-            n = jnp.where(there, list_ref[at * wide + jnp.minimum(first + g, wide - 1)], 0)
-            other = n // own_blocks
-            k = n - other * own_blocks
-            spot = jnp.where(
-                k < edge, inner + k, jnp.where(k >= own_blocks - edge, inner + k - inner, k - edge)
-            )
-            picked.append((there, n, other * own_blocks + spot))
-        rhs = jnp.concatenate([blocks_ref[spot] for _, _, spot in picked], axis=0)
+    def group_product(entries):
+        picked = [(entry & 0xFFFF, entry >> 16) for entry in entries]
+        rhs = jnp.concatenate([blocks_ref[spot] for _, spot in picked], axis=0)
 
         def lane_row(ref):
             halves = []
             for p in range(0, GROUP, 2):
-                a = ref[pl.ds(picked[p][1], 1), :]
-                b = ref[pl.ds(picked[p + 1][1], 1), :]
+                a = ref[pl.ds(picked[p][0], 1), :]
+                b = ref[pl.ds(picked[p + 1][0], 1), :]
                 halves.append(jnp.where(low_lane, a, b))
             return jnp.concatenate(halves, axis=1)
 
-        valid = jnp.concatenate(
-            [
-                jnp.where(
-                    low_lane,
-                    jnp.where(picked[p][0], 1.0, 0.0),
-                    jnp.where(picked[p + 1][0], 1.0, 0.0),
-                )
-                for p in range(0, GROUP, 2)
-            ],
-            axis=1,
-        ).astype(F32)
         left = lane_row(off_ref)
         right_w = lane_row(fx_ref).astype(F32) / 256.0
         lower_w = lane_row(fy_ref).astype(F32) / 256.0
@@ -271,13 +263,10 @@
         across = jnp.where(column == left, 1.0 - right_w, 0.0) + jnp.where(
             column == left + 1, right_w, 0.0
         )
-        band = jnp.concatenate(
-            [((1.0 - lower_w) * valid) * across, (lower_w * valid) * across], axis=0
-        ).astype(BF16)
+        band = jnp.concatenate([(1.0 - lower_w) * across, lower_w * across], axis=0).astype(BF16)
         return jnp.dot(band, rhs, preferred_element_type=F32)
 
-    def overfill(out, place, local, inside):
-        at = place * per + local
+    def overfill(out, at, inside):
         have = count_ref[at]
 
         @pl.when(have > GROUP)
@@ -286,7 +275,12 @@
 
             @pl.loop(0, (have + GROUP - 1) // GROUP)
             def _(m):
-                acc_ref[...] = acc_ref[...] + group_product(at, m * GROUP, have)
+                entries = []
+                for g in range(GROUP):
+                    index = m * GROUP + g
+                    entry = list_ref[at * wide + jnp.minimum(index, wide - 1)]
+                    entries.append(jnp.where(index < have, entry, wide))
+                acc_ref[...] = acc_ref[...] + group_product(entries)
 
             out[inside[0], inside[1]] = acc_ref[...].astype(BF16)
 
@@ -299,14 +293,15 @@
             values = []
             for n in range(BATCH):
                 at = base * per + m * BATCH + n
-                values.append(group_product(at, 0, count_ref[at]).astype(BF16))
+                entries = [list_ref[at * wide + g] for g in range(GROUP)]
+                values.append(group_product(entries).astype(BF16))
             for n in range(BATCH):
                 spot = m * BATCH + n
-                out[spot // per, spot % per] = values[n]
+                out[spot >> per_bits, spot & (per - 1)] = values[n]
 
         @pl.loop(0, (slots // 2) * per)
         def _(spot, out=out, base=base):
-            overfill(out, base + spot // per, spot % per, (spot // per, spot % per))
+            overfill(out, base * per + spot, (spot >> per_bits, spot & (per - 1)))
 
 
 def swap_low_bits(value):
@@ -334,7 +329,7 @@
         out_shape=[shape] * 2,
         scratch_shapes=[
             pltpu.VMEM((2 * own, BLK, chans), BF16),
-            pltpu.VMEM((3, 2 * own, 2 * BLK), jnp.int32),
+            pltpu.VMEM((3, 2 * own + 8, 2 * BLK), jnp.int32),
             pltpu.VMEM((2 * IMGW, chans), F32),
             pltpu.SMEM((slots * per,), jnp.int32),
             pltpu.SMEM((slots * per * 2 * own,), jnp.int32),
@@ -500,42 +495,56 @@
         return value
 
 
-def place_kernel(halves, order_ref, info_ref, *refs):
-    out_ref = refs[-1]
-    parts = order_ref.shape[0]
-    size = out_ref.shape[1] // (len(halves) * parts // 2)
-    for source_ref, half in zip(refs, halves):
-        for s in range(parts // 2):
-            place = order_ref[half * (parts // 2) + s]
-            if len(halves) == 1:
-                place = place & (parts // 2 - 1)
-            target = pl.multiple_of(place * size, size)
-            out_ref[:, pl.ds(target, size), :] = source_ref[:, s * size : (s + 1) * size, :]
-
-
-def place_parts(order, info, halves, sources, blocks, count, before):
-    taps, rows, chans = sources[0].shape
-    group = taps // len(blocks)
-
-    def target(t, order_ref, info_ref):
-        side = (info_ref[0] & 1) ^ halves[0] if len(halves) == 1 else 0
-        return (pick(t, blocks), side, 0)
-
+def place_kernel(spans, *refs):
+    tables = refs[: len(spans)]
+    sources = refs[len(spans) : 3 * len(spans)]
+    conv_ref, back_ref = refs[3 * len(spans) :]
+    step = pl.program_id(0)
+    start = 0
+    for n, span in enumerate(spans):
+        out_ref = back_ref if n == len(spans) - 1 else conv_ref
+        parts = tables[n].shape[0]
+        size = out_ref.shape[1] // parts
+
+        @pl.when((step >= start) & (step < start + span))
+        def _(n=n, out_ref=out_ref, parts=parts, size=size):
+            for half in range(2):
+                for s in range(parts // 2):
+                    place = tables[n][half * (parts // 2) + s]
+                    target = pl.multiple_of(place * size, size)
+                    out_ref[:, pl.ds(target, size), :] = sources[2 * n + half][
+                        :, s * size : (s + 1) * size, :
+                    ]
+
+        start += span
+
+
+def place_parts(tables, chunks):
+    chans = chunks[0][0].shape[2]
+    spans = tuple(max(1, mine.shape[0] // 3) for mine, _ in chunks)
+    starts = [sum(spans[:n]) for n in range(len(spans))]
+    groups = sum(spans) - 1
+    in_specs = [SMEM] * len(tables)
+    for (mine, _), span, start in zip(chunks, spans, starts):
+        block = (mine.shape[0] // span,) + mine.shape[1:]
+        index = lambda t, span=span, start=start: (jnp.clip(t - start, 0, span - 1), 0, 0)
+        in_specs += [pl.BlockSpec(block, index)] * 2
     return pl.pallas_call(
-        functools.partial(place_kernel, halves),
-        grid_spec=pltpu.PrefetchScalarGridSpec(
-            num_scalar_prefetch=2,
-            grid=(len(blocks),),
-            in_specs=[pl.BlockSpec((group, rows, chans), lambda t, o, i: (t, 0, 0))] * len(sources)
-            + [ANY] * len(before),
-            out_specs=pl.BlockSpec((group, len(halves) * rows, chans), target),
-        ),
-        out_shape=jax.ShapeDtypeStruct((count, 2 * rows, chans), BF16),
-        input_output_aliases={2 + len(sources): 0} if before else {},
+        functools.partial(place_kernel, spans),
+        grid=(sum(spans),),
+        in_specs=in_specs,
+        out_specs=[
+            pl.BlockSpec((3, chans, chans), lambda t: (jnp.minimum(t, groups - 1), 0, 0)),
+            pl.BlockSpec((1, chans, chans), lambda t: (0, 0, 0)),
+        ],
+        out_shape=[
+            jax.ShapeDtypeStruct((3 * groups, chans, chans), BF16),
+            jax.ShapeDtypeStruct((1, chans, chans), BF16),
+        ],
         compiler_params=params(),
-        cost_estimate=cost(0, 4 * taps * len(halves) * rows * chans),
+        cost_estimate=cost(0, 40 * chans * chans),
         name="place_parts",
-    )(order, info, *sources, *before)
+    )(*tables, *[half for chunk in chunks for half in chunk])
 
 
 def together(*values):
@@ -555,10 +564,12 @@
     own = rows * cols // BLK
     edge_blocks = cols // BLK
     steps = int(math.log2(pods * tiles))
-    levels = min(CONV_LEVELS, steps, int(math.log2(chans // 16)))
-    back_levels = min(2, levels)
-    order = part_order(my_pod, my_tile, pods, tiles, levels)
-    back_order = part_order(my_pod, my_tile, pods, tiles, back_levels)
+    most = min(steps, int(math.log2(chans // 16)))
+    early_levels, late_levels, back_levels = (
+        min(levels, most) for levels in (EARLY_LEVELS, LATE_LEVELS, BACK_LEVELS)
+    )
+    order_of = lambda levels: part_order(my_pod, my_tile, pods, tiles, levels)
+    early_order, late_order, back_order = map(order_of, (early_levels, late_levels, back_levels))
     cell_scale = 1.0 / math.sqrt(pods * tiles * rows * cols)
     pixel_scale = 1.0 / math.sqrt(pods * tiles * image.shape[0])
 
@@ -582,7 +593,7 @@
     as_blocks = lambda value: value.reshape(-1, BLK, chans)
     keep, send = warp_pieces(
         info,
-        route[0],
+        route,
         cells,
         cells_other,
         [as_blocks(v) for v in (inner, edge, inner_other, edge_other)],
@@ -605,36 +616,44 @@
             send = region_sum(warp, 0, extent // 2, extent).astype(BF16)
             extent //= 2
         warp.append(exchange(send, *sizes, lambda core: warp_masks[core][n]))
+        return send
 
     warp_step(0, send)
     early_taps = tuple((i, j) for j in (1, 0, 2) for i in (1, 0))
     late_taps = tuple((2, j) for j in (1, 0, 2))
     outs = wgrad(
-        order, act, grad, [low, high], early_taps, tuple(3 * i + j for i, j in early_taps), 6, [], [keep]
+        early_order,
+        act,
+        grad,
+        [low, high],
+        early_taps,
+        tuple(3 * i + j for i, j in early_taps),
+        6,
+        [],
+        [keep],
     )
-    early = Chain(*outs, sizes, levels, cell_scale)
+    early = Chain(*outs, sizes, early_levels, cell_scale)
     early.step()
-    outs = list(wgrad(order, act, grad, [low, high], late_taps, (1, 0, 2), 3, [], [outs[0]]))
+    outs = list(wgrad(late_order, act, grad, [low, high], late_taps, (1, 0, 2), 3, [], [outs[0]]))
     outs[0] = early.tie(outs[0])
-    late = Chain(*outs, sizes, levels, cell_scale)
+    late = Chain(*outs, sizes, late_levels, cell_scale)
     warp[1], late.sent = together(warp[1], late.sent)
 
-    warp_step(1, None)
+    sent = warp_step(1, None)
     late.step()
-    early.step(warp[1])
+    early.step(sent)
     warp[2] = late.tie(warp[2])
 
-    warp_step(2, None)
-    late.step(warp[2])
-    early.step()
-    late.step()
-    warp[3] = early.tie(warp[3])
-    warp[3] = late.tie(warp[3])
+    sent = warp_step(2, None)
+    early.step(sent)
+    late.step(sent)
     for n in range(3, last + 1):
         warp_step(n, None)
 
     image_grad, keep_img, send_img = image_layer(back_order, [warp], slope, image, backbone_weight)
     back = Chain(keep_img, send_img, sizes, back_levels, pixel_scale)
+    early.step()
+    early.recv, late.recv, _ = together(early.recv, late.recv, send_img)
     chains = [back, early, late]
     before = [send_img]
     while any(chain.more() for chain in chains):
@@ -644,10 +663,11 @@
                 chain.step(*before)
                 before = [] if held is None else [held]
 
-    conv_grad = place_parts(order, info, (0,), [early.sent], (0, 1), 9, [])
-    conv_grad = place_parts(order, info, (1,), [early.recv], (0, 1), 9, [conv_grad])
-    conv_grad = place_parts(order, info, (0, 1), [late.sent, late.recv], (2,), 9, [conv_grad])
-    backbone_grad = place_parts(back_order, info, (0, 1), [back.sent, back.recv], (0,), 1, [])[0]
+    conv_grad, backbone_grad = place_parts(
+        [early_order, late_order, back_order],
+        [(chain.sent, chain.recv) for chain in (early, late, back)],
+    )
+    backbone_grad = backbone_grad[0]
     conv_grad = jnp.transpose(conv_grad.reshape(3, 3, chans, chans), (2, 0, 1, 3))
     return (image_grad[None], conv_grad, backbone_grad)
 

time: 211 us -> 195 us (0.924)
  Pallas kernels: 72.2 us -> 63.7 us
  starting transfers between devices: 36.8 us -> 31.2 us
  local copies, waits for them, and re-layouts: 2.97 us -> 5.64 us
  other arithmetic: 18.6 us -> 16 us
    pallas_call x4 -> x1, Pallas kernels: 11.8 us -> 5.18 us  [place_parts(): pl.pallas_call(functools.partial(place_kernel, spans), grid=(sum(spans),)...]
    ppermute x26 -> x27, starting transfers between devices: 27 us -> 21.5 us  [exchange(): return lax.ppermute(value, ('dp', 'tile'), pairs)]
    unnamed x30 -> x34, local copies, waits for them, and re-layouts: 0.66 us -> 3.32 us
    ppermute x26 -> x27, waiting for transfers between devices: 79.3 us -> 77.4 us  [exchange(): return lax.ppermute(value, ('dp', 'tile'), pairs)]
    convert_element_type x5 -> x6, other arithmetic: 6.39 us -> 7.63 us  [step(): send = region_sum(self.terms, 1, self.extent // 2, self.extent).astype(BF16)]
  transfers between devices with their start and end apart: 31 -> 32, of which waited for: 16 -> 14; matrix products, arithmetic and copies ran while one was open for 9% -> 7% of each run, Pallas kernels for 28% -> 26%
where the time goes in v4:
time: 195 us
  waiting for transfers between devices  77.4 us (40%)
  Pallas kernels  63.7 us (33%)
  starting transfers between devices  31.2 us (16%)
  other arithmetic  16 us (8%)
  local copies, waits for them, and re-layouts  5.64 us (3%)
    ppermute x27, waiting for transfers between devices, exchange(): return lax.ppermute(value, ('dp', 'tile'), pairs)  77.4 us
    pallas_call x2, Pallas kernels, wgrad(): pl.pallas_call(functools.partial(wgrad_kernel, taps, len(halos) > 0), gri...  23 us
    ppermute x27, starting transfers between devices, exchange(): return lax.ppermute(value, ('dp', 'tile'), pairs)  21.5 us
    pallas_call x2, Pallas kernels, bev_rows(): pl.pallas_call(kernel, grid=(3,), in_specs=[whole(rows, cols, chans)] + [...  20.5 us
    pallas_call x1, Pallas kernels, warp_pieces(): pl.pallas_call(functools.partial(pieces_kernel, (own, per, bits, edge, le...  8.46 us
    convert_element_type x6, other arithmetic, step(): send = region_sum(self.terms, 1, self.extent // 2, self.extent).astype(BF16)  7.63 us
    pallas_call x1, Pallas kernels, place_parts(): pl.pallas_call(functools.partial(place_kernel, spans), grid=(sum(spans),)...  5.18 us
    ppermute x1, starting transfers between devices, body(): low = lax.ppermute(grad[rows - 1], 'tile', forward)  3.91 us
  transfers between devices with their start and end apart: 32, of which 14 were waited for; matrix products, arithmetic and copies ran while one was open for 7% of the time, Pallas kernels for 26%

profile of v4, /device:TPU:0, one launch (start us, length us, event | category | flops | bytes accessed | tf_op | source)
XLA Modules:
  0.0 194.8 jit_solution(5519857479089008593)
XLA Ops:
  0.7 2.2 %slice_bitcast_fusion = (bf16[640,512]{1,0:T(8,128)(2,1)}, bf16[640,512]{1,0:T(8,128)(2,1)S(1)}) fusion(bf16[1,4,640,512]{3,2,1,0:T(8,128)(2,1)} %param.9), kind=kLoop, calls=%fused_computation.8 | loop fusion | bytes 2621440 | tf_op jit(solution)/shard_map/squeeze | solution.py:579
  2.9 1.3 collective-permute-start.2
  4.2 3.9 %collective-permute-start.1 = (bf16[640,512]{1,0:T(8,128)(2,1)S(1)}, bf16[640,512]{1,0:T(8,128)(2,1)}, u32[]{:S(2)}, u32[]{:S(2)}) collective-permute-start(bf16[640,512]{1,0:T(8,128)(2,1)S(1)} %get-tuple-element.82), channel_id=1, source_target_pairs={{0,1},{1,2},{2,3},{3,4},{4,5},{5,6},{6,7},{7,8},{8,9},{9,10},{10,1... | collective-permute-start | bytes 1966088 | tf_op jit(solution)/shard_map/ppermute | solution.py:578
  8.2 1.8 collective-permute-start
  10.0 10.1 %bev_rows.2.refs_3_ = bf16[2,640,512]{2,1,0:T(8,128)(2,1)} custom-call(bf16[4,640,512]{2,1,0:T(8,128)(2,1)} %bitcast.23, bf16[3,3,512,512]{3,2,1,0:T(8,128)(2,1)} %bitcast.27), custom_call_target="tpu_custom_call" | custom-call | flops 6039797760 | bytes 9961472 | tf_op jit(solution)/shard_map/bev_rows/pallas_call | solution.py:90
  20.8 10.4 %bev_rows.3.refs_0_ = bf16[2,640,512]{2,1,0:T(8,128)(2,1)} custom-call(bf16[4,640,512]{2,1,0:T(8,128)(2,1)} %bitcast.24, bf16[640,512]{1,0:T(8,128)(2,1)} %collective-permute-done.1.refs_0_, bf16[640,512]{1,0:T(8,128)(2,1)} %collective-permute-done.2.refs_1_, bf16[3,3,512,512]{3,2,1,0:T(8,128)(2,1)} %bitcast.28, bf16[2,640,512]{2,1,0:T(8,128)(2,1)} %bev_rows.2.refs_3_, ...), custom_call_target="tpu_custom_call" | custom-call | flops 6039797760 | bytes 9961472 | tf_op jit(solution)/shard_map/bev_rows/pallas_call | solution.py:90
  31.1 2.8 %collective-permute-start.4 = (bf16[2,640,512]{2,1,0:T(8,128)(2,1)}, bf16[2,640,512]{2,1,0:T(8,128)(2,1)}, u32[]{:S(2)}, u32[]{:S(2)}) collective-permute-start(bf16[2,640,512]{2,1,0:T(8,128)(2,1)} %bev_rows.3.refs_0_), channel_id=1, source_target_pairs={{0,1},{1,0},{2,3},{3,2},{4,5},{5,4},{6,7},{7,6},{8,9},{9,8},{10,11... | collective-permute-start | bytes 3932168 | tf_op jit(solution)/shard_map/ppermute | solution.py:591
  34.6 2.8 %image_slope.1.refs_4_ = f32[512,512]{1,0:T(8,128)} custom-call(bf16[512,512]{1,0:T(8,128)(2,1)} %bitcast.20, bf16[512,512]{1,0:T(8,128)(2,1)} %refs_6_.1, bf16[2,640,512]{2,1,0:T(8,128)(2,1)} %bev_rows.3.refs_0_), custom_call_target="tpu_custom_call" | custom-call | flops 268435456 | bytes 2621440 | tf_op jit(solution)/shard_map/image_slope/pallas_call | solution.py:355
  37.3 8.5 %warp_pieces.1 = (bf16[4,4,128,512]{3,2,1,0:T(8,128)(2,1)}, bf16[4,4,128,512]{3,2,1,0:T(8,128)(2,1)}) custom-call(s32[1]{0:T(128)} %bitcast.info_ref, s32[1,640]{1,0:T(1,128)} %route_ref.1, s32[3,40,64]{2,1,0:T(8,128)} %copy-done.11, s32[3,40,64]{2,1,0:T(8,128)} %copy-done.12, bf16[20,64,512]{2,1,0:T(8,128)(2,1)} %bitcast.22, bf16[20,64,512]{2,1,0:T(8,128)(2,1)} %bitcast.19, ...), custom_call_target="tpu_custom_call" | custom-call | flops 1073741824 | bytes 9437184 | tf_op jit(solution)/shard_map/warp_pieces/pallas_call | solution.py:325
  45.8 3.0 %collective-permute-start.5 = (bf16[4,4,128,512]{3,2,1,0:T(8,128)(2,1)}, bf16[4,4,128,512]{3,2,1,0:T(8,128)(2,1)}, u32[]{:S(2)}, u32[]{:S(2)}) collective-permute-start(bf16[4,4,128,512]{3,2,1,0:T(8,128)(2,1)} %get-tuple-element.43), channel_id=1, source_target_pairs={{0,2},{1,5},{2,0},{3,7},{4,6},{5,1},{6,4},{7,3},{8,10},{9,13},{10,... | collective-permute-start | bytes 6291464 | tf_op jit(solution)/shard_map/ppermute | solution.py:410
  48.8 14.0 %wgrad.2 = (bf16[6,256,512]{2,1,0:T(8,128)(2,1)}, bf16[6,256,512]{2,1,0:T(8,128)(2,1)}) custom-call(s32[16]{0:T(128)} %pad_add_fusion.3.order_ref.refs_0_, bf16[4,640,512]{2,1,0:T(8,128)(2,1)} %bitcast.30, bf16[2560,512]{1,0:T(8,128)(2,1)} %bitcast.25, bf16[640,512]{1,0:T(8,128)(2,1)} %collective-permute-done.1.refs_0_, ...), custom_call_target="tpu_custom_call" | custom-call | flops 8053063680 | bytes 8388608 | tf_op jit(solution)/shard_map/wgrad/pallas_call | solution.py:166
  63.4 9.0 %wgrad.3 = (bf16[3,256,512]{2,1,0:T(8,128)(2,1)}, bf16[3,256,512]{2,1,0:T(8,128)(2,1)}) custom-call(s32[8]{0:T(128)} %pad_add_fusion.2.order_ref.refs_1_, bf16[4,640,512]{2,1,0:T(8,128)(2,1)} %bitcast.31, bf16[2560,512]{1,0:T(8,128)(2,1)} %bitcast.26, bf16[640,512]{1,0:T(8,128)(2,1)} %collective-permute-done.1.refs_0_, ...), custom_call_target="tpu_custom_call" | custom-call | flops 4026531840 | bytes 6815744 | tf_op jit(solution)/shard_map/wgrad/pallas_call | solution.py:166
  72.4 1.7 add_convert_fusion.1
  74.5 1.6 add_convert_fusion
  76.1 1.1 collective-permute-start.10
  77.2 1.6 collective-permute-start.7
  78.8 9.3 %collective-permute-done.10 = bf16[6,128,512]{2,1,0:T(8,128)(2,1)S(1)} collective-permute-done((bf16[6,128,512]{2,1,0:T(8,128)(2,1)S(1)}, bf16[6,128,512]{2,1,0:T(8,128)(2,1)S(1)}, u32[]{:S(2)}, u32[]{:S(2)}) %collective-permute-start.10) | collective-permute-done | bytes 786464 | tf_op jit(solution)/shard_map/ppermute | solution.py:410
  88.2 2.0 %add_convert_fusion.4 = bf16[6,64,512]{2,1,0:T(8,128)(2,1)} fusion(bf16[6,128,512]{2,1,0:T(8,128)(2,1)S(1)} %collective-permute-done.10, bf16[6,256,512]{2,1,0:T(8,128)(2,1)} %collective-permute-done.9, bf16[6,256,512]{2,1,0:T(8,128)(2,1)} %get-tuple-element.44.refs_2_), kind=kLoop, calls=%fused_computation.7 | loop fusion | flops 1179648 | bytes 1572864 | tf_op jit(solution)/shard_map/convert_element_type | solution.py:471
  90.2 1.8 collective-permute-done.7.refs_2_
  92.0 1.6 add_convert_fusion.2
  93.6 2.7 %collective-permute-start.11 = (bf16[6,64,512]{2,1,0:T(8,128)(2,1)}, bf16[6,64,512]{2,1,0:T(8,128)(2,1)S(1)}, u32[]{:S(2)}, u32[]{:S(2)}) collective-permute-start(bf16[6,64,512]{2,1,0:T(8,128)(2,1)} %add_convert_fusion.4), channel_id=1, source_target_pairs={{0,2},{1,17},{2,0},{3,19},{4,6},{5,21},{6,4},{7,23},{8,10},{9,25},... | collective-permute-start | bytes 1179656 | tf_op jit(solution)/shard_map/ppermute | solution.py:410
  97.0 0.8 add_convert_fusion.3
  98.4 4.7 %collective-permute-done.11 = bf16[6,64,512]{2,1,0:T(8,128)(2,1)S(1)} collective-permute-done((bf16[6,64,512]{2,1,0:T(8,128)(2,1)}, bf16[6,64,512]{2,1,0:T(8,128)(2,1)S(1)}, u32[]{:S(2)}, u32[]{:S(2)}) %collective-permute-start.11) | collective-permute-done | bytes 393248 | tf_op jit(solution)/shard_map/ppermute | solution.py:410
  103.1 0.7 copy-done.8
  103.9 1.8 add_convert_fusion.9
  105.7 1.2 collective-permute-start.12
  107.5 14.9 %collective-permute-done.8.refs_3_ = bf16[1,4,128,512]{3,2,1,0:T(8,128)(2,1)} collective-permute-done((bf16[1,4,128,512]{3,2,1,0:T(8,128)(2,1)S(1)}, bf16[1,4,128,512]{3,2,1,0:T(8,128)(2,1)}, u32[]{:S(2)}, u32[]{:S(2)}) %collective-permute-start.8) | collective-permute-done | bytes 524320 | tf_op jit(solution)/shard_map/ppermute | solution.py:410
  122.4 3.8 %image_layer.1 = (bf16[512,512]{1,0:T(8,128)(2,1)}, bf16[1,256,512]{2,1,0:T(8,128)(2,1)}, bf16[1,256,512]{2,1,0:T(8,128)(2,1)}) custom-call(s32[4]{0:T(128)} %pad_add_fusion.1.order_ref.refs_2_, bf16[4,4,128,512]{3,2,1,0:T(8,128)(2,1)} %get-tuple-element.42.refs_2_.refs_0_, bf16[4,4,128,512]{3,2,1,0:T(8,128)(2,1)} %collective-permute-done.5.refs_1_, ...), custom_call_target="tpu_custom_call" | custom-call | flops 536870912 | bytes 4194304 | tf_op jit(solution)/shard_map/image_layer/pallas_call | solution.py:389
  126.2 0.9 collective-permute-start.15
  127.1 1.2 add_convert_fusion.8
  128.4 1.2 add_convert_fusion.7
  129.8 9.6 %collective-permute-done.14 = bf16[6,32,512]{2,1,0:T(8,128)(2,1)S(1)} collective-permute-done((bf16[6,32,512]{2,1,0:T(8,128)(2,1)S(1)}, bf16[6,32,512]{2,1,0:T(8,128)(2,1)S(1)}, u32[]{:S(2)}, u32[]{:S(2)}) %collective-permute-start.14) | collective-permute-done | bytes 196640 | tf_op jit(solution)/shard_map/ppermute | solution.py:410
  140.2 6.1 %collective-permute-done.16 = bf16[6,32,512]{2,1,0:T(8,128)(2,1)S(1)} collective-permute-done((bf16[6,32,512]{2,1,0:T(8,128)(2,1)S(1)}, bf16[6,32,512]{2,1,0:T(8,128)(2,1)S(1)}, u32[]{:S(2)}, u32[]{:S(2)}) %collective-permute-start.16) | collective-permute-done | bytes 196640 | tf_op jit(solution)/shard_map/ppermute | solution.py:410
  146.6 1.2 add_convert_fusion.6
  148.2 2.0 %collective-permute-start.20 = (bf16[1,128,512]{2,1,0:T(8,128)(2,1)S(1)}, bf16[1,128,512]{2,1,0:T(8,128)(2,1)S(1)}, u32[]{:S(2)}, u32[]{:S(2)}) collective-permute-start(bf16[1,128,512]{2,1,0:T(8,128)(2,1)S(1)} %add_convert_fusion.12), channel_id=1, source_target_pairs={{0,2},{1,17},{2,0},{3,19},{4,6},{5,21},{6,4},{7,23},{8,10},{9,25},... | collective-permute-start | bytes 393224 | tf_op jit(solution)/shard_map/ppermute | solution.py:410
  150.2 4.1 %collective-permute-done.18 = bf16[6,64,512]{2,1,0:T(8,128)(2,1)S(1)} collective-permute-done((bf16[6,64,512]{2,1,0:T(8,128)(2,1)S(1)}, bf16[6,64,512]{2,1,0:T(8,128)(2,1)S(1)}, u32[]{:S(2)}, u32[]{:S(2)}) %collective-permute-start.18) | collective-permute-done | bytes 393248 | tf_op jit(solution)/shard_map/ppermute | solution.py:410
  154.3 1.3 collective-permute-done.20
  156.9 1.8 collective-permute-start.23
  158.7 7.3 %collective-permute-done.25 = bf16[3,64,512]{2,1,0:T(8,128)(2,1)S(1)} collective-permute-done((bf16[3,64,512]{2,1,0:T(8,128)(2,1)S(1)}, bf16[3,64,512]{2,1,0:T(8,128)(2,1)S(1)}, u32[]{:S(2)}, u32[]{:S(2)}) %collective-permute-start.25) | collective-permute-done | bytes 196640 | tf_op jit(solution)/shard_map/ppermute | solution.py:410
  166.1 1.8 collective-permute-start.26
  168.2 3.6 %collective-permute-done.26 = bf16[3,64,512]{2,1,0:T(8,128)(2,1)S(1)} collective-permute-done((bf16[3,64,512]{2,1,0:T(8,128)(2,1)S(1)}, bf16[3,64,512]{2,1,0:T(8,128)(2,1)S(1)}, u32[]{:S(2)}, u32[]{:S(2)}) %collective-permute-start.26) | collective-permute-done | bytes 196640 | tf_op jit(solution)/shard_map/ppermute | solution.py:410
  171.8 1.0 collective-permute-start.27
  173.0 6.7 %collective-permute-done.27 = bf16[3,128,512]{2,1,0:T(8,128)(2,1)S(1)} collective-permute-done((bf16[3,128,512]{2,1,0:T(8,128)(2,1)S(1)}, bf16[3,128,512]{2,1,0:T(8,128)(2,1)S(1)}, u32[]{:S(2)}, u32[]{:S(2)}) %collective-permute-start.27) | collective-permute-done | bytes 393248 | tf_op jit(solution)/shard_map/ppermute | solution.py:410
  179.8 1.5 collective-permute-done.28
  181.7 4.7 %collective-permute-done.30 = bf16[1,128,512]{2,1,0:T(8,128)(2,1)S(1)} collective-permute-done((bf16[1,128,512]{2,1,0:T(8,128)(2,1)S(1)}, bf16[1,128,512]{2,1,0:T(8,128)(2,1)S(1)}, u32[]{:S(2)}, u32[]{:S(2)}) %collective-permute-start.30) | collective-permute-done | bytes 131104 | tf_op jit(solution)/shard_map/ppermute | solution.py:410
  186.5 1.5 collective-permute-done.31.refs_8_
  188.7 0.9 copy-done.5
  189.6 5.2 %place_parts.1 = (bf16[9,512,512]{2,1,0:T(8,128)(2,1)}, bf16[1,512,512]{2,1,0:T(8,128)(2,1)}) custom-call(s32[16]{0:T(128)} %pad_add_fusion.3.order_ref.refs_0_, s32[8]{0:T(128)} %pad_add_fusion.2.order_ref.refs_1_, s32[4]{0:T(128)} %pad_add_fusion.1.order_ref.refs_2_, bf16[6,256,512]{2,1,0:T(8,128)(2,1)} %copy-done.1, ...), custom_call_target="tpu_custom_call" | custom-call | bytes 10485760 | tf_op jit(solution)/shard_map/place_parts/pallas_call | solution.py:532
  (90 shorter events, 9.0 us)
Async XLA Ops:
  0.6 7.5 %copy-start.13 = (s32[1,2560]{1,0:T(1,128)S(1)}, s32[1,2560]{1,0:T(1,128)}, u32[]{:S(2)}) copy-start(s32[1,2560]{1,0:T(1,128)} %param.17) | copy-start | bytes 30724
  0.6 7.4 %copy-start.14 = (s32[1,2560]{1,0:T(1,128)S(1)}, s32[1,2560]{1,0:T(1,128)}, u32[]{:S(2)}) copy-start(s32[1,2560]{1,0:T(1,128)} %param.16) | copy-start | bytes 30724
  0.7 7.4 %copy-start.15 = (s32[1,2560]{1,0:T(1,128)S(1)}, s32[1,2560]{1,0:T(1,128)}, u32[]{:S(2)}) copy-start(s32[1,2560]{1,0:T(1,128)} %param.15) | copy-start | bytes 30724
  2.9 17.2 %collective-permute-start.2 = (bf16[640,512]{1,0:T(8,128)(2,1)}, bf16[640,512]{1,0:T(8,128)(2,1)}, u32[]{:S(2)}, u32[]{:S(2)}) collective-permute-start(bf16[640,512]{1,0:T(8,128)(2,1)} %get-tuple-element.81), channel_id=1, source_target_pairs={{1,0},{2,1},{3,2},{4,3},{5,4},{6,5},{7,6},{8,7},{9,8},{10,9},{11,1... | collective-permute-start | bytes 1966088 | tf_op jit(solution)/shard_map/ppermute | solution.py:579
  4.2 16.0 %collective-permute-start.1 = (bf16[640,512]{1,0:T(8,128)(2,1)S(1)}, bf16[640,512]{1,0:T(8,128)(2,1)}, u32[]{:S(2)}, u32[]{:S(2)}) collective-permute-start(bf16[640,512]{1,0:T(8,128)(2,1)S(1)} %get-tuple-element.82), channel_id=1, source_target_pairs={{0,1},{1,2},{2,3},{3,4},{4,5},{5,6},{6,7},{7,8},{8,9},{9,10},{10,1... | collective-permute-start | bytes 1966088 | tf_op jit(solution)/shard_map/ppermute | solution.py:578
  8.2 11.9 %copy-start.11 = (s32[3,40,64]{2,1,0:T(8,128)}, s32[3,40,64]{2,1,0:T(8,128)S(1)}, u32[]{:S(2)}) copy-start(s32[3,40,64]{2,1,0:T(8,128)S(1)} %reshape.32.mine_ref) | copy-start | bytes 92164
  8.2 11.9 %collective-permute-start = (s32[3,40,64]{2,1,0:T(8,128)S(1)}, s32[3,40,64]{2,1,0:T(8,128)S(1)}, u32[]{:S(2)}, u32[]{:S(2)}) collective-permute-start(s32[3,40,64]{2,1,0:T(8,128)S(1)} %reshape.32.mine_ref), channel_id=1, source_target_pairs={{0,1},{1,0},{2,3},{3,2},{4,5},{5,4},{6,7},{7,6},{8,9},{9,8},{10,11... | collective-permute-start | bytes 92168 | tf_op jit(solution)/shard_map/ppermute | solution.py:583
  20.1 17.3 %collective-permute-start.3 = (bf16[2,640,512]{2,1,0:T(8,128)(2,1)}, bf16[2,640,512]{2,1,0:T(8,128)(2,1)}, u32[]{:S(2)}, u32[]{:S(2)}) collective-permute-start(bf16[2,640,512]{2,1,0:T(8,128)(2,1)} %bev_rows.2.refs_3_), channel_id=1, source_target_pairs={{0,1},{1,0},{2,3},{3,2},{4,5},{5,4},{6,7},{7,6},{8,9},{9,8},{10,11... | collective-permute-start | bytes 3932168 | tf_op jit(solution)/shard_map/ppermute | solution.py:587
  31.1 6.2 %collective-permute-start.4 = (bf16[2,640,512]{2,1,0:T(8,128)(2,1)}, bf16[2,640,512]{2,1,0:T(8,128)(2,1)}, u32[]{:S(2)}, u32[]{:S(2)}) collective-permute-start(bf16[2,640,512]{2,1,0:T(8,128)(2,1)} %bev_rows.3.refs_0_), channel_id=1, source_target_pairs={{0,1},{1,0},{2,3},{3,2},{4,5},{5,4},{6,7},{7,6},{8,9},{9,8},{10,11... | collective-permute-start | bytes 3932168 | tf_op jit(solution)/shard_map/ppermute | solution.py:591
  45.8 28.4 %collective-permute-start.5 = (bf16[4,4,128,512]{3,2,1,0:T(8,128)(2,1)}, bf16[4,4,128,512]{3,2,1,0:T(8,128)(2,1)}, u32[]{:S(2)}, u32[]{:S(2)}) collective-permute-start(bf16[4,4,128,512]{3,2,1,0:T(8,128)(2,1)} %get-tuple-element.43), channel_id=1, source_target_pairs={{0,2},{1,5},{2,0},{3,7},{4,6},{5,1},{6,4},{7,3},{8,10},{9,13},{10,... | collective-permute-start | bytes 6291464 | tf_op jit(solution)/shard_map/ppermute | solution.py:410
  62.8 9.6 %collective-permute-start.9 = (bf16[6,256,512]{2,1,0:T(8,128)(2,1)}, bf16[6,256,512]{2,1,0:T(8,128)(2,1)}, u32[]{:S(2)}, u32[]{:S(2)}) collective-permute-start(bf16[6,256,512]{2,1,0:T(8,128)(2,1)} %get-tuple-element.50), channel_id=1, source_target_pairs={{0,1},{1,0},{2,3},{3,2},{4,5},{5,4},{6,7},{7,6},{8,9},{9,8},{10,11... | collective-permute-start | bytes 4718600 | tf_op jit(solution)/shard_map/ppermute | solution.py:410
  72.4 2.1 %copy-start = (bf16[4,4,128,512]{3,2,1,0:T(8,128)(2,1)S(1)}, bf16[4,4,128,512]{3,2,1,0:T(8,128)(2,1)}, u32[]{:S(2)}) copy-start(bf16[4,4,128,512]{3,2,1,0:T(8,128)(2,1)} %get-tuple-element.42.refs_2_.refs_0_) | copy-start | bytes 6291460
  74.5 4.3 %copy-start.16 = (bf16[3,256,512]{2,1,0:T(8,128)(2,1)S(1)}, bf16[3,256,512]{2,1,0:T(8,128)(2,1)}, u32[]{:S(2)}) copy-start(bf16[3,256,512]{2,1,0:T(8,128)(2,1)} %get-tuple-element.47) | copy-start | bytes 2359300
  76.1 21.0 %copy-start.6 = (bf16[3,256,512]{2,1,0:T(8,128)(2,1)S(1)}, bf16[3,256,512]{2,1,0:T(8,128)(2,1)}, u32[]{:S(2)}) copy-start(bf16[3,256,512]{2,1,0:T(8,128)(2,1)} %get-tuple-element.55) | copy-start | bytes 2359300
  76.1 12.1 %collective-permute-start.10 = (bf16[6,128,512]{2,1,0:T(8,128)(2,1)S(1)}, bf16[6,128,512]{2,1,0:T(8,128)(2,1)S(1)}, u32[]{:S(2)}, u32[]{:S(2)}) collective-permute-start(bf16[6,128,512]{2,1,0:T(8,128)(2,1)S(1)} %add_convert_fusion.1), channel_id=1, source_target_pairs={{0,16},{1,3},{2,18},{3,1},{4,20},{5,7},{6,22},{7,5},{8,24},{9,11},... | collective-permute-start | bytes 2359304 | tf_op jit(solution)/shard_map/ppermute | solution.py:410
  77.2 14.8 %collective-permute-start.7 = (bf16[2,4,128,512]{3,2,1,0:T(8,128)(2,1)S(1)}, bf16[2,4,128,512]{3,2,1,0:T(8,128)(2,1)S(1)}, u32[]{:S(2)}, u32[]{:S(2)}) collective-permute-start(bf16[2,4,128,512]{3,2,1,0:T(8,128)(2,1)S(1)} %add_convert_fusion), channel_id=1, source_target_pairs={{0,4},{1,3},{2,6},{3,1},{4,0},{5,7},{6,2},{7,5},{8,12},{9,11},{10,... | collective-permute-start | bytes 3145736 | tf_op jit(solution)/shard_map/ppermute | solution.py:410
  78.8 11.4 %collective-permute-start.6 = (bf16[3,256,512]{2,1,0:T(8,128)(2,1)S(1)}, bf16[3,256,512]{2,1,0:T(8,128)(2,1)S(1)}, u32[]{:S(2)}, u32[]{:S(2)}) collective-permute-start(bf16[3,256,512]{2,1,0:T(8,128)(2,1)S(1)} %copy-done.16), channel_id=1, source_target_pairs={{0,1},{1,0},{2,3},{3,2},{4,5},{5,4},{6,7},{7,6},{8,9},{9,8},{10,11... | collective-permute-start | bytes 2359304 | tf_op jit(solution)/shard_map/ppermute | solution.py:410
  90.2 7.7 %copy-start.7 = (bf16[3,256,512]{2,1,0:T(8,128)(2,1)}, bf16[3,256,512]{2,1,0:T(8,128)(2,1)S(1)}, u32[]{:S(2)}) copy-start(bf16[3,256,512]{2,1,0:T(8,128)(2,1)S(1)} %collective-permute-done.6) | copy-start | bytes 2359300
  92.0 1.6 copy-start.3
  93.6 9.5 %collective-permute-start.11 = (bf16[6,64,512]{2,1,0:T(8,128)(2,1)}, bf16[6,64,512]{2,1,0:T(8,128)(2,1)S(1)}, u32[]{:S(2)}, u32[]{:S(2)}) collective-permute-start(bf16[6,64,512]{2,1,0:T(8,128)(2,1)} %add_convert_fusion.4), channel_id=1, source_target_pairs={{0,2},{1,17},{2,0},{3,19},{4,6},{5,21},{6,4},{7,23},{8,10},{9,25},... | collective-permute-start | bytes 1179656 | tf_op jit(solution)/shard_map/ppermute | solution.py:410
  96.4 26.1 %collective-permute-start.8 = (bf16[1,4,128,512]{3,2,1,0:T(8,128)(2,1)S(1)}, bf16[1,4,128,512]{3,2,1,0:T(8,128)(2,1)}, u32[]{:S(2)}, u32[]{:S(2)}) collective-permute-start(bf16[1,4,128,512]{3,2,1,0:T(8,128)(2,1)S(1)} %add_convert_fusion.2), channel_id=1, source_target_pairs={{0,8},{1,9},{2,10},{3,11},{4,12},{5,13},{6,14},{7,15},{8,0},{9,1},... | collective-permute-start | bytes 1572872 | tf_op jit(solution)/shard_map/ppermute | solution.py:410
  97.9 29.2 %collective-permute-start.13 = (bf16[3,128,512]{2,1,0:T(8,128)(2,1)}, bf16[3,128,512]{2,1,0:T(8,128)(2,1)}, u32[]{:S(2)}, u32[]{:S(2)}) collective-permute-start(bf16[3,128,512]{2,1,0:T(8,128)(2,1)} %add_convert_fusion.3), channel_id=1, source_target_pairs={{0,16},{1,3},{2,18},{3,1},{4,20},{5,7},{6,22},{7,5},{8,24},{9,11},... | collective-permute-start | bytes 1179656 | tf_op jit(solution)/shard_map/ppermute | solution.py:410
  103.1 0.7 copy-start.8
  105.7 21.4 %collective-permute-start.12 = (bf16[6,32,512]{2,1,0:T(8,128)(2,1)}, bf16[6,32,512]{2,1,0:T(8,128)(2,1)S(1)}, u32[]{:S(2)}, u32[]{:S(2)}) collective-permute-start(bf16[6,32,512]{2,1,0:T(8,128)(2,1)} %add_convert_fusion.9), channel_id=1, source_target_pairs={{0,4},{1,5},{2,6},{3,7},{4,0},{5,1},{6,2},{7,3},{8,12},{9,13},{10,... | collective-permute-start | bytes 589832 | tf_op jit(solution)/shard_map/ppermute | solution.py:410
  126.2 13.3 %copy-start.10 = (bf16[1,256,512]{2,1,0:T(8,128)(2,1)S(1)}, bf16[1,256,512]{2,1,0:T(8,128)(2,1)}, u32[]{:S(2)}) copy-start(bf16[1,256,512]{2,1,0:T(8,128)(2,1)} %get-tuple-element.62) | copy-start | bytes 786436
  126.2 13.2 %collective-permute-start.15 = (bf16[1,256,512]{2,1,0:T(8,128)(2,1)}, bf16[1,256,512]{2,1,0:T(8,128)(2,1)S(1)}, u32[]{:S(2)}, u32[]{:S(2)}) collective-permute-start(bf16[1,256,512]{2,1,0:T(8,128)(2,1)} %get-tuple-element.60), channel_id=1, source_target_pairs={{0,1},{1,0},{2,3},{3,2},{4,5},{5,4},{6,7},{7,6},{8,9},{9,8},{10,11... | collective-permute-start | bytes 786440 | tf_op jit(solution)/shard_map/ppermute | solution.py:410
  128.4 11.0 %collective-permute-start.14 = (bf16[6,32,512]{2,1,0:T(8,128)(2,1)S(1)}, bf16[6,32,512]{2,1,0:T(8,128)(2,1)S(1)}, u32[]{:S(2)}, u32[]{:S(2)}) collective-permute-start(bf16[6,32,512]{2,1,0:T(8,128)(2,1)S(1)} %add_convert_fusion.8), channel_id=1, source_target_pairs={{0,8},{1,9},{2,10},{3,11},{4,12},{5,13},{6,14},{7,15},{8,0},{9,1},... | collective-permute-start | bytes 589832 | tf_op jit(solution)/shard_map/ppermute | solution.py:410
  129.6 17.0 %collective-permute-start.19 = (bf16[3,64,512]{2,1,0:T(8,128)(2,1)S(1)}, bf16[3,64,512]{2,1,0:T(8,128)(2,1)S(1)}, u32[]{:S(2)}, u32[]{:S(2)}) collective-permute-start(bf16[3,64,512]{2,1,0:T(8,128)(2,1)S(1)} %add_convert_fusion.7), channel_id=1, source_target_pairs={{0,2},{1,17},{2,0},{3,19},{4,6},{5,21},{6,4},{7,23},{8,10},{9,25},... | collective-permute-start | bytes 589832 | tf_op jit(solution)/shard_map/ppermute | solution.py:410
  139.5 6.9 %collective-permute-start.16 = (bf16[6,32,512]{2,1,0:T(8,128)(2,1)S(1)}, bf16[6,32,512]{2,1,0:T(8,128)(2,1)S(1)}, u32[]{:S(2)}, u32[]{:S(2)}) collective-permute-start(bf16[6,32,512]{2,1,0:T(8,128)(2,1)S(1)} %multiply_convert_fusion.1), channel_id=1, source_target_pairs={{0,4},{1,5},{2,6},{3,7},{4,0},{5,1},{6,2},{7,3},{8,12},{9,13},{10,... | collective-permute-start | bytes 589832 | tf_op jit(solution)/shard_map/ppermute | solution.py:410
  139.6 6.8 %collective-permute-start.17 = (bf16[1,128,512]{2,1,0:T(8,128)(2,1)S(1)}, bf16[1,128,512]{2,1,0:T(8,128)(2,1)S(1)}, u32[]{:S(2)}, u32[]{:S(2)}) collective-permute-start(bf16[1,128,512]{2,1,0:T(8,128)(2,1)S(1)} %add_convert_fusion.13), channel_id=1, source_target_pairs={{0,16},{1,3},{2,18},{3,1},{4,20},{5,7},{6,22},{7,5},{8,24},{9,11},... | collective-permute-start | bytes 393224 | tf_op jit(solution)/shard_map/ppermute | solution.py:410
  146.4 7.8 %collective-permute-start.18 = (bf16[6,64,512]{2,1,0:T(8,128)(2,1)S(1)}, bf16[6,64,512]{2,1,0:T(8,128)(2,1)S(1)}, u32[]{:S(2)}, u32[]{:S(2)}) collective-permute-start(bf16[6,64,512]{2,1,0:T(8,128)(2,1)S(1)} %pad_maximum_fusion.3), channel_id=1, source_target_pairs={{0,2},{1,17},{2,0},{3,19},{4,6},{5,21},{6,4},{7,23},{8,10},{9,25},... | collective-permute-start | bytes 1179656 | tf_op jit(solution)/shard_map/ppermute | solution.py:410
  147.8 8.4 %collective-permute-start.22 = (bf16[3,64,512]{2,1,0:T(8,128)(2,1)S(1)}, bf16[3,64,512]{2,1,0:T(8,128)(2,1)S(1)}, u32[]{:S(2)}, u32[]{:S(2)}) collective-permute-start(bf16[3,64,512]{2,1,0:T(8,128)(2,1)S(1)} %add_convert_fusion.6), channel_id=1, source_target_pairs={{0,4},{1,5},{2,6},{3,7},{4,0},{5,1},{6,2},{7,3},{8,12},{9,13},{10,... | collective-permute-start | bytes 589832 | tf_op jit(solution)/shard_map/ppermute | solution.py:410
  148.2 7.4 %collective-permute-start.20 = (bf16[1,128,512]{2,1,0:T(8,128)(2,1)S(1)}, bf16[1,128,512]{2,1,0:T(8,128)(2,1)S(1)}, u32[]{:S(2)}, u32[]{:S(2)}) collective-permute-start(bf16[1,128,512]{2,1,0:T(8,128)(2,1)S(1)} %add_convert_fusion.12), channel_id=1, source_target_pairs={{0,2},{1,17},{2,0},{3,19},{4,6},{5,21},{6,4},{7,23},{8,10},{9,25},... | collective-permute-start | bytes 393224 | tf_op jit(solution)/shard_map/ppermute | solution.py:410
  155.6 12.3 %collective-permute-start.21 = (bf16[6,128,512]{2,1,0:T(8,128)(2,1)S(1)}, bf16[6,128,512]{2,1,0:T(8,128)(2,1)S(1)}, u32[]{:S(2)}, u32[]{:S(2)}) collective-permute-start(bf16[6,128,512]{2,1,0:T(8,128)(2,1)S(1)} %pad_maximum_fusion.1), channel_id=1, source_target_pairs={{0,16},{1,3},{2,18},{3,1},{4,20},{5,7},{6,22},{7,5},{8,24},{9,11},... | collective-permute-start | bytes 2359304 | tf_op jit(solution)/shard_map/ppermute | solution.py:410
  156.3 9.8 %collective-permute-start.25 = (bf16[3,64,512]{2,1,0:T(8,128)(2,1)S(1)}, bf16[3,64,512]{2,1,0:T(8,128)(2,1)S(1)}, u32[]{:S(2)}, u32[]{:S(2)}) collective-permute-start(bf16[3,64,512]{2,1,0:T(8,128)(2,1)S(1)} %add_convert_fusion.5), channel_id=1, source_target_pairs={{0,8},{1,9},{2,10},{3,11},{4,12},{5,13},{6,14},{7,15},{8,0},{9,1},... | collective-permute-start | bytes 589832 | tf_op jit(solution)/shard_map/ppermute | solution.py:410
  156.9 11.2 %collective-permute-start.23 = (bf16[1,128,512]{2,1,0:T(8,128)(2,1)S(1)}, bf16[1,128,512]{2,1,0:T(8,128)(2,1)S(1)}, u32[]{:S(2)}, u32[]{:S(2)}) collective-permute-start(bf16[1,128,512]{2,1,0:T(8,128)(2,1)S(1)} %add_convert_fusion.11), channel_id=1, source_target_pairs={{0,4},{1,5},{2,6},{3,7},{4,0},{5,1},{6,2},{7,3},{8,12},{9,13},{10,... | collective-permute-start | bytes 393224 | tf_op jit(solution)/shard_map/ppermute | solution.py:410
  166.1 5.7 %collective-permute-start.26 = (bf16[3,64,512]{2,1,0:T(8,128)(2,1)S(1)}, bf16[3,64,512]{2,1,0:T(8,128)(2,1)S(1)}, u32[]{:S(2)}, u32[]{:S(2)}) collective-permute-start(bf16[3,64,512]{2,1,0:T(8,128)(2,1)S(1)} %multiply_convert_fusion), channel_id=1, source_target_pairs={{0,2},{1,17},{2,0},{3,19},{4,6},{5,21},{6,4},{7,23},{8,10},{9,25},... | collective-permute-start | bytes 589832 | tf_op jit(solution)/shard_map/ppermute | solution.py:410
  168.1 18.3 %copy-start.1 = (bf16[6,256,512]{2,1,0:T(8,128)(2,1)}, bf16[6,256,512]{2,1,0:T(8,128)(2,1)S(1)}, u32[]{:S(2)}) copy-start(bf16[6,256,512]{2,1,0:T(8,128)(2,1)S(1)} %pad_maximum_fusion.refs_3_) | copy-start | bytes 4718596
  168.1 21.5 %collective-permute-start.24 = (bf16[6,256,512]{2,1,0:T(8,128)(2,1)S(1)}, bf16[6,256,512]{2,1,0:T(8,128)(2,1)}, u32[]{:S(2)}, u32[]{:S(2)}) collective-permute-start(bf16[6,256,512]{2,1,0:T(8,128)(2,1)S(1)} %pad_maximum_fusion.refs_3_), channel_id=1, source_target_pairs={{0,1},{1,0},{2,3},{3,2},{4,5},{5,4},{6,7},{7,6},{8,9},{9,8},{10,11... | collective-permute-start | bytes 4718600 | tf_op jit(solution)/shard_map/ppermute | solution.py:410
  171.8 7.8 %collective-permute-start.27 = (bf16[3,128,512]{2,1,0:T(8,128)(2,1)S(1)}, bf16[3,128,512]{2,1,0:T(8,128)(2,1)S(1)}, u32[]{:S(2)}, u32[]{:S(2)}) collective-permute-start(bf16[3,128,512]{2,1,0:T(8,128)(2,1)S(1)} %pad_maximum_fusion.4), channel_id=1, source_target_pairs={{0,16},{1,3},{2,18},{3,1},{4,20},{5,7},{6,22},{7,5},{8,24},{9,11},... | collective-permute-start | bytes 1179656 | tf_op jit(solution)/shard_map/ppermute | solution.py:410
  172.9 8.4 %collective-permute-start.28 = (bf16[1,128,512]{2,1,0:T(8,128)(2,1)S(1)}, bf16[1,128,512]{2,1,0:T(8,128)(2,1)S(1)}, u32[]{:S(2)}, u32[]{:S(2)}) collective-permute-start(bf16[1,128,512]{2,1,0:T(8,128)(2,1)S(1)} %add_convert_fusion.10), channel_id=1, source_target_pairs={{0,8},{1,9},{2,10},{3,11},{4,12},{5,13},{6,14},{7,15},{8,0},{9,1},... | collective-permute-start | bytes 393224 | tf_op jit(solution)/shard_map/ppermute | solution.py:410
  179.7 9.9 %copy-start.2 = (bf16[3,256,512]{2,1,0:T(8,128)(2,1)}, bf16[3,256,512]{2,1,0:T(8,128)(2,1)S(1)}, u32[]{:S(2)}) copy-start(bf16[3,256,512]{2,1,0:T(8,128)(2,1)S(1)} %pad_maximum_fusion.2.refs_5_) | copy-start | bytes 2359300
  181.3 6.7 %collective-permute-start.29 = (bf16[3,256,512]{2,1,0:T(8,128)(2,1)S(1)}, bf16[3,256,512]{2,1,0:T(8,128)(2,1)S(1)}, u32[]{:S(2)}, u32[]{:S(2)}) collective-permute-start(bf16[3,256,512]{2,1,0:T(8,128)(2,1)S(1)} %pad_maximum_fusion.2.refs_5_), channel_id=1, source_target_pairs={{0,1},{1,0},{2,3},{3,2},{4,5},{5,4},{6,7},{7,6},{8,9},{9,8},{10,11... | collective-permute-start | bytes 2359304 | tf_op jit(solution)/shard_map/ppermute | solution.py:410
  181.3 5.0 %collective-permute-start.30 = (bf16[1,128,512]{2,1,0:T(8,128)(2,1)S(1)}, bf16[1,128,512]{2,1,0:T(8,128)(2,1)S(1)}, u32[]{:S(2)}, u32[]{:S(2)}) collective-permute-start(bf16[1,128,512]{2,1,0:T(8,128)(2,1)S(1)} %multiply_convert_fusion.2), channel_id=1, source_target_pairs={{0,16},{1,3},{2,18},{3,1},{4,20},{5,7},{6,22},{7,5},{8,24},{9,11},... | collective-permute-start | bytes 393224 | tf_op jit(solution)/shard_map/ppermute | solution.py:410
  186.4 1.6 copy-start.4
  186.4 1.6 collective-permute-start.31
  188.0 0.7 copy-start.9
  188.7 0.9 copy-start.5
  (1 other events, 0.6 us)

commit v5 on v4

--- a/solution.py
+++ b/solution.py
@@ -15,6 +15,8 @@
 EARLY_LEVELS = 4
 LATE_LEVELS = 3
 BACK_LEVELS = 2
+EARLY_WAITS = (0, 0, 0, 0, 0, 2, 3, 4, 6)
+LATE_WAITS = (0, 0, 0, 0, 1, 3, 4, 5)
 VMEM_BYTES = 63 * 1024 * 1024
 F32 = jnp.float32
 BF16 = jnp.bfloat16
@@ -116,10 +118,12 @@
             target[0, s * size : (s + 1) * size, :] = value_ref[pl.ds(source, size), :].astype(BF16)
 
 
-def wgrad_kernel(taps, halo, order_ref, a_ref, g_ref, *refs):
-    if halo:
-        low_ref, high_ref = refs[:2]
-    keep_ref, send_ref, moved_ref, wide_ref = refs[-4:]
+def wgrad_kernel(taps, groups, *refs):
+    count = max(groups) + 1
+    orders = refs[:count]
+    a_ref, g_ref, low_ref, high_ref = refs[count : count + 4]
+    outs = refs[-2 * count - 2 : -2]
+    moved_ref, wide_ref = refs[-2:]
     rows, cols, chans = a_ref.shape
     total = rows * cols
     step = pl.program_id(0)
@@ -127,7 +131,7 @@
         fresh = j != 1 and (t == 0 or taps[t - 1][1] != j)
 
         @pl.when(step == t)
-        def _(i=i, j=j, fresh=fresh):
+        def _(i=i, j=j, fresh=fresh, group=groups[t]):
             if fresh:
                 for u in range(rows):
                     moved_ref[u * cols : (u + 1) * cols, :] = column_shift(
@@ -147,7 +151,7 @@
                 wide_ref[...] = tn_dot(act(1, rows), g_ref[: total - cols, :]) + tn_dot(
                     act(0, 1), low_ref[...]
                 )
-            spread(wide_ref, order_ref, keep_ref, send_ref)
+            spread(wide_ref, orders[group], *outs[2 * group : 2 * group + 2])
 
 
 def pick(index, values):
@@ -157,29 +161,36 @@
     return result
 
 
-def wgrad(order, act, grad, halos, taps, places, count, before, after):
+def wgrad(orders, act, grad, halos, taps, groups, places, after):
     rows, cols, chans = grad.shape
     whole = lambda *shape: pl.BlockSpec(shape, lambda t: (0,) * len(shape))
-    half_spec = pl.BlockSpec((1, chans // 2, chans), lambda t: (pick(t, places), 0, 0))
-    shape = jax.ShapeDtypeStruct((count, chans // 2, chans), BF16)
-    ahead = 3 + len(halos)
+    out_specs, out_shape = [], []
+    for group in range(len(orders)):
+        mine = [n for n in range(len(taps)) if groups[n] == group]
+        visited = [places[max([n for n in mine if n <= t], default=mine[0])] for t in range(len(taps))]
+        spec = pl.BlockSpec(
+            (1, chans // 2, chans), lambda t, visited=visited: (pick(t, visited), 0, 0)
+        )
+        shape = jax.ShapeDtypeStruct((len(mine), chans // 2, chans), BF16)
+        out_specs += [spec, spec]
+        out_shape += [shape, shape]
     return pl.pallas_call(
-        functools.partial(wgrad_kernel, taps, len(halos) > 0),
+        functools.partial(wgrad_kernel, taps, groups),
         grid=(len(taps),),
-        in_specs=[SMEM, whole(rows, cols, chans), whole(rows * cols, chans)]
-        + [whole(cols, chans)] * len(halos)
-        + [ANY] * (len(before) + len(after)),
-        out_specs=[half_spec, half_spec],
-        out_shape=[shape, shape],
+        in_specs=[SMEM] * len(orders)
+        + [whole(rows, cols, chans), whole(rows * cols, chans)]
+        + [whole(cols, chans)] * 2
+        + [ANY] * len(after),
+        out_specs=out_specs,
+        out_shape=out_shape,
         scratch_shapes=[pltpu.VMEM((rows * cols, chans), BF16), pltpu.VMEM((chans, chans), F32)],
-        input_output_aliases={ahead: 0, ahead + 1: 1} if before else {},
         compiler_params=params(),
         cost_estimate=cost(
             2 * len(taps) * rows * cols * chans * chans,
             2 * (2 * rows * cols * chans + len(taps) * chans * chans),
         ),
         name="wgrad",
-    )(order, act, grad.reshape(rows * cols, chans), *halos, *before, *after)
+    )(*orders, act, grad.reshape(rows * cols, chans), *halos, *after)
 
 
 def pieces_kernel(
@@ -187,8 +198,8 @@
 ):
     own_blocks, per, tile_bits, edge, after = plan
     sources = refs[:4]
-    outs = refs[4 + after : 6 + after]
-    blocks_ref, cells_ref, acc_ref, count_ref, list_ref, sems = refs[6 + after :]
+    outs = refs[4 + after : 8 + after]
+    blocks_ref, cells_ref, acc_ref, count_ref, list_ref, sems = refs[8 + after :]
     off_ref, fx_ref, fy_ref = cells_ref.at[0], cells_ref.at[1], cells_ref.at[2]
     copies = []
     start = 0
@@ -284,24 +295,31 @@
 
             out[inside[0], inside[1]] = acc_ref[...].astype(BF16)
 
-    for half in (1, 0):
-        out = outs[half]
-        base = half * (slots // 2)
-
-        @pl.loop(0, (slots // 2) * per // BATCH)
-        def _(m, out=out, base=base):
-            values = []
-            for n in range(BATCH):
-                at = base * per + m * BATCH + n
-                entries = [list_ref[at * wide + g] for g in range(GROUP)]
-                values.append(group_product(entries).astype(BF16))
-            for n in range(BATCH):
-                spot = m * BATCH + n
-                out[spot >> per_bits, spot & (per - 1)] = values[n]
-
-        @pl.loop(0, (slots // 2) * per)
-        def _(spot, out=out, base=base):
-            overfill(out, base * per + spot, (spot >> per_bits, spot & (per - 1)))
+    inside = outs[0].shape[1]
+    for chunk in range(2):
+        for half in (1, 0):
+            out = outs[2 * chunk + half]
+            base = half * (slots // 2) * per + chunk * inside
+
+            def visit(spot, base=base):
+                place = spot // inside
+                local = spot - place * inside
+                return place, local, base + place * per + local
+
+            @pl.loop(0, (slots // 2) * inside // BATCH)
+            def _(m, out=out, visit=visit):
+                found = []
+                for n in range(BATCH):
+                    place, local, at = visit(m * BATCH + n)
+                    entries = [list_ref[at * wide + g] for g in range(GROUP)]
+                    found.append((place, local, group_product(entries).astype(BF16)))
+                for place, local, value in found:
+                    out[place, local] = value
+
+            @pl.loop(0, (slots // 2) * inside)
+            def _(spot, out=out, visit=visit):
+                place, local, at = visit(spot)
+                overfill(out, at, (place, local))
 
 
 def swap_low_bits(value):
@@ -321,12 +339,12 @@
     chans = sources[0].shape[2]
     bits = int(math.log2(tiles)) - 1
     slots = tiles // 2
-    shape = jax.ShapeDtypeStruct((slots // 2, per, 2 * IMGW, chans), BF16)
+    shape = jax.ShapeDtypeStruct((slots // 2, per // 2, 2 * IMGW, chans), BF16)
     return pl.pallas_call(
         functools.partial(pieces_kernel, (own, per, bits, edge, len(after))),
         in_specs=[SMEM, SMEM, VMEM, VMEM] + [ANY] * (4 + len(after)),
-        out_specs=[VMEM] * 2,
-        out_shape=[shape] * 2,
+        out_specs=[VMEM] * 4,
+        out_shape=[shape] * 4,
         scratch_shapes=[
             pltpu.VMEM((2 * own, BLK, chans), BF16),
             pltpu.VMEM((3, 2 * own + 8, 2 * BLK), jnp.int32),
@@ -460,6 +478,9 @@
         if self.done <= self.levels:
             return region_sum(self.terms[:-1] + [self.recv], 1, 0, self.extent)
         return self.sent.astype(F32) + self.recv.astype(F32)
+
+    def hold(self, *values):
+        self.recv = together(self.recv, *values)[0]
 
     def step(self, *after):
         n = self.done
@@ -591,7 +612,7 @@
     edge_other = lax.ppermute(edge, "tile", core_swap)
     slope = image_slope(image, backbone_weight, [edge])
     as_blocks = lambda value: value.reshape(-1, BLK, chans)
-    keep, send = warp_pieces(
+    keep_a, send_a, keep_b, send_b = warp_pieces(
         info,
         route,
         cells,
@@ -606,62 +627,61 @@
     tile_masks = [(0, 1 << n) for n in range(1, int(math.log2(tiles)))]
     swapped = [tile_masks[1], tile_masks[0]] + tile_masks[2:] if len(tile_masks) > 1 else tile_masks
     warp_masks = (tile_masks, swapped)
-    warp = [keep]
-    extent = keep.shape[0]
-    last = len(tile_masks) - 1
-
-    def warp_step(n, send):
-        nonlocal extent
+
+    def warp_step(terms, n, send):
         if n > 0:
-            send = region_sum(warp, 0, extent // 2, extent).astype(BF16)
-            extent //= 2
-        warp.append(exchange(send, *sizes, lambda core: warp_masks[core][n]))
+            extent = keep_a.shape[0] >> (n - 1)
+            send = region_sum(terms, 0, extent // 2, extent).astype(BF16)
+        terms.append(exchange(send, *sizes, lambda core: warp_masks[core][n]))
         return send
 
-    warp_step(0, send)
-    early_taps = tuple((i, j) for j in (1, 0, 2) for i in (1, 0))
-    late_taps = tuple((2, j) for j in (1, 0, 2))
-    outs = wgrad(
-        early_order,
-        act,
-        grad,
-        [low, high],
-        early_taps,
-        tuple(3 * i + j for i, j in early_taps),
-        6,
-        [],
-        [keep],
+    a, b = [keep_a], [keep_b]
+    warp_step(a, 0, send_a)
+    warp_step(b, 0, send_b)
+    taps = tuple((i, j) for j in (1, 0, 2) for i in (1, 0, 2))
+    groups = tuple(int(i == 2) for i, _ in taps)
+    places = tuple(j if i == 2 else 3 * i + j for i, j in taps)
+    keep_early, send_early, keep_late, send_late = wgrad(
+        (early_order, late_order), act, grad, [low, high], taps, groups, places, [keep_a]
     )
-    early = Chain(*outs, sizes, early_levels, cell_scale)
+    a[1], b[1], send_early, send_late = together(a[1], b[1], send_early, send_late)
+    early = Chain(keep_early, send_early, sizes, early_levels, cell_scale)
+    late = Chain(keep_late, send_late, sizes, late_levels, cell_scale)
+    warp_step(a, 1, None)
+    sent = warp_step(b, 1, None)
     early.step()
-    outs = list(wgrad(late_order, act, grad, [low, high], late_taps, (1, 0, 2), 3, [], [outs[0]]))
-    outs[0] = early.tie(outs[0])
-    late = Chain(*outs, sizes, late_levels, cell_scale)
-    warp[1], late.sent = together(warp[1], late.sent)
-
-    sent = warp_step(1, None)
-    late.step()
+    late.step(sent)
+    early.hold(a[2])
+    sent = warp_step(a, 2, None)
     early.step(sent)
-    warp[2] = late.tie(warp[2])
-
-    sent = warp_step(2, None)
-    early.step(sent)
+    late.hold(b[2])
+    sent = warp_step(b, 2, None)
     late.step(sent)
-    for n in range(3, last + 1):
-        warp_step(n, None)
-
-    image_grad, keep_img, send_img = image_layer(back_order, [warp], slope, image, backbone_weight)
+    early.hold(a[3])
+    early.step()
+    for n in range(3, len(tile_masks)):
+        for terms in (a, b):
+            warp_step(terms, n, None)
+
+    image_grad, keep_img, send_img = image_layer(back_order, [a, b], slope, image, backbone_weight)
     back = Chain(keep_img, send_img, sizes, back_levels, pixel_scale)
     early.step()
+    late.step()
     early.recv, late.recv, _ = together(early.recv, late.recv, send_img)
-    chains = [back, early, late]
-    before = [send_img]
-    while any(chain.more() for chain in chains):
-        for chain in chains:
-            if chain.more():
-                held = chain.recv
-                chain.step(*before)
-                before = [] if held is None else [held]
+    received = []
+    for n in range(back.count):
+        back.step()
+        for chain, waits in ((early, EARLY_WAITS), (late, LATE_WAITS)):
+            while chain.more() and waits[min(chain.done, len(waits) - 1)] <= n:
+                wait = waits[min(chain.done, len(waits) - 1)]
+                if wait > 0:
+                    chain.hold(received[wait - 1])
+                chain.step()
+        received.append(back.recv)
+    for chain in (early, late):
+        while chain.more():
+            chain.hold(received[-1])
+            chain.step()
 
     conv_grad, backbone_grad = place_parts(
         [early_order, late_order, back_order],

time: 195 us -> 191 us (0.979)
  waiting for transfers between devices: 77.4 us -> 69.2 us
  starting transfers between devices: 31.2 us -> 34.9 us
  Pallas kernels: 63.7 us -> 60.9 us
    ppermute x27 -> x30, waiting for transfers between devices: 77.4 us -> 69.2 us  [exchange(): return lax.ppermute(value, ('dp', 'tile'), pairs)]
    ppermute x27 -> x30, starting transfers between devices: 21.5 us -> 25.1 us  [exchange(): return lax.ppermute(value, ('dp', 'tile'), pairs)]
    pallas_call x2 -> x1, Pallas kernels: 23 us -> 20.2 us  [wgrad(): pl.pallas_call(functools.partial(wgrad_kernel, taps, groups), grid=(len(t...]
    convert_element_type x2 -> x4, other arithmetic: 3.21 us -> 5.82 us  [warp_step(): send = region_sum(terms, 0, extent // 2, extent).astype(BF16)]
    unnamed x34 -> x42, local copies, waits for them, and re-layouts: 3.32 us -> 4.47 us
  transfers between devices with their start and end apart: 32 -> 35, of which waited for: 14 -> 20; matrix products, arithmetic and copies ran while one was open for 7% -> 9% of each run, Pallas kernels for 26% -> 25%
where the time goes in v5:
time: 191 us; the launch traced here: 190 us
  waiting for transfers between devices  69.2 us (36%)
  Pallas kernels  60.9 us (32%)
  starting transfers between devices  34.9 us (18%)
  other arithmetic  17.6 us (9%)
  local copies, waits for them, and re-layouts  6.77 us (4%)
    ppermute x30, waiting for transfers between devices, exchange(): return lax.ppermute(value, ('dp', 'tile'), pairs)  69.2 us
    ppermute x30, starting transfers between devices, exchange(): return lax.ppermute(value, ('dp', 'tile'), pairs)  25.1 us
    pallas_call x2, Pallas kernels, bev_rows(): pl.pallas_call(kernel, grid=(3,), in_specs=[whole(rows, cols, chans)] + [...  20.4 us
    pallas_call x1, Pallas kernels, wgrad(): pl.pallas_call(functools.partial(wgrad_kernel, taps, groups), grid=(len(t...  20.2 us
    pallas_call x1, Pallas kernels, warp_pieces(): pl.pallas_call(functools.partial(pieces_kernel, (own, per, bits, edge, le...  8.6 us
    convert_element_type x6, other arithmetic, step(): send = region_sum(self.terms, 1, self.extent // 2, self.extent).astype(BF16)  6.59 us
    convert_element_type x4, other arithmetic, warp_step(): send = region_sum(terms, 0, extent // 2, extent).astype(BF16)  5.82 us
    pallas_call x1, Pallas kernels, place_parts(): pl.pallas_call(functools.partial(place_kernel, spans), grid=(sum(spans),)...  5.18 us
  transfers between devices with their start and end apart: 35, of which 20 were waited for; matrix products, arithmetic and copies ran while one was open for 9% of the time, Pallas kernels for 25%

profile of v5, /device:TPU:0, one launch (start us, length us, event | category | flops | bytes accessed | tf_op | source)
XLA Modules:
  0.0 190.4 jit_solution(8426785669402472503)
XLA Ops:
  0.7 2.2 %slice_bitcast_fusion = (bf16[640,512]{1,0:T(8,128)(2,1)}, bf16[640,512]{1,0:T(8,128)(2,1)S(1)}) fusion(bf16[1,4,640,512]{3,2,1,0:T(8,128)(2,1)} %param.9), kind=kLoop, calls=%fused_computation.8 | loop fusion | bytes 2621440 | tf_op jit(solution)/shard_map/squeeze | solution.py:600
  2.9 1.3 collective-permute-start.2
  4.2 3.9 %collective-permute-start.1 = (bf16[640,512]{1,0:T(8,128)(2,1)S(1)}, bf16[640,512]{1,0:T(8,128)(2,1)}, u32[]{:S(2)}, u32[]{:S(2)}) collective-permute-start(bf16[640,512]{1,0:T(8,128)(2,1)S(1)} %get-tuple-element.70), channel_id=1, source_target_pairs={{0,1},{1,2},{2,3},{3,4},{4,5},{5,6},{6,7},{7,8},{8,9},{9,10},{10,1... | collective-permute-start | bytes 1966088 | tf_op jit(solution)/shard_map/ppermute | solution.py:599
  8.2 1.8 collective-permute-start
  10.0 10.0 %bev_rows.2.refs_3_ = bf16[2,640,512]{2,1,0:T(8,128)(2,1)} custom-call(bf16[4,640,512]{2,1,0:T(8,128)(2,1)} %bitcast.23, bf16[3,3,512,512]{3,2,1,0:T(8,128)(2,1)} %bitcast.26), custom_call_target="tpu_custom_call" | custom-call | flops 6039797760 | bytes 9961472 | tf_op jit(solution)/shard_map/bev_rows/pallas_call | solution.py:92
  20.7 10.4 %bev_rows.3.refs_0_ = bf16[2,640,512]{2,1,0:T(8,128)(2,1)} custom-call(bf16[4,640,512]{2,1,0:T(8,128)(2,1)} %bitcast.24, bf16[640,512]{1,0:T(8,128)(2,1)} %collective-permute-done.1.refs_0_.refs_4_, bf16[640,512]{1,0:T(8,128)(2,1)} %collective-permute-done.2.refs_1_.refs_5_, bf16[3,3,512,512]{3,2,1,0:T(8,128)(2,1)} %bitcast.27, ...), custom_call_target="tpu_custom_call" | custom-call | flops 6039797760 | bytes 9961472 | tf_op jit(solution)/shard_map/bev_rows/pallas_call | solution.py:92
  31.1 2.8 %collective-permute-start.4 = (bf16[2,640,512]{2,1,0:T(8,128)(2,1)}, bf16[2,640,512]{2,1,0:T(8,128)(2,1)}, u32[]{:S(2)}, u32[]{:S(2)}) collective-permute-start(bf16[2,640,512]{2,1,0:T(8,128)(2,1)} %bev_rows.3.refs_0_), channel_id=1, source_target_pairs={{0,1},{1,0},{2,3},{3,2},{4,5},{5,4},{6,7},{7,6},{8,9},{9,8},{10,11... | collective-permute-start | bytes 3932168 | tf_op jit(solution)/shard_map/ppermute | solution.py:612
  35.1 2.8 %image_slope.1.refs_4_.refs_8_ = f32[512,512]{1,0:T(8,128)} custom-call(bf16[512,512]{1,0:T(8,128)(2,1)} %bitcast.20, bf16[512,512]{1,0:T(8,128)(2,1)} %refs_10_.1, bf16[2,640,512]{2,1,0:T(8,128)(2,1)} %bev_rows.3.refs_0_), custom_call_target="tpu_custom_call" | custom-call | flops 268435456 | bytes 2621440 | tf_op jit(solution)/shard_map/image_slope/pallas_call | solution.py:373
  37.9 8.6 %warp_pieces.1 = (bf16[4,2,128,512]{3,2,1,0:T(8,128)(2,1)}, bf16[4,2,128,512]{3,2,1,0:T(8,128)(2,1)}, bf16[4,2,128,512]{3,2,1,0:T(8,128)(2,1)}, bf16[4,2,128,512]{3,2,1,0:T(8,128)(2,1)}) custom-call(s32[1]{0:T(128)} %bitcast.info_ref, s32[1,640]{1,0:T(1,128)} %route_ref.1, s32[3,40,64]{2,1,0:T(8,128)} %copy-done.15, s32[3,40,64]{2,1,0:T(8,128)} %copy-done.16, ...), custom_call_target="tpu_custom_call" | custom-call | flops 1073741824 | bytes 9437184 | tf_op jit(solution)/shard_map/warp_pieces/pallas_call | solution.py:343
  46.5 2.9 %collective-permute-start.5 = (bf16[4,2,128,512]{3,2,1,0:T(8,128)(2,1)}, bf16[4,2,128,512]{3,2,1,0:T(8,128)(2,1)}, u32[]{:S(2)}, u32[]{:S(2)}) collective-permute-start(bf16[4,2,128,512]{3,2,1,0:T(8,128)(2,1)} %get-tuple-element.37), channel_id=1, source_target_pairs={{0,2},{1,5},{2,0},{3,7},{4,6},{5,1},{6,4},{7,3},{8,10},{9,13},{10,... | collective-permute-start | bytes 3145736 | tf_op jit(solution)/shard_map/ppermute | solution.py:428
  49.5 20.2 %wgrad.1 = (bf16[6,256,512]{2,1,0:T(8,128)(2,1)}, bf16[6,256,512]{2,1,0:T(8,128)(2,1)}, bf16[3,256,512]{2,1,0:T(8,128)(2,1)}, bf16[3,256,512]{2,1,0:T(8,128)(2,1)}) custom-call(s32[16]{0:T(128)} %pad_add_fusion.2.refs_0_, s32[8]{0:T(128)} %pad_add_fusion.3.refs_1_, bf16[4,640,512]{2,1,0:T(8,128)(2,1)} %bitcast.29, bf16[2560,512]{1,0:T(8,128)(2,1)} %bitcast.25, ...), custom_call_target="tpu_custom_call" | custom-call | flops 12079595520 | bytes 9961472 | tf_op jit(solution)/shard_map/wgrad/pallas_call | solution.py:177
  69.7 4.1 %collective-permute-done.6.refs_5_ = bf16[4,2,128,512]{3,2,1,0:T(8,128)(2,1)} collective-permute-done((bf16[4,2,128,512]{3,2,1,0:T(8,128)(2,1)}, bf16[4,2,128,512]{3,2,1,0:T(8,128)(2,1)}, u32[]{:S(2)}, u32[]{:S(2)}) %collective-permute-start.6) | collective-permute-done | bytes 1048608 | tf_op jit(solution)/shard_map/ppermute | solution.py:428
  73.8 1.4 add_convert_fusion.2
  75.2 1.2 collective-permute-start.7
  76.4 1.2 add_convert_fusion.1
  78.8 5.6 %collective-permute-done.7.refs_2_ = bf16[2,2,128,512]{3,2,1,0:T(8,128)(2,1)S(1)} collective-permute-done((bf16[2,2,128,512]{3,2,1,0:T(8,128)(2,1)S(1)}, bf16[2,2,128,512]{3,2,1,0:T(8,128)(2,1)S(1)}, u32[]{:S(2)}, u32[]{:S(2)}) %collective-permute-start.7) | collective-permute-done | bytes 524320 | tf_op jit(solution)/shard_map/ppermute | solution.py:428
  84.5 1.3 add_convert_fusion.6
  86.1 1.2 collective-permute-start.12
  87.2 2.6 %collective-permute-start.8 = (bf16[1,2,128,512]{3,2,1,0:T(8,128)(2,1)S(1)}, bf16[1,2,128,512]{3,2,1,0:T(8,128)(2,1)S(1)}, u32[]{:S(2)}, u32[]{:S(2)}) collective-permute-start(bf16[1,2,128,512]{3,2,1,0:T(8,128)(2,1)S(1)} %add_convert_fusion.6), channel_id=1, source_target_pairs={{0,8},{1,9},{2,10},{3,11},{4,12},{5,13},{6,14},{7,15},{8,0},{9,1},... | collective-permute-start | bytes 786440 | tf_op jit(solution)/shard_map/ppermute | solution.py:428
  90.1 1.9 %add_convert_fusion.5 = bf16[1,2,128,512]{3,2,1,0:T(8,128)(2,1)} fusion(bf16[2,2,128,512]{3,2,1,0:T(8,128)(2,1)S(1)} %collective-permute-done.9.refs_6_, bf16[4,2,128,512]{3,2,1,0:T(8,128)(2,1)} %collective-permute-done.6.refs_5_, bf16[4,2,128,512]{3,2,1,0:T(8,128)(2,1)S(1)} %copy-done.1), kind=kLoop, calls=%fused_computation.10 | loop fusion | flops 786432 | bytes 1048576 | tf_op jit(solution)/shard_map/convert_element_type | solution.py:634
  92.0 1.0 add_convert_fusion.3
  93.0 1.1 collective-permute-start.16
  94.1 8.1 %collective-permute-done.8.refs_3_ = bf16[1,2,128,512]{3,2,1,0:T(8,128)(2,1)S(1)} collective-permute-done((bf16[1,2,128,512]{3,2,1,0:T(8,128)(2,1)S(1)}, bf16[1,2,128,512]{3,2,1,0:T(8,128)(2,1)S(1)}, u32[]{:S(2)}, u32[]{:S(2)}) %collective-permute-start.8) | collective-permute-done | bytes 262176 | tf_op jit(solution)/shard_map/ppermute | solution.py:428
  102.2 1.0 copy-done.9
  104.5 1.9 add_convert_fusion.10
  106.4 1.7 collective-permute-start.17
  108.1 4.1 %collective-permute-done.13 = bf16[6,64,512]{2,1,0:T(8,128)(2,1)S(1)} collective-permute-done((bf16[6,64,512]{2,1,0:T(8,128)(2,1)}, bf16[6,64,512]{2,1,0:T(8,128)(2,1)S(1)}, u32[]{:S(2)}, u32[]{:S(2)}) %collective-permute-start.13) | collective-permute-done | bytes 393248 | tf_op jit(solution)/shard_map/ppermute | solution.py:428
  112.1 1.7 add_convert_fusion.11
  114.5 2.9 %collective-permute-done.10.refs_7_ = bf16[1,2,128,512]{3,2,1,0:T(8,128)(2,1)} collective-permute-done((bf16[1,2,128,512]{3,2,1,0:T(8,128)(2,1)}, bf16[1,2,128,512]{3,2,1,0:T(8,128)(2,1)}, u32[]{:S(2)}, u32[]{:S(2)}) %collective-permute-start.10) | collective-permute-done | bytes 262176 | tf_op jit(solution)/shard_map/ppermute | solution.py:428
  117.4 3.8 %image_layer.1 = (bf16[512,512]{1,0:T(8,128)(2,1)}, bf16[1,256,512]{2,1,0:T(8,128)(2,1)}, bf16[1,256,512]{2,1,0:T(8,128)(2,1)}) custom-call(s32[4]{0:T(128)} %pad_add_fusion.1.order_ref.refs_2_, bf16[4,2,128,512]{3,2,1,0:T(8,128)(2,1)} %get-tuple-element.36.refs_6_.refs_0_, bf16[4,2,128,512]{3,2,1,0:T(8,128)(2,1)} %collective-permute-done.5.refs_1_, ...), custom_call_target="tpu_custom_call" | custom-call | flops 536870912 | bytes 4194304 | tf_op jit(solution)/shard_map/image_layer/pallas_call | solution.py:407
  121.4 1.2 add_convert_fusion.9
  125.0 4.4 %collective-permute-done.20 = bf16[1,128,512]{2,1,0:T(8,128)(2,1)S(1)} collective-permute-done((bf16[1,128,512]{2,1,0:T(8,128)(2,1)S(1)}, bf16[1,128,512]{2,1,0:T(8,128)(2,1)S(1)}, u32[]{:S(2)}, u32[]{:S(2)}) %collective-permute-start.20) | collective-permute-done | bytes 131104 | tf_op jit(solution)/shard_map/ppermute | solution.py:428
  129.4 5.4 %collective-permute-done.18 = bf16[6,32,512]{2,1,0:T(8,128)(2,1)S(1)} collective-permute-done((bf16[6,32,512]{2,1,0:T(8,128)(2,1)S(1)}, bf16[6,32,512]{2,1,0:T(8,128)(2,1)S(1)}, u32[]{:S(2)}, u32[]{:S(2)}) %collective-permute-start.18) | collective-permute-done | bytes 196640 | tf_op jit(solution)/shard_map/ppermute | solution.py:428
  135.0 1.6 collective-permute-start.22
  136.7 3.4 %collective-permute-done.22 = bf16[1,128,512]{2,1,0:T(8,128)(2,1)S(1)} collective-permute-done((bf16[1,128,512]{2,1,0:T(8,128)(2,1)S(1)}, bf16[1,128,512]{2,1,0:T(8,128)(2,1)S(1)}, u32[]{:S(2)}, u32[]{:S(2)}) %collective-permute-start.22) | collective-permute-done | bytes 131104 | tf_op jit(solution)/shard_map/ppermute | solution.py:428
  140.1 1.7 collective-permute-done.21
  141.8 1.6 collective-permute-start.23
  143.9 1.3 add_convert_fusion.8
  145.2 1.8 collective-permute-start.29
  147.0 2.4 %collective-permute-done.24 = bf16[1,128,512]{2,1,0:T(8,128)(2,1)S(1)} collective-permute-done((bf16[1,128,512]{2,1,0:T(8,128)(2,1)S(1)}, bf16[1,128,512]{2,1,0:T(8,128)(2,1)S(1)}, u32[]{:S(2)}, u32[]{:S(2)}) %collective-permute-start.24) | collective-permute-done | bytes 131104 | tf_op jit(solution)/shard_map/ppermute | solution.py:428
  151.5 2.2 %collective-permute-start.30 = (bf16[3,64,512]{2,1,0:T(8,128)(2,1)S(1)}, bf16[3,64,512]{2,1,0:T(8,128)(2,1)S(1)}, u32[]{:S(2)}, u32[]{:S(2)}) collective-permute-start(bf16[3,64,512]{2,1,0:T(8,128)(2,1)S(1)} %add_convert_fusion.7), channel_id=1, source_target_pairs={{0,8},{1,9},{2,10},{3,11},{4,12},{5,13},{6,14},{7,15},{8,0},{9,1},... | collective-permute-start | bytes 589832 | tf_op jit(solution)/shard_map/ppermute | solution.py:428
  153.7 9.3 %collective-permute-done.26 = bf16[1,128,512]{2,1,0:T(8,128)(2,1)S(1)} collective-permute-done((bf16[1,128,512]{2,1,0:T(8,128)(2,1)S(1)}, bf16[1,128,512]{2,1,0:T(8,128)(2,1)S(1)}, u32[]{:S(2)}, u32[]{:S(2)}) %collective-permute-start.26) | collective-permute-done | bytes 131104 | tf_op jit(solution)/shard_map/ppermute | solution.py:428
  163.7 3.4 %collective-permute-done.30 = bf16[3,64,512]{2,1,0:T(8,128)(2,1)S(1)} collective-permute-done((bf16[3,64,512]{2,1,0:T(8,128)(2,1)S(1)}, bf16[3,64,512]{2,1,0:T(8,128)(2,1)S(1)}, u32[]{:S(2)}, u32[]{:S(2)}) %collective-permute-start.30) | collective-permute-done | bytes 196640 | tf_op jit(solution)/shard_map/ppermute | solution.py:428
  168.3 1.2 copy-done
  169.5 3.4 %collective-permute-done.31 = bf16[3,64,512]{2,1,0:T(8,128)(2,1)S(1)} collective-permute-done((bf16[3,64,512]{2,1,0:T(8,128)(2,1)S(1)}, bf16[3,64,512]{2,1,0:T(8,128)(2,1)S(1)}, u32[]{:S(2)}, u32[]{:S(2)}) %collective-permute-start.31) | collective-permute-done | bytes 196640 | tf_op jit(solution)/shard_map/ppermute | solution.py:428
  173.6 7.2 %collective-permute-done.32 = bf16[3,128,512]{2,1,0:T(8,128)(2,1)S(1)} collective-permute-done((bf16[3,128,512]{2,1,0:T(8,128)(2,1)S(1)}, bf16[3,128,512]{2,1,0:T(8,128)(2,1)S(1)}, u32[]{:S(2)}, u32[]{:S(2)}) %collective-permute-start.32) | collective-permute-done | bytes 393248 | tf_op jit(solution)/shard_map/ppermute | solution.py:428
  181.5 2.1 %collective-permute-done.34.refs_8_ = bf16[1,256,512]{2,1,0:T(8,128)(2,1)S(1)} collective-permute-done((bf16[1,256,512]{2,1,0:T(8,128)(2,1)S(1)}, bf16[1,256,512]{2,1,0:T(8,128)(2,1)S(1)}, u32[]{:S(2)}, u32[]{:S(2)}) %collective-permute-start.34) | collective-permute-done | bytes 262176 | tf_op jit(solution)/shard_map/ppermute | solution.py:428
  185.2 5.2 %place_parts.1 = (bf16[9,512,512]{2,1,0:T(8,128)(2,1)}, bf16[1,512,512]{2,1,0:T(8,128)(2,1)}) custom-call(s32[16]{0:T(128)} %pad_add_fusion.2.refs_0_, s32[8]{0:T(128)} %pad_add_fusion.3.refs_1_, s32[4]{0:T(128)} %pad_add_fusion.1.order_ref.refs_2_, bf16[6,256,512]{2,1,0:T(8,128)(2,1)} %copy-done, bf16[6,256,512]{2,1,0:T(8,128)(2,1)} %collective-permute-done.28.refs_4_, ...), custom_call_target="tpu_custom_call" | custom-call | bytes 10485760 | tf_op jit(solution)/shard_map/place_parts/pallas_call | solution.py:553
  (105 shorter events, 16.0 us)
Async XLA Ops:
  0.6 7.4 %copy-start.17 = (s32[1,2560]{1,0:T(1,128)S(1)}, s32[1,2560]{1,0:T(1,128)}, u32[]{:S(2)}) copy-start(s32[1,2560]{1,0:T(1,128)} %param.17) | copy-start | bytes 30724
  0.6 7.4 %copy-start.18 = (s32[1,2560]{1,0:T(1,128)S(1)}, s32[1,2560]{1,0:T(1,128)}, u32[]{:S(2)}) copy-start(s32[1,2560]{1,0:T(1,128)} %param.16) | copy-start | bytes 30724
  0.7 7.4 %copy-start.19 = (s32[1,2560]{1,0:T(1,128)S(1)}, s32[1,2560]{1,0:T(1,128)}, u32[]{:S(2)}) copy-start(s32[1,2560]{1,0:T(1,128)} %param.15) | copy-start | bytes 30724
  2.9 17.2 %collective-permute-start.2 = (bf16[640,512]{1,0:T(8,128)(2,1)}, bf16[640,512]{1,0:T(8,128)(2,1)}, u32[]{:S(2)}, u32[]{:S(2)}) collective-permute-start(bf16[640,512]{1,0:T(8,128)(2,1)} %get-tuple-element.69), channel_id=1, source_target_pairs={{1,0},{2,1},{3,2},{4,3},{5,4},{6,5},{7,6},{8,7},{9,8},{10,9},{11,1... | collective-permute-start | bytes 1966088 | tf_op jit(solution)/shard_map/ppermute | solution.py:600
  4.2 15.9 %collective-permute-start.1 = (bf16[640,512]{1,0:T(8,128)(2,1)S(1)}, bf16[640,512]{1,0:T(8,128)(2,1)}, u32[]{:S(2)}, u32[]{:S(2)}) collective-permute-start(bf16[640,512]{1,0:T(8,128)(2,1)S(1)} %get-tuple-element.70), channel_id=1, source_target_pairs={{0,1},{1,2},{2,3},{3,4},{4,5},{5,6},{6,7},{7,8},{8,9},{9,10},{10,1... | collective-permute-start | bytes 1966088 | tf_op jit(solution)/shard_map/ppermute | solution.py:599
  8.2 11.9 %copy-start.15 = (s32[3,40,64]{2,1,0:T(8,128)}, s32[3,40,64]{2,1,0:T(8,128)S(1)}, u32[]{:S(2)}) copy-start(s32[3,40,64]{2,1,0:T(8,128)S(1)} %reshape.32.mine_ref) | copy-start | bytes 92164
  8.2 11.9 %collective-permute-start = (s32[3,40,64]{2,1,0:T(8,128)S(1)}, s32[3,40,64]{2,1,0:T(8,128)S(1)}, u32[]{:S(2)}, u32[]{:S(2)}) collective-permute-start(s32[3,40,64]{2,1,0:T(8,128)S(1)} %reshape.32.mine_ref), channel_id=1, source_target_pairs={{0,1},{1,0},{2,3},{3,2},{4,5},{5,4},{6,7},{7,6},{8,9},{9,8},{10,11... | collective-permute-start | bytes 92168 | tf_op jit(solution)/shard_map/ppermute | solution.py:604
  20.0 17.9 %collective-permute-start.3 = (bf16[2,640,512]{2,1,0:T(8,128)(2,1)}, bf16[2,640,512]{2,1,0:T(8,128)(2,1)}, u32[]{:S(2)}, u32[]{:S(2)}) collective-permute-start(bf16[2,640,512]{2,1,0:T(8,128)(2,1)} %bev_rows.2.refs_3_), channel_id=1, source_target_pairs={{0,1},{1,0},{2,3},{3,2},{4,5},{5,4},{6,7},{7,6},{8,9},{9,8},{10,11... | collective-permute-start | bytes 3932168 | tf_op jit(solution)/shard_map/ppermute | solution.py:608
  31.1 6.8 %collective-permute-start.4 = (bf16[2,640,512]{2,1,0:T(8,128)(2,1)}, bf16[2,640,512]{2,1,0:T(8,128)(2,1)}, u32[]{:S(2)}, u32[]{:S(2)}) collective-permute-start(bf16[2,640,512]{2,1,0:T(8,128)(2,1)} %bev_rows.3.refs_0_), channel_id=1, source_target_pairs={{0,1},{1,0},{2,3},{3,2},{4,5},{5,4},{6,7},{7,6},{8,9},{9,8},{10,11... | collective-permute-start | bytes 3932168 | tf_op jit(solution)/shard_map/ppermute | solution.py:612
  46.5 23.2 %collective-permute-start.5 = (bf16[4,2,128,512]{3,2,1,0:T(8,128)(2,1)}, bf16[4,2,128,512]{3,2,1,0:T(8,128)(2,1)}, u32[]{:S(2)}, u32[]{:S(2)}) collective-permute-start(bf16[4,2,128,512]{3,2,1,0:T(8,128)(2,1)} %get-tuple-element.37), channel_id=1, source_target_pairs={{0,2},{1,5},{2,0},{3,7},{4,6},{5,1},{6,4},{7,3},{8,10},{9,13},{10,... | collective-permute-start | bytes 3145736 | tf_op jit(solution)/shard_map/ppermute | solution.py:428
  49.4 24.3 %collective-permute-start.6 = (bf16[4,2,128,512]{3,2,1,0:T(8,128)(2,1)}, bf16[4,2,128,512]{3,2,1,0:T(8,128)(2,1)}, u32[]{:S(2)}, u32[]{:S(2)}) collective-permute-start(bf16[4,2,128,512]{3,2,1,0:T(8,128)(2,1)} %get-tuple-element.38), channel_id=1, source_target_pairs={{0,2},{1,5},{2,0},{3,7},{4,6},{5,1},{6,4},{7,3},{8,10},{9,13},{10,... | collective-permute-start | bytes 3145736 | tf_op jit(solution)/shard_map/ppermute | solution.py:428
  69.7 6.7 %copy-start.1 = (bf16[4,2,128,512]{3,2,1,0:T(8,128)(2,1)S(1)}, bf16[4,2,128,512]{3,2,1,0:T(8,128)(2,1)}, u32[]{:S(2)}) copy-start(bf16[4,2,128,512]{3,2,1,0:T(8,128)(2,1)} %get-tuple-element.42.refs_4_) | copy-start | bytes 3145732
  73.8 4.8 %copy-start.20 = (bf16[3,256,512]{2,1,0:T(8,128)(2,1)S(1)}, bf16[3,256,512]{2,1,0:T(8,128)(2,1)}, u32[]{:S(2)}) copy-start(bf16[3,256,512]{2,1,0:T(8,128)(2,1)} %get-tuple-element.52) | copy-start | bytes 2359300
  73.8 12.0 %collective-permute-start.11 = (bf16[6,256,512]{2,1,0:T(8,128)(2,1)}, bf16[6,256,512]{2,1,0:T(8,128)(2,1)S(1)}, u32[]{:S(2)}, u32[]{:S(2)}) collective-permute-start(bf16[6,256,512]{2,1,0:T(8,128)(2,1)} %get-tuple-element.46), channel_id=1, source_target_pairs={{0,1},{1,0},{2,3},{3,2},{4,5},{5,4},{6,7},{7,6},{8,9},{9,8},{10,11... | collective-permute-start | bytes 4718600 | tf_op jit(solution)/shard_map/ppermute | solution.py:428
  75.2 10.6 %copy-start.3 = (bf16[6,256,512]{2,1,0:T(8,128)(2,1)S(1)}, bf16[6,256,512]{2,1,0:T(8,128)(2,1)}, u32[]{:S(2)}) copy-start(bf16[6,256,512]{2,1,0:T(8,128)(2,1)} %get-tuple-element.45) | copy-start | bytes 4718596
  75.2 9.2 %collective-permute-start.7 = (bf16[2,2,128,512]{3,2,1,0:T(8,128)(2,1)S(1)}, bf16[2,2,128,512]{3,2,1,0:T(8,128)(2,1)S(1)}, u32[]{:S(2)}, u32[]{:S(2)}) collective-permute-start(bf16[2,2,128,512]{3,2,1,0:T(8,128)(2,1)S(1)} %add_convert_fusion.2), channel_id=1, source_target_pairs={{0,4},{1,3},{2,6},{3,1},{4,0},{5,7},{6,2},{7,5},{8,12},{9,11},{10,... | collective-permute-start | bytes 1572872 | tf_op jit(solution)/shard_map/ppermute | solution.py:428
  77.6 12.4 %collective-permute-start.9 = (bf16[2,2,128,512]{3,2,1,0:T(8,128)(2,1)S(1)}, bf16[2,2,128,512]{3,2,1,0:T(8,128)(2,1)S(1)}, u32[]{:S(2)}, u32[]{:S(2)}) collective-permute-start(bf16[2,2,128,512]{3,2,1,0:T(8,128)(2,1)S(1)} %add_convert_fusion.1), channel_id=1, source_target_pairs={{0,4},{1,3},{2,6},{3,1},{4,0},{5,7},{6,2},{7,5},{8,12},{9,11},{10,... | collective-permute-start | bytes 1572872 | tf_op jit(solution)/shard_map/ppermute | solution.py:428
  78.5 13.4 %collective-permute-start.15 = (bf16[3,256,512]{2,1,0:T(8,128)(2,1)S(1)}, bf16[3,256,512]{2,1,0:T(8,128)(2,1)S(1)}, u32[]{:S(2)}, u32[]{:S(2)}) collective-permute-start(bf16[3,256,512]{2,1,0:T(8,128)(2,1)S(1)} %copy-done.20), channel_id=1, source_target_pairs={{0,1},{1,0},{2,3},{3,2},{4,5},{5,4},{6,7},{7,6},{8,9},{9,8},{10,11... | collective-permute-start | bytes 2359304 | tf_op jit(solution)/shard_map/ppermute | solution.py:428
  85.8 26.3 %copy-start.4 = (bf16[6,256,512]{2,1,0:T(8,128)(2,1)}, bf16[6,256,512]{2,1,0:T(8,128)(2,1)S(1)}, u32[]{:S(2)}) copy-start(bf16[6,256,512]{2,1,0:T(8,128)(2,1)S(1)} %collective-permute-done.11) | copy-start | bytes 4718596
  85.8 6.2 %copy-start.10 = (bf16[3,256,512]{2,1,0:T(8,128)(2,1)S(1)}, bf16[3,256,512]{2,1,0:T(8,128)(2,1)}, u32[]{:S(2)}) copy-start(bf16[3,256,512]{2,1,0:T(8,128)(2,1)} %get-tuple-element.50) | copy-start | bytes 2359300
  86.1 16.1 %collective-permute-start.12 = (bf16[6,128,512]{2,1,0:T(8,128)(2,1)S(1)}, bf16[6,128,512]{2,1,0:T(8,128)(2,1)S(1)}, u32[]{:S(2)}, u32[]{:S(2)}) collective-permute-start(bf16[6,128,512]{2,1,0:T(8,128)(2,1)S(1)} %add_convert_fusion), channel_id=1, source_target_pairs={{0,16},{1,3},{2,18},{3,1},{4,20},{5,7},{6,22},{7,5},{8,24},{9,11},... | collective-permute-start | bytes 2359304 | tf_op jit(solution)/shard_map/ppermute | solution.py:428
  87.2 15.0 %collective-permute-start.8 = (bf16[1,2,128,512]{3,2,1,0:T(8,128)(2,1)S(1)}, bf16[1,2,128,512]{3,2,1,0:T(8,128)(2,1)S(1)}, u32[]{:S(2)}, u32[]{:S(2)}) collective-permute-start(bf16[1,2,128,512]{3,2,1,0:T(8,128)(2,1)S(1)} %add_convert_fusion.6), channel_id=1, source_target_pairs={{0,8},{1,9},{2,10},{3,11},{4,12},{5,13},{6,14},{7,15},{8,0},{9,1},... | collective-permute-start | bytes 786440 | tf_op jit(solution)/shard_map/ppermute | solution.py:428
  90.1 14.0 %copy-start.6 = (bf16[2,2,128,512]{3,2,1,0:T(8,128)(2,1)}, bf16[2,2,128,512]{3,2,1,0:T(8,128)(2,1)S(1)}, u32[]{:S(2)}) copy-start(bf16[2,2,128,512]{3,2,1,0:T(8,128)(2,1)S(1)} %collective-permute-done.9.refs_6_) | copy-start | bytes 1572868
  92.0 12.1 %copy-start.11 = (bf16[3,256,512]{2,1,0:T(8,128)(2,1)}, bf16[3,256,512]{2,1,0:T(8,128)(2,1)S(1)}, u32[]{:S(2)}) copy-start(bf16[3,256,512]{2,1,0:T(8,128)(2,1)S(1)} %collective-permute-done.15) | copy-start | bytes 2359300
  93.0 11.6 %collective-permute-start.16 = (bf16[3,128,512]{2,1,0:T(8,128)(2,1)}, bf16[3,128,512]{2,1,0:T(8,128)(2,1)}, u32[]{:S(2)}, u32[]{:S(2)}) collective-permute-start(bf16[3,128,512]{2,1,0:T(8,128)(2,1)} %add_convert_fusion.3), channel_id=1, source_target_pairs={{0,16},{1,3},{2,18},{3,1},{4,20},{5,7},{6,22},{7,5},{8,24},{9,11},... | collective-permute-start | bytes 1179656 | tf_op jit(solution)/shard_map/ppermute | solution.py:428
  104.1 8.0 %collective-permute-start.13 = (bf16[6,64,512]{2,1,0:T(8,128)(2,1)}, bf16[6,64,512]{2,1,0:T(8,128)(2,1)S(1)}, u32[]{:S(2)}, u32[]{:S(2)}) collective-permute-start(bf16[6,64,512]{2,1,0:T(8,128)(2,1)} %add_convert_fusion.4), channel_id=1, source_target_pairs={{0,2},{1,17},{2,0},{3,19},{4,6},{5,21},{6,4},{7,23},{8,10},{9,25},... | collective-permute-start | bytes 1179656 | tf_op jit(solution)/shard_map/ppermute | solution.py:428
  104.5 12.8 %collective-permute-start.10 = (bf16[1,2,128,512]{3,2,1,0:T(8,128)(2,1)}, bf16[1,2,128,512]{3,2,1,0:T(8,128)(2,1)}, u32[]{:S(2)}, u32[]{:S(2)}) collective-permute-start(bf16[1,2,128,512]{3,2,1,0:T(8,128)(2,1)} %add_convert_fusion.5), channel_id=1, source_target_pairs={{0,8},{1,9},{2,10},{3,11},{4,12},{5,13},{6,14},{7,15},{8,0},{9,1},... | collective-permute-start | bytes 786440 | tf_op jit(solution)/shard_map/ppermute | solution.py:428
  106.4 14.8 %collective-permute-start.17 = (bf16[3,64,512]{2,1,0:T(8,128)(2,1)}, bf16[3,64,512]{2,1,0:T(8,128)(2,1)}, u32[]{:S(2)}, u32[]{:S(2)}) collective-permute-start(bf16[3,64,512]{2,1,0:T(8,128)(2,1)} %add_convert_fusion.10), channel_id=1, source_target_pairs={{0,2},{1,17},{2,0},{3,19},{4,6},{5,21},{6,4},{7,23},{8,10},{9,25},... | collective-permute-start | bytes 589832 | tf_op jit(solution)/shard_map/ppermute | solution.py:428
  113.8 7.5 %collective-permute-start.14 = (bf16[6,32,512]{2,1,0:T(8,128)(2,1)}, bf16[6,32,512]{2,1,0:T(8,128)(2,1)S(1)}, u32[]{:S(2)}, u32[]{:S(2)}) collective-permute-start(bf16[6,32,512]{2,1,0:T(8,128)(2,1)} %add_convert_fusion.11), channel_id=1, source_target_pairs={{0,4},{1,5},{2,6},{3,7},{4,0},{5,1},{6,2},{7,3},{8,12},{9,13},{10,... | collective-permute-start | bytes 589832 | tf_op jit(solution)/shard_map/ppermute | solution.py:428
  121.2 13.8 %copy-start.14 = (bf16[1,256,512]{2,1,0:T(8,128)(2,1)S(1)}, bf16[1,256,512]{2,1,0:T(8,128)(2,1)}, u32[]{:S(2)}) copy-start(bf16[1,256,512]{2,1,0:T(8,128)(2,1)} %get-tuple-element.57) | copy-start | bytes 786436
  121.2 2.2 %collective-permute-start.19 = (bf16[1,256,512]{2,1,0:T(8,128)(2,1)}, bf16[1,256,512]{2,1,0:T(8,128)(2,1)S(1)}, u32[]{:S(2)}, u32[]{:S(2)}) collective-permute-start(bf16[1,256,512]{2,1,0:T(8,128)(2,1)} %get-tuple-element.55), channel_id=1, source_target_pairs={{0,1},{1,0},{2,3},{3,2},{4,5},{5,4},{6,7},{7,6},{8,9},{9,8},{10,11... | collective-permute-start | bytes 786440 | tf_op jit(solution)/shard_map/ppermute | solution.py:428
  122.6 12.2 %collective-permute-start.18 = (bf16[6,32,512]{2,1,0:T(8,128)(2,1)S(1)}, bf16[6,32,512]{2,1,0:T(8,128)(2,1)S(1)}, u32[]{:S(2)}, u32[]{:S(2)}) collective-permute-start(bf16[6,32,512]{2,1,0:T(8,128)(2,1)S(1)} %add_convert_fusion.9), channel_id=1, source_target_pairs={{0,8},{1,9},{2,10},{3,11},{4,12},{5,13},{6,14},{7,15},{8,0},{9,1},... | collective-permute-start | bytes 589832 | tf_op jit(solution)/shard_map/ppermute | solution.py:428
  124.3 5.0 %collective-permute-start.20 = (bf16[1,128,512]{2,1,0:T(8,128)(2,1)S(1)}, bf16[1,128,512]{2,1,0:T(8,128)(2,1)S(1)}, u32[]{:S(2)}, u32[]{:S(2)}) collective-permute-start(bf16[1,128,512]{2,1,0:T(8,128)(2,1)S(1)} %add_convert_fusion.15), channel_id=1, source_target_pairs={{0,16},{1,3},{2,18},{3,1},{4,20},{5,7},{6,22},{7,5},{8,24},{9,11},... | collective-permute-start | bytes 393224 | tf_op jit(solution)/shard_map/ppermute | solution.py:428
  134.9 6.9 %collective-permute-start.21 = (bf16[6,32,512]{2,1,0:T(8,128)(2,1)S(1)}, bf16[6,32,512]{2,1,0:T(8,128)(2,1)S(1)}, u32[]{:S(2)}, u32[]{:S(2)}) collective-permute-start(bf16[6,32,512]{2,1,0:T(8,128)(2,1)S(1)} %multiply_convert_fusion.1), channel_id=1, source_target_pairs={{0,4},{1,5},{2,6},{3,7},{4,0},{5,1},{6,2},{7,3},{8,12},{9,13},{10,... | collective-permute-start | bytes 589832 | tf_op jit(solution)/shard_map/ppermute | solution.py:428
  135.0 5.0 %collective-permute-start.22 = (bf16[1,128,512]{2,1,0:T(8,128)(2,1)S(1)}, bf16[1,128,512]{2,1,0:T(8,128)(2,1)S(1)}, u32[]{:S(2)}, u32[]{:S(2)}) collective-permute-start(bf16[1,128,512]{2,1,0:T(8,128)(2,1)S(1)} %add_convert_fusion.14), channel_id=1, source_target_pairs={{0,2},{1,17},{2,0},{3,19},{4,6},{5,21},{6,4},{7,23},{8,10},{9,25},... | collective-permute-start | bytes 393224 | tf_op jit(solution)/shard_map/ppermute | solution.py:428
  141.8 7.8 %collective-permute-start.23 = (bf16[6,64,512]{2,1,0:T(8,128)(2,1)S(1)}, bf16[6,64,512]{2,1,0:T(8,128)(2,1)S(1)}, u32[]{:S(2)}, u32[]{:S(2)}) collective-permute-start(bf16[6,64,512]{2,1,0:T(8,128)(2,1)S(1)} %pad_maximum_fusion.3), channel_id=1, source_target_pairs={{0,2},{1,17},{2,0},{3,19},{4,6},{5,21},{6,4},{7,23},{8,10},{9,25},... | collective-permute-start | bytes 1179656 | tf_op jit(solution)/shard_map/ppermute | solution.py:428
  143.5 5.8 %collective-permute-start.24 = (bf16[1,128,512]{2,1,0:T(8,128)(2,1)S(1)}, bf16[1,128,512]{2,1,0:T(8,128)(2,1)S(1)}, u32[]{:S(2)}, u32[]{:S(2)}) collective-permute-start(bf16[1,128,512]{2,1,0:T(8,128)(2,1)S(1)} %add_convert_fusion.13), channel_id=1, source_target_pairs={{0,4},{1,5},{2,6},{3,7},{4,0},{5,1},{6,2},{7,3},{8,12},{9,13},{10,... | collective-permute-start | bytes 393224 | tf_op jit(solution)/shard_map/ppermute | solution.py:428
  145.2 6.3 %collective-permute-start.29 = (bf16[3,64,512]{2,1,0:T(8,128)(2,1)S(1)}, bf16[3,64,512]{2,1,0:T(8,128)(2,1)S(1)}, u32[]{:S(2)}, u32[]{:S(2)}) collective-permute-start(bf16[3,64,512]{2,1,0:T(8,128)(2,1)S(1)} %add_convert_fusion.8), channel_id=1, source_target_pairs={{0,4},{1,5},{2,6},{3,7},{4,0},{5,1},{6,2},{7,3},{8,12},{9,13},{10,... | collective-permute-start | bytes 589832 | tf_op jit(solution)/shard_map/ppermute | solution.py:428
  149.8 18.4 %collective-permute-start.25 = (bf16[6,128,512]{2,1,0:T(8,128)(2,1)S(1)}, bf16[6,128,512]{2,1,0:T(8,128)(2,1)S(1)}, u32[]{:S(2)}, u32[]{:S(2)}) collective-permute-start(bf16[6,128,512]{2,1,0:T(8,128)(2,1)S(1)} %pad_maximum_fusion.1), channel_id=1, source_target_pairs={{0,16},{1,3},{2,18},{3,1},{4,20},{5,7},{6,22},{7,5},{8,24},{9,11},... | collective-permute-start | bytes 2359304 | tf_op jit(solution)/shard_map/ppermute | solution.py:428
  150.6 12.4 %collective-permute-start.26 = (bf16[1,128,512]{2,1,0:T(8,128)(2,1)S(1)}, bf16[1,128,512]{2,1,0:T(8,128)(2,1)S(1)}, u32[]{:S(2)}, u32[]{:S(2)}) collective-permute-start(bf16[1,128,512]{2,1,0:T(8,128)(2,1)S(1)} %add_convert_fusion.12), channel_id=1, source_target_pairs={{0,8},{1,9},{2,10},{3,11},{4,12},{5,13},{6,14},{7,15},{8,0},{9,1},... | collective-permute-start | bytes 393224 | tf_op jit(solution)/shard_map/ppermute | solution.py:428
  151.5 15.6 %collective-permute-start.30 = (bf16[3,64,512]{2,1,0:T(8,128)(2,1)S(1)}, bf16[3,64,512]{2,1,0:T(8,128)(2,1)S(1)}, u32[]{:S(2)}, u32[]{:S(2)}) collective-permute-start(bf16[3,64,512]{2,1,0:T(8,128)(2,1)S(1)} %add_convert_fusion.7), channel_id=1, source_target_pairs={{0,8},{1,9},{2,10},{3,11},{4,12},{5,13},{6,14},{7,15},{8,0},{9,1},... | collective-permute-start | bytes 589832 | tf_op jit(solution)/shard_map/ppermute | solution.py:428
  163.1 5.0 %collective-permute-start.27 = (bf16[1,128,512]{2,1,0:T(8,128)(2,1)S(1)}, bf16[1,128,512]{2,1,0:T(8,128)(2,1)S(1)}, u32[]{:S(2)}, u32[]{:S(2)}) collective-permute-start(bf16[1,128,512]{2,1,0:T(8,128)(2,1)S(1)} %multiply_convert_fusion.2), channel_id=1, source_target_pairs={{0,16},{1,3},{2,18},{3,1},{4,20},{5,7},{6,22},{7,5},{8,24},{9,11},... | collective-permute-start | bytes 393224 | tf_op jit(solution)/shard_map/ppermute | solution.py:428
  167.2 5.7 %collective-permute-start.31 = (bf16[3,64,512]{2,1,0:T(8,128)(2,1)S(1)}, bf16[3,64,512]{2,1,0:T(8,128)(2,1)S(1)}, u32[]{:S(2)}, u32[]{:S(2)}) collective-permute-start(bf16[3,64,512]{2,1,0:T(8,128)(2,1)S(1)} %multiply_convert_fusion), channel_id=1, source_target_pairs={{0,2},{1,17},{2,0},{3,19},{4,6},{5,21},{6,4},{7,23},{8,10},{9,25},... | collective-permute-start | bytes 589832 | tf_op jit(solution)/shard_map/ppermute | solution.py:428
  169.5 15.7 %collective-permute-start.28 = (bf16[6,256,512]{2,1,0:T(8,128)(2,1)S(1)}, bf16[6,256,512]{2,1,0:T(8,128)(2,1)}, u32[]{:S(2)}, u32[]{:S(2)}) collective-permute-start(bf16[6,256,512]{2,1,0:T(8,128)(2,1)S(1)} %pad_maximum_fusion.refs_3_), channel_id=1, source_target_pairs={{0,1},{1,0},{2,3},{3,2},{4,5},{5,4},{6,7},{7,6},{8,9},{9,8},{10,11... | collective-permute-start | bytes 4718600 | tf_op jit(solution)/shard_map/ppermute | solution.py:428
  172.9 7.8 %collective-permute-start.32 = (bf16[3,128,512]{2,1,0:T(8,128)(2,1)S(1)}, bf16[3,128,512]{2,1,0:T(8,128)(2,1)S(1)}, u32[]{:S(2)}, u32[]{:S(2)}) collective-permute-start(bf16[3,128,512]{2,1,0:T(8,128)(2,1)S(1)} %pad_maximum_fusion.4), channel_id=1, source_target_pairs={{0,16},{1,3},{2,18},{3,1},{4,20},{5,7},{6,22},{7,5},{8,24},{9,11},... | collective-permute-start | bytes 1179656 | tf_op jit(solution)/shard_map/ppermute | solution.py:428
  180.8 4.4 %copy-start.2 = (bf16[3,256,512]{2,1,0:T(8,128)(2,1)}, bf16[3,256,512]{2,1,0:T(8,128)(2,1)S(1)}, u32[]{:S(2)}) copy-start(bf16[3,256,512]{2,1,0:T(8,128)(2,1)S(1)} %pad_maximum_fusion.2.refs_5_) | copy-start | bytes 2359300
  180.9 2.7 %collective-permute-start.33 = (bf16[3,256,512]{2,1,0:T(8,128)(2,1)S(1)}, bf16[3,256,512]{2,1,0:T(8,128)(2,1)S(1)}, u32[]{:S(2)}, u32[]{:S(2)}) collective-permute-start(bf16[3,256,512]{2,1,0:T(8,128)(2,1)S(1)} %pad_maximum_fusion.2.refs_5_), channel_id=1, source_target_pairs={{0,1},{1,0},{2,3},{3,2},{4,5},{5,4},{6,7},{7,6},{8,9},{9,8},{10,11... | collective-permute-start | bytes 2359304 | tf_op jit(solution)/shard_map/ppermute | solution.py:428
  181.0 2.6 %collective-permute-start.34 = (bf16[1,256,512]{2,1,0:T(8,128)(2,1)S(1)}, bf16[1,256,512]{2,1,0:T(8,128)(2,1)S(1)}, u32[]{:S(2)}, u32[]{:S(2)}) collective-permute-start(bf16[1,256,512]{2,1,0:T(8,128)(2,1)S(1)} %pad_maximum_fusion.5.refs_7_), channel_id=1, source_target_pairs={{0,1},{1,0},{2,3},{3,2},{4,5},{5,4},{6,7},{7,6},{8,9},{9,8},{10,11... | collective-permute-start | bytes 786440 | tf_op jit(solution)/shard_map/ppermute | solution.py:428
  (8 other events, 10.3 us)

commit v6 on v5

--- a/solution.py
+++ b/solution.py
@@ -11,12 +11,12 @@
 BLK = 64
 IMGW = 64
 GROUP = 4
-BATCH = 4
+BATCH = 8
 EARLY_LEVELS = 4
 LATE_LEVELS = 3
 BACK_LEVELS = 2
 EARLY_WAITS = (0, 0, 0, 0, 0, 2, 3, 4, 6)
-LATE_WAITS = (0, 0, 0, 0, 1, 3, 4, 5)
+LATE_WAITS = (0, 0, 0, 0, 1, 3, 4, 6)
 VMEM_BYTES = 63 * 1024 * 1024
 F32 = jnp.float32
 BF16 = jnp.bfloat16

time: 191 us -> 191 us (level)
  no operation moved by 1% of the time
where the time goes in v6:
time: 191 us; the launch traced here: 190 us
  waiting for transfers between devices  68 us (36%)
  Pallas kernels  60.6 us (32%)
  starting transfers between devices  36.1 us (19%)
  other arithmetic  17.6 us (9%)
  local copies, waits for them, and re-layouts  6.77 us (4%)
    ppermute x30, waiting for transfers between devices, exchange(): return lax.ppermute(value, ('dp', 'tile'), pairs)  68 us
    ppermute x30, starting transfers between devices, exchange(): return lax.ppermute(value, ('dp', 'tile'), pairs)  26.3 us
    pallas_call x2, Pallas kernels, bev_rows(): pl.pallas_call(kernel, grid=(3,), in_specs=[whole(rows, cols, chans)] + [...  20.4 us
    pallas_call x1, Pallas kernels, wgrad(): pl.pallas_call(functools.partial(wgrad_kernel, taps, groups), grid=(len(t...  20.2 us
    pallas_call x1, Pallas kernels, warp_pieces(): pl.pallas_call(functools.partial(pieces_kernel, (own, per, bits, edge, le...  8.29 us
    convert_element_type x6, other arithmetic, step(): send = region_sum(self.terms, 1, self.extent // 2, self.extent).astype(BF16)  6.59 us
    convert_element_type x4, other arithmetic, warp_step(): send = region_sum(terms, 0, extent // 2, extent).astype(BF16)  5.82 us
    pallas_call x1, Pallas kernels, place_parts(): pl.pallas_call(functools.partial(place_kernel, spans), grid=(sum(spans),)...  5.18 us
  transfers between devices with their start and end apart: 35, of which 20 were waited for; matrix products, arithmetic and copies ran while one was open for 9% of the time, Pallas kernels for 25%

profile of v6, /device:TPU:0, one launch (start us, length us, event | category | flops | bytes accessed | tf_op | source)
XLA Modules:
  0.0 190.1 jit_solution(5517204122794099681)
XLA Ops:
  0.7 2.2 %slice_bitcast_fusion = (bf16[640,512]{1,0:T(8,128)(2,1)}, bf16[640,512]{1,0:T(8,128)(2,1)S(1)}) fusion(bf16[1,4,640,512]{3,2,1,0:T(8,128)(2,1)} %param.9), kind=kLoop, calls=%fused_computation.8 | loop fusion | bytes 2621440 | tf_op jit(solution)/shard_map/squeeze | solution.py:600
  2.9 1.3 collective-permute-start.2
  4.2 3.9 %collective-permute-start.1 = (bf16[640,512]{1,0:T(8,128)(2,1)S(1)}, bf16[640,512]{1,0:T(8,128)(2,1)}, u32[]{:S(2)}, u32[]{:S(2)}) collective-permute-start(bf16[640,512]{1,0:T(8,128)(2,1)S(1)} %get-tuple-element.70), channel_id=1, source_target_pairs={{0,1},{1,2},{2,3},{3,4},{4,5},{5,6},{6,7},{7,8},{8,9},{9,10},{10,1... | collective-permute-start | bytes 1966088 | tf_op jit(solution)/shard_map/ppermute | solution.py:599
  8.2 1.8 collective-permute-start
  10.0 10.0 %bev_rows.2.refs_3_ = bf16[2,640,512]{2,1,0:T(8,128)(2,1)} custom-call(bf16[4,640,512]{2,1,0:T(8,128)(2,1)} %bitcast.23, bf16[3,3,512,512]{3,2,1,0:T(8,128)(2,1)} %bitcast.26), custom_call_target="tpu_custom_call" | custom-call | flops 6039797760 | bytes 9961472 | tf_op jit(solution)/shard_map/bev_rows/pallas_call | solution.py:92
  20.7 10.4 %bev_rows.3.refs_0_ = bf16[2,640,512]{2,1,0:T(8,128)(2,1)} custom-call(bf16[4,640,512]{2,1,0:T(8,128)(2,1)} %bitcast.24, bf16[640,512]{1,0:T(8,128)(2,1)} %collective-permute-done.1.refs_0_.refs_4_, bf16[640,512]{1,0:T(8,128)(2,1)} %collective-permute-done.2.refs_1_.refs_5_, bf16[3,3,512,512]{3,2,1,0:T(8,128)(2,1)} %bitcast.27, ...), custom_call_target="tpu_custom_call" | custom-call | flops 6039797760 | bytes 9961472 | tf_op jit(solution)/shard_map/bev_rows/pallas_call | solution.py:92
  31.1 2.8 %collective-permute-start.4 = (bf16[2,640,512]{2,1,0:T(8,128)(2,1)}, bf16[2,640,512]{2,1,0:T(8,128)(2,1)}, u32[]{:S(2)}, u32[]{:S(2)}) collective-permute-start(bf16[2,640,512]{2,1,0:T(8,128)(2,1)} %bev_rows.3.refs_0_), channel_id=1, source_target_pairs={{0,1},{1,0},{2,3},{3,2},{4,5},{5,4},{6,7},{7,6},{8,9},{9,8},{10,11... | collective-permute-start | bytes 3932168 | tf_op jit(solution)/shard_map/ppermute | solution.py:612
  35.1 2.8 %image_slope.1.refs_4_.refs_8_ = f32[512,512]{1,0:T(8,128)} custom-call(bf16[512,512]{1,0:T(8,128)(2,1)} %bitcast.20, bf16[512,512]{1,0:T(8,128)(2,1)} %refs_10_.1, bf16[2,640,512]{2,1,0:T(8,128)(2,1)} %bev_rows.3.refs_0_), custom_call_target="tpu_custom_call" | custom-call | flops 268435456 | bytes 2621440 | tf_op jit(solution)/shard_map/image_slope/pallas_call | solution.py:373
  37.9 8.3 %warp_pieces.1 = (bf16[4,2,128,512]{3,2,1,0:T(8,128)(2,1)}, bf16[4,2,128,512]{3,2,1,0:T(8,128)(2,1)}, bf16[4,2,128,512]{3,2,1,0:T(8,128)(2,1)}, bf16[4,2,128,512]{3,2,1,0:T(8,128)(2,1)}) custom-call(s32[1]{0:T(128)} %bitcast.info_ref, s32[1,640]{1,0:T(1,128)} %route_ref.1, s32[3,40,64]{2,1,0:T(8,128)} %copy-done.15, s32[3,40,64]{2,1,0:T(8,128)} %copy-done.16, ...), custom_call_target="tpu_custom_call" | custom-call | flops 1073741824 | bytes 9437184 | tf_op jit(solution)/shard_map/warp_pieces/pallas_call | solution.py:343
  46.2 2.1 %collective-permute-start.5 = (bf16[4,2,128,512]{3,2,1,0:T(8,128)(2,1)}, bf16[4,2,128,512]{3,2,1,0:T(8,128)(2,1)}, u32[]{:S(2)}, u32[]{:S(2)}) collective-permute-start(bf16[4,2,128,512]{3,2,1,0:T(8,128)(2,1)} %get-tuple-element.37), channel_id=1, source_target_pairs={{0,2},{1,5},{2,0},{3,7},{4,6},{5,1},{6,4},{7,3},{8,10},{9,13},{10,... | collective-permute-start | bytes 3145736 | tf_op jit(solution)/shard_map/ppermute | solution.py:428
  48.4 20.2 %wgrad.1 = (bf16[6,256,512]{2,1,0:T(8,128)(2,1)}, bf16[6,256,512]{2,1,0:T(8,128)(2,1)}, bf16[3,256,512]{2,1,0:T(8,128)(2,1)}, bf16[3,256,512]{2,1,0:T(8,128)(2,1)}) custom-call(s32[16]{0:T(128)} %pad_add_fusion.2.refs_0_, s32[8]{0:T(128)} %pad_add_fusion.3.refs_1_, bf16[4,640,512]{2,1,0:T(8,128)(2,1)} %bitcast.29, bf16[2560,512]{1,0:T(8,128)(2,1)} %bitcast.25, ...), custom_call_target="tpu_custom_call" | custom-call | flops 12079595520 | bytes 9961472 | tf_op jit(solution)/shard_map/wgrad/pallas_call | solution.py:177
  68.5 4.1 %collective-permute-done.6.refs_5_ = bf16[4,2,128,512]{3,2,1,0:T(8,128)(2,1)} collective-permute-done((bf16[4,2,128,512]{3,2,1,0:T(8,128)(2,1)}, bf16[4,2,128,512]{3,2,1,0:T(8,128)(2,1)}, u32[]{:S(2)}, u32[]{:S(2)}) %collective-permute-start.6) | collective-permute-done | bytes 1048608 | tf_op jit(solution)/shard_map/ppermute | solution.py:428
  72.6 1.4 add_convert_fusion.2
  74.0 1.7 collective-permute-start.7
  75.7 1.2 add_convert_fusion.1
  77.7 5.6 %collective-permute-done.7.refs_2_ = bf16[2,2,128,512]{3,2,1,0:T(8,128)(2,1)S(1)} collective-permute-done((bf16[2,2,128,512]{3,2,1,0:T(8,128)(2,1)S(1)}, bf16[2,2,128,512]{3,2,1,0:T(8,128)(2,1)S(1)}, u32[]{:S(2)}, u32[]{:S(2)}) %collective-permute-start.7) | collective-permute-done | bytes 524320 | tf_op jit(solution)/shard_map/ppermute | solution.py:428
  83.3 1.3 add_convert_fusion.6
  84.9 2.0 %collective-permute-start.12 = (bf16[6,128,512]{2,1,0:T(8,128)(2,1)S(1)}, bf16[6,128,512]{2,1,0:T(8,128)(2,1)S(1)}, u32[]{:S(2)}, u32[]{:S(2)}) collective-permute-start(bf16[6,128,512]{2,1,0:T(8,128)(2,1)S(1)} %add_convert_fusion), channel_id=1, source_target_pairs={{0,16},{1,3},{2,18},{3,1},{4,20},{5,7},{6,22},{7,5},{8,24},{9,11},... | collective-permute-start | bytes 2359304 | tf_op jit(solution)/shard_map/ppermute | solution.py:428
  86.9 2.6 %collective-permute-start.8 = (bf16[1,2,128,512]{3,2,1,0:T(8,128)(2,1)S(1)}, bf16[1,2,128,512]{3,2,1,0:T(8,128)(2,1)S(1)}, u32[]{:S(2)}, u32[]{:S(2)}) collective-permute-start(bf16[1,2,128,512]{3,2,1,0:T(8,128)(2,1)S(1)} %add_convert_fusion.6), channel_id=1, source_target_pairs={{0,8},{1,9},{2,10},{3,11},{4,12},{5,13},{6,14},{7,15},{8,0},{9,1},... | collective-permute-start | bytes 786440 | tf_op jit(solution)/shard_map/ppermute | solution.py:428
  89.5 1.9 %add_convert_fusion.5 = bf16[1,2,128,512]{3,2,1,0:T(8,128)(2,1)} fusion(bf16[2,2,128,512]{3,2,1,0:T(8,128)(2,1)S(1)} %collective-permute-done.9.refs_6_, bf16[4,2,128,512]{3,2,1,0:T(8,128)(2,1)} %collective-permute-done.6.refs_5_, bf16[4,2,128,512]{3,2,1,0:T(8,128)(2,1)S(1)} %copy-done.1), kind=kLoop, calls=%fused_computation.10 | loop fusion | flops 786432 | bytes 1048576 | tf_op jit(solution)/shard_map/convert_element_type | solution.py:634
  92.4 1.4 collective-permute-start.16
  93.7 7.6 %collective-permute-done.8.refs_3_ = bf16[1,2,128,512]{3,2,1,0:T(8,128)(2,1)S(1)} collective-permute-done((bf16[1,2,128,512]{3,2,1,0:T(8,128)(2,1)S(1)}, bf16[1,2,128,512]{3,2,1,0:T(8,128)(2,1)S(1)}, u32[]{:S(2)}, u32[]{:S(2)}) %collective-permute-start.8) | collective-permute-done | bytes 262176 | tf_op jit(solution)/shard_map/ppermute | solution.py:428
  101.4 1.0 copy-done.9
  103.9 1.9 add_convert_fusion.10
  105.8 1.5 collective-permute-start.17
  107.3 4.1 %collective-permute-done.13 = bf16[6,64,512]{2,1,0:T(8,128)(2,1)S(1)} collective-permute-done((bf16[6,64,512]{2,1,0:T(8,128)(2,1)}, bf16[6,64,512]{2,1,0:T(8,128)(2,1)S(1)}, u32[]{:S(2)}, u32[]{:S(2)}) %collective-permute-start.13) | collective-permute-done | bytes 393248 | tf_op jit(solution)/shard_map/ppermute | solution.py:428
  111.4 1.7 add_convert_fusion.11
  113.7 2.9 %collective-permute-done.10.refs_7_ = bf16[1,2,128,512]{3,2,1,0:T(8,128)(2,1)} collective-permute-done((bf16[1,2,128,512]{3,2,1,0:T(8,128)(2,1)}, bf16[1,2,128,512]{3,2,1,0:T(8,128)(2,1)}, u32[]{:S(2)}, u32[]{:S(2)}) %collective-permute-start.10) | collective-permute-done | bytes 262176 | tf_op jit(solution)/shard_map/ppermute | solution.py:428
  116.6 3.8 %image_layer.1 = (bf16[512,512]{1,0:T(8,128)(2,1)}, bf16[1,256,512]{2,1,0:T(8,128)(2,1)}, bf16[1,256,512]{2,1,0:T(8,128)(2,1)}) custom-call(s32[4]{0:T(128)} %pad_add_fusion.1.order_ref.refs_2_, bf16[4,2,128,512]{3,2,1,0:T(8,128)(2,1)} %get-tuple-element.36.refs_6_.refs_0_, bf16[4,2,128,512]{3,2,1,0:T(8,128)(2,1)} %collective-permute-done.5.refs_1_, ...), custom_call_target="tpu_custom_call" | custom-call | flops 536870912 | bytes 4194304 | tf_op jit(solution)/shard_map/image_layer/pallas_call | solution.py:407
  120.6 1.2 add_convert_fusion.9
  124.0 4.2 %collective-permute-done.20 = bf16[1,128,512]{2,1,0:T(8,128)(2,1)S(1)} collective-permute-done((bf16[1,128,512]{2,1,0:T(8,128)(2,1)S(1)}, bf16[1,128,512]{2,1,0:T(8,128)(2,1)S(1)}, u32[]{:S(2)}, u32[]{:S(2)}) %collective-permute-start.20) | collective-permute-done | bytes 131104 | tf_op jit(solution)/shard_map/ppermute | solution.py:428
  128.2 5.9 %collective-permute-done.18 = bf16[6,32,512]{2,1,0:T(8,128)(2,1)S(1)} collective-permute-done((bf16[6,32,512]{2,1,0:T(8,128)(2,1)S(1)}, bf16[6,32,512]{2,1,0:T(8,128)(2,1)S(1)}, u32[]{:S(2)}, u32[]{:S(2)}) %collective-permute-start.18) | collective-permute-done | bytes 196640 | tf_op jit(solution)/shard_map/ppermute | solution.py:428
  134.2 2.1 %collective-permute-start.22 = (bf16[1,128,512]{2,1,0:T(8,128)(2,1)S(1)}, bf16[1,128,512]{2,1,0:T(8,128)(2,1)S(1)}, u32[]{:S(2)}, u32[]{:S(2)}) collective-permute-start(bf16[1,128,512]{2,1,0:T(8,128)(2,1)S(1)} %add_convert_fusion.14), channel_id=1, source_target_pairs={{0,2},{1,17},{2,0},{3,19},{4,6},{5,21},{6,4},{7,23},{8,10},{9,25},... | collective-permute-start | bytes 393224 | tf_op jit(solution)/shard_map/ppermute | solution.py:428
  136.3 2.9 %collective-permute-done.22 = bf16[1,128,512]{2,1,0:T(8,128)(2,1)S(1)} collective-permute-done((bf16[1,128,512]{2,1,0:T(8,128)(2,1)S(1)}, bf16[1,128,512]{2,1,0:T(8,128)(2,1)S(1)}, u32[]{:S(2)}, u32[]{:S(2)}) %collective-permute-start.22) | collective-permute-done | bytes 131104 | tf_op jit(solution)/shard_map/ppermute | solution.py:428
  139.3 1.7 collective-permute-done.21
  141.0 2.1 %collective-permute-start.23 = (bf16[6,64,512]{2,1,0:T(8,128)(2,1)S(1)}, bf16[6,64,512]{2,1,0:T(8,128)(2,1)S(1)}, u32[]{:S(2)}, u32[]{:S(2)}) collective-permute-start(bf16[6,64,512]{2,1,0:T(8,128)(2,1)S(1)} %pad_maximum_fusion.3), channel_id=1, source_target_pairs={{0,2},{1,17},{2,0},{3,19},{4,6},{5,21},{6,4},{7,23},{8,10},{9,25},... | collective-permute-start | bytes 1179656 | tf_op jit(solution)/shard_map/ppermute | solution.py:428
  143.5 1.3 add_convert_fusion.8
  144.8 1.8 collective-permute-start.29
  146.7 1.7 collective-permute-done.24
  149.0 1.2 collective-permute-start.25
  150.6 2.6 %collective-permute-start.30 = (bf16[3,64,512]{2,1,0:T(8,128)(2,1)S(1)}, bf16[3,64,512]{2,1,0:T(8,128)(2,1)S(1)}, u32[]{:S(2)}, u32[]{:S(2)}) collective-permute-start(bf16[3,64,512]{2,1,0:T(8,128)(2,1)S(1)} %add_convert_fusion.7), channel_id=1, source_target_pairs={{0,8},{1,9},{2,10},{3,11},{4,12},{5,13},{6,14},{7,15},{8,0},{9,1},... | collective-permute-start | bytes 589832 | tf_op jit(solution)/shard_map/ppermute | solution.py:428
  153.3 9.4 %collective-permute-done.26 = bf16[1,128,512]{2,1,0:T(8,128)(2,1)S(1)} collective-permute-done((bf16[1,128,512]{2,1,0:T(8,128)(2,1)S(1)}, bf16[1,128,512]{2,1,0:T(8,128)(2,1)S(1)}, u32[]{:S(2)}, u32[]{:S(2)}) %collective-permute-start.26) | collective-permute-done | bytes 131104 | tf_op jit(solution)/shard_map/ppermute | solution.py:428
  163.4 3.4 %collective-permute-done.30 = bf16[3,64,512]{2,1,0:T(8,128)(2,1)S(1)} collective-permute-done((bf16[3,64,512]{2,1,0:T(8,128)(2,1)S(1)}, bf16[3,64,512]{2,1,0:T(8,128)(2,1)S(1)}, u32[]{:S(2)}, u32[]{:S(2)}) %collective-permute-start.30) | collective-permute-done | bytes 196640 | tf_op jit(solution)/shard_map/ppermute | solution.py:428
  168.0 1.2 copy-done
  169.2 3.4 %collective-permute-done.31 = bf16[3,64,512]{2,1,0:T(8,128)(2,1)S(1)} collective-permute-done((bf16[3,64,512]{2,1,0:T(8,128)(2,1)S(1)}, bf16[3,64,512]{2,1,0:T(8,128)(2,1)S(1)}, u32[]{:S(2)}, u32[]{:S(2)}) %collective-permute-start.31) | collective-permute-done | bytes 196640 | tf_op jit(solution)/shard_map/ppermute | solution.py:428
  173.2 7.2 %collective-permute-done.32 = bf16[3,128,512]{2,1,0:T(8,128)(2,1)S(1)} collective-permute-done((bf16[3,128,512]{2,1,0:T(8,128)(2,1)S(1)}, bf16[3,128,512]{2,1,0:T(8,128)(2,1)S(1)}, u32[]{:S(2)}, u32[]{:S(2)}) %collective-permute-start.32) | collective-permute-done | bytes 393248 | tf_op jit(solution)/shard_map/ppermute | solution.py:428
  181.2 2.1 %collective-permute-done.34.refs_8_ = bf16[1,256,512]{2,1,0:T(8,128)(2,1)S(1)} collective-permute-done((bf16[1,256,512]{2,1,0:T(8,128)(2,1)S(1)}, bf16[1,256,512]{2,1,0:T(8,128)(2,1)S(1)}, u32[]{:S(2)}, u32[]{:S(2)}) %collective-permute-start.34) | collective-permute-done | bytes 262176 | tf_op jit(solution)/shard_map/ppermute | solution.py:428
  184.9 5.2 %place_parts.1 = (bf16[9,512,512]{2,1,0:T(8,128)(2,1)}, bf16[1,512,512]{2,1,0:T(8,128)(2,1)}) custom-call(s32[16]{0:T(128)} %pad_add_fusion.2.refs_0_, s32[8]{0:T(128)} %pad_add_fusion.3.refs_1_, s32[4]{0:T(128)} %pad_add_fusion.1.order_ref.refs_2_, bf16[6,256,512]{2,1,0:T(8,128)(2,1)} %copy-done, bf16[6,256,512]{2,1,0:T(8,128)(2,1)} %collective-permute-done.28.refs_4_, ...), custom_call_target="tpu_custom_call" | custom-call | bytes 10485760 | tf_op jit(solution)/shard_map/place_parts/pallas_call | solution.py:553
  (105 shorter events, 15.1 us)
Async XLA Ops:
  0.6 7.4 %copy-start.17 = (s32[1,2560]{1,0:T(1,128)S(1)}, s32[1,2560]{1,0:T(1,128)}, u32[]{:S(2)}) copy-start(s32[1,2560]{1,0:T(1,128)} %param.17) | copy-start | bytes 30724
  0.6 7.4 %copy-start.18 = (s32[1,2560]{1,0:T(1,128)S(1)}, s32[1,2560]{1,0:T(1,128)}, u32[]{:S(2)}) copy-start(s32[1,2560]{1,0:T(1,128)} %param.16) | copy-start | bytes 30724
  0.7 7.4 %copy-start.19 = (s32[1,2560]{1,0:T(1,128)S(1)}, s32[1,2560]{1,0:T(1,128)}, u32[]{:S(2)}) copy-start(s32[1,2560]{1,0:T(1,128)} %param.15) | copy-start | bytes 30724
  2.9 17.2 %collective-permute-start.2 = (bf16[640,512]{1,0:T(8,128)(2,1)}, bf16[640,512]{1,0:T(8,128)(2,1)}, u32[]{:S(2)}, u32[]{:S(2)}) collective-permute-start(bf16[640,512]{1,0:T(8,128)(2,1)} %get-tuple-element.69), channel_id=1, source_target_pairs={{1,0},{2,1},{3,2},{4,3},{5,4},{6,5},{7,6},{8,7},{9,8},{10,9},{11,1... | collective-permute-start | bytes 1966088 | tf_op jit(solution)/shard_map/ppermute | solution.py:600
  4.2 15.9 %collective-permute-start.1 = (bf16[640,512]{1,0:T(8,128)(2,1)S(1)}, bf16[640,512]{1,0:T(8,128)(2,1)}, u32[]{:S(2)}, u32[]{:S(2)}) collective-permute-start(bf16[640,512]{1,0:T(8,128)(2,1)S(1)} %get-tuple-element.70), channel_id=1, source_target_pairs={{0,1},{1,2},{2,3},{3,4},{4,5},{5,6},{6,7},{7,8},{8,9},{9,10},{10,1... | collective-permute-start | bytes 1966088 | tf_op jit(solution)/shard_map/ppermute | solution.py:599
  8.2 11.9 %copy-start.15 = (s32[3,40,64]{2,1,0:T(8,128)}, s32[3,40,64]{2,1,0:T(8,128)S(1)}, u32[]{:S(2)}) copy-start(s32[3,40,64]{2,1,0:T(8,128)S(1)} %reshape.32.mine_ref) | copy-start | bytes 92164
  8.2 11.9 %collective-permute-start = (s32[3,40,64]{2,1,0:T(8,128)S(1)}, s32[3,40,64]{2,1,0:T(8,128)S(1)}, u32[]{:S(2)}, u32[]{:S(2)}) collective-permute-start(s32[3,40,64]{2,1,0:T(8,128)S(1)} %reshape.32.mine_ref), channel_id=1, source_target_pairs={{0,1},{1,0},{2,3},{3,2},{4,5},{5,4},{6,7},{7,6},{8,9},{9,8},{10,11... | collective-permute-start | bytes 92168 | tf_op jit(solution)/shard_map/ppermute | solution.py:604
  20.0 17.9 %collective-permute-start.3 = (bf16[2,640,512]{2,1,0:T(8,128)(2,1)}, bf16[2,640,512]{2,1,0:T(8,128)(2,1)}, u32[]{:S(2)}, u32[]{:S(2)}) collective-permute-start(bf16[2,640,512]{2,1,0:T(8,128)(2,1)} %bev_rows.2.refs_3_), channel_id=1, source_target_pairs={{0,1},{1,0},{2,3},{3,2},{4,5},{5,4},{6,7},{7,6},{8,9},{9,8},{10,11... | collective-permute-start | bytes 3932168 | tf_op jit(solution)/shard_map/ppermute | solution.py:608
  31.1 6.8 %collective-permute-start.4 = (bf16[2,640,512]{2,1,0:T(8,128)(2,1)}, bf16[2,640,512]{2,1,0:T(8,128)(2,1)}, u32[]{:S(2)}, u32[]{:S(2)}) collective-permute-start(bf16[2,640,512]{2,1,0:T(8,128)(2,1)} %bev_rows.3.refs_0_), channel_id=1, source_target_pairs={{0,1},{1,0},{2,3},{3,2},{4,5},{5,4},{6,7},{7,6},{8,9},{9,8},{10,11... | collective-permute-start | bytes 3932168 | tf_op jit(solution)/shard_map/ppermute | solution.py:612
  46.2 22.3 %collective-permute-start.5 = (bf16[4,2,128,512]{3,2,1,0:T(8,128)(2,1)}, bf16[4,2,128,512]{3,2,1,0:T(8,128)(2,1)}, u32[]{:S(2)}, u32[]{:S(2)}) collective-permute-start(bf16[4,2,128,512]{3,2,1,0:T(8,128)(2,1)} %get-tuple-element.37), channel_id=1, source_target_pairs={{0,2},{1,5},{2,0},{3,7},{4,6},{5,1},{6,4},{7,3},{8,10},{9,13},{10,... | collective-permute-start | bytes 3145736 | tf_op jit(solution)/shard_map/ppermute | solution.py:428
  48.3 24.3 %collective-permute-start.6 = (bf16[4,2,128,512]{3,2,1,0:T(8,128)(2,1)}, bf16[4,2,128,512]{3,2,1,0:T(8,128)(2,1)}, u32[]{:S(2)}, u32[]{:S(2)}) collective-permute-start(bf16[4,2,128,512]{3,2,1,0:T(8,128)(2,1)} %get-tuple-element.38), channel_id=1, source_target_pairs={{0,2},{1,5},{2,0},{3,7},{4,6},{5,1},{6,4},{7,3},{8,10},{9,13},{10,... | collective-permute-start | bytes 3145736 | tf_op jit(solution)/shard_map/ppermute | solution.py:428
  68.5 7.2 %copy-start.1 = (bf16[4,2,128,512]{3,2,1,0:T(8,128)(2,1)S(1)}, bf16[4,2,128,512]{3,2,1,0:T(8,128)(2,1)}, u32[]{:S(2)}) copy-start(bf16[4,2,128,512]{3,2,1,0:T(8,128)(2,1)} %get-tuple-element.42.refs_4_) | copy-start | bytes 3145732
  72.6 4.8 %copy-start.20 = (bf16[3,256,512]{2,1,0:T(8,128)(2,1)S(1)}, bf16[3,256,512]{2,1,0:T(8,128)(2,1)}, u32[]{:S(2)}) copy-start(bf16[3,256,512]{2,1,0:T(8,128)(2,1)} %get-tuple-element.52) | copy-start | bytes 2359300
  72.6 12.0 %collective-permute-start.11 = (bf16[6,256,512]{2,1,0:T(8,128)(2,1)}, bf16[6,256,512]{2,1,0:T(8,128)(2,1)S(1)}, u32[]{:S(2)}, u32[]{:S(2)}) collective-permute-start(bf16[6,256,512]{2,1,0:T(8,128)(2,1)} %get-tuple-element.46), channel_id=1, source_target_pairs={{0,1},{1,0},{2,3},{3,2},{4,5},{5,4},{6,7},{7,6},{8,9},{9,8},{10,11... | collective-permute-start | bytes 4718600 | tf_op jit(solution)/shard_map/ppermute | solution.py:428
  74.0 10.6 %copy-start.3 = (bf16[6,256,512]{2,1,0:T(8,128)(2,1)S(1)}, bf16[6,256,512]{2,1,0:T(8,128)(2,1)}, u32[]{:S(2)}) copy-start(bf16[6,256,512]{2,1,0:T(8,128)(2,1)} %get-tuple-element.45) | copy-start | bytes 4718596
  74.0 9.2 %collective-permute-start.7 = (bf16[2,2,128,512]{3,2,1,0:T(8,128)(2,1)S(1)}, bf16[2,2,128,512]{3,2,1,0:T(8,128)(2,1)S(1)}, u32[]{:S(2)}, u32[]{:S(2)}) collective-permute-start(bf16[2,2,128,512]{3,2,1,0:T(8,128)(2,1)S(1)} %add_convert_fusion.2), channel_id=1, source_target_pairs={{0,4},{1,3},{2,6},{3,1},{4,0},{5,7},{6,2},{7,5},{8,12},{9,11},{10,... | collective-permute-start | bytes 1572872 | tf_op jit(solution)/shard_map/ppermute | solution.py:428
  76.9 12.6 %collective-permute-start.9 = (bf16[2,2,128,512]{3,2,1,0:T(8,128)(2,1)S(1)}, bf16[2,2,128,512]{3,2,1,0:T(8,128)(2,1)S(1)}, u32[]{:S(2)}, u32[]{:S(2)}) collective-permute-start(bf16[2,2,128,512]{3,2,1,0:T(8,128)(2,1)S(1)} %add_convert_fusion.1), channel_id=1, source_target_pairs={{0,4},{1,3},{2,6},{3,1},{4,0},{5,7},{6,2},{7,5},{8,12},{9,11},{10,... | collective-permute-start | bytes 1572872 | tf_op jit(solution)/shard_map/ppermute | solution.py:428
  77.4 14.0 %collective-permute-start.15 = (bf16[3,256,512]{2,1,0:T(8,128)(2,1)S(1)}, bf16[3,256,512]{2,1,0:T(8,128)(2,1)S(1)}, u32[]{:S(2)}, u32[]{:S(2)}) collective-permute-start(bf16[3,256,512]{2,1,0:T(8,128)(2,1)S(1)} %copy-done.20), channel_id=1, source_target_pairs={{0,1},{1,0},{2,3},{3,2},{4,5},{5,4},{6,7},{7,6},{8,9},{9,8},{10,11... | collective-permute-start | bytes 2359304 | tf_op jit(solution)/shard_map/ppermute | solution.py:428
  84.6 26.7 %copy-start.4 = (bf16[6,256,512]{2,1,0:T(8,128)(2,1)}, bf16[6,256,512]{2,1,0:T(8,128)(2,1)S(1)}, u32[]{:S(2)}) copy-start(bf16[6,256,512]{2,1,0:T(8,128)(2,1)S(1)} %collective-permute-done.11) | copy-start | bytes 4718596
  84.7 6.7 %copy-start.10 = (bf16[3,256,512]{2,1,0:T(8,128)(2,1)S(1)}, bf16[3,256,512]{2,1,0:T(8,128)(2,1)}, u32[]{:S(2)}) copy-start(bf16[3,256,512]{2,1,0:T(8,128)(2,1)} %get-tuple-element.50) | copy-start | bytes 2359300
  84.9 16.5 %collective-permute-start.12 = (bf16[6,128,512]{2,1,0:T(8,128)(2,1)S(1)}, bf16[6,128,512]{2,1,0:T(8,128)(2,1)S(1)}, u32[]{:S(2)}, u32[]{:S(2)}) collective-permute-start(bf16[6,128,512]{2,1,0:T(8,128)(2,1)S(1)} %add_convert_fusion), channel_id=1, source_target_pairs={{0,16},{1,3},{2,18},{3,1},{4,20},{5,7},{6,22},{7,5},{8,24},{9,11},... | collective-permute-start | bytes 2359304 | tf_op jit(solution)/shard_map/ppermute | solution.py:428
  86.9 14.5 %collective-permute-start.8 = (bf16[1,2,128,512]{3,2,1,0:T(8,128)(2,1)S(1)}, bf16[1,2,128,512]{3,2,1,0:T(8,128)(2,1)S(1)}, u32[]{:S(2)}, u32[]{:S(2)}) collective-permute-start(bf16[1,2,128,512]{3,2,1,0:T(8,128)(2,1)S(1)} %add_convert_fusion.6), channel_id=1, source_target_pairs={{0,8},{1,9},{2,10},{3,11},{4,12},{5,13},{6,14},{7,15},{8,0},{9,1},... | collective-permute-start | bytes 786440 | tf_op jit(solution)/shard_map/ppermute | solution.py:428
  89.5 13.8 %copy-start.6 = (bf16[2,2,128,512]{3,2,1,0:T(8,128)(2,1)}, bf16[2,2,128,512]{3,2,1,0:T(8,128)(2,1)S(1)}, u32[]{:S(2)}) copy-start(bf16[2,2,128,512]{3,2,1,0:T(8,128)(2,1)S(1)} %collective-permute-done.9.refs_6_) | copy-start | bytes 1572868
  91.4 11.9 %copy-start.11 = (bf16[3,256,512]{2,1,0:T(8,128)(2,1)}, bf16[3,256,512]{2,1,0:T(8,128)(2,1)S(1)}, u32[]{:S(2)}) copy-start(bf16[3,256,512]{2,1,0:T(8,128)(2,1)S(1)} %collective-permute-done.15) | copy-start | bytes 2359300
  92.4 11.6 %collective-permute-start.16 = (bf16[3,128,512]{2,1,0:T(8,128)(2,1)}, bf16[3,128,512]{2,1,0:T(8,128)(2,1)}, u32[]{:S(2)}, u32[]{:S(2)}) collective-permute-start(bf16[3,128,512]{2,1,0:T(8,128)(2,1)} %add_convert_fusion.3), channel_id=1, source_target_pairs={{0,16},{1,3},{2,18},{3,1},{4,20},{5,7},{6,22},{7,5},{8,24},{9,11},... | collective-permute-start | bytes 1179656 | tf_op jit(solution)/shard_map/ppermute | solution.py:428
  103.3 8.0 %collective-permute-start.13 = (bf16[6,64,512]{2,1,0:T(8,128)(2,1)}, bf16[6,64,512]{2,1,0:T(8,128)(2,1)S(1)}, u32[]{:S(2)}, u32[]{:S(2)}) collective-permute-start(bf16[6,64,512]{2,1,0:T(8,128)(2,1)} %add_convert_fusion.4), channel_id=1, source_target_pairs={{0,2},{1,17},{2,0},{3,19},{4,6},{5,21},{6,4},{7,23},{8,10},{9,25},... | collective-permute-start | bytes 1179656 | tf_op jit(solution)/shard_map/ppermute | solution.py:428
  103.7 12.9 %collective-permute-start.10 = (bf16[1,2,128,512]{3,2,1,0:T(8,128)(2,1)}, bf16[1,2,128,512]{3,2,1,0:T(8,128)(2,1)}, u32[]{:S(2)}, u32[]{:S(2)}) collective-permute-start(bf16[1,2,128,512]{3,2,1,0:T(8,128)(2,1)} %add_convert_fusion.5), channel_id=1, source_target_pairs={{0,8},{1,9},{2,10},{3,11},{4,12},{5,13},{6,14},{7,15},{8,0},{9,1},... | collective-permute-start | bytes 786440 | tf_op jit(solution)/shard_map/ppermute | solution.py:428
  105.8 14.7 %collective-permute-start.17 = (bf16[3,64,512]{2,1,0:T(8,128)(2,1)}, bf16[3,64,512]{2,1,0:T(8,128)(2,1)}, u32[]{:S(2)}, u32[]{:S(2)}) collective-permute-start(bf16[3,64,512]{2,1,0:T(8,128)(2,1)} %add_convert_fusion.10), channel_id=1, source_target_pairs={{0,2},{1,17},{2,0},{3,19},{4,6},{5,21},{6,4},{7,23},{8,10},{9,25},... | collective-permute-start | bytes 589832 | tf_op jit(solution)/shard_map/ppermute | solution.py:428
  113.1 7.6 %collective-permute-start.14 = (bf16[6,32,512]{2,1,0:T(8,128)(2,1)}, bf16[6,32,512]{2,1,0:T(8,128)(2,1)S(1)}, u32[]{:S(2)}, u32[]{:S(2)}) collective-permute-start(bf16[6,32,512]{2,1,0:T(8,128)(2,1)} %add_convert_fusion.11), channel_id=1, source_target_pairs={{0,4},{1,5},{2,6},{3,7},{4,0},{5,1},{6,2},{7,3},{8,12},{9,13},{10,... | collective-permute-start | bytes 589832 | tf_op jit(solution)/shard_map/ppermute | solution.py:428
  120.4 13.7 %copy-start.14 = (bf16[1,256,512]{2,1,0:T(8,128)(2,1)S(1)}, bf16[1,256,512]{2,1,0:T(8,128)(2,1)}, u32[]{:S(2)}) copy-start(bf16[1,256,512]{2,1,0:T(8,128)(2,1)} %get-tuple-element.57) | copy-start | bytes 786436
  120.4 1.7 collective-permute-start.19
  121.9 12.1 %collective-permute-start.18 = (bf16[6,32,512]{2,1,0:T(8,128)(2,1)S(1)}, bf16[6,32,512]{2,1,0:T(8,128)(2,1)S(1)}, u32[]{:S(2)}, u32[]{:S(2)}) collective-permute-start(bf16[6,32,512]{2,1,0:T(8,128)(2,1)S(1)} %add_convert_fusion.9), channel_id=1, source_target_pairs={{0,8},{1,9},{2,10},{3,11},{4,12},{5,13},{6,14},{7,15},{8,0},{9,1},... | collective-permute-start | bytes 589832 | tf_op jit(solution)/shard_map/ppermute | solution.py:428
  123.1 5.0 %collective-permute-start.20 = (bf16[1,128,512]{2,1,0:T(8,128)(2,1)S(1)}, bf16[1,128,512]{2,1,0:T(8,128)(2,1)S(1)}, u32[]{:S(2)}, u32[]{:S(2)}) collective-permute-start(bf16[1,128,512]{2,1,0:T(8,128)(2,1)S(1)} %add_convert_fusion.15), channel_id=1, source_target_pairs={{0,16},{1,3},{2,18},{3,1},{4,20},{5,7},{6,22},{7,5},{8,24},{9,11},... | collective-permute-start | bytes 393224 | tf_op jit(solution)/shard_map/ppermute | solution.py:428
  134.1 6.9 %collective-permute-start.21 = (bf16[6,32,512]{2,1,0:T(8,128)(2,1)S(1)}, bf16[6,32,512]{2,1,0:T(8,128)(2,1)S(1)}, u32[]{:S(2)}, u32[]{:S(2)}) collective-permute-start(bf16[6,32,512]{2,1,0:T(8,128)(2,1)S(1)} %multiply_convert_fusion.1), channel_id=1, source_target_pairs={{0,4},{1,5},{2,6},{3,7},{4,0},{5,1},{6,2},{7,3},{8,12},{9,13},{10,... | collective-permute-start | bytes 589832 | tf_op jit(solution)/shard_map/ppermute | solution.py:428
  134.2 5.0 %collective-permute-start.22 = (bf16[1,128,512]{2,1,0:T(8,128)(2,1)S(1)}, bf16[1,128,512]{2,1,0:T(8,128)(2,1)S(1)}, u32[]{:S(2)}, u32[]{:S(2)}) collective-permute-start(bf16[1,128,512]{2,1,0:T(8,128)(2,1)S(1)} %add_convert_fusion.14), channel_id=1, source_target_pairs={{0,2},{1,17},{2,0},{3,19},{4,6},{5,21},{6,4},{7,23},{8,10},{9,25},... | collective-permute-start | bytes 393224 | tf_op jit(solution)/shard_map/ppermute | solution.py:428
  141.0 7.9 %collective-permute-start.23 = (bf16[6,64,512]{2,1,0:T(8,128)(2,1)S(1)}, bf16[6,64,512]{2,1,0:T(8,128)(2,1)S(1)}, u32[]{:S(2)}, u32[]{:S(2)}) collective-permute-start(bf16[6,64,512]{2,1,0:T(8,128)(2,1)S(1)} %pad_maximum_fusion.3), channel_id=1, source_target_pairs={{0,2},{1,17},{2,0},{3,19},{4,6},{5,21},{6,4},{7,23},{8,10},{9,25},... | collective-permute-start | bytes 1179656 | tf_op jit(solution)/shard_map/ppermute | solution.py:428
  143.2 5.1 %collective-permute-start.24 = (bf16[1,128,512]{2,1,0:T(8,128)(2,1)S(1)}, bf16[1,128,512]{2,1,0:T(8,128)(2,1)S(1)}, u32[]{:S(2)}, u32[]{:S(2)}) collective-permute-start(bf16[1,128,512]{2,1,0:T(8,128)(2,1)S(1)} %add_convert_fusion.13), channel_id=1, source_target_pairs={{0,4},{1,5},{2,6},{3,7},{4,0},{5,1},{6,2},{7,3},{8,12},{9,13},{10,... | collective-permute-start | bytes 393224 | tf_op jit(solution)/shard_map/ppermute | solution.py:428
  144.8 5.7 %collective-permute-start.29 = (bf16[3,64,512]{2,1,0:T(8,128)(2,1)S(1)}, bf16[3,64,512]{2,1,0:T(8,128)(2,1)S(1)}, u32[]{:S(2)}, u32[]{:S(2)}) collective-permute-start(bf16[3,64,512]{2,1,0:T(8,128)(2,1)S(1)} %add_convert_fusion.8), channel_id=1, source_target_pairs={{0,4},{1,5},{2,6},{3,7},{4,0},{5,1},{6,2},{7,3},{8,12},{9,13},{10,... | collective-permute-start | bytes 589832 | tf_op jit(solution)/shard_map/ppermute | solution.py:428
  149.0 18.8 %collective-permute-start.25 = (bf16[6,128,512]{2,1,0:T(8,128)(2,1)S(1)}, bf16[6,128,512]{2,1,0:T(8,128)(2,1)S(1)}, u32[]{:S(2)}, u32[]{:S(2)}) collective-permute-start(bf16[6,128,512]{2,1,0:T(8,128)(2,1)S(1)} %pad_maximum_fusion.1), channel_id=1, source_target_pairs={{0,16},{1,3},{2,18},{3,1},{4,20},{5,7},{6,22},{7,5},{8,24},{9,11},... | collective-permute-start | bytes 2359304 | tf_op jit(solution)/shard_map/ppermute | solution.py:428
  150.2 12.5 %collective-permute-start.26 = (bf16[1,128,512]{2,1,0:T(8,128)(2,1)S(1)}, bf16[1,128,512]{2,1,0:T(8,128)(2,1)S(1)}, u32[]{:S(2)}, u32[]{:S(2)}) collective-permute-start(bf16[1,128,512]{2,1,0:T(8,128)(2,1)S(1)} %add_convert_fusion.12), channel_id=1, source_target_pairs={{0,8},{1,9},{2,10},{3,11},{4,12},{5,13},{6,14},{7,15},{8,0},{9,1},... | collective-permute-start | bytes 393224 | tf_op jit(solution)/shard_map/ppermute | solution.py:428
  150.6 16.1 %collective-permute-start.30 = (bf16[3,64,512]{2,1,0:T(8,128)(2,1)S(1)}, bf16[3,64,512]{2,1,0:T(8,128)(2,1)S(1)}, u32[]{:S(2)}, u32[]{:S(2)}) collective-permute-start(bf16[3,64,512]{2,1,0:T(8,128)(2,1)S(1)} %add_convert_fusion.7), channel_id=1, source_target_pairs={{0,8},{1,9},{2,10},{3,11},{4,12},{5,13},{6,14},{7,15},{8,0},{9,1},... | collective-permute-start | bytes 589832 | tf_op jit(solution)/shard_map/ppermute | solution.py:428
  162.7 5.0 %collective-permute-start.27 = (bf16[1,128,512]{2,1,0:T(8,128)(2,1)S(1)}, bf16[1,128,512]{2,1,0:T(8,128)(2,1)S(1)}, u32[]{:S(2)}, u32[]{:S(2)}) collective-permute-start(bf16[1,128,512]{2,1,0:T(8,128)(2,1)S(1)} %multiply_convert_fusion.2), channel_id=1, source_target_pairs={{0,16},{1,3},{2,18},{3,1},{4,20},{5,7},{6,22},{7,5},{8,24},{9,11},... | collective-permute-start | bytes 393224 | tf_op jit(solution)/shard_map/ppermute | solution.py:428
  166.8 5.7 %collective-permute-start.31 = (bf16[3,64,512]{2,1,0:T(8,128)(2,1)S(1)}, bf16[3,64,512]{2,1,0:T(8,128)(2,1)S(1)}, u32[]{:S(2)}, u32[]{:S(2)}) collective-permute-start(bf16[3,64,512]{2,1,0:T(8,128)(2,1)S(1)} %multiply_convert_fusion), channel_id=1, source_target_pairs={{0,2},{1,17},{2,0},{3,19},{4,6},{5,21},{6,4},{7,23},{8,10},{9,25},... | collective-permute-start | bytes 589832 | tf_op jit(solution)/shard_map/ppermute | solution.py:428
  169.2 15.7 %collective-permute-start.28 = (bf16[6,256,512]{2,1,0:T(8,128)(2,1)S(1)}, bf16[6,256,512]{2,1,0:T(8,128)(2,1)}, u32[]{:S(2)}, u32[]{:S(2)}) collective-permute-start(bf16[6,256,512]{2,1,0:T(8,128)(2,1)S(1)} %pad_maximum_fusion.refs_3_), channel_id=1, source_target_pairs={{0,1},{1,0},{2,3},{3,2},{4,5},{5,4},{6,7},{7,6},{8,9},{9,8},{10,11... | collective-permute-start | bytes 4718600 | tf_op jit(solution)/shard_map/ppermute | solution.py:428
  172.6 7.8 %collective-permute-start.32 = (bf16[3,128,512]{2,1,0:T(8,128)(2,1)S(1)}, bf16[3,128,512]{2,1,0:T(8,128)(2,1)S(1)}, u32[]{:S(2)}, u32[]{:S(2)}) collective-permute-start(bf16[3,128,512]{2,1,0:T(8,128)(2,1)S(1)} %pad_maximum_fusion.4), channel_id=1, source_target_pairs={{0,16},{1,3},{2,18},{3,1},{4,20},{5,7},{6,22},{7,5},{8,24},{9,11},... | collective-permute-start | bytes 1179656 | tf_op jit(solution)/shard_map/ppermute | solution.py:428
  180.5 4.4 %copy-start.2 = (bf16[3,256,512]{2,1,0:T(8,128)(2,1)}, bf16[3,256,512]{2,1,0:T(8,128)(2,1)S(1)}, u32[]{:S(2)}) copy-start(bf16[3,256,512]{2,1,0:T(8,128)(2,1)S(1)} %pad_maximum_fusion.2.refs_5_) | copy-start | bytes 2359300
  180.5 2.7 %collective-permute-start.33 = (bf16[3,256,512]{2,1,0:T(8,128)(2,1)S(1)}, bf16[3,256,512]{2,1,0:T(8,128)(2,1)S(1)}, u32[]{:S(2)}, u32[]{:S(2)}) collective-permute-start(bf16[3,256,512]{2,1,0:T(8,128)(2,1)S(1)} %pad_maximum_fusion.2.refs_5_), channel_id=1, source_target_pairs={{0,1},{1,0},{2,3},{3,2},{4,5},{5,4},{6,7},{7,6},{8,9},{9,8},{10,11... | collective-permute-start | bytes 2359304 | tf_op jit(solution)/shard_map/ppermute | solution.py:428
  180.6 2.6 %collective-permute-start.34 = (bf16[1,256,512]{2,1,0:T(8,128)(2,1)S(1)}, bf16[1,256,512]{2,1,0:T(8,128)(2,1)S(1)}, u32[]{:S(2)}, u32[]{:S(2)}) collective-permute-start(bf16[1,256,512]{2,1,0:T(8,128)(2,1)S(1)} %pad_maximum_fusion.5.refs_7_), channel_id=1, source_target_pairs={{0,1},{1,0},{2,3},{3,2},{4,5},{5,4},{6,7},{7,6},{8,9},{9,8},{10,11... | collective-permute-start | bytes 786440 | tf_op jit(solution)/shard_map/ppermute | solution.py:428
  (8 other events, 10.3 us)
